TPU v7x, 512 devices: a whole 4x8x8 slice. The times are simulated.
512 devices in a mesh: gx: 8 (over z), gy: 64 (over y, x, core).
Axes of the slice: x: 4, y: 8, z: 8, core: 2. Of those that a mesh axis runs over, the one named last changes fastest.
Arguments:
- level_set: float32 [64, 2048, 128], P('gx', 'gy'), may hold values from -3 to 3
- velocity: float32 [3, 64, 2048, 128], P(None, 'gx', 'gy'), may hold values from -5 to 5
- source: float32 [64, 2048, 128], P('gx', 'gy'), may hold values from -6 to 6
- wick_solid: int32 [8, 256, 16], P('gx', 'gy'), may hold values 0 or 1
Outputs:
- level_new: float32 [64, 2048, 128], P('gx', 'gy')
- pressure: float32 [64, 2048, 128], P('gx', 'gy')
All inputs are finite; a program needn't handle non-finite values. No bound on the sum of `wick_solid` on one device may be relied on, other than what follows from the above.
Results may differ from a plain program's by a relative error of at most 0.00055.
Values sent between devices are 32-bit elements; how exact they have to be, the bound alone decides.
No kernel may reach another device: no remote copies, remote signals or barrier semaphores. Data moves between devices by JAX's collectives and lax.ppermute only.
A program may use at most 64 MiB of HBM per device.

v0:
```python
import jax
import jax.numpy as jnp
import numpy as np
from jax import lax
from jax.sharding import PartitionSpec as P

EZ = 1
EY = 4
EX = 16
ITERS = 2


TIME_STEP = 0.02
HELM_COEF = 0.25
LEVEL_WIDTH = 0.25
GAS_RATIO = 10.0
SOLID_FACTOR = 0.25
SCHWARZ_SCALE = 0.5
SCHWARZ_SHIFT = 0.05


def extended(block, sides, width):
    for axis, dim in sides:
        count = lax.axis_size(axis)
        forward = [(i, i + 1) for i in range(count - 1)]
        backward = [(target, source) for source, target in forward]
        low = lax.ppermute(
            lax.slice_in_dim(block, block.shape[dim] - width, None, axis=dim), axis, forward
        )
        high = lax.ppermute(lax.slice_in_dim(block, 0, width, axis=dim), axis, backward)
        block = jnp.concatenate([low, block, high], axis=dim)
    return block


def gll_tables():
    gll_nodes = np.array(
        [
            -1.0,
            -0.8717401485096066,
            -0.5917001814331423,
            -0.2092992179024789,
            0.2092992179024789,
            0.5917001814331423,
            0.8717401485096066,
            1.0,
        ]
    )
    weight_np = np.array(
        [
            1.0 / 28.0,
            0.21070422714350603,
            0.3411226924835044,
            0.4124587946587038,
            0.4124587946587038,
            0.3411226924835044,
            0.21070422714350603,
            1.0 / 28.0,
        ]
    )
    bary_weights = np.array(
        [1.0 / np.prod([gll_nodes[i] - gll_nodes[j] for j in range(8) if j != i]) for i in range(8)]
    )
    derivative = np.zeros((8, 8))
    for i in range(8):
        for j in range(8):
            if i != j:
                derivative[i, j] = bary_weights[j] / bary_weights[i] / (gll_nodes[i] - gll_nodes[j])
        derivative[i, i] = -np.sum(derivative[i])
    return (weight_np, derivative)


def sine_tables():
    indices = np.arange(10) + 1.0
    sine_basis = np.sqrt(2.0 / 11.0) * np.sin(np.pi * np.outer(indices, indices) / 11.0)
    eigen_vals = 2.0 - 2.0 * np.cos(np.pi * indices / 11.0)
    return (sine_basis, eigen_vals)


def apply_blocks(values, matrix, axis_id):
    block_size = matrix.shape[0]
    dim_shape = values.shape
    if axis_id == 2:
        big_table = jnp.kron(jnp.eye(dim_shape[2] // block_size, dtype=jnp.float32), matrix.T)
        return jnp.dot(values, big_table, precision=lax.Precision.HIGHEST)
    if axis_id == 0:
        parted = values.reshape(dim_shape[0] // block_size, block_size, dim_shape[1], dim_shape[2])
        return jnp.einsum("ij,ajyx->aiyx", matrix, parted, precision=lax.Precision.HIGHEST).reshape(
            dim_shape
        )
    parted = values.reshape(dim_shape[0], dim_shape[1] // block_size, block_size, dim_shape[2])
    return jnp.einsum("ij,zajx->zaix", matrix, parted, precision=lax.Precision.HIGHEST).reshape(
        dim_shape
    )


def node_weights(weight_np, grid_shape):
    weight_row = jnp.asarray(weight_np, dtype=jnp.float32)
    along_z = jnp.tile(weight_row, grid_shape[0] // 8)
    along_y = jnp.tile(weight_row, grid_shape[1] // 8)
    along_x = jnp.tile(weight_row, grid_shape[2] // 8)
    return along_z[:, None, None] * along_y[None, :, None] * along_x[None, None, :]


def axis_count(length, start, total):
    position = jnp.arange(length) + start
    node_pos = jnp.arange(length) % 8
    inner_lo = jnp.logical_and(node_pos == 0, position > 0).astype(jnp.float32)
    inner_hi = jnp.logical_and(node_pos == 7, position < total - 1).astype(jnp.float32)
    return 1.0 + inner_lo + inner_hi


def fold_axis(padded, axis_id):
    length = padded.shape[axis_id] - 2
    node_pos = jnp.arange(length) % 8
    mask_shape = [1, 1, 1]
    mask_shape[axis_id] = length
    first_mask = (node_pos == 0).astype(jnp.float32).reshape(mask_shape)
    last_mask = (node_pos == 7).astype(jnp.float32).reshape(mask_shape)
    middle = lax.slice_in_dim(padded, 1, length + 1, axis=axis_id)
    lower_rim = lax.slice_in_dim(padded, 0, length, axis=axis_id)
    upper_rim = lax.slice_in_dim(padded, 2, length + 2, axis=axis_id)
    return middle + first_mask * lower_rim + last_mask * upper_rim


def fold_all(padded):
    summed = fold_axis(padded, 1)
    summed = fold_axis(summed, 0)
    summed = jnp.pad(summed, ((0, 0), (0, 0), (1, 1)))
    return fold_axis(summed, 2)


def extend_axis(padded, axis_id):
    length = padded.shape[axis_id] - 4
    blocks = length // 8
    dim_shape = list(padded.shape)
    part_shape = dim_shape[:axis_id] + [blocks, 8] + dim_shape[axis_id + 1 :]
    center_part = lax.slice_in_dim(padded, 2, length + 2, axis=axis_id).reshape(part_shape)
    lower_part = lax.slice_in_dim(padded, 0, length, axis=axis_id).reshape(part_shape)
    upper_part = lax.slice_in_dim(padded, 4, length + 4, axis=axis_id).reshape(part_shape)
    lower_rim = lax.slice_in_dim(lower_part, 0, 1, axis=axis_id + 1)
    upper_rim = lax.slice_in_dim(upper_part, 7, 8, axis=axis_id + 1)
    joined = jnp.concatenate([lower_rim, center_part, upper_rim], axis=axis_id + 1)
    return joined.reshape(dim_shape[:axis_id] + [blocks * 10] + dim_shape[axis_id + 1 :])


def extend_all(padded):
    widened = extend_axis(padded, 1)
    widened = extend_axis(widened, 0)
    widened = jnp.pad(widened, ((0, 0), (0, 0), (2, 2)))
    return extend_axis(widened, 2)


def inner_axis(values, axis_id):
    dim_shape = list(values.shape)
    blocks = dim_shape[axis_id] // 10
    parted = values.reshape(dim_shape[:axis_id] + [blocks, 10] + dim_shape[axis_id + 1 :])
    kept_nodes = lax.slice_in_dim(parted, 1, 9, axis=axis_id + 1)
    return kept_nodes.reshape(dim_shape[:axis_id] + [blocks * 8] + dim_shape[axis_id + 1 :])


def schwarz_solve(widened, sine_basis, eigen_vals):
    spectral = apply_blocks(
        apply_blocks(apply_blocks(widened, sine_basis, 0), sine_basis, 1), sine_basis, 2
    )
    lam_z = jnp.tile(eigen_vals, widened.shape[0] // 10)
    lam_y = jnp.tile(eigen_vals, widened.shape[1] // 10)
    lam_x = jnp.tile(eigen_vals, widened.shape[2] // 10)
    denominator = (
        SCHWARZ_SCALE * (lam_z[:, None, None] + lam_y[None, :, None] + lam_x[None, None, :])
        + SCHWARZ_SHIFT
    )
    spectral = spectral / denominator
    restored = apply_blocks(
        apply_blocks(apply_blocks(spectral, sine_basis, 0), sine_basis, 1), sine_basis, 2
    )
    return inner_axis(inner_axis(inner_axis(restored, 0), 1), 2)


def coarse_matrix(kbar):
    rows_gx, rows_gy = kbar.shape
    along_z = 2.0 * kbar[:-1] * kbar[1:] / (kbar[:-1] + kbar[1:]) * (EY * EX / EZ)
    along_y = 2.0 * kbar[:, :-1] * kbar[:, 1:] / (kbar[:, :-1] + kbar[:, 1:]) * (EZ * EX / EY)
    diagonal = (
        HELM_COEF * EZ * EY * EX
        + jnp.pad(along_z, ((1, 0), (0, 0)))
        + jnp.pad(along_z, ((0, 1), (0, 0)))
    )
    diagonal = diagonal + jnp.pad(along_y, ((0, 0), (1, 0))) + jnp.pad(along_y, ((0, 0), (0, 1)))
    total = rows_gx * rows_gy
    z_links = jnp.pad(along_z, ((0, 1), (0, 0))).reshape(total)[: total - rows_gy]
    y_links = jnp.pad(along_y, ((0, 0), (0, 1))).reshape(total)[: total - 1]
    matrix = (
        jnp.diag(diagonal.reshape(total)) - jnp.diag(z_links, rows_gy) - jnp.diag(z_links, -rows_gy)
    )
    return matrix - jnp.diag(y_links, 1) - jnp.diag(y_links, -1)


def chol_solve(factor, rhs_vec):
    column = rhs_vec.reshape(-1, 1)
    middle = lax.linalg.triangular_solve(factor, column, left_side=True, lower=True)
    return lax.linalg.triangular_solve(
        factor, middle, left_side=True, lower=True, transpose_a=True
    ).reshape(-1)


def pad_one(values):
    slabs = extended(values, (("gx", 0),), 1)
    return extended(slabs, (("gy", 1),), 1)


def pad_two(values):
    slabs = extended(values, (("gx", 0),), 2)
    return extended(slabs, (("gy", 1),), 2)


def body(level_set, velocity, source, wick_solid):
    weight_np, deriv_np = gll_tables()
    deriv = jnp.asarray(deriv_np, dtype=jnp.float32)
    deriv_t = jnp.asarray(deriv_np.T, dtype=jnp.float32)
    basis_np, eigen_np = sine_tables()
    sine_basis = jnp.asarray(basis_np, dtype=jnp.float32)
    eigen_vals = jnp.asarray(eigen_np, dtype=jnp.float32)
    grid_shape = level_set.shape
    count_gx = lax.axis_size("gx")
    count_gy = lax.axis_size("gy")
    index_gx = lax.axis_index("gx")
    index_gy = lax.axis_index("gy")
    node_w = node_weights(weight_np, grid_shape)
    mass_w = 0.125 * node_w
    mult_z = axis_count(grid_shape[0], index_gx * grid_shape[0], grid_shape[0] * count_gx)
    mult_y = axis_count(grid_shape[1], index_gy * grid_shape[1], grid_shape[1] * count_gy)
    mult_x = axis_count(grid_shape[2], 0, grid_shape[2])
    mult = mult_z[:, None, None] * mult_y[None, :, None] * mult_x[None, None, :]
    inv_mult = 1.0 / mult
    own_index = index_gx * count_gy + index_gy

    def assemble(values):
        return fold_all(pad_one(values))

    advect = velocity[0] * 2.0 * apply_blocks(level_set, deriv, 0)
    advect = advect + velocity[1] * 2.0 * apply_blocks(level_set, deriv, 1)
    advect = advect + velocity[2] * 2.0 * apply_blocks(level_set, deriv, 2)
    moved = level_set - TIME_STEP * advect
    diverge = 2.0 * (
        apply_blocks(velocity[0], deriv, 0)
        + apply_blocks(velocity[1], deriv, 1)
        + apply_blocks(velocity[2], deriv, 2)
    )
    level_term = mass_w * moved
    rhs_term = mass_w * (source - TIME_STEP * diverge)
    level_sum = assemble(level_term)
    rhs = assemble(rhs_term)
    level_new = level_sum / (mass_w * mult)
    heavi = jax.nn.sigmoid(level_new / LEVEL_WIDTH)
    solid_pts = jnp.repeat(
        jnp.repeat(jnp.repeat(wick_solid, 8, axis=0), 8, axis=1), 8, axis=2
    ).astype(jnp.float32)
    coef = (GAS_RATIO - (GAS_RATIO - 1.0) * heavi) * (1.0 - (1.0 - SOLID_FACTOR) * solid_pts)
    flux_w = 0.5 * coef * node_w
    means = lax.all_gather(jnp.reshape(jnp.mean(coef), (1,)), ("gx", "gy"), axis=0, tiled=True)
    factor = jnp.linalg.cholesky(coarse_matrix(means.reshape(count_gx, count_gy)))

    def coarse_value(residual):
        partial_total = jnp.sum(residual * inv_mult)
        everyone = lax.all_gather(
            jnp.reshape(partial_total, (1,)), ("gx", "gy"), axis=0, tiled=True
        )
        solved = chol_solve(factor, everyone)
        return lax.dynamic_index_in_dim(solved, own_index, keepdims=False)

    def precond(residual):
        widened = extend_all(pad_two(residual))
        local = schwarz_solve(widened, sine_basis, eigen_vals)
        coarse_now = coarse_value(residual)
        return assemble(inv_mult * (local + coarse_now))

    def inner(left, right):
        return lax.psum(jnp.sum(left * right * inv_mult), ("gx", "gy"))

    pressure = jnp.zeros_like(rhs)
    residual = rhs
    precon = precond(residual)
    rz_now = inner(residual, precon)
    search = precon
    for sweep_id in range(ITERS):
        result = HELM_COEF * mass_w * search
        for axis_id in range(3):
            result = result + apply_blocks(
                flux_w * apply_blocks(search, deriv, axis_id), deriv_t, axis_id
            )
        applied = assemble(result)
        step_len = rz_now / inner(search, applied)
        pressure = pressure + step_len * search
        residual = residual - step_len * applied
        if sweep_id + 1 < ITERS:
            precon = precond(residual)
            rz_next = inner(residual, precon)
            search = precon + rz_next / rz_now * search
            rz_now = rz_next
    return (level_new, pressure)


def solution(mesh):
    placed = (
        P("gx", "gy", None),
        P(None, "gx", "gy", None),
        P("gx", "gy", None),
        P("gx", "gy", None),
    )
    return jax.shard_map(
        body,
        mesh=mesh,
        in_specs=placed,
        out_specs=(P("gx", "gy", None), P("gx", "gy", None)),
        check_vma=False,
    )
```

profile of v0, /device:TPU:1, one launch (start us, length us, event | category | flops | bytes accessed | tf_op | source)
XLA Modules:
  0.0 855.2 jit_solution(1053228595222556291)
XLA Ops:
  7.7 5.5 collective-permute-start.4
  15.7 4.6 collective-permute-start
  23.6 7.8 collective-permute-start.7
  31.4 1.9 collective-permute-start.6
  33.4 2.4 collective-permute-start.3
  35.8 3.2 collective-permute-start.2
  43.3 104.5 %all-reduce.20 = (f32[512]{0:T(512)S(1)}, f32[512]{0:T(512)S(1)}) all-reduce(f32[512]{0:T(512)S(1)} %dynamic-update-slice.27, f32[512]{0:T(512)S(1)} %dynamic-update-slice.28), channel_id=1, replica_groups=mesh['gx'=8,'gy'=64] {'gx','gy'}, use_global_device_ids=true, to_apply=%add.16 | all-reduce | flops 1024 | bytes 8192
  149.2 4.3 collective-permute-start.8
  155.3 11.7 %cholesky.103 = f32[128,128]{1,0:T(8,128)S(1)} custom-call(f32[128,128]{1,0:T(8,128)S(1)} %cholesky.263), custom_call_target="Cholesky" | custom-call | tf_op jit(solution)/shard_map/jit(cholesky)/cholesky | solution.py:261
  167.2 9.8 %custom-call.33 = f32[1,128,128]{1,2,0:T(8,128)S(1)} custom-call(f32[1,128,128]{2,1,0:T(8,128)S(1)} %get-tuple-element.127), custom_call_target="InvertDiagBlocksLowerTriangular" | custom-call | tf_op jit(solution)/shard_map/jit(cholesky)/cholesky | solution.py:261
  177.7 11.7 %cholesky.215 = f32[128,128]{1,0:T(8,128)S(1)} custom-call(f32[128,128]{1,0:T(8,128)S(1)} %cholesky.267), custom_call_target="Cholesky" | custom-call | tf_op jit(solution)/shard_map/jit(cholesky)/cholesky | solution.py:261
  189.4 10.4 %custom-call.34 = f32[1,128,128]{1,2,0:T(8,128)S(1)} custom-call(f32[1,128,128]{2,1,0:T(8,128)S(1)} %get-tuple-element.124), custom_call_target="InvertDiagBlocksLowerTriangular" | custom-call | tf_op jit(solution)/shard_map/jit(cholesky)/cholesky | solution.py:261
  200.5 11.7 %cholesky.236 = f32[128,128]{1,0:T(8,128)S(1)} custom-call(f32[128,128]{1,0:T(8,128)S(1)} %cholesky.272), custom_call_target="Cholesky" | custom-call | tf_op jit(solution)/shard_map/jit(cholesky)/cholesky | solution.py:261
  212.2 9.8 %custom-call.35 = f32[1,128,128]{1,2,0:T(8,128)S(1)} custom-call(f32[1,128,128]{2,1,0:T(8,128)S(1)} %get-tuple-element.121), custom_call_target="InvertDiagBlocksLowerTriangular" | custom-call | tf_op jit(solution)/shard_map/jit(cholesky)/cholesky | solution.py:261
  222.7 11.9 %cholesky.253 = f32[128,128]{1,0:T(8,128)S(1)} custom-call(f32[128,128]{1,0:T(8,128)S(1)} %convolution_subtract_fusion.2), custom_call_target="Cholesky" | custom-call | tf_op jit(solution)/shard_map/jit(cholesky)/cholesky | solution.py:261
  240.0 8.3 while.8
  248.3 39.3 %custom-call.39 = f32[4,128,128]{1,2,0:T(8,128)S(1)} custom-call(f32[4,128,128]{2,1,0:T(8,128)S(1)} %get-tuple-element.33), custom_call_target="InvertDiagBlocksLowerTriangular" | custom-call | tf_op jit(solution)/shard_map/triangular_solve/custom-call.8 | solution.py:201
  290.5 4.8 collective-permute-start.10
  295.3 1.9 collective-permute-start.11
  309.1 2.1 copy.157
  311.2 1.8 slice.785
  318.3 1.9 copy.158
  325.1 2.5 reshape.970
  327.6 2.2 slice.788
  329.8 1.8 copy.209
  331.7 1.8 add_bitcast_fusion.1
  335.2 4.1 collective-permute-start.12
  340.3 1.9 collective-permute-start.15
  342.2 5.2 collective-permute-start.14
  351.7 4.5 collective-permute-start.16
  357.2 1.9 collective-permute-start.19
  359.1 4.9 collective-permute-start.18
  365.9 108.4 %all-reduce.19 = (f32[]{:T(128)}, f32[]{:T(128)}) all-reduce(f32[]{:T(128)} %get-tuple-element.45, f32[]{:T(128)} %get-tuple-element.44), channel_id=1, replica_groups=mesh['gx'=8,'gy'=64] {'gx','gy'}, use_global_device_ids=true, to_apply=%region_11.14 | all-reduce | flops 2 | bytes 16 | tf_op jit(solution)/shard_map/psum | solution.py:278
  477.6 4.0 collective-permute-start.20
  482.4 96.5 %all-reduce.18 = f32[512]{0:T(512)S(1)} all-reduce(f32[512]{0:T(512)S(1)} %dynamic-update-slice.29), channel_id=1, replica_groups=mesh['gx'=8,'gy'=64] {'gx','gy'}, use_global_device_ids=true, to_apply=%add.18 | all-reduce | flops 512 | bytes 4096
  581.7 3.4 collective-permute-start.22
  585.1 1.9 collective-permute-start.23
  595.0 2.1 copy.178
  606.4 2.5 reshape.974
  609.0 2.2 slice.832
  614.6 4.0 collective-permute-start.24
  619.5 1.9 collective-permute-start.27
  621.5 4.9 collective-permute-start.26
  628.2 104.3 %psum.30 = f32[]{:T(128)} all-reduce(f32[]{:T(128)} %get-tuple-element.58), channel_id=1, replica_groups=mesh['gx'=8,'gy'=64] {'gx','gy'}, use_global_device_ids=true, to_apply=%region_16.19 | all-reduce | flops 1 | bytes 8 | tf_op jit(solution)/shard_map/psum | solution.py:278
  737.3 4.7 collective-permute-start.28
  742.9 3.4 collective-permute-start.31
  746.3 3.6 collective-permute-start.30
  752.4 100.6 %psum.31 = f32[]{:T(128)} all-reduce(f32[]{:T(128)} %fusion.97), channel_id=1, replica_groups=mesh['gx'=8,'gy'=64] {'gx','gy'}, use_global_device_ids=true, to_apply=%region_18.21 | all-reduce | flops 1 | bytes 8 | tf_op jit(solution)/shard_map/psum | solution.py:278
  (426 shorter events, 102.5 us)
Async XLA Ops:
  5.6 34.4 %copy-start.24 = (f32[128]{0:T(128)}, f32[128]{0:T(128)S(1)}, u32[]{:S(2)}) copy-start(f32[128]{0:T(128)S(1)} %mul.719) | copy-start | bytes 1540
  5.7 34.4 %copy-start.7 = (f32[8,32]{0,1:T(8,128)}, f32[8,32]{0,1:T(8,128)S(1)}, u32[]{:S(2)}) copy-start(f32[8,32]{0,1:T(8,128)S(1)} %get-tuple-element.150) | copy-start | bytes 3076
  6.4 17.1 %collective-permute-start.5 = (f32[1,32,128]{2,0,1:T(1,128)S(1)}, f32[1,32,128]{2,0,1:T(1,128)S(1)}, u32[]{:S(2)}, u32[]{:S(2)}) collective-permute-start(f32[1,32,128]{2,0,1:T(1,128)S(1)} %get-tuple-element.115), channel_id=1, source_target_pairs={{64,0},{128,64},{192,128},{256,192},{320,256},{384,320},{448,384},... | collective-permute-start | bytes 49160 | tf_op jit(solution)/shard_map/ppermute | solution.py:30
  7.7 15.8 %collective-permute-start.4 = (f32[1,32,128]{2,0,1:T(1,128)S(1)}, f32[1,32,128]{2,0,1:T(1,128)S(1)}, u32[]{:S(2)}, u32[]{:S(2)}) collective-permute-start(f32[1,32,128]{2,0,1:T(1,128)S(1)} %get-tuple-element.114), channel_id=1, source_target_pairs={{0,64},{64,128},{128,192},{192,256},{256,320},{320,384},{384,448},... | collective-permute-start | bytes 49160 | tf_op jit(solution)/shard_map/ppermute | solution.py:27
  14.4 18.9 %collective-permute-start.1 = (f32[1,32,128]{2,0,1:T(1,128)S(1)}, f32[1,32,128]{2,0,1:T(1,128)S(1)}, u32[]{:S(2)}, u32[]{:S(2)}) collective-permute-start(f32[1,32,128]{2,0,1:T(1,128)S(1)} %get-tuple-element.117), channel_id=1, source_target_pairs={{64,0},{128,64},{192,128},{256,192},{320,256},{384,320},{448,384},... | collective-permute-start | bytes 49160 | tf_op jit(solution)/shard_map/ppermute | solution.py:30
  15.7 17.6 %collective-permute-start = (f32[1,32,128]{2,0,1:T(1,128)S(1)}, f32[1,32,128]{2,0,1:T(1,128)S(1)}, u32[]{:S(2)}, u32[]{:S(2)}) collective-permute-start(f32[1,32,128]{2,0,1:T(1,128)S(1)} %get-tuple-element.116), channel_id=1, source_target_pairs={{0,64},{64,128},{128,192},{192,256},{256,320},{320,384},{384,448},... | collective-permute-start | bytes 49160 | tf_op jit(solution)/shard_map/ppermute | solution.py:27
  20.4 19.7 %copy-start.33 = (f32[128]{0:T(128)}, f32[128]{0:T(128)S(1)}, u32[]{:S(2)}) copy-start(f32[128]{0:T(128)S(1)} %fusion.172) | copy-start | bytes 1540
  20.4 19.7 %copy-start.27 = (f32[128]{0:T(128)}, f32[128]{0:T(128)S(1)}, u32[]{:S(2)}) copy-start(f32[128]{0:T(128)S(1)} %get-tuple-element.143) | copy-start | bytes 1540
  20.4 19.7 %copy-start.30 = (f32[128]{0:T(128)}, f32[128]{0:T(128)S(1)}, u32[]{:S(2)}) copy-start(f32[128]{0:T(128)S(1)} %get-tuple-element.144) | copy-start | bytes 1540
  20.4 19.4 %copy-start.36 = (f32[32]{0:T(128)}, f32[32]{0:T(128)S(1)}, u32[]{:S(2)}) copy-start(f32[32]{0:T(128)S(1)} %get-tuple-element.147) | copy-start | bytes 388
  20.4 19.4 %copy-start.39 = (f32[32]{0:T(128)}, f32[32]{0:T(128)S(1)}, u32[]{:S(2)}) copy-start(f32[32]{0:T(128)S(1)} %get-tuple-element.148) | copy-start | bytes 388
  20.4 19.5 %copy-start.49 = (f32[8]{0:T(128)}, f32[8]{0:T(128)S(1)}, u32[]{:S(2)}) copy-start(f32[8]{0:T(128)S(1)} %get-tuple-element.145) | copy-start | bytes 100
  20.5 19.5 %copy-start.52 = (f32[8]{0:T(128)}, f32[8]{0:T(128)S(1)}, u32[]{:S(2)}) copy-start(f32[8]{0:T(128)S(1)} %get-tuple-element.146) | copy-start | bytes 100
  21.6 18.5 %copy-start.13 = (f32[32,128]{1,0:T(8,128)}, f32[32,128]{1,0:T(8,128)S(1)}, u32[]{:S(2)}) copy-start(f32[32,128]{1,0:T(8,128)S(1)} %copy.166) | copy-start | bytes 49156
  23.6 15.4 %collective-permute-start.7 = (f32[10,1,128]{2,0,1:T(8,128)S(1)}, f32[10,1,128]{2,0,1:T(8,128)S(1)}, u32[]{:S(2)}, u32[]{:S(2)}) collective-permute-start(f32[10,1,128]{2,0,1:T(8,128)S(1)} %get-tuple-element.95), channel_id=1, source_target_pairs={{1,0},{2,1},{3,2},{4,3},{5,4},{6,5},{7,6},{8,7},{9,8},{10,9},{11,1... | collective-permute-start | bytes 15368 | tf_op jit(solution)/shard_map/ppermute | solution.py:30
  31.4 7.6 collective-permute-start.6
  33.4 5.8 collective-permute-start.3
  35.8 3.9 collective-permute-start.2
  39.0 115.0 %copy-start.65 = (pred[512]{0:T(512)(128)(4,1)S(1)}, pred[512]{0:T(512)(128)(4,1)}, u32[]{:S(2)}) copy-start(pred[512]{0:T(512)(128)(4,1)} %constant.333.clone.1) | copy-start | bytes 1540
  147.9 142.4 %collective-permute-start.9 = (f32[2,32,128]{2,0,1:T(2,128)S(1)}, f32[2,32,128]{2,0,1:T(2,128)S(1)}, u32[]{:S(2)}, u32[]{:S(2)}) collective-permute-start(f32[2,32,128]{2,0,1:T(2,128)S(1)} %get-tuple-element.113), channel_id=1, source_target_pairs={{64,0},{128,64},{192,128},{256,192},{320,256},{384,320},{448,384},... | collective-permute-start | bytes 98312 | tf_op jit(solution)/shard_map/ppermute | solution.py:30
  149.2 141.2 %collective-permute-start.8 = (f32[2,32,128]{2,0,1:T(2,128)S(1)}, f32[2,32,128]{2,0,1:T(2,128)S(1)}, u32[]{:S(2)}, u32[]{:S(2)}) collective-permute-start(f32[2,32,128]{2,0,1:T(2,128)S(1)} %get-tuple-element.112), channel_id=1, source_target_pairs={{0,64},{64,128},{128,192},{192,256},{256,320},{320,384},{384,448},... | collective-permute-start | bytes 98312 | tf_op jit(solution)/shard_map/ppermute | solution.py:27
  290.5 11.3 %collective-permute-start.10 = (f32[12,2,128]{2,0,1:T(8,128)S(1)}, f32[12,2,128]{2,0,1:T(8,128)S(1)}, u32[]{:S(2)}, u32[]{:S(2)}) collective-permute-start(f32[12,2,128]{2,0,1:T(8,128)S(1)} %get-tuple-element.92), channel_id=1, source_target_pairs={{0,1},{1,2},{2,3},{3,4},{4,5},{5,6},{6,7},{7,8},{8,9},{9,10},{10,1... | collective-permute-start | bytes 36872 | tf_op jit(solution)/shard_map/ppermute | solution.py:27
  295.3 6.4 collective-permute-start.11
  333.9 5.5 collective-permute-start.13
  335.2 5.0 collective-permute-start.12
  340.3 7.6 collective-permute-start.15
  342.2 5.7 collective-permute-start.14
  350.4 5.9 collective-permute-start.17
  351.7 5.4 collective-permute-start.16
  357.2 6.8 collective-permute-start.19
  359.1 5.6 collective-permute-start.18
  476.3 105.3 %collective-permute-start.21 = (f32[2,32,128]{2,0,1:T(2,128)S(1)}, f32[2,32,128]{2,0,1:T(2,128)S(1)}, u32[]{:S(2)}, u32[]{:S(2)}) collective-permute-start(f32[2,32,128]{2,0,1:T(2,128)S(1)} %get-tuple-element.107), channel_id=1, source_target_pairs={{64,0},{128,64},{192,128},{256,192},{320,256},{384,320},{448,384},... | collective-permute-start | bytes 98312 | tf_op jit(solution)/shard_map/ppermute | solution.py:30
  477.6 104.0 %collective-permute-start.20 = (f32[2,32,128]{2,0,1:T(2,128)S(1)}, f32[2,32,128]{2,0,1:T(2,128)S(1)}, u32[]{:S(2)}, u32[]{:S(2)}) collective-permute-start(f32[2,32,128]{2,0,1:T(2,128)S(1)} %get-tuple-element.106), channel_id=1, source_target_pairs={{0,64},{64,128},{128,192},{192,256},{256,320},{320,384},{384,448},... | collective-permute-start | bytes 98312 | tf_op jit(solution)/shard_map/ppermute | solution.py:27
  581.7 9.8 %collective-permute-start.22 = (f32[12,2,128]{2,0,1:T(8,128)S(1)}, f32[12,2,128]{2,0,1:T(8,128)S(1)}, u32[]{:S(2)}, u32[]{:S(2)}) collective-permute-start(f32[12,2,128]{2,0,1:T(8,128)S(1)} %get-tuple-element.86), channel_id=1, source_target_pairs={{0,1},{1,2},{2,3},{3,4},{4,5},{5,6},{6,7},{7,8},{8,9},{9,10},{10,1... | collective-permute-start | bytes 36872 | tf_op jit(solution)/shard_map/ppermute | solution.py:27
  585.1 6.4 collective-permute-start.23
  612.9 120.9 %copy-start.2 = (f32[8,32,128]{2,0,1:T(8,128)S(1)}, f32[8,32,128]{2,0,1:T(8,128)}, u32[]{:S(2)}) copy-start(f32[8,32,128]{2,0,1:T(8,128)} %copy-done.1) | copy-start | bytes 393220
  613.1 120.8 %copy-start.26 = (f32[128]{0:T(128)S(1)}, f32[128]{0:T(128)}, u32[]{:S(2)}) copy-start(f32[128]{0:T(128)} %copy-done.24) | copy-start | bytes 1540
  613.1 120.8 %copy-start.46 = (f32[8,8,1]{1,0,2:T(8,128)S(1)}, f32[8,8,1]{1,0,2:T(8,128)}, u32[]{:S(2)}) copy-start(f32[8,8,1]{1,0,2:T(8,128)} %constant.438) | copy-start | bytes 772
  613.3 5.3 collective-permute-start.25
  614.6 4.9 collective-permute-start.24
  619.5 6.8 collective-permute-start.27
  621.5 112.8 %copy-start.12 = (f32[128,128,1]{1,0,2:T(8,128)S(1)}, f32[128,128,1]{1,0,2:T(8,128)}, u32[]{:S(2)}) copy-start(f32[128,128,1]{1,0,2:T(8,128)} %copy-done.10) | copy-start | bytes 196612
  621.5 5.7 collective-permute-start.26
  627.4 107.1 %copy-start.23 = (f32[8,8,1,1]{1,0,3,2:T(8,128)S(1)}, f32[8,8,1,1]{1,0,3,2:T(8,128)}, u32[]{:S(2)}) copy-start(f32[8,8,1,1]{1,0,3,2:T(8,128)} %constant.439) | copy-start | bytes 772
  736.0 6.0 collective-permute-start.29
  737.3 5.6 collective-permute-start.28
  742.9 7.0 collective-permute-start.31
  746.3 4.4 collective-permute-start.30
  (50 other events, 373.0 us)
where the time goes:
time: 863 us; the launch traced here: 855 us
  blocking collectives  514 us (60%)
  other arithmetic  143 us (17%)
  starting transfers between devices  101 us (12%)
  local copies, waits for them, and re-layouts  57.1 us (7%)
  matrix products  22.6 us (3%)
  between operations  10.4 us (1%)
    psum x3, blocking collectives, inner(): return lax.psum(jnp.sum(left * right * inv_mult), ('gx', 'gy'))  313 us
    unnamed x2, blocking collectives  201 us
    another operation x15, other arithmetic, body(): jnp.linalg.cholesky(coarse_matrix(means.reshape(count_gx, count_gy)))  79.8 us
    ppermute x16, starting transfers between devices, extended(): lax.ppermute(lax.slice_in_dim(block, block.shape[dim] - width, None, axis...  67.5 us
    another operation x10, other arithmetic, chol_solve(): lax.linalg.triangular_solve(factor, middle, left_side=True, lower=True, t...  46.9 us
    ppermute x16, starting transfers between devices, extended(): lax.ppermute(lax.slice_in_dim(block, 0, width, axis=dim), axis, backward)  33.6 us
  transfers between devices with their start and end apart: 32, of which 8 were waited for; matrix products, arithmetic and copies ran while one was open for 18% of the time, Pallas kernels for 0%

commit v1 on v0

v1 whole, which is shorter than its diff:
```python
import functools

import jax
import jax.numpy as jnp
import numpy as np
from jax import lax
from jax.experimental import pallas as pl
from jax.experimental.pallas import tpu as pltpu
from jax.sharding import PartitionSpec as P

EZ = 1
EY = 4
EX = 16
ROWS = 8 * EY
LANES = 8 * EX

TIME_STEP = 0.02
HELM_COEF = 0.25
LEVEL_WIDTH = 0.25
GAS_RATIO = 10.0
SOLID_FACTOR = 0.25
SCHWARZ_SCALE = 0.5
SCHWARZ_SHIFT = 0.05

F32 = jnp.float32
BF16 = jnp.bfloat16
VMEM = pltpu.VMEM
SMEM = pltpu.SMEM
LIMIT = 24 * 1024 * 1024
PAIRS = ((0, 0), (0, 1), (0, 2), (1, 1), (1, 2), (2, 2))


def gll_tables():
    gll_nodes = np.array(
        [
            -1.0,
            -0.8717401485096066,
            -0.5917001814331423,
            -0.2092992179024789,
            0.2092992179024789,
            0.5917001814331423,
            0.8717401485096066,
            1.0,
        ]
    )
    weight_np = np.array(
        [
            1.0 / 28.0,
            0.21070422714350603,
            0.3411226924835044,
            0.4124587946587038,
            0.4124587946587038,
            0.3411226924835044,
            0.21070422714350603,
            1.0 / 28.0,
        ]
    )
    bary_weights = np.array(
        [1.0 / np.prod([gll_nodes[i] - gll_nodes[j] for j in range(8) if j != i]) for i in range(8)]
    )
    derivative = np.zeros((8, 8))
    for i in range(8):
        for j in range(8):
            if i != j:
                derivative[i, j] = bary_weights[j] / bary_weights[i] / (gll_nodes[i] - gll_nodes[j])
        derivative[i, i] = -np.sum(derivative[i])
    return (weight_np, derivative)


def sine_tables():
    indices = np.arange(10) + 1.0
    sine_basis = np.sqrt(2.0 / 11.0) * np.sin(np.pi * np.outer(indices, indices) / 11.0)
    eigen_vals = 2.0 - 2.0 * np.cos(np.pi * indices / 11.0)
    return (sine_basis, eigen_vals)


WEIGHT, DERIV = gll_tables()
SINE, EIGEN = sine_tables()


def split_const(matrix):
    single = matrix.astype(np.float32)
    high = single.astype(jnp.bfloat16)
    low = (single - high.astype(np.float32)).astype(jnp.bfloat16)
    return high, low


def line_maps(count):
    length = 8 * count
    total = length + 4

    def column(position):
        if 0 <= position < length:
            return position
        return {-2: length, -1: length + 1, length: length + 2, length + 1: length + 3}[position]

    assembled = {}
    for position in range(-2, length + 2):
        row = np.zeros(total)
        row[column(position)] = 1.0
        if 0 <= position < length:
            if position % 8 == 0:
                row[column(position - 1)] += 1.0
            if position % 8 == 7:
                row[column(position + 1)] += 1.0
        assembled[position] = row
    forward = np.zeros((10 * count, total))
    for element in range(count):
        places = [8 * element - 2] + list(range(8 * element, 8 * element + 8)) + [8 * element + 9]
        forward[10 * element : 10 * element + 10] = SINE @ np.stack([assembled[p] for p in places])
    backward = np.zeros((length, 10 * count))
    for element in range(count):
        backward[8 * element : 8 * element + 8, 10 * element : 10 * element + 10] = SINE[1:9]
    for element in range(count - 1):
        first, second = 8 * element + 7, 8 * element + 8
        mean = 0.5 * (backward[first] + backward[second])
        backward[first] = mean
        backward[second] = mean
    return forward, backward


FZ, BZ = line_maps(1)
FY, BY = line_maps(EY)
FY = np.pad(FY, ((0, 0), (0, 4)))
FX, BX = line_maps(EX)
FX = FX[:, :LANES]


def denominators():
    lam_y = np.tile(EIGEN, EY)
    lam_x = np.tile(EIGEN, EX)
    total = EIGEN[:, None, None] + lam_y[None, :, None] + lam_x[None, None, :]
    return (1.0 / (SCHWARZ_SCALE * total + SCHWARZ_SHIFT)).astype(np.float32)


INV_DEN = denominators()
DX_H, DX_L = split_const(np.kron(np.eye(EX), DERIV.T))
DXT_H, DXT_L = split_const(np.kron(np.eye(EX), DERIV))
FY_H, FY_L = split_const(FY)
BY_H, BY_L = split_const(BY)
FX_H, FX_L = split_const(FX.T.copy())
BX_H, BX_L = split_const(BX.T.copy())


def roll_table():
    table = np.zeros((2, 8, 8, LANES), np.float32)
    for kind, matrix in enumerate((DERIV, DERIV.T)):
        for k in range(8):
            for i in range(8):
                table[kind, k, i, :] = matrix[i, (i + k) % 8]
    return table


ROLLS = roll_table()
WY = np.tile(WEIGHT, EY)
WX = np.tile(WEIGHT, EX)
PLANE_W = (WY[:, None] * WX[None, :]).astype(np.float32)


def inner_count(count):
    mult = np.ones(8 * count)
    position = np.arange(8 * count)
    mult[(position % 8 == 0) & (position > 0)] += 1.0
    mult[(position % 8 == 7) & (position < 8 * count - 1)] += 1.0
    return mult


INV_MASS = (8.0 / (WY * inner_count(EY))[:, None] / (WX * inner_count(EX))[None, :]).astype(
    np.float32
)
SPREAD = np.kron(np.eye(EX), np.ones((1, 8))).astype(jnp.bfloat16)


def shape_functions(count, has_low, has_high):
    length = 8 * count
    pieces = np.zeros((3, length))
    pieces[1] = 1.0
    if has_low:
        pieces[0, 0] = 0.5
        pieces[1, 0] = 0.5
    if has_high:
        pieces[2, -1] = 0.5
        pieces[1, -1] = 0.5
    slopes = np.stack([np.kron(np.eye(count), DERIV) @ piece for piece in pieces])
    return pieces, slopes


CASES = ((False, True), (True, True), (True, False))


def z_table():
    table = np.zeros((3, 16, 8))
    for case, (low, high) in enumerate(CASES):
        pieces, slopes = shape_functions(1, low, high)
        for index, (first, second) in enumerate(PAIRS):
            table[case, index] = slopes[first] * slopes[second]
            table[case, 6 + index] = pieces[first] * pieces[second]
            mass = np.sum(WEIGHT * pieces[first] * pieces[second])
            table[case, 15, index] = HELM_COEF / 8.0 * np.sum(WX) * mass
        table[case, 12:15] = pieces
    return table.astype(np.float32)


def y_table():
    table = np.zeros((3, 3, ROWS, LANES))
    for case, (low, high) in enumerate(CASES):
        pieces, slopes = shape_functions(EY, low, high)
        for first in range(3):
            table[case, 2, :, first] = pieces[first]
            for second in range(3):
                table[case, 0, :, 3 * first + second] = pieces[first] * pieces[second]
                table[case, 1, :, 3 * first + second] = slopes[first] * slopes[second]
    return table.astype(np.float32)


Z_TABLE = z_table()
Y_TABLE = y_table()


def parts(values):
    high = values.astype(BF16)
    low = (values - high.astype(F32)).astype(BF16)
    return high, low


def dot(left, right):
    return jnp.dot(left, right, preferred_element_type=F32)


def left_table(table, values):
    high, low = parts(values)
    return dot(table[0][...], high) + dot(table[0][...], low) + dot(table[1][...], high)


def right_table(values, table):
    high, low = parts(values)
    return dot(high, table[0][...]) + dot(low, table[0][...]) + dot(high, table[1][...])


def along_z(values, matrix):
    rows = []
    for i in range(matrix.shape[0]):
        total = None
        for j in range(matrix.shape[1]):
            if matrix[i, j] == 0.0:
                continue
            term = float(matrix[i, j]) * values[j]
            total = term if total is None else total + term
        rows.append(total)
    return rows


def along_y(values, rolls, kind):
    grouped = values.reshape(8 * EY, 8, LANES)
    total = rolls[kind, 0][None] * grouped
    for k in range(1, 8):
        total = total + rolls[kind, k][None] * pltpu.roll(grouped, 8 - k, 1)
    return total.reshape(8, ROWS, LANES)


def along_x(values, table):
    return right_table(values.reshape(8 * ROWS, LANES), table).reshape(8, ROWS, LANES)


def stack(planes):
    return jnp.concatenate([plane[None] for plane in planes], axis=0)


def edge_rows(rows, low, high):
    position = lax.broadcasted_iota(jnp.int32, (rows, LANES), 0)
    return jnp.where(position == 0, low, jnp.where(position == rows - 1, high, 1.0))


def local_operator(values, flux, plane_w, rolls, dx, dxt):
    gz = along_z([values[i] for i in range(8)], DERIV)
    fz = along_z([flux[i] * gz[i] for i in range(8)], DERIV.T)
    total = along_y(flux * along_y(values, rolls, 0), rolls, 1)
    total = total + along_x(flux * along_x(values, dx), dxt)
    planes = [
        total[i] + fz[i] + (HELM_COEF * 0.125 * float(WEIGHT[i])) * (plane_w * values[i])
        for i in range(8)
    ]
    return stack(planes)


def add_faces(own, low_z, high_z, low_y, high_y):
    row = lax.broadcasted_iota(jnp.int32, (ROWS, LANES), 0)
    planes = []
    for i in range(8):
        plane = own[i]
        first = low_y[i : i + 1]
        last = high_y[i : i + 1]
        if i == 0:
            plane = plane + low_z
            first = first + low_y[8:9]
            last = last + high_y[8:9]
        if i == 7:
            plane = plane + high_z
            first = first + low_y[9:10]
            last = last + high_y[9:10]
        plane = plane + jnp.where(row == 0, first, jnp.where(row == ROWS - 1, last, 0.0))
        planes.append(plane)
    return stack(planes)


def schwarz(ext, tables, inv_den, near, out_ref, low_ref, high_ref):
    fy, fx, bx, by = tables
    spectral = along_z([ext[i] for i in range(12)], FZ)
    spectral = [left_table(fy, plane) for plane in spectral]
    wide = right_table(jnp.concatenate(spectral, axis=0), fx)
    wide = wide * inv_den[...].reshape(10 * 10 * EY, 10 * EX)
    back = right_table(wide, bx)
    step = 10 * EY
    back = [left_table(by, back[step * i : step * (i + 1)]) for i in range(10)]
    planes = along_z(back, BZ)
    edge = edge_rows(ROWS, near[2], near[3])
    planes = [plane * edge for plane in planes]
    planes[0] = planes[0] * near[0]
    planes[7] = planes[7] * near[1]
    for i in range(8):
        out_ref[i] = planes[i]
    low_ref[...] = planes[0]
    high_ref[...] = planes[7]


def fill_ext(ext, own, low_z, high_z, low_y, high_y):
    for i in range(8):
        ext[i, 0:ROWS] = own[i]
    for i in range(2):
        ext[8 + i, 0:ROWS] = low_z[i]
        ext[10 + i, 0:ROWS] = high_z[i]
    zeros = jnp.zeros((4, LANES), F32)
    for i in range(12):
        ext[i, ROWS : ROWS + 8] = jnp.concatenate(
            [low_y[2 * i : 2 * i + 2], high_y[2 * i : 2 * i + 2], zeros], axis=0
        )


def partition_total(ext, near):
    total = near[0] * ext[0] + near[1] * ext[7] + 0.5 * (ext[9] + ext[10])
    for i in range(1, 7):
        total = total + ext[i]
    row = lax.broadcasted_iota(jnp.int32, (ROWS + 8, LANES), 0)
    weight = jnp.where(row < ROWS, 1.0, 0.0)
    weight = jnp.where(row == 0, near[2], weight)
    weight = jnp.where(row == ROWS - 1, near[3], weight)
    weight = jnp.where((row == ROWS + 1) | (row == ROWS + 2), 0.5, weight)
    return jnp.sum(total * weight)


def lane_row(entries):
    lane = lax.broadcasted_iota(jnp.int32, (1, LANES), 1)
    row = jnp.zeros((1, LANES), F32)
    for index, value in enumerate(entries):
        row = jnp.where(lane == index, value, row)
    return row


def advect_kernel(lev, vel, src, plane_w, rolls, dxh, dxl, b_ref, l_ref, zlo, zhi):
    dx = (dxh, dxl)
    level = lev[...]
    v0, v1, v2 = vel[0], vel[1], vel[2]
    gz = stack(along_z([level[i] for i in range(8)], DERIV))
    advect = v0 * gz + v1 * along_y(level, rolls, 0) + v2 * along_x(level, dx)
    moved = level - (2.0 * TIME_STEP) * advect
    diverge = stack(along_z([v0[i] for i in range(8)], DERIV))
    diverge = diverge + along_y(v1, rolls, 0) + along_x(v2, dx)
    force = src[...] - (2.0 * TIME_STEP) * diverge
    weights = plane_w[...]
    for i in range(8):
        mass = (0.125 * float(WEIGHT[i])) * weights
        term = mass * force[i]
        moved_i = mass * moved[i]
        b_ref[i] = term
        l_ref[i] = moved_i
        if i < 2:
            zlo[i] = term
        if i == 0:
            zlo[2] = moved_i
        if i > 5:
            zhi[i - 6] = term
        if i == 7:
            zhi[2] = moved_i


def rim_kernel(kinds, *refs):
    count = len(kinds)
    own = refs[:count]
    low_z, high_z, low_y, high_y = refs[count:]
    at = 0
    for (width, start), array in zip(kinds, own, strict=True):
        for i in range(8):
            low_y[at : at + width] = array[i, 0:width]
            high_y[at : at + width] = array[i, ROWS - width : ROWS]
            at += width
        for planes in (low_z, high_z):
            for i in range(width):
                low_y[at : at + width] = planes[start + i, 0:width]
                high_y[at : at + width] = planes[start + i, ROWS - width : ROWS]
                at += width
    rest = low_y.shape[0] - at
    if rest:
        low_y[at : at + rest] = jnp.zeros((rest, LANES), F32)
        high_y[at : at + rest] = jnp.zeros((rest, LANES), F32)


def level_kernel(
    near, solid, spread, inv_mass, plane_w, inv_den, fyh, fyl, fxh, fxl, bxh, bxl, byh, byl,
    b, l, zlo, zhi, ylo, yhi, level_ref, flux_ref, w_ref, wlo, whi, stat, ext,
):
    own = add_faces(
        l[...], zlo[2], zhi[2], ylo[24:34], yhi[24:34]
    )
    row = lax.broadcasted_iota(jnp.int32, (8, ROWS, LANES), 1)
    lane = lax.broadcasted_iota(jnp.int32, (8, ROWS, LANES), 2)
    before = jnp.where((row % 8 == 0) & (row > 0), pltpu.roll(own, 1, 1), 0.0)
    after = jnp.where((row % 8 == 7) & (row < ROWS - 1), pltpu.roll(own, ROWS - 1, 1), 0.0)
    own = own + before + after
    before = jnp.where((lane % 8 == 0) & (lane > 0), pltpu.roll(own, 1, 2), 0.0)
    after = jnp.where((lane % 8 == 7) & (lane < LANES - 1), pltpu.roll(own, LANES - 1, 2), 0.0)
    own = own + before + after
    inverse = inv_mass[...] * edge_rows(ROWS, near[2], near[3])
    in_solid = dot(solid[...].astype(BF16), spread[...])
    open_part = jnp.concatenate(
        [jnp.broadcast_to(1.0 - (1.0 - SOLID_FACTOR) * in_solid[e : e + 1], (8, LANES)) for e in range(EY)],
        axis=0,
    )
    total = jnp.zeros((ROWS, LANES), F32)
    for i in range(8):
        scale = 1.0 / float(WEIGHT[i])
        plane = own[i] * (inverse * scale)
        if i == 0:
            plane = plane * near[0]
        if i == 7:
            plane = plane * near[1]
        level_ref[i] = plane
        liquid = jax.nn.sigmoid(plane * (1.0 / LEVEL_WIDTH))
        coef = (GAS_RATIO - (GAS_RATIO - 1.0) * liquid) * open_part
        total = total + coef
        flux_ref[i] = (0.5 * float(WEIGHT[i])) * (coef * plane_w[...])
    kbar = jnp.sum(total) * (1.0 / (8 * ROWS * LANES))
    fill_ext(ext, b, zlo, zhi, ylo, yhi)
    stat[...] = lane_row([kbar, partition_total(ext, near)])
    schwarz(ext, ((fyh, fyl), (fxh, fxl), (bxh, bxl), (byh, byl)), inv_den, near, w_ref, wlo, whi)


def schwarz_kernel(
    near, inv_den, fyh, fyl, fxh, fxl, bxh, bxl, byh, byl, b, zlo, zhi, ylo, yhi,
    w_ref, wlo, whi, ext,
):
    fill_ext(ext, b, zlo, zhi, ylo, yhi)
    schwarz(ext, ((fyh, fyl), (fxh, fxl), (bxh, bxl), (byh, byl)), inv_den, near, w_ref, wlo, whi)


def galerkin_kernel(
    zt, yt, wy, plane_w, rolls, dxh, dxl, dxth, dxtl, stat_in, flux, w, zlo, zhi, ylo, yhi,
    zl_ref, stat,
):
    local = add_faces(w[...], zlo[...], zhi[...], ylo[...], yhi[...])
    zl_ref[...] = local
    fluxes = flux[...]
    applied = local_operator(local, fluxes, plane_w[...], rolls, (dxh, dxl), (dxth, dxtl))

    def combine(index, planes):
        total = zt[index, 0] * planes[0]
        for i in range(1, 8):
            total = total + zt[index, i] * planes[i]
        return jnp.sum(total, axis=1, keepdims=True)

    total = jnp.zeros((ROWS, LANES), F32)
    for a in range(3):
        placed = pltpu.roll(yt[2], 2 + 3 * a, 1)
        total = total + combine(12 + a, applied) * placed
    for index in range(6):
        shift = 11 + 9 * index
        slope_z = combine(index, fluxes) + zt[15, index] * wy[...]
        slope_y = combine(6 + index, fluxes)
        total = total + slope_z * pltpu.roll(yt[0], shift, 1)
        total = total + slope_y * pltpu.roll(yt[1], shift, 1)
    stat[...] = stat_in[...] + jnp.sum(total, axis=0, keepdims=True)


def invert(blocks, sub):
    for k in range(8):
        pivot = 1.0 / blocks[k][k : k + 1]
        scaled = jnp.where(sub == k, pivot, blocks[k] * pivot)
        rows = []
        for r in range(8):
            if r == k:
                rows.append(scaled)
            else:
                rest = jnp.where(sub == k, 0.0, blocks[r])
                rows.append(rest - blocks[r][k : k + 1] * scaled)
        blocks = rows
    return blocks


def multiply(left, right):
    rows = []
    for r in range(8):
        total = left[r][0:1] * right[0]
        for k in range(1, 8):
            total = total + left[r][k : k + 1] * right[k]
        rows.append(total)
    return rows


def matvec(terms, sub):
    result = jnp.zeros_like(terms[0][1])
    for r in range(8):
        product = terms[0][0][r] * terms[0][1]
        for blocks, column in terms[1:]:
            product = product + blocks[r] * column
        result = jnp.where(sub == r, jnp.sum(product, axis=0, keepdims=True), result)
    return result


def coarse_kernel(count, place, gathered, out_ref, wide, values):
    lanes = LANES
    wide[...] = jnp.zeros((LANES, LANES), F32)
    for i in range(8):
        wide[0:count] = gathered[:, i, :]
        values[i] = wide[...].T
    sub = lax.broadcasted_iota(jnp.int32, (8, lanes), 0)
    lane = lax.broadcasted_iota(jnp.int32, (8, lanes), 1)

    def value(index):
        return jnp.concatenate([values[i, index : index + 1] for i in range(8)], axis=0)

    def move(array, dz, dy):
        if dz:
            array = pltpu.roll(array, (-dz) % 8, 0)
        if dy:
            array = pltpu.roll(array, (-dy) % lanes, 1)
        return array

    kbar = jnp.where(lane < count, value(0), 1.0)
    above = move(kbar, 1, 0)
    link_z = jnp.where(sub < 7, 2.0 * kbar * above / (kbar + above) * (EY * EX / EZ), 0.0)
    link_z = jnp.where(lane < count, link_z, 0.0)
    beside = move(kbar, 0, 1)
    link_y = 2.0 * kbar * beside / (kbar + beside) * (EZ * EX / EY)
    link_y = jnp.where(lane < count - 1, link_y, 0.0)
    back_z = move(link_z, -1, 0)
    back_y = move(link_y, 0, -1)
    diagonal = HELM_COEF * EZ * EY * EX + link_z + back_z + link_y + back_y
    blocks, lower, upper = [], [], []
    for r in range(8):
        row = jnp.where(sub == r, diagonal, 0.0)
        row = jnp.where(sub == r + 1, -back_z, row)
        row = jnp.where(sub == r - 1, -link_z, row)
        blocks.append(row)
        lower.append(jnp.where(sub == r, -back_y, 0.0))
        upper.append(jnp.where(sub == r, -link_y, 0.0))
    levels = []
    step = 1
    while step < count:
        inverse = invert(blocks, sub)
        down = multiply(lower, [move(row, 0, -step) for row in inverse])
        up = multiply(upper, [move(row, 0, step) for row in inverse])
        levels.append((step, down, up))
        before_u = multiply(down, [move(row, 0, -step) for row in upper])
        after_l = multiply(up, [move(row, 0, step) for row in lower])
        if 2 * step < count:
            new_lower = multiply(down, [move(row, 0, -step) for row in lower])
            new_upper = multiply(up, [move(row, 0, step) for row in upper])
            lower = [-row for row in new_lower]
            upper = [-row for row in new_upper]
        blocks = [blocks[r] - before_u[r] - after_l[r] for r in range(8)]
        step *= 2
    inverse = invert(blocks, sub)

    def solve(column):
        for distance, down, up in levels:
            pulled = matvec(
                [(down, move(column, 0, -distance)), (up, move(column, 0, distance))], sub
            )
            column = column - pulled
        return matvec([(inverse, column)], sub)

    offsets = [(a - 1, b - 1) for a in range(3) for b in range(3)]
    first = solve(value(1))
    near_first = [move(first, dz, dy) for dz, dy in offsets]
    totals = jnp.zeros((8, lanes), F32)
    for d, (dz, dy) in enumerate(offsets):
        term = value(2 + d)
        for e in range(9):
            a, b, c, f = d // 3, d % 3, e // 3, e % 3
            if a > c:
                a, b, c, f = c, f, a, b
            term = term + value(11 + 9 * PAIRS.index((a, c)) + 3 * b + f) * near_first[e]
        totals = totals + move(term, -dz, -dy)
    totals = jnp.where(lane < count, totals, 0.0)
    second = solve(totals)
    near_second = [move(second, dz, dy) for dz, dy in offsets]
    mine = (sub == place[0]) & (lane == place[1])
    for d in range(9):
        out_ref[d : d + 1] = jnp.full((1, lanes), jnp.sum(jnp.where(mine, near_first[d], 0.0)))
        out_ref[16 + d : 17 + d] = jnp.full(
            (1, lanes), jnp.sum(jnp.where(mine, near_second[d], 0.0))
        )


def add_coarse(local, zt, yt, coarse, start):
    columns = []
    for a in range(3):
        total = yt[2, :, 0:1] * coarse[start + 3 * a : start + 3 * a + 1]
        for b in range(1, 3):
            total = total + yt[2, :, b : b + 1] * coarse[start + 3 * a + b : start + 3 * a + b + 1]
        columns.append(total)
    planes = []
    for i in range(8):
        plane = local[i] + zt[13, i] * columns[1]
        if i == 0:
            plane = plane + zt[12, i] * columns[0]
        if i == 7:
            plane = plane + zt[14, i] * columns[2]
        planes.append(plane)
    return stack(planes)


def apply_kernel(
    zt, yt, plane_w, rolls, dxh, dxl, dxth, dxtl, coarse, flux, b, zl,
    z_ref, y_ref, ylo, yhi, stat,
):
    field = add_coarse(zl[...], zt, yt, coarse, 0)
    z_ref[...] = field
    applied = local_operator(field, flux[...], plane_w[...], rolls, (dxh, dxl), (dxth, dxtl))
    y_ref[...] = applied
    ylo[...] = applied[0:2]
    yhi[...] = applied[6:8]
    stat[...] = lane_row([jnp.sum(b[...] * field), jnp.sum(field * applied)])


def second_kernel(
    zt, yt, plane_w, rolls, dxh, dxl, dxth, dxtl, coarse, flux, b, y, w, zlo, zhi, ylo, yhi,
    stat_in, q_ref, stat,
):
    local = add_faces(w[...], zlo[...], zhi[...], ylo[...], yhi[...])
    field = add_coarse(local, zt, yt, coarse, 16)
    q_ref[...] = field
    applied = local_operator(field, flux[...], plane_w[...], rolls, (dxh, dxl), (dxth, dxtl))
    sums = [0.0, 0.0, jnp.sum(b[...] * field), jnp.sum(y[...] * field), jnp.sum(field * applied)]
    stat[...] = stat_in[...] + lane_row(sums)


def combine_kernel(sums, z, q, p_ref):
    total = jnp.sum(sums[...], axis=0, keepdims=True)
    rz, pap, rq, aq, qhq = (total[:, k : k + 1] for k in range(5))
    step = rz / pap
    rz_next = step * (step * aq - rq)
    beta = rz_next / rz
    grown = 1.0 + beta
    curved = grown * grown * pap - 2.0 * step * grown * aq + step * step * qhq
    step_next = rz_next / curved
    on_z = step + step_next * grown
    on_q = step_next * step
    p_ref[...] = on_z.reshape(1, 1, 1) * z[...] - on_q.reshape(1, 1, 1) * q[...]


def call(kernel, outs, specs, args, scratch=(), flops=1000000):
    nbytes = sum(4 * int(np.prod(out)) for out in outs) * 2
    return pl.pallas_call(
        kernel,
        out_shape=[jax.ShapeDtypeStruct(out, F32) for out in outs],
        in_specs=[pl.BlockSpec(memory_space=SMEM if spec else VMEM) for spec in specs],
        out_specs=[pl.BlockSpec(memory_space=VMEM) for _ in outs],
        scratch_shapes=list(scratch),
        compiler_params=pltpu.CompilerParams(vmem_limit_bytes=LIMIT),
        cost_estimate=pl.CostEstimate(flops=flops, bytes_accessed=nbytes, transcendentals=0),
    )(*args)


def run(kernel, outs, smem, args, scratch=(), flops=1000000):
    specs = [True] * len(smem) + [False] * len(args)
    return call(kernel, outs, specs, list(smem) + list(args), scratch, flops)


def shift(axis, low_face, high_face):
    count = lax.axis_size(axis)
    forward = [(i, i + 1) for i in range(count - 1)]
    backward = [(target, source) for source, target in forward]
    return lax.ppermute(high_face, axis, forward), lax.ppermute(low_face, axis, backward)


def gather_tiles(row, count_gx, count_gy):
    tile = jnp.broadcast_to(row, (count_gx, LANES))
    tile = lax.all_to_all(tile, "gx", 0, 0, tiled=True)
    wide = jnp.broadcast_to(tile[None], (count_gy, count_gx, LANES))
    return lax.all_to_all(wide, "gy", 0, 0, tiled=True)


def body(level_set, velocity, source, wick_solid):
    block = level_set.shape
    count_gx = lax.axis_size("gx")
    count_gy = lax.axis_size("gy")
    index_gx = lax.axis_index("gx")
    index_gy = lax.axis_index("gy")

    def ends(index, count):
        return [jnp.where(index > 0, 0.5, 1.0), jnp.where(index < count - 1, 0.5, 1.0)]

    def case(index, count):
        return jnp.where(index == 0, 0, jnp.where(index == count - 1, 2, 1))

    near = jnp.stack(ends(index_gx, count_gx) + ends(index_gy, count_gy)).astype(F32)
    zt = lax.dynamic_index_in_dim(jnp.asarray(Z_TABLE), case(index_gx, count_gx), 0, False)
    yt = lax.dynamic_index_in_dim(jnp.asarray(Y_TABLE), case(index_gy, count_gy), 0, False)
    place = jnp.stack([index_gx, index_gy]).astype(jnp.int32)
    plane_w = jnp.asarray(PLANE_W)
    rolls = jnp.asarray(ROLLS)
    dx = (jnp.asarray(DX_H), jnp.asarray(DX_L))
    dxt = (jnp.asarray(DXT_H), jnp.asarray(DXT_L))
    wy = jnp.asarray(WY.astype(np.float32)[:, None])
    operator = (plane_w, rolls, *dx, *dxt)
    solver = (INV_DEN, FY_H, FY_L, FX_H, FX_L, BX_H, BX_L, BY_H, BY_L)
    solver = tuple(jnp.asarray(table) for table in solver)
    face = (ROWS, LANES)
    ext = VMEM((12, ROWS + 8, LANES), F32)
    solid = wick_solid.reshape(EY, EX).astype(F32)

    b, l, zlo, zhi = run(
        advect_kernel,
        [block, block, (3, *face), (3, *face)],
        [],
        [level_set, velocity, source, plane_w, rolls, *dx],
    )
    zlo, zhi = shift("gx", zlo, zhi)
    ylo, yhi = run(
        functools.partial(rim_kernel, ((2, 0), (1, 2))), [(40, LANES)] * 2, [], [b, l, zlo, zhi]
    )
    ylo, yhi = shift("gy", ylo, yhi)
    level_new, flux, w, wlo, whi, stat = run(
        level_kernel,
        [block, block, block, face, face, (1, LANES)],
        [near],
        [
            solid, jnp.asarray(SPREAD), jnp.asarray(INV_MASS), plane_w, *solver,
            b, l, zlo, zhi, ylo, yhi,
        ],
        [ext],
    )

    def exchange_one(w, wlo, whi):
        zlo, zhi = shift("gx", wlo, whi)
        ylo, yhi = run(
            functools.partial(rim_kernel, ((1, 0),)), [(16, LANES)] * 2, [],
            [w, zlo[None], zhi[None]],
        )
        ylo, yhi = shift("gy", ylo, yhi)
        return zlo, zhi, ylo, yhi

    faces = exchange_one(w, wlo, whi)
    zl, stat = run(
        galerkin_kernel,
        [block, (1, LANES)],
        [zt],
        [yt, wy, *operator, stat, flux, w, *faces],
    )
    gathered = gather_tiles(stat, count_gx, count_gy)
    (coarse,) = run(
        functools.partial(coarse_kernel, count_gy),
        [(32, LANES)],
        [place],
        [gathered],
        [VMEM((LANES, LANES), F32), VMEM((8, LANES, LANES), F32)],
    )
    z, y, zlo, zhi, sums = run(
        apply_kernel,
        [block, block, (2, *face), (2, *face), (1, LANES)],
        [zt],
        [yt, *operator, coarse, flux, b, zl],
    )
    zlo, zhi = shift("gx", zlo, zhi)
    ylo, yhi = run(
        functools.partial(rim_kernel, ((2, 0),)), [(24, LANES)] * 2, [], [y, zlo, zhi]
    )
    ylo, yhi = shift("gy", ylo, yhi)
    w, wlo, whi = run(
        schwarz_kernel,
        [block, face, face],
        [near],
        [*solver, y, zlo, zhi, ylo, yhi],
        [ext],
    )
    faces = exchange_one(w, wlo, whi)
    q, sums = run(
        second_kernel,
        [block, (1, LANES)],
        [zt],
        [yt, *operator, coarse, flux, b, y, w, *faces, sums],
    )
    tile = jnp.broadcast_to(sums, (count_gx, LANES))
    tile = lax.all_to_all(tile, "gx", 0, 0, tiled=True)
    wide = jnp.broadcast_to(jnp.sum(tile, axis=0, keepdims=True), (count_gy, LANES))
    wide = lax.all_to_all(wide, "gy", 0, 0, tiled=True)
    (pressure,) = run(combine_kernel, [block], [], [wide, z, q])
    return (level_new, pressure)


def solution(mesh):
    placed = (
        P("gx", "gy", None),
        P(None, "gx", "gy", None),
        P("gx", "gy", None),
        P("gx", "gy", None),
    )
    return jax.shard_map(
        body,
        mesh=mesh,
        in_specs=placed,
        out_specs=(P("gx", "gy", None), P("gx", "gy", None)),
        check_vma=False,
    )
```

time: 863 us -> 164 us (0.19)
  blocking collectives: 514 us -> 44.2 us
  other arithmetic: 143 us -> 0.18 us
  local copies, waits for them, and re-layouts: 57.1 us -> 7.57 us
  starting transfers between devices: 101 us -> 57.6 us
  waiting for transfers between devices: 6.3 us -> 39.1 us
  matrix products: 22.6 us -> 0 us
  Pallas kernels: 0 us -> 13 us
  between operations: 10.4 us -> 1.12 us
    psum x3 -> x0, blocking collectives: 313 us -> none  [inner(): return lax.psum(jnp.sum(left * right * inv_mult), ('gx', 'gy'))]
    unnamed x2 -> x0, blocking collectives: 201 us -> none
    another operation x25 -> x2, other arithmetic: 127 us -> 0.16 us  [the longest x1 0.08 us: body(): jnp.stack(ends(index_gx, count_gx) + ends(index_gy, count_gy)).astype(F32)]
    ppermute x32 -> x16, starting transfers between devices: 101 us -> 42.1 us  [the longest x8 28.9 us: shift(): lax.ppermute(high_face, axis, forward)]
    all_to_all x0 -> x3, blocking collectives: none -> 44.2 us  [the longest x1 21.4 us: body(): wide = lax.all_to_all(wide, 'gy', 0, 0, tiled=True)]
    slice x53 -> x0, local copies, waits for them, and re-layouts: 24.4 us -> none  [the longest x8 4.69 us: inner_axis(): kept_nodes = lax.slice_in_dim(parted, 1, 9, axis=axis_id + 1)]
    ppermute x32 -> x16, waiting for transfers between devices: 6.3 us -> 26 us  [the longest x8 26 us: shift(): lax.ppermute(low_face, axis, backward)]
    another operation x27 -> x0, local copies, waits for them, and re-layouts: 17.9 us -> none  [the longest x13 8.26 us: chol_solve(): lax.linalg.triangular_solve(factor, middle, left_side=True, lower=True, t...]
  transfers between devices with their start and end apart: 32 -> 17, of which waited for: 8 -> 9; matrix products, arithmetic and copies ran while one was open for 18% -> 1% of each run, Pallas kernels for 0% -> 0%
where the time goes in v1:
time: 164 us; the launch traced here: 163 us
  starting transfers between devices  57.6 us (35%)
  blocking collectives  44.2 us (27%)
  waiting for transfers between devices  39.1 us (24%)
  Pallas kernels  13 us (8%)
  local copies, waits for them, and re-layouts  7.57 us (5%)
    ppermute x8, starting transfers between devices, shift(): lax.ppermute(high_face, axis, forward)  28.9 us
    ppermute x8, waiting for transfers between devices, shift(): lax.ppermute(low_face, axis, backward)  26 us
    all_to_all x1, blocking collectives, body(): wide = lax.all_to_all(wide, 'gy', 0, 0, tiled=True)  21.4 us
    all_to_all x1, starting transfers between devices, gather_tiles(): return lax.all_to_all(wide, 'gy', 0, 0, tiled=True)  15.6 us
    ppermute x8, starting transfers between devices, shift(): lax.ppermute(low_face, axis, backward)  13.1 us
    all_to_all x1, waiting for transfers between devices, gather_tiles(): return lax.all_to_all(wide, 'gy', 0, 0, tiled=True)  13.1 us
    pallas_call x12, Pallas kernels, call(): pl.pallas_call(kernel, out_shape=[jax.ShapeDtypeStruct(out, F32) for out...  13 us
    all_to_all x1, blocking collectives, gather_tiles(): tile = lax.all_to_all(tile, 'gx', 0, 0, tiled=True)  12.9 us
  transfers between devices with their start and end apart: 17, of which 9 were waited for; matrix products, arithmetic and copies ran while one was open for 1% of the time, Pallas kernels for 0%

profile of v1, /device:TPU:1, one launch (start us, length us, event | category | flops | bytes accessed | tf_op | source)
XLA Modules:
  0.0 162.9 jit_solution(12024950709789712445)
XLA Ops:
  0.7 0.7 copy-done.3
  1.4 0.8 copy-done.1
  2.2 0.8 copy-done.4
  3.0 1.0 copy-done.7
  4.0 0.9 copy-done.14
  4.9 0.9 copy-done.15
  5.9 0.5 shard_map.239
  6.4 5.0 %collective-permute-start = (f32[3,32,128]{2,1,0:T(8,128)S(1)}, f32[3,32,128]{2,1,0:T(8,128)S(1)}, u32[]{:S(2)}, u32[]{:S(2)}) collective-permute-start(f32[3,32,128]{2,1,0:T(8,128)S(1)} %get-tuple-element.34), channel_id=1, source_target_pairs={{0,64},{64,128},{128,192},{192,256},{256,320},{320,384},{384,448},... | collective-permute-start | bytes 147464 | tf_op jit(solution)/shard_map/ppermute | solution.py:683
  11.4 1.3 collective-permute-start.1
  12.7 4.1 %collective-permute-done.1.refs_3_.zhi = f32[3,32,128]{2,1,0:T(8,128)S(1)} collective-permute-done((f32[3,32,128]{2,1,0:T(8,128)S(1)}, f32[3,32,128]{2,1,0:T(8,128)S(1)}, u32[]{:S(2)}, u32[]{:S(2)}) %collective-permute-start.1) | collective-permute-done | bytes 49184 | tf_op jit(solution)/shard_map/ppermute | solution.py:683
  16.9 4.8 %collective-permute-start.2 = (f32[40,128]{1,0:T(8,128)S(1)}, f32[40,128]{1,0:T(8,128)S(1)}, u32[]{:S(2)}, u32[]{:S(2)}) collective-permute-start(f32[40,128]{1,0:T(8,128)S(1)} %get-tuple-element.36), channel_id=1, source_target_pairs={{0,1},{1,2},{2,3},{3,4},{4,5},{5,6},{6,7},{7,8},{8,9},{9,10},{10,1... | collective-permute-start | bytes 61448 | tf_op jit(solution)/shard_map/ppermute | solution.py:683
  21.7 2.2 %collective-permute-start.3 = (f32[40,128]{1,0:T(8,128)S(1)}, f32[40,128]{1,0:T(8,128)S(1)}, u32[]{:S(2)}, u32[]{:S(2)}) collective-permute-start(f32[40,128]{1,0:T(8,128)S(1)} %get-tuple-element.37), channel_id=1, source_target_pairs={{1,0},{2,1},{3,2},{4,3},{5,4},{6,5},{7,6},{8,7},{9,8},{10,9},{11,1... | collective-permute-start | bytes 61448 | tf_op jit(solution)/shard_map/ppermute | solution.py:683
  24.0 0.1 pad_maximum_fusion.near
  24.1 2.8 %collective-permute-done.3.yhi = f32[40,128]{1,0:T(8,128)S(1)} collective-permute-done((f32[40,128]{1,0:T(8,128)S(1)}, f32[40,128]{1,0:T(8,128)S(1)}, u32[]{:S(2)}, u32[]{:S(2)}) %collective-permute-start.3) | collective-permute-done | bytes 20512 | tf_op jit(solution)/shard_map/ppermute | solution.py:683
  26.9 2.4 %shard_map.241 = (f32[8,32,128]{2,1,0:T(8,128)}, f32[8,32,128]{2,1,0:T(8,128)S(1)}, f32[8,32,128]{2,1,0:T(8,128)S(1)}, f32[32,128]{1,0:T(8,128)S(1)}, f32[32,128]{1,0:T(8,128)S(1)}, /*index=5*/f32[1,128]{1,0:T(1,128)S(1)}) custom-call(f32[4]{0:T(128)S(1)} %pad_maximum_fusion.near, f32[4,16]{1,0:T(4,128)S(1)} %convert_bitcast_fusion.solid, ...), custom_call_target="tpu_custom_call" | custom-call | flops 1000000 | bytes 852992 | tf_op jit(solution)/shard_map/pallas_call | solution.py:663
  29.4 4.0 %collective-permute-start.4 = (f32[32,128]{1,0:T(8,128)S(1)}, f32[32,128]{1,0:T(8,128)S(1)}, u32[]{:S(2)}, u32[]{:S(2)}) collective-permute-start(f32[32,128]{1,0:T(8,128)S(1)} %get-tuple-element.42), channel_id=1, source_target_pairs={{0,64},{64,128},{128,192},{192,256},{256,320},{320,384},{384,448},... | collective-permute-start | bytes 49160 | tf_op jit(solution)/shard_map/ppermute | solution.py:683
  33.4 1.3 collective-permute-start.5
  34.7 0.8 dynamic-slice_bitcast_fusion.yt
  35.5 4.2 %collective-permute-done.5.zhi = f32[32,128]{1,0:T(8,128)S(1)} collective-permute-done((f32[32,128]{1,0:T(8,128)S(1)}, f32[32,128]{1,0:T(8,128)S(1)}, u32[]{:S(2)}, u32[]{:S(2)}) %collective-permute-start.5) | collective-permute-done | bytes 16416 | tf_op jit(solution)/shard_map/ppermute | solution.py:683
  39.7 3.2 %collective-permute-start.6 = (f32[16,128]{1,0:T(8,128)S(1)}, f32[16,128]{1,0:T(8,128)S(1)}, u32[]{:S(2)}, u32[]{:S(2)}) collective-permute-start(f32[16,128]{1,0:T(8,128)S(1)} %get-tuple-element.44), channel_id=1, source_target_pairs={{0,1},{1,2},{2,3},{3,4},{4,5},{5,6},{6,7},{7,8},{8,9},{9,10},{10,1... | collective-permute-start | bytes 24584 | tf_op jit(solution)/shard_map/ppermute | solution.py:683
  42.9 1.9 %collective-permute-start.7 = (f32[16,128]{1,0:T(8,128)S(1)}, f32[16,128]{1,0:T(8,128)S(1)}, u32[]{:S(2)}, u32[]{:S(2)}) collective-permute-start(f32[16,128]{1,0:T(8,128)S(1)} %get-tuple-element.45), channel_id=1, source_target_pairs={{1,0},{2,1},{3,2},{4,3},{5,4},{6,5},{7,6},{8,7},{9,8},{10,9},{11,1... | collective-permute-start | bytes 24584 | tf_op jit(solution)/shard_map/ppermute | solution.py:683
  44.9 0.7 dynamic-slice_bitcast_fusion.1
  45.6 2.3 %collective-permute-done.7.yhi = f32[16,128]{1,0:T(8,128)S(1)} collective-permute-done((f32[16,128]{1,0:T(8,128)S(1)}, f32[16,128]{1,0:T(8,128)S(1)}, u32[]{:S(2)}, u32[]{:S(2)}) %collective-permute-start.7) | collective-permute-done | bytes 8224 | tf_op jit(solution)/shard_map/ppermute | solution.py:683
  47.9 1.5 shard_map.243
  49.4 12.9 %all_to_all.25 = f32[8,1,128]{2,1,0:T(1,128)S(1)} all-to-all(f32[8,1,128]{2,1,0:T(1,128)S(1)} %broadcast_in_dim.38), channel_id=1, replica_groups=mesh['gx'=8,'gy'=64] {'gx'}, dimensions={0} | all-to-all | bytes 8192 | tf_op jit(solution)/shard_map/all_to_all | solution.py:688
  62.3 0.7 broadcast_in_dim.40
  63.1 15.6 %all-to-all-start.1 = ((f32[64,8,128]{2,1,0:T(8,128)}), f32[64,8,128]{2,1,0:T(8,128)S(1)}, u32[]{:S(2)}, u32[]{:S(2)}) async-start(f32[64,8,128]{2,1,0:T(8,128)} %broadcast_in_dim.40), calls=%async_computation.1 | async-start | bytes 524288 | tf_op jit(solution)/shard_map/all_to_all | solution.py:690
  78.7 0.1 pad_add_fusion.place
  78.7 13.1 %all-to-all-done.1.gathered = f32[64,8,128]{2,1,0:T(8,128)S(1)} async-done(((f32[64,8,128]{2,1,0:T(8,128)}), f32[64,8,128]{2,1,0:T(8,128)S(1)}, u32[]{:S(2)}, u32[]{:S(2)}) %all-to-all-start.1) | async-done | bytes 262176 | tf_op jit(solution)/shard_map/all_to_all | solution.py:690
  91.8 3.4 %shard_map.244.coarse = f32[32,128]{1,0:T(8,128)S(1)} custom-call(s32[2]{0:T(128)S(1)} %pad_add_fusion.place, f32[64,8,128]{2,1,0:T(8,128)S(1)} %all-to-all-done.1.gathered), custom_call_target="tpu_custom_call" | custom-call | flops 1000000 | bytes 32768 | tf_op jit(solution)/shard_map/pallas_call | solution.py:663
  95.2 1.3 shard_map.245
  96.5 2.2 %collective-permute-start.8 = (f32[2,32,128]{2,1,0:T(8,128)S(1)}, f32[2,32,128]{2,1,0:T(8,128)S(1)}, u32[]{:S(2)}, u32[]{:S(2)}) collective-permute-start(f32[2,32,128]{2,1,0:T(8,128)S(1)} %get-tuple-element.49), channel_id=1, source_target_pairs={{0,64},{64,128},{128,192},{192,256},{256,320},{320,384},{384,448},... | collective-permute-start | bytes 98312 | tf_op jit(solution)/shard_map/ppermute | solution.py:683
  98.7 1.3 collective-permute-start.9
  100.0 3.3 %collective-permute-done.9.refs_2_.zhi = f32[2,32,128]{2,1,0:T(8,128)S(1)} collective-permute-done((f32[2,32,128]{2,1,0:T(8,128)S(1)}, f32[2,32,128]{2,1,0:T(8,128)S(1)}, u32[]{:S(2)}, u32[]{:S(2)}) %collective-permute-start.9) | collective-permute-done | bytes 32800 | tf_op jit(solution)/shard_map/ppermute | solution.py:683
  103.4 4.0 %collective-permute-start.10 = (f32[24,128]{1,0:T(8,128)S(1)}, f32[24,128]{1,0:T(8,128)S(1)}, u32[]{:S(2)}, u32[]{:S(2)}) collective-permute-start(f32[24,128]{1,0:T(8,128)S(1)} %get-tuple-element.51), channel_id=1, source_target_pairs={{0,1},{1,2},{2,3},{3,4},{4,5},{5,6},{6,7},{7,8},{8,9},{9,10},{10,1... | collective-permute-start | bytes 36872 | tf_op jit(solution)/shard_map/ppermute | solution.py:683
  107.4 1.9 %collective-permute-start.11 = (f32[24,128]{1,0:T(8,128)S(1)}, f32[24,128]{1,0:T(8,128)S(1)}, u32[]{:S(2)}, u32[]{:S(2)}) collective-permute-start(f32[24,128]{1,0:T(8,128)S(1)} %get-tuple-element.52), channel_id=1, source_target_pairs={{1,0},{2,1},{3,2},{4,3},{5,4},{6,5},{7,6},{8,7},{9,8},{10,9},{11,1... | collective-permute-start | bytes 36872 | tf_op jit(solution)/shard_map/ppermute | solution.py:683
  109.4 3.1 %collective-permute-done.11.yhi = f32[24,128]{1,0:T(8,128)S(1)} collective-permute-done((f32[24,128]{1,0:T(8,128)S(1)}, f32[24,128]{1,0:T(8,128)S(1)}, u32[]{:S(2)}, u32[]{:S(2)}) %collective-permute-start.11) | collective-permute-done | bytes 12320 | tf_op jit(solution)/shard_map/ppermute | solution.py:683
  112.5 1.8 %shard_map.247 = (f32[8,32,128]{2,1,0:T(8,128)S(1)}, f32[32,128]{1,0:T(8,128)S(1)}, f32[32,128]{1,0:T(8,128)S(1)}) custom-call(f32[4]{0:T(128)S(1)} %pad_maximum_fusion.near, f32[10,40,160]{2,1,0:T(8,128)S(1)} %copy-done, bf16[40,40]{1,0:T(8,128)(2,1)S(1)} %copy-done.17, bf16[40,40]{1,0:T(8,128)(2,1)S(1)} %copy-done.16, bf16[128,160]{1,0:T(8,128)(2,1)S(1)} %copy-done.11, ...), custom_call_target="tpu_custom_call" | custom-call | flops 1000000 | bytes 327680 | tf_op jit(solution)/shard_map/pallas_call | solution.py:663
  114.2 2.2 %collective-permute-start.12 = (f32[32,128]{1,0:T(8,128)S(1)}, f32[32,128]{1,0:T(8,128)S(1)}, u32[]{:S(2)}, u32[]{:S(2)}) collective-permute-start(f32[32,128]{1,0:T(8,128)S(1)} %get-tuple-element.54), channel_id=1, source_target_pairs={{0,64},{64,128},{128,192},{192,256},{256,320},{320,384},{384,448},... | collective-permute-start | bytes 49160 | tf_op jit(solution)/shard_map/ppermute | solution.py:683
  116.4 1.3 collective-permute-start.13
  117.7 3.2 %collective-permute-done.13.zhi = f32[32,128]{1,0:T(8,128)S(1)} collective-permute-done((f32[32,128]{1,0:T(8,128)S(1)}, f32[32,128]{1,0:T(8,128)S(1)}, u32[]{:S(2)}, u32[]{:S(2)}) %collective-permute-start.13) | collective-permute-done | bytes 16416 | tf_op jit(solution)/shard_map/ppermute | solution.py:683
  120.9 3.5 %collective-permute-start.14 = (f32[16,128]{1,0:T(8,128)S(1)}, f32[16,128]{1,0:T(8,128)S(1)}, u32[]{:S(2)}, u32[]{:S(2)}) collective-permute-start(f32[16,128]{1,0:T(8,128)S(1)} %get-tuple-element.56), channel_id=1, source_target_pairs={{0,1},{1,2},{2,3},{3,4},{4,5},{5,6},{6,7},{7,8},{8,9},{9,10},{10,1... | collective-permute-start | bytes 24584 | tf_op jit(solution)/shard_map/ppermute | solution.py:683
  124.4 1.9 %collective-permute-start.15 = (f32[16,128]{1,0:T(8,128)S(1)}, f32[16,128]{1,0:T(8,128)S(1)}, u32[]{:S(2)}, u32[]{:S(2)}) collective-permute-start(f32[16,128]{1,0:T(8,128)S(1)} %get-tuple-element.57), channel_id=1, source_target_pairs={{1,0},{2,1},{3,2},{4,3},{5,4},{6,5},{7,6},{8,7},{9,8},{10,9},{11,1... | collective-permute-start | bytes 24584 | tf_op jit(solution)/shard_map/ppermute | solution.py:683
  126.4 3.0 %collective-permute-done.15.yhi = f32[16,128]{1,0:T(8,128)S(1)} collective-permute-done((f32[16,128]{1,0:T(8,128)S(1)}, f32[16,128]{1,0:T(8,128)S(1)}, u32[]{:S(2)}, u32[]{:S(2)}) %collective-permute-start.15) | collective-permute-done | bytes 8224 | tf_op jit(solution)/shard_map/ppermute | solution.py:683
  129.4 1.3 shard_map.249
  130.7 10.0 %all_to_all.26 = f32[8,1,128]{2,1,0:T(1,128)S(1)} all-to-all(f32[8,1,128]{2,1,0:T(1,128)S(1)} %broadcast_in_dim.43), channel_id=1, replica_groups=mesh['gx'=8,'gy'=64] {'gx'}, dimensions={0} | all-to-all | bytes 8192 | tf_op jit(solution)/shard_map/all_to_all | solution.py:794
  140.7 21.4 %all_to_all.27 = f32[64,1,128]{2,1,0:T(1,128)S(1)} all-to-all(f32[64,1,128]{2,1,0:T(1,128)S(1)} %broadcast_in_dim.44), channel_id=1, replica_groups=mesh['gx'=8,'gy'=64] {'gy'}, dimensions={0} | all-to-all | bytes 65536 | tf_op jit(solution)/shard_map/all_to_all | solution.py:796
  162.1 0.8 shard_map.250
  (60 shorter events, 0.3 us)
Async XLA Ops:
  0.6 0.8 copy-start.3
  0.6 0.8 copy-start.6
  1.4 0.8 copy-start.1
  2.2 0.8 copy-start.4
  3.0 1.0 copy-start.7
  4.0 0.9 copy-start.14
  4.9 0.9 copy-start.15
  5.8 6.9 %copy-start.23 = (s32[1,4,16]{2,1,0:T(4,128)S(1)}, s32[1,4,16]{2,1,0:T(4,128)}, u32[]{:S(2)}) copy-start(s32[1,4,16]{2,1,0:T(4,128)} %param.27) | copy-start | bytes 772
  5.8 21.0 %copy-start.10 = (bf16[128,160]{1,0:T(8,128)(2,1)S(1)}, bf16[128,160]{1,0:T(8,128)(2,1)}, u32[]{:S(2)}) copy-start(bf16[128,160]{1,0:T(8,128)(2,1)} %constant.88.clone.fxl) | copy-start | bytes 122884
  5.8 21.0 %copy-start.11 = (bf16[128,160]{1,0:T(8,128)(2,1)S(1)}, bf16[128,160]{1,0:T(8,128)(2,1)}, u32[]{:S(2)}) copy-start(bf16[128,160]{1,0:T(8,128)(2,1)} %constant.87.clone.fxh) | copy-start | bytes 122884
  5.8 21.0 %copy-start.12 = (bf16[160,128]{1,0:T(8,128)(2,1)S(1)}, bf16[160,128]{1,0:T(8,128)(2,1)}, u32[]{:S(2)}) copy-start(bf16[160,128]{1,0:T(8,128)(2,1)} %constant.90.clone.bxl) | copy-start | bytes 122884
  5.8 21.0 %copy-start.13 = (bf16[160,128]{1,0:T(8,128)(2,1)S(1)}, bf16[160,128]{1,0:T(8,128)(2,1)}, u32[]{:S(2)}) copy-start(bf16[160,128]{1,0:T(8,128)(2,1)} %constant.89.clone.bxh) | copy-start | bytes 122884
  5.8 21.0 %copy-start.17 = (bf16[40,40]{1,0:T(8,128)(2,1)S(1)}, bf16[40,40]{1,0:T(8,128)(2,1)}, u32[]{:S(2)}) copy-start(bf16[40,40]{1,0:T(8,128)(2,1)} %constant.85.clone.fyh) | copy-start | bytes 9604
  5.8 21.0 %copy-start.18 = (bf16[32,40]{1,0:T(8,128)(2,1)S(1)}, bf16[32,40]{1,0:T(8,128)(2,1)}, u32[]{:S(2)}) copy-start(bf16[32,40]{1,0:T(8,128)(2,1)} %constant.92.clone.byl) | copy-start | bytes 7684
  5.8 21.0 %copy-start.19 = (bf16[32,40]{1,0:T(8,128)(2,1)S(1)}, bf16[32,40]{1,0:T(8,128)(2,1)}, u32[]{:S(2)}) copy-start(bf16[32,40]{1,0:T(8,128)(2,1)} %constant.91.clone.byh) | copy-start | bytes 7684
  5.9 21.0 %copy-start.20 = (f32[32,128]{1,0:T(8,128)S(1)}, f32[32,128]{1,0:T(8,128)}, u32[]{:S(2)}) copy-start(f32[32,128]{1,0:T(8,128)} %constant.94.clone.inv_mass) | copy-start | bytes 49156
  5.9 21.0 %copy-start.22 = (bf16[16,128]{1,0:T(8,128)(2,1)S(1)}, bf16[16,128]{1,0:T(8,128)(2,1)}, u32[]{:S(2)}) copy-start(bf16[16,128]{1,0:T(8,128)(2,1)} %constant.93.clone.spread) | copy-start | bytes 12292
  6.4 20.5 %copy-start = (f32[10,40,160]{2,1,0:T(8,128)S(1)}, f32[10,40,160]{2,1,0:T(8,128)}, u32[]{:S(2)}) copy-start(f32[10,40,160]{2,1,0:T(8,128)} %constant.84.clone.inv_den) | copy-start | bytes 768004
  6.4 6.3 %collective-permute-start = (f32[3,32,128]{2,1,0:T(8,128)S(1)}, f32[3,32,128]{2,1,0:T(8,128)S(1)}, u32[]{:S(2)}, u32[]{:S(2)}) collective-permute-start(f32[3,32,128]{2,1,0:T(8,128)S(1)} %get-tuple-element.34), channel_id=1, source_target_pairs={{0,64},{64,128},{128,192},{192,256},{256,320},{320,384},{384,448},... | collective-permute-start | bytes 147464 | tf_op jit(solution)/shard_map/ppermute | solution.py:683
  11.4 5.5 %collective-permute-start.1 = (f32[3,32,128]{2,1,0:T(8,128)S(1)}, f32[3,32,128]{2,1,0:T(8,128)S(1)}, u32[]{:S(2)}, u32[]{:S(2)}) collective-permute-start(f32[3,32,128]{2,1,0:T(8,128)S(1)} %get-tuple-element.35), channel_id=1, source_target_pairs={{64,0},{128,64},{192,128},{256,192},{320,256},{384,320},{448,384},... | collective-permute-start | bytes 147464 | tf_op jit(solution)/shard_map/ppermute | solution.py:683
  16.9 10.0 %copy-start.16 = (bf16[40,40]{1,0:T(8,128)(2,1)S(1)}, bf16[40,40]{1,0:T(8,128)(2,1)}, u32[]{:S(2)}) copy-start(bf16[40,40]{1,0:T(8,128)(2,1)} %constant.86.clone.fyl) | copy-start | bytes 9604
  16.9 7.2 %collective-permute-start.2 = (f32[40,128]{1,0:T(8,128)S(1)}, f32[40,128]{1,0:T(8,128)S(1)}, u32[]{:S(2)}, u32[]{:S(2)}) collective-permute-start(f32[40,128]{1,0:T(8,128)S(1)} %get-tuple-element.36), channel_id=1, source_target_pairs={{0,1},{1,2},{2,3},{3,4},{4,5},{5,6},{6,7},{7,8},{8,9},{9,10},{10,1... | collective-permute-start | bytes 61448 | tf_op jit(solution)/shard_map/ppermute | solution.py:683
  21.7 5.1 %collective-permute-start.3 = (f32[40,128]{1,0:T(8,128)S(1)}, f32[40,128]{1,0:T(8,128)S(1)}, u32[]{:S(2)}, u32[]{:S(2)}) collective-permute-start(f32[40,128]{1,0:T(8,128)S(1)} %get-tuple-element.37), channel_id=1, source_target_pairs={{1,0},{2,1},{3,2},{4,3},{5,4},{6,5},{7,6},{8,7},{9,8},{10,9},{11,1... | collective-permute-start | bytes 61448 | tf_op jit(solution)/shard_map/ppermute | solution.py:683
  29.4 6.1 %collective-permute-start.4 = (f32[32,128]{1,0:T(8,128)S(1)}, f32[32,128]{1,0:T(8,128)S(1)}, u32[]{:S(2)}, u32[]{:S(2)}) collective-permute-start(f32[32,128]{1,0:T(8,128)S(1)} %get-tuple-element.42), channel_id=1, source_target_pairs={{0,64},{64,128},{128,192},{192,256},{256,320},{320,384},{384,448},... | collective-permute-start | bytes 49160 | tf_op jit(solution)/shard_map/ppermute | solution.py:683
  33.4 6.3 %collective-permute-start.5 = (f32[32,128]{1,0:T(8,128)S(1)}, f32[32,128]{1,0:T(8,128)S(1)}, u32[]{:S(2)}, u32[]{:S(2)}) collective-permute-start(f32[32,128]{1,0:T(8,128)S(1)} %get-tuple-element.43), channel_id=1, source_target_pairs={{64,0},{128,64},{192,128},{256,192},{320,256},{384,320},{448,384},... | collective-permute-start | bytes 49160 | tf_op jit(solution)/shard_map/ppermute | solution.py:683
  39.7 8.2 %copy-start.2 = (f32[2,8,8,128]{3,2,1,0:T(8,128)S(1)}, f32[2,8,8,128]{3,2,1,0:T(8,128)}, u32[]{:S(2)}) copy-start(f32[2,8,8,128]{3,2,1,0:T(8,128)} %constant.78.clone.rolls) | copy-start | bytes 196612
  39.7 8.2 %copy-start.5 = (bf16[128,128]{1,0:T(8,128)(2,1)S(1)}, bf16[128,128]{1,0:T(8,128)(2,1)}, u32[]{:S(2)}) copy-start(bf16[128,128]{1,0:T(8,128)(2,1)} %constant.79.clone.dxh) | copy-start | bytes 98308
  39.7 8.2 %copy-start.8 = (bf16[128,128]{1,0:T(8,128)(2,1)S(1)}, bf16[128,128]{1,0:T(8,128)(2,1)}, u32[]{:S(2)}) copy-start(bf16[128,128]{1,0:T(8,128)(2,1)} %constant.82.clone.dxtl) | copy-start | bytes 98308
  39.7 8.2 %copy-start.9 = (bf16[128,128]{1,0:T(8,128)(2,1)S(1)}, bf16[128,128]{1,0:T(8,128)(2,1)}, u32[]{:S(2)}) copy-start(bf16[128,128]{1,0:T(8,128)(2,1)} %constant.81.clone.dxth) | copy-start | bytes 98308
  39.7 8.2 %copy-start.21 = (f32[32,1]{1,0:T(8,128)S(1)}, f32[32,1]{1,0:T(8,128)}, u32[]{:S(2)}) copy-start(f32[32,1]{1,0:T(8,128)} %constant.83.clone.wy) | copy-start | bytes 388
  39.7 5.9 %collective-permute-start.6 = (f32[16,128]{1,0:T(8,128)S(1)}, f32[16,128]{1,0:T(8,128)S(1)}, u32[]{:S(2)}, u32[]{:S(2)}) collective-permute-start(f32[16,128]{1,0:T(8,128)S(1)} %get-tuple-element.44), channel_id=1, source_target_pairs={{0,1},{1,2},{2,3},{3,4},{4,5},{5,6},{6,7},{7,8},{8,9},{9,10},{10,1... | collective-permute-start | bytes 24584 | tf_op jit(solution)/shard_map/ppermute | solution.py:683
  42.9 5.0 %collective-permute-start.7 = (f32[16,128]{1,0:T(8,128)S(1)}, f32[16,128]{1,0:T(8,128)S(1)}, u32[]{:S(2)}, u32[]{:S(2)}) collective-permute-start(f32[16,128]{1,0:T(8,128)S(1)} %get-tuple-element.45), channel_id=1, source_target_pairs={{1,0},{2,1},{3,2},{4,3},{5,4},{6,5},{7,6},{8,7},{9,8},{10,9},{11,1... | collective-permute-start | bytes 24584 | tf_op jit(solution)/shard_map/ppermute | solution.py:683
  63.1 28.8 %all-to-all-start.1 = ((f32[64,8,128]{2,1,0:T(8,128)}), f32[64,8,128]{2,1,0:T(8,128)S(1)}, u32[]{:S(2)}, u32[]{:S(2)}) async-start(f32[64,8,128]{2,1,0:T(8,128)} %broadcast_in_dim.40), calls=%async_computation.1 | async-start | bytes 524288 | tf_op jit(solution)/shard_map/all_to_all | solution.py:690
  96.5 3.5 %collective-permute-start.8 = (f32[2,32,128]{2,1,0:T(8,128)S(1)}, f32[2,32,128]{2,1,0:T(8,128)S(1)}, u32[]{:S(2)}, u32[]{:S(2)}) collective-permute-start(f32[2,32,128]{2,1,0:T(8,128)S(1)} %get-tuple-element.49), channel_id=1, source_target_pairs={{0,64},{64,128},{128,192},{192,256},{256,320},{320,384},{384,448},... | collective-permute-start | bytes 98312 | tf_op jit(solution)/shard_map/ppermute | solution.py:683
  98.7 4.7 %collective-permute-start.9 = (f32[2,32,128]{2,1,0:T(8,128)S(1)}, f32[2,32,128]{2,1,0:T(8,128)S(1)}, u32[]{:S(2)}, u32[]{:S(2)}) collective-permute-start(f32[2,32,128]{2,1,0:T(8,128)S(1)} %get-tuple-element.50), channel_id=1, source_target_pairs={{64,0},{128,64},{192,128},{256,192},{320,256},{384,320},{448,384},... | collective-permute-start | bytes 98312 | tf_op jit(solution)/shard_map/ppermute | solution.py:683
  103.4 6.0 %collective-permute-start.10 = (f32[24,128]{1,0:T(8,128)S(1)}, f32[24,128]{1,0:T(8,128)S(1)}, u32[]{:S(2)}, u32[]{:S(2)}) collective-permute-start(f32[24,128]{1,0:T(8,128)S(1)} %get-tuple-element.51), channel_id=1, source_target_pairs={{0,1},{1,2},{2,3},{3,4},{4,5},{5,6},{6,7},{7,8},{8,9},{9,10},{10,1... | collective-permute-start | bytes 36872 | tf_op jit(solution)/shard_map/ppermute | solution.py:683
  107.4 5.0 %collective-permute-start.11 = (f32[24,128]{1,0:T(8,128)S(1)}, f32[24,128]{1,0:T(8,128)S(1)}, u32[]{:S(2)}, u32[]{:S(2)}) collective-permute-start(f32[24,128]{1,0:T(8,128)S(1)} %get-tuple-element.52), channel_id=1, source_target_pairs={{1,0},{2,1},{3,2},{4,3},{5,4},{6,5},{7,6},{8,7},{9,8},{10,9},{11,1... | collective-permute-start | bytes 36872 | tf_op jit(solution)/shard_map/ppermute | solution.py:683
  114.2 3.5 %collective-permute-start.12 = (f32[32,128]{1,0:T(8,128)S(1)}, f32[32,128]{1,0:T(8,128)S(1)}, u32[]{:S(2)}, u32[]{:S(2)}) collective-permute-start(f32[32,128]{1,0:T(8,128)S(1)} %get-tuple-element.54), channel_id=1, source_target_pairs={{0,64},{64,128},{128,192},{192,256},{256,320},{320,384},{384,448},... | collective-permute-start | bytes 49160 | tf_op jit(solution)/shard_map/ppermute | solution.py:683
  116.4 4.5 %collective-permute-start.13 = (f32[32,128]{1,0:T(8,128)S(1)}, f32[32,128]{1,0:T(8,128)S(1)}, u32[]{:S(2)}, u32[]{:S(2)}) collective-permute-start(f32[32,128]{1,0:T(8,128)S(1)} %get-tuple-element.55), channel_id=1, source_target_pairs={{64,0},{128,64},{192,128},{256,192},{320,256},{384,320},{448,384},... | collective-permute-start | bytes 49160 | tf_op jit(solution)/shard_map/ppermute | solution.py:683
  120.9 5.5 %collective-permute-start.14 = (f32[16,128]{1,0:T(8,128)S(1)}, f32[16,128]{1,0:T(8,128)S(1)}, u32[]{:S(2)}, u32[]{:S(2)}) collective-permute-start(f32[16,128]{1,0:T(8,128)S(1)} %get-tuple-element.56), channel_id=1, source_target_pairs={{0,1},{1,2},{2,3},{3,4},{4,5},{5,6},{6,7},{7,8},{8,9},{9,10},{10,1... | collective-permute-start | bytes 24584 | tf_op jit(solution)/shard_map/ppermute | solution.py:683
  124.4 5.0 %collective-permute-start.15 = (f32[16,128]{1,0:T(8,128)S(1)}, f32[16,128]{1,0:T(8,128)S(1)}, u32[]{:S(2)}, u32[]{:S(2)}) collective-permute-start(f32[16,128]{1,0:T(8,128)S(1)} %get-tuple-element.57), channel_id=1, source_target_pairs={{1,0},{2,1},{3,2},{4,3},{5,4},{6,5},{7,6},{8,7},{9,8},{10,9},{11,1... | collective-permute-start | bytes 24584 | tf_op jit(solution)/shard_map/ppermute | solution.py:683

commit v2 on v1

--- a/solution.py
+++ b/solution.py
@@ -119,23 +119,39 @@
     return forward, backward
 
 
+def wide_maps():
+    count = EY + 2
+    forward, backward = line_maps(count)
+    length = 8 * count
+    columns = np.zeros((10 * count, ROWS + 2 * TILE))
+    columns[:, :ROWS] = forward[:, 8 : 8 + ROWS]
+    columns[:, ROWS : ROWS + 2] = forward[:, length : length + 2]
+    columns[:, ROWS + 2 : ROWS + 10] = forward[:, :8]
+    columns[:, ROWS + TILE : ROWS + TILE + 8] = forward[:, length - 8 : length]
+    columns[:, ROWS + TILE + 8 : ROWS + TILE + 10] = forward[:, length + 2 : length + 4]
+    _, own = line_maps(EY)
+    rows = np.zeros((ROWS + 8, 10 * count))
+    rows[:ROWS, 10 : 10 + 10 * EY] = own
+    rows[ROWS, :10] = SINE[8]
+    rows[ROWS + 1, 10 + 10 * EY :] = SINE[1]
+    return columns, rows
+
+
+TILE = 16
 FZ, BZ = line_maps(1)
-FY, BY = line_maps(EY)
-FY = np.pad(FY, ((0, 0), (0, 4)))
+FY, BY = wide_maps()
 FX, BX = line_maps(EX)
 FX = FX[:, :LANES]
 
 
 def denominators():
-    lam_y = np.tile(EIGEN, EY)
+    lam_y = np.tile(EIGEN, EY + 2)
     lam_x = np.tile(EIGEN, EX)
     total = EIGEN[:, None, None] + lam_y[None, :, None] + lam_x[None, None, :]
     return (1.0 / (SCHWARZ_SCALE * total + SCHWARZ_SHIFT)).astype(np.float32)
 
 
 INV_DEN = denominators()
-DX_H, DX_L = split_const(np.kron(np.eye(EX), DERIV.T))
-DXT_H, DXT_L = split_const(np.kron(np.eye(EX), DERIV))
 FY_H, FY_L = split_const(FY)
 BY_H, BY_L = split_const(BY)
 FX_H, FX_L = split_const(FX.T.copy())
@@ -143,18 +159,27 @@
 
 
 def roll_table():
-    table = np.zeros((2, 8, 8, LANES), np.float32)
+    table = np.zeros((2, 8, 8, LANES))
     for kind, matrix in enumerate((DERIV, DERIV.T)):
         for k in range(8):
             for i in range(8):
                 table[kind, k, i, :] = matrix[i, (i + k) % 8]
-    return table
-
-
-ROLLS = roll_table()
+    return table.reshape(2 * 64, LANES)
+
+
 WY = np.tile(WEIGHT, EY)
 WX = np.tile(WEIGHT, EX)
-PLANE_W = (WY[:, None] * WX[None, :]).astype(np.float32)
+AT_ROLLS = ROWS
+AT_DX = AT_ROLLS + 128
+AT_DXT = AT_DX + LANES
+PACKED = np.concatenate(
+    [
+        WY[:, None] * WX[None, :],
+        roll_table(),
+        np.kron(np.eye(EX), DERIV.T),
+        np.kron(np.eye(EX), DERIV),
+    ]
+).astype(np.float32)
 
 
 def inner_count(count):
@@ -250,16 +275,21 @@
     return rows
 
 
-def along_y(values, rolls, kind):
+def along_y(values, packed, kind):
     grouped = values.reshape(8 * EY, 8, LANES)
-    total = rolls[kind, 0][None] * grouped
+    start = AT_ROLLS + 64 * kind
+    total = packed[start : start + 8][None] * grouped
     for k in range(1, 8):
-        total = total + rolls[kind, k][None] * pltpu.roll(grouped, 8 - k, 1)
+        total = total + packed[start + 8 * k : start + 8 * k + 8][None] * pltpu.roll(grouped, 8 - k, 1)
     return total.reshape(8, ROWS, LANES)
 
 
-def along_x(values, table):
-    return right_table(values.reshape(8 * ROWS, LANES), table).reshape(8, ROWS, LANES)
+def along_x(values, packed, kind):
+    start = AT_DXT if kind else AT_DX
+    high, low = parts(packed[start : start + LANES])
+    first, rest = parts(values.reshape(8 * ROWS, LANES))
+    total = dot(first, high) + dot(rest, high) + dot(first, low)
+    return total.reshape(8, ROWS, LANES)
 
 
 def stack(planes):
@@ -271,11 +301,12 @@
     return jnp.where(position == 0, low, jnp.where(position == rows - 1, high, 1.0))
 
 
-def local_operator(values, flux, plane_w, rolls, dx, dxt):
+def local_operator(values, flux, packed):
+    plane_w = packed[0:ROWS]
     gz = along_z([values[i] for i in range(8)], DERIV)
     fz = along_z([flux[i] * gz[i] for i in range(8)], DERIV.T)
-    total = along_y(flux * along_y(values, rolls, 0), rolls, 1)
-    total = total + along_x(flux * along_x(values, dx), dxt)
+    total = along_y(flux * along_y(values, packed, 0), packed, 1)
+    total = total + along_x(flux * along_x(values, packed, 0), packed, 1)
     planes = [
         total[i] + fz[i] + (HELM_COEF * 0.125 * float(WEIGHT[i])) * (plane_w * values[i])
         for i in range(8)
@@ -283,38 +314,34 @@
     return stack(planes)
 
 
-def add_faces(own, low_z, high_z, low_y, high_y):
-    row = lax.broadcasted_iota(jnp.int32, (ROWS, LANES), 0)
-    planes = []
-    for i in range(8):
-        plane = own[i]
-        first = low_y[i : i + 1]
-        last = high_y[i : i + 1]
-        if i == 0:
-            plane = plane + low_z
-            first = first + low_y[8:9]
-            last = last + high_y[8:9]
-        if i == 7:
-            plane = plane + high_z
-            first = first + low_y[9:10]
-            last = last + high_y[9:10]
-        plane = plane + jnp.where(row == 0, first, jnp.where(row == ROWS - 1, last, 0.0))
-        planes.append(plane)
+def add_planes(own, low_z, high_z):
+    planes = [own[i] for i in range(8)]
+    planes[0] = planes[0] + low_z
+    planes[7] = planes[7] + high_z
     return stack(planes)
 
 
-def schwarz(ext, tables, inv_den, near, out_ref, low_ref, high_ref):
+def schwarz(own, low_z, high_z, low_y, high_y, tables, inv_den, near, out_ref, low_ref, high_ref):
     fy, fx, bx, by = tables
-    spectral = along_z([ext[i] for i in range(12)], FZ)
-    spectral = [left_table(fy, plane) for plane in spectral]
+    middle = along_z([own[i] for i in range(8)] + [low_z[0], low_z[1], high_z[0], high_z[1]], FZ)
+    below = along_z([low_y[i] for i in range(12)], FZ)
+    above = along_z([high_y[i] for i in range(12)], FZ)
+    spectral = [
+        left_table(fy, jnp.concatenate([middle[i], below[i], above[i]], axis=0)) for i in range(10)
+    ]
+    step = 10 * (EY + 2)
     wide = right_table(jnp.concatenate(spectral, axis=0), fx)
-    wide = wide * inv_den[...].reshape(10 * 10 * EY, 10 * EX)
+    wide = wide * inv_den[...].reshape(10 * step, 10 * EX)
     back = right_table(wide, bx)
-    step = 10 * EY
     back = [left_table(by, back[step * i : step * (i + 1)]) for i in range(10)]
     planes = along_z(back, BZ)
     edge = edge_rows(ROWS, near[2], near[3])
-    planes = [plane * edge for plane in planes]
+    row = lax.broadcasted_iota(jnp.int32, (ROWS, LANES), 0)
+    for i in range(8):
+        first = (1.0 - near[2]) * planes[i][ROWS : ROWS + 1]
+        last = (1.0 - near[3]) * planes[i][ROWS + 1 : ROWS + 2]
+        other = jnp.where(row == 0, first, jnp.where(row == ROWS - 1, last, 0.0))
+        planes[i] = planes[i][0:ROWS] * edge + other
     planes[0] = planes[0] * near[0]
     planes[7] = planes[7] * near[1]
     for i in range(8):
@@ -323,29 +350,18 @@
     high_ref[...] = planes[7]
 
 
-def fill_ext(ext, own, low_z, high_z, low_y, high_y):
-    for i in range(8):
-        ext[i, 0:ROWS] = own[i]
-    for i in range(2):
-        ext[8 + i, 0:ROWS] = low_z[i]
-        ext[10 + i, 0:ROWS] = high_z[i]
-    zeros = jnp.zeros((4, LANES), F32)
-    for i in range(12):
-        ext[i, ROWS : ROWS + 8] = jnp.concatenate(
-            [low_y[2 * i : 2 * i + 2], high_y[2 * i : 2 * i + 2], zeros], axis=0
-        )
-
-
-def partition_total(ext, near):
-    total = near[0] * ext[0] + near[1] * ext[7] + 0.5 * (ext[9] + ext[10])
-    for i in range(1, 7):
-        total = total + ext[i]
-    row = lax.broadcasted_iota(jnp.int32, (ROWS + 8, LANES), 0)
-    weight = jnp.where(row < ROWS, 1.0, 0.0)
-    weight = jnp.where(row == 0, near[2], weight)
-    weight = jnp.where(row == ROWS - 1, near[3], weight)
-    weight = jnp.where((row == ROWS + 1) | (row == ROWS + 2), 0.5, weight)
-    return jnp.sum(total * weight)
+def partition_total(own, low_z, high_z, low_y, high_y, near):
+    def planes(array):
+        total = near[0] * array[0] + near[1] * array[7]
+        for i in range(1, 7):
+            total = total + array[i]
+        return total
+
+    total = planes(own) + 0.5 * (low_z[1] + high_z[0])
+    below = planes(low_y) + 0.5 * (low_y[9] + low_y[10])
+    above = planes(high_y) + 0.5 * (high_y[9] + high_y[10])
+    faces = 0.5 * (below[9:10] + above[0:1])
+    return jnp.sum(total * edge_rows(ROWS, near[2], near[3])) + jnp.sum(faces)
 
 
 def lane_row(entries):
@@ -356,17 +372,16 @@
     return row
 
 
-def advect_kernel(lev, vel, src, plane_w, rolls, dxh, dxl, b_ref, l_ref, zlo, zhi):
-    dx = (dxh, dxl)
+def advect_kernel(lev, vel, src, packed, b_ref, l_ref, zlo, zhi):
     level = lev[...]
     v0, v1, v2 = vel[0], vel[1], vel[2]
     gz = stack(along_z([level[i] for i in range(8)], DERIV))
-    advect = v0 * gz + v1 * along_y(level, rolls, 0) + v2 * along_x(level, dx)
+    advect = v0 * gz + v1 * along_y(level, packed, 0) + v2 * along_x(level, packed, 0)
     moved = level - (2.0 * TIME_STEP) * advect
     diverge = stack(along_z([v0[i] for i in range(8)], DERIV))
-    diverge = diverge + along_y(v1, rolls, 0) + along_x(v2, dx)
+    diverge = diverge + along_y(v1, packed, 0) + along_x(v2, packed, 0)
     force = src[...] - (2.0 * TIME_STEP) * diverge
-    weights = plane_w[...]
+    weights = packed[0:ROWS]
     for i in range(8):
         mass = (0.125 * float(WEIGHT[i])) * weights
         term = mass * force[i]
@@ -383,34 +398,49 @@
             zhi[2] = moved_i
 
 
-def rim_kernel(kinds, *refs):
-    count = len(kinds)
+def rim_kernel(count, *refs):
     own = refs[:count]
     low_z, high_z, low_y, high_y = refs[count:]
-    at = 0
-    for (width, start), array in zip(kinds, own, strict=True):
+    zeros = jnp.zeros((TILE - 10 - (count - 1), LANES), F32)
+
+    def rows(planes, level, at, far):
+        pieces = [planes[at, ROWS - 10 : ROWS] if far else planes[at, 0:10]]
+        if count == 2:
+            if level is None:
+                pieces.append(jnp.zeros((1, LANES), F32))
+            else:
+                array, index = level
+                pieces.append(array[index, ROWS - 1 : ROWS] if far else array[index, 0:1])
+        return jnp.concatenate(pieces + [zeros], axis=0)
+
+    for far, out in ((False, low_y), (True, high_y)):
         for i in range(8):
-            low_y[at : at + width] = array[i, 0:width]
-            high_y[at : at + width] = array[i, ROWS - width : ROWS]
-            at += width
-        for planes in (low_z, high_z):
-            for i in range(width):
-                low_y[at : at + width] = planes[start + i, 0:width]
-                high_y[at : at + width] = planes[start + i, ROWS - width : ROWS]
-                at += width
-    rest = low_y.shape[0] - at
-    if rest:
-        low_y[at : at + rest] = jnp.zeros((rest, LANES), F32)
-        high_y[at : at + rest] = jnp.zeros((rest, LANES), F32)
+            out[i] = rows(own[0], (own[-1], i), i, far)
+        for i in range(2):
+            out[8 + i] = rows(low_z, (low_z, 2) if i == 1 else None, i, far)
+            out[10 + i] = rows(high_z, (high_z, 2) if i == 0 else None, i, far)
 
 
 def level_kernel(
-    near, solid, spread, inv_mass, plane_w, inv_den, fyh, fyl, fxh, fxl, bxh, bxl, byh, byl,
-    b, l, zlo, zhi, ylo, yhi, level_ref, flux_ref, w_ref, wlo, whi, stat, ext,
+    near, solid, spread, inv_mass, packed, inv_den, fyh, fyl, fxh, fxl, bxh, bxl, byh, byl,
+    b, l, zlo, zhi, ylo, yhi, level_ref, flux_ref, w_ref, wlo, whi, stat,
 ):
-    own = add_faces(
-        l[...], zlo[2], zhi[2], ylo[24:34], yhi[24:34]
-    )
+    row = lax.broadcasted_iota(jnp.int32, (ROWS, LANES), 0)
+    planes = []
+    for i in range(8):
+        plane = l[i]
+        first = ylo[i, 10:11]
+        last = yhi[i, 10:11]
+        if i == 0:
+            plane = plane + zlo[2]
+            first = first + ylo[9, 10:11]
+            last = last + yhi[9, 10:11]
+        if i == 7:
+            plane = plane + zhi[2]
+            first = first + ylo[10, 10:11]
+            last = last + yhi[10, 10:11]
+        planes.append(plane + jnp.where(row == 0, first, jnp.where(row == ROWS - 1, last, 0.0)))
+    own = stack(planes)
     row = lax.broadcasted_iota(jnp.int32, (8, ROWS, LANES), 1)
     lane = lax.broadcasted_iota(jnp.int32, (8, ROWS, LANES), 2)
     before = jnp.where((row % 8 == 0) & (row > 0), pltpu.roll(own, 1, 1), 0.0)
@@ -425,6 +455,7 @@
         [jnp.broadcast_to(1.0 - (1.0 - SOLID_FACTOR) * in_solid[e : e + 1], (8, LANES)) for e in range(EY)],
         axis=0,
     )
+    plane_w = packed[0:ROWS]
     total = jnp.zeros((ROWS, LANES), F32)
     for i in range(8):
         scale = 1.0 / float(WEIGHT[i])
@@ -437,29 +468,26 @@
         liquid = jax.nn.sigmoid(plane * (1.0 / LEVEL_WIDTH))
         coef = (GAS_RATIO - (GAS_RATIO - 1.0) * liquid) * open_part
         total = total + coef
-        flux_ref[i] = (0.5 * float(WEIGHT[i])) * (coef * plane_w[...])
+        flux_ref[i] = (0.5 * float(WEIGHT[i])) * (coef * plane_w)
     kbar = jnp.sum(total) * (1.0 / (8 * ROWS * LANES))
-    fill_ext(ext, b, zlo, zhi, ylo, yhi)
-    stat[...] = lane_row([kbar, partition_total(ext, near)])
-    schwarz(ext, ((fyh, fyl), (fxh, fxl), (bxh, bxl), (byh, byl)), inv_den, near, w_ref, wlo, whi)
+    stat[...] = lane_row([kbar, partition_total(b, zlo, zhi, ylo, yhi, near)])
+    tables = ((fyh, fyl), (fxh, fxl), (bxh, bxl), (byh, byl))
+    schwarz(b, zlo, zhi, ylo, yhi, tables, inv_den, near, w_ref, wlo, whi)
 
 
 def schwarz_kernel(
     near, inv_den, fyh, fyl, fxh, fxl, bxh, bxl, byh, byl, b, zlo, zhi, ylo, yhi,
-    w_ref, wlo, whi, ext,
+    w_ref, wlo, whi,
 ):
-    fill_ext(ext, b, zlo, zhi, ylo, yhi)
-    schwarz(ext, ((fyh, fyl), (fxh, fxl), (bxh, bxl), (byh, byl)), inv_den, near, w_ref, wlo, whi)
-
-
-def galerkin_kernel(
-    zt, yt, wy, plane_w, rolls, dxh, dxl, dxth, dxtl, stat_in, flux, w, zlo, zhi, ylo, yhi,
-    zl_ref, stat,
-):
-    local = add_faces(w[...], zlo[...], zhi[...], ylo[...], yhi[...])
+    tables = ((fyh, fyl), (fxh, fxl), (bxh, bxl), (byh, byl))
+    schwarz(b, zlo, zhi, ylo, yhi, tables, inv_den, near, w_ref, wlo, whi)
+
+
+def galerkin_kernel(zt, yt, wy, packed, stat_in, flux, w, zlo, zhi, zl_ref, stat):
+    local = add_planes(w, zlo[...], zhi[...])
     zl_ref[...] = local
     fluxes = flux[...]
-    applied = local_operator(local, fluxes, plane_w[...], rolls, (dxh, dxl), (dxth, dxtl))
+    applied = local_operator(local, fluxes, packed)
 
     def combine(index, planes):
         total = zt[index, 0] * planes[0]
@@ -519,7 +547,7 @@
     lanes = LANES
     wide[...] = jnp.zeros((LANES, LANES), F32)
     for i in range(8):
-        wide[0:count] = gathered[:, i, :]
+        wide[0:count] = gathered[count * i : count * (i + 1)]
         values[i] = wide[...].T
     sub = lax.broadcasted_iota(jnp.int32, (8, lanes), 0)
     lane = lax.broadcasted_iota(jnp.int32, (8, lanes), 1)
@@ -620,12 +648,12 @@
 
 
 def apply_kernel(
-    zt, yt, plane_w, rolls, dxh, dxl, dxth, dxtl, coarse, flux, b, zl,
+    zt, yt, packed, coarse, flux, b, zl,
     z_ref, y_ref, ylo, yhi, stat,
 ):
     field = add_coarse(zl[...], zt, yt, coarse, 0)
     z_ref[...] = field
-    applied = local_operator(field, flux[...], plane_w[...], rolls, (dxh, dxl), (dxth, dxtl))
+    applied = local_operator(field, flux[...], packed)
     y_ref[...] = applied
     ylo[...] = applied[0:2]
     yhi[...] = applied[6:8]
@@ -633,13 +661,13 @@
 
 
 def second_kernel(
-    zt, yt, plane_w, rolls, dxh, dxl, dxth, dxtl, coarse, flux, b, y, w, zlo, zhi, ylo, yhi,
+    zt, yt, packed, coarse, flux, b, y, w, zlo, zhi,
     stat_in, q_ref, stat,
 ):
-    local = add_faces(w[...], zlo[...], zhi[...], ylo[...], yhi[...])
+    local = add_planes(w, zlo[...], zhi[...])
     field = add_coarse(local, zt, yt, coarse, 16)
     q_ref[...] = field
-    applied = local_operator(field, flux[...], plane_w[...], rolls, (dxh, dxl), (dxth, dxtl))
+    applied = local_operator(field, flux[...], packed)
     sums = [0.0, 0.0, jnp.sum(b[...] * field), jnp.sum(y[...] * field), jnp.sum(field * applied)]
     stat[...] = stat_in[...] + lane_row(sums)
 
@@ -683,13 +711,6 @@
     return lax.ppermute(high_face, axis, forward), lax.ppermute(low_face, axis, backward)
 
 
-def gather_tiles(row, count_gx, count_gy):
-    tile = jnp.broadcast_to(row, (count_gx, LANES))
-    tile = lax.all_to_all(tile, "gx", 0, 0, tiled=True)
-    wide = jnp.broadcast_to(tile[None], (count_gy, count_gx, LANES))
-    return lax.all_to_all(wide, "gy", 0, 0, tiled=True)
-
-
 def body(level_set, velocity, source, wick_solid):
     block = level_set.shape
     count_gx = lax.axis_size("gx")
@@ -707,57 +728,41 @@
     zt = lax.dynamic_index_in_dim(jnp.asarray(Z_TABLE), case(index_gx, count_gx), 0, False)
     yt = lax.dynamic_index_in_dim(jnp.asarray(Y_TABLE), case(index_gy, count_gy), 0, False)
     place = jnp.stack([index_gx, index_gy]).astype(jnp.int32)
-    plane_w = jnp.asarray(PLANE_W)
-    rolls = jnp.asarray(ROLLS)
-    dx = (jnp.asarray(DX_H), jnp.asarray(DX_L))
-    dxt = (jnp.asarray(DXT_H), jnp.asarray(DXT_L))
+    packed = jnp.asarray(PACKED)
     wy = jnp.asarray(WY.astype(np.float32)[:, None])
-    operator = (plane_w, rolls, *dx, *dxt)
     solver = (INV_DEN, FY_H, FY_L, FX_H, FX_L, BX_H, BX_L, BY_H, BY_L)
     solver = tuple(jnp.asarray(table) for table in solver)
     face = (ROWS, LANES)
-    ext = VMEM((12, ROWS + 8, LANES), F32)
+    rim = (12, TILE, LANES)
     solid = wick_solid.reshape(EY, EX).astype(F32)
 
     b, l, zlo, zhi = run(
         advect_kernel,
         [block, block, (3, *face), (3, *face)],
         [],
-        [level_set, velocity, source, plane_w, rolls, *dx],
+        [level_set, velocity, source, packed],
     )
     zlo, zhi = shift("gx", zlo, zhi)
-    ylo, yhi = run(
-        functools.partial(rim_kernel, ((2, 0), (1, 2))), [(40, LANES)] * 2, [], [b, l, zlo, zhi]
-    )
+    ylo, yhi = run(functools.partial(rim_kernel, 2), [rim, rim], [], [b, l, zlo, zhi])
     ylo, yhi = shift("gy", ylo, yhi)
     level_new, flux, w, wlo, whi, stat = run(
         level_kernel,
         [block, block, block, face, face, (1, LANES)],
         [near],
         [
-            solid, jnp.asarray(SPREAD), jnp.asarray(INV_MASS), plane_w, *solver,
+            solid, jnp.asarray(SPREAD), jnp.asarray(INV_MASS), packed, *solver,
             b, l, zlo, zhi, ylo, yhi,
         ],
-        [ext],
-    )
-
-    def exchange_one(w, wlo, whi):
-        zlo, zhi = shift("gx", wlo, whi)
-        ylo, yhi = run(
-            functools.partial(rim_kernel, ((1, 0),)), [(16, LANES)] * 2, [],
-            [w, zlo[None], zhi[None]],
-        )
-        ylo, yhi = shift("gy", ylo, yhi)
-        return zlo, zhi, ylo, yhi
-
-    faces = exchange_one(w, wlo, whi)
+    )
+    zlo, zhi = shift("gx", wlo, whi)
     zl, stat = run(
         galerkin_kernel,
         [block, (1, LANES)],
         [zt],
-        [yt, wy, *operator, stat, flux, w, *faces],
-    )
-    gathered = gather_tiles(stat, count_gx, count_gy)
+        [yt, wy, packed, stat, flux, w, zlo, zhi],
+    )
+    wide = jnp.broadcast_to(stat, (count_gx * count_gy, LANES))
+    gathered = lax.all_to_all(wide, ("gx", "gy"), 0, 0, tiled=True)
     (coarse,) = run(
         functools.partial(coarse_kernel, count_gy),
         [(32, LANES)],
@@ -769,26 +774,23 @@
         apply_kernel,
         [block, block, (2, *face), (2, *face), (1, LANES)],
         [zt],
-        [yt, *operator, coarse, flux, b, zl],
+        [yt, packed, coarse, flux, b, zl],
     )
     zlo, zhi = shift("gx", zlo, zhi)
-    ylo, yhi = run(
-        functools.partial(rim_kernel, ((2, 0),)), [(24, LANES)] * 2, [], [y, zlo, zhi]
-    )
+    ylo, yhi = run(functools.partial(rim_kernel, 1), [rim, rim], [], [y, zlo, zhi])
     ylo, yhi = shift("gy", ylo, yhi)
     w, wlo, whi = run(
         schwarz_kernel,
         [block, face, face],
         [near],
         [*solver, y, zlo, zhi, ylo, yhi],
-        [ext],
-    )
-    faces = exchange_one(w, wlo, whi)
+    )
+    zlo, zhi = shift("gx", wlo, whi)
     q, sums = run(
         second_kernel,
         [block, (1, LANES)],
         [zt],
-        [yt, *operator, coarse, flux, b, y, w, *faces, sums],
+        [yt, packed, coarse, flux, b, y, w, zlo, zhi, sums],
     )
     tile = jnp.broadcast_to(sums, (count_gx, LANES))
     tile = lax.all_to_all(tile, "gx", 0, 0, tiled=True)

time: 164 us -> 140 us (0.85)
  blocking collectives: 44.2 us -> 28.3 us
  starting transfers between devices: 57.6 us -> 51.1 us
    all_to_all x1 -> x0, blocking collectives: 12.9 us -> none  [gather_tiles(): tile = lax.all_to_all(tile, 'gx', 0, 0, tiled=True)]
    ppermute x8 -> x6, starting transfers between devices: 28.9 us -> 22.7 us  [shift(): lax.ppermute(high_face, axis, forward)]
    ppermute x8 -> x6, waiting for transfers between devices: 26 us -> 21 us  [shift(): lax.ppermute(low_face, axis, backward)]
    all_to_all x1, waiting for transfers between devices: 13.1 us -> 17.4 us  [body(): gathered = lax.all_to_all(wide, ('gx', 'gy'), 0, 0, tiled=True)]
    all_to_all x1, blocking collectives: 21.4 us -> 17.2 us  [body(): wide = lax.all_to_all(wide, 'gy', 0, 0, tiled=True)]
    ppermute x8 -> x6, starting transfers between devices: 13.1 us -> 9.31 us  [shift(): lax.ppermute(low_face, axis, backward)]
    all_to_all x1, starting transfers between devices: 15.6 us -> 19.1 us  [body(): gathered = lax.all_to_all(wide, ('gx', 'gy'), 0, 0, tiled=True)]
    unnamed x48 -> x36, local copies, waits for them, and re-layouts: 5.24 us -> 4.46 us
  transfers between devices with their start and end apart: 17 -> 13, of which waited for: 9 -> 7; matrix products, arithmetic and copies ran while one was open for 1% -> 1% of each run, Pallas kernels for 0% -> 0%
where the time goes in v2:
time: 140 us
  starting transfers between devices  51.1 us (36%)
  waiting for transfers between devices  38.4 us (27%)
  blocking collectives  28.3 us (20%)
  Pallas kernels  13.7 us (10%)
  local copies, waits for them, and re-layouts  6.94 us (5%)
    ppermute x6, starting transfers between devices, shift(): lax.ppermute(high_face, axis, forward)  22.7 us
    ppermute x6, waiting for transfers between devices, shift(): lax.ppermute(low_face, axis, backward)  21 us
    all_to_all x1, starting transfers between devices, body(): gathered = lax.all_to_all(wide, ('gx', 'gy'), 0, 0, tiled=True)  19.1 us
    all_to_all x1, waiting for transfers between devices, body(): gathered = lax.all_to_all(wide, ('gx', 'gy'), 0, 0, tiled=True)  17.4 us
    all_to_all x1, blocking collectives, body(): wide = lax.all_to_all(wide, 'gy', 0, 0, tiled=True)  17.2 us
    pallas_call x10, Pallas kernels, call(): pl.pallas_call(kernel, out_shape=[jax.ShapeDtypeStruct(out, F32) for out...  13.7 us
    all_to_all x1, blocking collectives, body(): tile = lax.all_to_all(tile, 'gx', 0, 0, tiled=True)  11.1 us
    ppermute x6, starting transfers between devices, shift(): lax.ppermute(low_face, axis, backward)  9.31 us
  transfers between devices with their start and end apart: 13, of which 7 were waited for; matrix products, arithmetic and copies ran while one was open for 1% of the time, Pallas kernels for 0%

profile of v2, /device:TPU:1, one launch (start us, length us, event | category | flops | bytes accessed | tf_op | source)
XLA Modules:
  0.0 139.6 jit_solution(16402450490596791704)
XLA Ops:
  0.6 0.0 copy-start
  0.6 0.9 copy-done
  1.6 1.0 copy-done.3
  2.6 0.9 copy-done.8
  3.5 0.9 copy-done.9
  4.4 0.5 shard_map.194
  4.9 4.8 %collective-permute-start = (f32[3,32,128]{2,1,0:T(8,128)S(1)}, f32[3,32,128]{2,1,0:T(8,128)S(1)}, u32[]{:S(2)}, u32[]{:S(2)}) collective-permute-start(f32[3,32,128]{2,1,0:T(8,128)S(1)} %get-tuple-element.30), channel_id=1, source_target_pairs={{0,64},{64,128},{128,192},{192,256},{256,320},{320,384},{384,448},... | collective-permute-start | bytes 147464 | tf_op jit(solution)/shard_map/ppermute | solution.py:711
  9.7 1.3 collective-permute-start.1
  11.0 0.0 copy-start.17
  11.1 0.7 copy-done.17
  11.7 0.0 copy-start.13
  11.7 0.0 copy-start.14
  11.8 0.9 dynamic-slice_bitcast_fusion.yt
  12.6 0.0 collective-permute-done.refs_2_.zlo
  12.6 2.6 %collective-permute-done.1.refs_3_.zhi = f32[3,32,128]{2,1,0:T(8,128)S(1)} collective-permute-done((f32[3,32,128]{2,1,0:T(8,128)S(1)}, f32[3,32,128]{2,1,0:T(8,128)S(1)}, u32[]{:S(2)}, u32[]{:S(2)}) %collective-permute-start.1) | collective-permute-done | bytes 49184 | tf_op jit(solution)/shard_map/ppermute | solution.py:711
  15.3 5.0 %collective-permute-start.2 = (f32[12,16,128]{2,1,0:T(8,128)S(1)}, f32[12,16,128]{2,1,0:T(8,128)S(1)}, u32[]{:S(2)}, u32[]{:S(2)}) collective-permute-start(f32[12,16,128]{2,1,0:T(8,128)S(1)} %get-tuple-element.32), channel_id=1, source_target_pairs={{0,1},{1,2},{2,3},{3,4},{4,5},{5,6},{6,7},{7,8},{8,9},{9,10},{10,1... | collective-permute-start | bytes 294920 | tf_op jit(solution)/shard_map/ppermute | solution.py:711
  20.2 2.2 %collective-permute-start.3 = (f32[12,16,128]{2,1,0:T(8,128)S(1)}, f32[12,16,128]{2,1,0:T(8,128)S(1)}, u32[]{:S(2)}, u32[]{:S(2)}) collective-permute-start(f32[12,16,128]{2,1,0:T(8,128)S(1)} %get-tuple-element.33), channel_id=1, source_target_pairs={{1,0},{2,1},{3,2},{4,3},{5,4},{6,5},{7,6},{8,7},{9,8},{10,9},{11,1... | collective-permute-start | bytes 294920 | tf_op jit(solution)/shard_map/ppermute | solution.py:711
  22.5 0.0 copy-start.16
  22.5 0.1 pad_maximum_fusion.near
  22.6 3.6 %collective-permute-done.3.yhi = f32[12,16,128]{2,1,0:T(8,128)S(1)} collective-permute-done((f32[12,16,128]{2,1,0:T(8,128)S(1)}, f32[12,16,128]{2,1,0:T(8,128)S(1)}, u32[]{:S(2)}, u32[]{:S(2)}) %collective-permute-start.3) | collective-permute-done | bytes 98336 | tf_op jit(solution)/shard_map/ppermute | solution.py:711
  26.3 2.7 %shard_map.196 = (f32[8,32,128]{2,1,0:T(8,128)}, f32[8,32,128]{2,1,0:T(8,128)S(1)}, f32[8,32,128]{2,1,0:T(8,128)S(1)}, f32[32,128]{1,0:T(8,128)S(1)}, f32[32,128]{1,0:T(8,128)S(1)}, /*index=5*/f32[1,128]{1,0:T(1,128)S(1)}) custom-call(f32[4]{0:T(128)S(1)} %pad_maximum_fusion.near, f32[4,16]{1,0:T(4,128)S(1)} %convert_bitcast_fusion.solid, ...), custom_call_target="tpu_custom_call" | custom-call | flops 1000000 | bytes 852992 | tf_op jit(solution)/shard_map/pallas_call | solution.py:691
  29.0 4.1 %collective-permute-start.4 = (f32[32,128]{1,0:T(8,128)S(1)}, f32[32,128]{1,0:T(8,128)S(1)}, u32[]{:S(2)}, u32[]{:S(2)}) collective-permute-start(f32[32,128]{1,0:T(8,128)S(1)} %get-tuple-element.38), channel_id=1, source_target_pairs={{0,64},{64,128},{128,192},{192,256},{256,320},{320,384},{384,448},... | collective-permute-start | bytes 49160 | tf_op jit(solution)/shard_map/ppermute | solution.py:711
  33.1 1.3 collective-permute-start.5
  34.4 0.7 dynamic-slice_bitcast_fusion.1
  35.1 0.1 copy.32.zt
  35.2 0.0 collective-permute-done.4.zlo
  35.2 4.3 %collective-permute-done.5.zhi = f32[32,128]{1,0:T(8,128)S(1)} collective-permute-done((f32[32,128]{1,0:T(8,128)S(1)}, f32[32,128]{1,0:T(8,128)S(1)}, u32[]{:S(2)}, u32[]{:S(2)}) %collective-permute-start.5) | collective-permute-done | bytes 16416 | tf_op jit(solution)/shard_map/ppermute | solution.py:711
  39.5 1.5 %shard_map.197 = (f32[8,32,128]{2,1,0:T(8,128)S(1)}, f32[1,128]{1,0:T(1,128)S(1)}) custom-call(f32[16,8]{1,0:T(8,128)S(1)} %copy.32.zt, f32[3,32,128]{2,1,0:T(8,128)S(1)} %dynamic-slice_bitcast_fusion.yt, f32[32,1]{1,0:T(8,128)S(1)} %copy-done.15, f32[416,128]{1,0:T(8,128)S(1)} %copy-done.1, f32[1,128]{1,0:T(1,128)S(1)} %get-tuple-element.35.stat_in, ...), custom_call_target="tpu_custom_call" | custom-call | flops 1000000 | bytes 263168 | tf_op jit(solution)/shard_map/pallas_call | solution.py:691
  40.9 0.8 broadcast_in_dim.6
  41.8 19.1 %all-to-all-start = ((f32[512,1,128]{2,1,0:T(1,128)}), f32[512,1,128]{2,1,0:T(1,128)S(1)}, u32[]{:S(2)}, u32[]{:S(2)}) async-start(f32[512,1,128]{2,1,0:T(1,128)} %broadcast_in_dim.6), calls=%async_computation | async-start | bytes 524288 | tf_op jit(solution)/shard_map/all_to_all | solution.py:765
  60.9 0.1 pad_add_fusion.place
  61.0 17.4 %all-to-all-done = f32[512,1,128]{2,1,0:T(1,128)S(1)} async-done(((f32[512,1,128]{2,1,0:T(1,128)}), f32[512,1,128]{2,1,0:T(1,128)S(1)}, u32[]{:S(2)}, u32[]{:S(2)}) %all-to-all-start) | async-done | bytes 262176 | tf_op jit(solution)/shard_map/all_to_all | solution.py:765
  78.4 3.3 %shard_map.198.coarse = f32[32,128]{1,0:T(8,128)S(1)} custom-call(s32[2]{0:T(128)S(1)} %pad_add_fusion.place, f32[512,128]{1,0:T(8,128)S(1)} %bitcast.17), custom_call_target="tpu_custom_call" | custom-call | flops 1000000 | bytes 32768 | tf_op jit(solution)/shard_map/pallas_call | solution.py:691
  81.7 1.3 shard_map.199
  83.0 2.7 %collective-permute-start.6 = (f32[2,32,128]{2,1,0:T(8,128)S(1)}, f32[2,32,128]{2,1,0:T(8,128)S(1)}, u32[]{:S(2)}, u32[]{:S(2)}) collective-permute-start(f32[2,32,128]{2,1,0:T(8,128)S(1)} %get-tuple-element.43), channel_id=1, source_target_pairs={{0,64},{64,128},{128,192},{192,256},{256,320},{320,384},{384,448},... | collective-permute-start | bytes 98312 | tf_op jit(solution)/shard_map/ppermute | solution.py:711
  85.7 1.3 collective-permute-start.7
  87.0 3.3 %collective-permute-done.7.refs_2_.zhi = f32[2,32,128]{2,1,0:T(8,128)S(1)} collective-permute-done((f32[2,32,128]{2,1,0:T(8,128)S(1)}, f32[2,32,128]{2,1,0:T(8,128)S(1)}, u32[]{:S(2)}, u32[]{:S(2)}) %collective-permute-start.7) | collective-permute-done | bytes 32800 | tf_op jit(solution)/shard_map/ppermute | solution.py:711
  90.4 3.7 %collective-permute-start.8 = (f32[12,16,128]{2,1,0:T(8,128)S(1)}, f32[12,16,128]{2,1,0:T(8,128)S(1)}, u32[]{:S(2)}, u32[]{:S(2)}) collective-permute-start(f32[12,16,128]{2,1,0:T(8,128)S(1)} %get-tuple-element.45), channel_id=1, source_target_pairs={{0,1},{1,2},{2,3},{3,4},{4,5},{5,6},{6,7},{7,8},{8,9},{9,10},{10,1... | collective-permute-start | bytes 294920 | tf_op jit(solution)/shard_map/ppermute | solution.py:711
  94.1 1.9 %collective-permute-start.9 = (f32[12,16,128]{2,1,0:T(8,128)S(1)}, f32[12,16,128]{2,1,0:T(8,128)S(1)}, u32[]{:S(2)}, u32[]{:S(2)}) collective-permute-start(f32[12,16,128]{2,1,0:T(8,128)S(1)} %get-tuple-element.46), channel_id=1, source_target_pairs={{1,0},{2,1},{3,2},{4,3},{5,4},{6,5},{7,6},{8,7},{9,8},{10,9},{11,1... | collective-permute-start | bytes 294920 | tf_op jit(solution)/shard_map/ppermute | solution.py:711
  96.0 4.0 %collective-permute-done.9.yhi = f32[12,16,128]{2,1,0:T(8,128)S(1)} collective-permute-done((f32[12,16,128]{2,1,0:T(8,128)S(1)}, f32[12,16,128]{2,1,0:T(8,128)S(1)}, u32[]{:S(2)}, u32[]{:S(2)}) %collective-permute-start.9) | collective-permute-done | bytes 98336 | tf_op jit(solution)/shard_map/ppermute | solution.py:711
  100.0 2.2 %shard_map.201 = (f32[8,32,128]{2,1,0:T(8,128)S(1)}, f32[32,128]{1,0:T(8,128)S(1)}, f32[32,128]{1,0:T(8,128)S(1)}) custom-call(f32[4]{0:T(128)S(1)} %pad_maximum_fusion.near, f32[10,60,160]{2,1,0:T(8,128)S(1)} %copy-done.2, bf16[60,64]{1,0:T(8,128)(2,1)S(1)} %copy-done.11, bf16[60,64]{1,0:T(8,128)(2,1)S(1)} %copy-done.10, bf16[128,160]{1,0:T(8,128)(2,1)S(1)} %copy-done.5, ...), custom_call_target="tpu_custom_call" | custom-call | flops 1000000 | bytes 327680 | tf_op jit(solution)/shard_map/pallas_call | solution.py:691
  102.2 2.4 %collective-permute-start.10 = (f32[32,128]{1,0:T(8,128)S(1)}, f32[32,128]{1,0:T(8,128)S(1)}, u32[]{:S(2)}, u32[]{:S(2)}) collective-permute-start(f32[32,128]{1,0:T(8,128)S(1)} %get-tuple-element.48), channel_id=1, source_target_pairs={{0,64},{64,128},{128,192},{192,256},{256,320},{320,384},{384,448},... | collective-permute-start | bytes 49160 | tf_op jit(solution)/shard_map/ppermute | solution.py:711
  104.6 1.3 collective-permute-start.11
  105.9 3.2 %collective-permute-done.11.zhi = f32[32,128]{1,0:T(8,128)S(1)} collective-permute-done((f32[32,128]{1,0:T(8,128)S(1)}, f32[32,128]{1,0:T(8,128)S(1)}, u32[]{:S(2)}, u32[]{:S(2)}) %collective-permute-start.11) | collective-permute-done | bytes 16416 | tf_op jit(solution)/shard_map/ppermute | solution.py:711
  109.1 1.3 shard_map.202
  110.4 11.1 %all_to_all.22 = f32[8,1,128]{2,1,0:T(1,128)S(1)} all-to-all(f32[8,1,128]{2,1,0:T(1,128)S(1)} %broadcast_in_dim.7), channel_id=1, replica_groups=mesh['gx'=8,'gy'=64] {'gx'}, dimensions={0} | all-to-all | bytes 8192 | tf_op jit(solution)/shard_map/all_to_all | solution.py:796
  121.6 17.2 %all_to_all.23 = f32[64,1,128]{2,1,0:T(1,128)S(1)} all-to-all(f32[64,1,128]{2,1,0:T(1,128)S(1)} %broadcast_in_dim.8), channel_id=1, replica_groups=mesh['gx'=8,'gy'=64] {'gy'}, dimensions={0} | all-to-all | bytes 65536 | tf_op jit(solution)/shard_map/all_to_all | solution.py:798
  138.8 0.8 shard_map.203
  (36 shorter events, 0.1 us)
Async XLA Ops:
  0.6 0.9 copy-start
  1.6 1.0 copy-start.3
  2.6 0.9 copy-start.8
  3.5 0.9 copy-start.9
  4.4 21.8 %copy-start.2 = (f32[10,60,160]{2,1,0:T(8,128)S(1)}, f32[10,60,160]{2,1,0:T(8,128)}, u32[]{:S(2)}) copy-start(f32[10,60,160]{2,1,0:T(8,128)} %constant.69.clone.inv_den) | copy-start | bytes 1152004
  4.9 7.7 %collective-permute-start = (f32[3,32,128]{2,1,0:T(8,128)S(1)}, f32[3,32,128]{2,1,0:T(8,128)S(1)}, u32[]{:S(2)}, u32[]{:S(2)}) collective-permute-start(f32[3,32,128]{2,1,0:T(8,128)S(1)} %get-tuple-element.30), channel_id=1, source_target_pairs={{0,64},{64,128},{128,192},{192,256},{256,320},{320,384},{384,448},... | collective-permute-start | bytes 147464 | tf_op jit(solution)/shard_map/ppermute | solution.py:711
  9.7 5.5 %collective-permute-start.1 = (f32[3,32,128]{2,1,0:T(8,128)S(1)}, f32[3,32,128]{2,1,0:T(8,128)S(1)}, u32[]{:S(2)}, u32[]{:S(2)}) collective-permute-start(f32[3,32,128]{2,1,0:T(8,128)S(1)} %get-tuple-element.31), channel_id=1, source_target_pairs={{64,0},{128,64},{192,128},{256,192},{320,256},{384,320},{448,384},... | collective-permute-start | bytes 147464 | tf_op jit(solution)/shard_map/ppermute | solution.py:711
  11.0 0.7 copy-start.17
  11.7 14.4 %copy-start.7 = (bf16[160,128]{1,0:T(8,128)(2,1)S(1)}, bf16[160,128]{1,0:T(8,128)(2,1)}, u32[]{:S(2)}) copy-start(bf16[160,128]{1,0:T(8,128)(2,1)} %constant.74.clone.bxh) | copy-start | bytes 122884
  11.7 14.4 %copy-start.11 = (bf16[60,64]{1,0:T(8,128)(2,1)S(1)}, bf16[60,64]{1,0:T(8,128)(2,1)}, u32[]{:S(2)}) copy-start(bf16[60,64]{1,0:T(8,128)(2,1)} %constant.70.clone.fyh) | copy-start | bytes 23044
  11.7 14.4 %copy-start.12 = (bf16[40,60]{1,0:T(8,128)(2,1)S(1)}, bf16[40,60]{1,0:T(8,128)(2,1)}, u32[]{:S(2)}) copy-start(bf16[40,60]{1,0:T(8,128)(2,1)} %constant.77.clone.byl) | copy-start | bytes 14404
  11.7 14.5 %copy-start.13 = (bf16[40,60]{1,0:T(8,128)(2,1)S(1)}, bf16[40,60]{1,0:T(8,128)(2,1)}, u32[]{:S(2)}) copy-start(bf16[40,60]{1,0:T(8,128)(2,1)} %constant.76.clone.byh) | copy-start | bytes 14404
  11.7 14.4 %copy-start.14 = (f32[32,128]{1,0:T(8,128)S(1)}, f32[32,128]{1,0:T(8,128)}, u32[]{:S(2)}) copy-start(f32[32,128]{1,0:T(8,128)} %constant.79.clone.inv_mass) | copy-start | bytes 49156
  12.6 13.6 %copy-start.1 = (f32[416,128]{1,0:T(8,128)S(1)}, f32[416,128]{1,0:T(8,128)}, u32[]{:S(2)}) copy-start(f32[416,128]{1,0:T(8,128)} %constant.67.clone.packed) | copy-start | bytes 638980
  15.2 11.0 %copy-start.4 = (bf16[128,160]{1,0:T(8,128)(2,1)S(1)}, bf16[128,160]{1,0:T(8,128)(2,1)}, u32[]{:S(2)}) copy-start(bf16[128,160]{1,0:T(8,128)(2,1)} %constant.73.clone.fxl) | copy-start | bytes 122884
  15.2 11.0 %copy-start.5 = (bf16[128,160]{1,0:T(8,128)(2,1)S(1)}, bf16[128,160]{1,0:T(8,128)(2,1)}, u32[]{:S(2)}) copy-start(bf16[128,160]{1,0:T(8,128)(2,1)} %constant.72.clone.fxh) | copy-start | bytes 122884
  15.2 11.0 %copy-start.6 = (bf16[160,128]{1,0:T(8,128)(2,1)S(1)}, bf16[160,128]{1,0:T(8,128)(2,1)}, u32[]{:S(2)}) copy-start(bf16[160,128]{1,0:T(8,128)(2,1)} %constant.75.clone.bxl) | copy-start | bytes 122884
  15.2 11.0 %copy-start.10 = (bf16[60,64]{1,0:T(8,128)(2,1)S(1)}, bf16[60,64]{1,0:T(8,128)(2,1)}, u32[]{:S(2)}) copy-start(bf16[60,64]{1,0:T(8,128)(2,1)} %constant.71.clone.fyl) | copy-start | bytes 23044
  15.3 7.3 %collective-permute-start.2 = (f32[12,16,128]{2,1,0:T(8,128)S(1)}, f32[12,16,128]{2,1,0:T(8,128)S(1)}, u32[]{:S(2)}, u32[]{:S(2)}) collective-permute-start(f32[12,16,128]{2,1,0:T(8,128)S(1)} %get-tuple-element.32), channel_id=1, source_target_pairs={{0,1},{1,2},{2,3},{3,4},{4,5},{5,6},{6,7},{7,8},{8,9},{9,10},{10,1... | collective-permute-start | bytes 294920 | tf_op jit(solution)/shard_map/ppermute | solution.py:711
  20.2 5.9 %collective-permute-start.3 = (f32[12,16,128]{2,1,0:T(8,128)S(1)}, f32[12,16,128]{2,1,0:T(8,128)S(1)}, u32[]{:S(2)}, u32[]{:S(2)}) collective-permute-start(f32[12,16,128]{2,1,0:T(8,128)S(1)} %get-tuple-element.33), channel_id=1, source_target_pairs={{1,0},{2,1},{3,2},{4,3},{5,4},{6,5},{7,6},{8,7},{9,8},{10,9},{11,1... | collective-permute-start | bytes 294920 | tf_op jit(solution)/shard_map/ppermute | solution.py:711
  22.5 3.8 %copy-start.16 = (bf16[16,128]{1,0:T(8,128)(2,1)S(1)}, bf16[16,128]{1,0:T(8,128)(2,1)}, u32[]{:S(2)}) copy-start(bf16[16,128]{1,0:T(8,128)(2,1)} %constant.78.clone.spread) | copy-start | bytes 12292
  29.0 10.5 %copy-start.15 = (f32[32,1]{1,0:T(8,128)S(1)}, f32[32,1]{1,0:T(8,128)}, u32[]{:S(2)}) copy-start(f32[32,1]{1,0:T(8,128)} %constant.68.clone.wy) | copy-start | bytes 388
  29.0 6.2 %collective-permute-start.4 = (f32[32,128]{1,0:T(8,128)S(1)}, f32[32,128]{1,0:T(8,128)S(1)}, u32[]{:S(2)}, u32[]{:S(2)}) collective-permute-start(f32[32,128]{1,0:T(8,128)S(1)} %get-tuple-element.38), channel_id=1, source_target_pairs={{0,64},{64,128},{128,192},{192,256},{256,320},{320,384},{384,448},... | collective-permute-start | bytes 49160 | tf_op jit(solution)/shard_map/ppermute | solution.py:711
  33.1 6.3 %collective-permute-start.5 = (f32[32,128]{1,0:T(8,128)S(1)}, f32[32,128]{1,0:T(8,128)S(1)}, u32[]{:S(2)}, u32[]{:S(2)}) collective-permute-start(f32[32,128]{1,0:T(8,128)S(1)} %get-tuple-element.39), channel_id=1, source_target_pairs={{64,0},{128,64},{192,128},{256,192},{320,256},{384,320},{448,384},... | collective-permute-start | bytes 49160 | tf_op jit(solution)/shard_map/ppermute | solution.py:711
  41.8 36.6 %all-to-all-start = ((f32[512,1,128]{2,1,0:T(1,128)}), f32[512,1,128]{2,1,0:T(1,128)S(1)}, u32[]{:S(2)}, u32[]{:S(2)}) async-start(f32[512,1,128]{2,1,0:T(1,128)} %broadcast_in_dim.6), calls=%async_computation | async-start | bytes 524288 | tf_op jit(solution)/shard_map/all_to_all | solution.py:765
  83.0 4.0 %collective-permute-start.6 = (f32[2,32,128]{2,1,0:T(8,128)S(1)}, f32[2,32,128]{2,1,0:T(8,128)S(1)}, u32[]{:S(2)}, u32[]{:S(2)}) collective-permute-start(f32[2,32,128]{2,1,0:T(8,128)S(1)} %get-tuple-element.43), channel_id=1, source_target_pairs={{0,64},{64,128},{128,192},{192,256},{256,320},{320,384},{384,448},... | collective-permute-start | bytes 98312 | tf_op jit(solution)/shard_map/ppermute | solution.py:711
  85.7 4.7 %collective-permute-start.7 = (f32[2,32,128]{2,1,0:T(8,128)S(1)}, f32[2,32,128]{2,1,0:T(8,128)S(1)}, u32[]{:S(2)}, u32[]{:S(2)}) collective-permute-start(f32[2,32,128]{2,1,0:T(8,128)S(1)} %get-tuple-element.44), channel_id=1, source_target_pairs={{64,0},{128,64},{192,128},{256,192},{320,256},{384,320},{448,384},... | collective-permute-start | bytes 98312 | tf_op jit(solution)/shard_map/ppermute | solution.py:711
  90.4 5.6 %collective-permute-start.8 = (f32[12,16,128]{2,1,0:T(8,128)S(1)}, f32[12,16,128]{2,1,0:T(8,128)S(1)}, u32[]{:S(2)}, u32[]{:S(2)}) collective-permute-start(f32[12,16,128]{2,1,0:T(8,128)S(1)} %get-tuple-element.45), channel_id=1, source_target_pairs={{0,1},{1,2},{2,3},{3,4},{4,5},{5,6},{6,7},{7,8},{8,9},{9,10},{10,1... | collective-permute-start | bytes 294920 | tf_op jit(solution)/shard_map/ppermute | solution.py:711
  94.1 5.9 %collective-permute-start.9 = (f32[12,16,128]{2,1,0:T(8,128)S(1)}, f32[12,16,128]{2,1,0:T(8,128)S(1)}, u32[]{:S(2)}, u32[]{:S(2)}) collective-permute-start(f32[12,16,128]{2,1,0:T(8,128)S(1)} %get-tuple-element.46), channel_id=1, source_target_pairs={{1,0},{2,1},{3,2},{4,3},{5,4},{6,5},{7,6},{8,7},{9,8},{10,9},{11,1... | collective-permute-start | bytes 294920 | tf_op jit(solution)/shard_map/ppermute | solution.py:711
  102.2 3.7 %collective-permute-start.10 = (f32[32,128]{1,0:T(8,128)S(1)}, f32[32,128]{1,0:T(8,128)S(1)}, u32[]{:S(2)}, u32[]{:S(2)}) collective-permute-start(f32[32,128]{1,0:T(8,128)S(1)} %get-tuple-element.48), channel_id=1, source_target_pairs={{0,64},{64,128},{128,192},{192,256},{256,320},{320,384},{384,448},... | collective-permute-start | bytes 49160 | tf_op jit(solution)/shard_map/ppermute | solution.py:711
  104.6 4.5 %collective-permute-start.11 = (f32[32,128]{1,0:T(8,128)S(1)}, f32[32,128]{1,0:T(8,128)S(1)}, u32[]{:S(2)}, u32[]{:S(2)}) collective-permute-start(f32[32,128]{1,0:T(8,128)S(1)} %get-tuple-element.49), channel_id=1, source_target_pairs={{64,0},{128,64},{192,128},{256,192},{320,256},{384,320},{448,384},... | collective-permute-start | bytes 49160 | tf_op jit(solution)/shard_map/ppermute | solution.py:711

commit v3 on v2

--- a/solution.py
+++ b/solution.py
@@ -27,7 +27,6 @@
 VMEM = pltpu.VMEM
 SMEM = pltpu.SMEM
 LIMIT = 24 * 1024 * 1024
-PAIRS = ((0, 0), (0, 1), (0, 2), (1, 1), (1, 2), (2, 2))
 
 
 def gll_tables():
@@ -172,12 +171,15 @@
 AT_ROLLS = ROWS
 AT_DX = AT_ROLLS + 128
 AT_DXT = AT_DX + LANES
+AT_SQUARE = AT_DXT + LANES
 PACKED = np.concatenate(
     [
         WY[:, None] * WX[None, :],
         roll_table(),
         np.kron(np.eye(EX), DERIV.T),
         np.kron(np.eye(EX), DERIV),
+        np.repeat(DERIV[:, :1] ** 2, LANES, axis=1),
+        np.repeat(DERIV[:, 7:] ** 2, LANES, axis=1),
     ]
 ).astype(np.float32)
 
@@ -194,52 +196,6 @@
     np.float32
 )
 SPREAD = np.kron(np.eye(EX), np.ones((1, 8))).astype(jnp.bfloat16)
-
-
-def shape_functions(count, has_low, has_high):
-    length = 8 * count
-    pieces = np.zeros((3, length))
-    pieces[1] = 1.0
-    if has_low:
-        pieces[0, 0] = 0.5
-        pieces[1, 0] = 0.5
-    if has_high:
-        pieces[2, -1] = 0.5
-        pieces[1, -1] = 0.5
-    slopes = np.stack([np.kron(np.eye(count), DERIV) @ piece for piece in pieces])
-    return pieces, slopes
-
-
-CASES = ((False, True), (True, True), (True, False))
-
-
-def z_table():
-    table = np.zeros((3, 16, 8))
-    for case, (low, high) in enumerate(CASES):
-        pieces, slopes = shape_functions(1, low, high)
-        for index, (first, second) in enumerate(PAIRS):
-            table[case, index] = slopes[first] * slopes[second]
-            table[case, 6 + index] = pieces[first] * pieces[second]
-            mass = np.sum(WEIGHT * pieces[first] * pieces[second])
-            table[case, 15, index] = HELM_COEF / 8.0 * np.sum(WX) * mass
-        table[case, 12:15] = pieces
-    return table.astype(np.float32)
-
-
-def y_table():
-    table = np.zeros((3, 3, ROWS, LANES))
-    for case, (low, high) in enumerate(CASES):
-        pieces, slopes = shape_functions(EY, low, high)
-        for first in range(3):
-            table[case, 2, :, first] = pieces[first]
-            for second in range(3):
-                table[case, 0, :, 3 * first + second] = pieces[first] * pieces[second]
-                table[case, 1, :, 3 * first + second] = slopes[first] * slopes[second]
-    return table.astype(np.float32)
-
-
-Z_TABLE = z_table()
-Y_TABLE = y_table()
 
 
 def parts(values):
@@ -372,7 +328,19 @@
     return row
 
 
-def advect_kernel(lev, vel, src, packed, b_ref, l_ref, zlo, zhi):
+def advect_kernel(
+    lev_in, vel_in, src_in, packed_in, b_ref, l_ref, zlo, zhi, lev, vel, src, packed, sems
+):
+    copies = [
+        pltpu.make_async_copy(source, target, sems.at[index])
+        for index, (source, target) in enumerate(
+            ((vel_in, vel), (lev_in, lev), (packed_in, packed), (src_in, src))
+        )
+    ]
+    for copy in copies:
+        copy.start()
+    for copy in copies:
+        copy.wait()
     level = lev[...]
     v0, v1, v2 = vel[0], vel[1], vel[2]
     gz = stack(along_z([level[i] for i in range(8)], DERIV))
@@ -422,8 +390,7 @@
 
 
 def level_kernel(
-    near, solid, spread, inv_mass, packed, inv_den, fyh, fyl, fxh, fxl, bxh, bxl, byh, byl,
-    b, l, zlo, zhi, ylo, yhi, level_ref, flux_ref, w_ref, wlo, whi, stat,
+    near, solid, spread, inv_mass, packed, b, l, zlo, zhi, ylo, yhi, level_ref, flux_ref, stat
 ):
     row = lax.broadcasted_iota(jnp.int32, (ROWS, LANES), 0)
     planes = []
@@ -457,6 +424,7 @@
     )
     plane_w = packed[0:ROWS]
     total = jnp.zeros((ROWS, LANES), F32)
+    fluxes = []
     for i in range(8):
         scale = 1.0 / float(WEIGHT[i])
         plane = own[i] * (inverse * scale)
@@ -468,11 +436,22 @@
         liquid = jax.nn.sigmoid(plane * (1.0 / LEVEL_WIDTH))
         coef = (GAS_RATIO - (GAS_RATIO - 1.0) * liquid) * open_part
         total = total + coef
-        flux_ref[i] = (0.5 * float(WEIGHT[i])) * (coef * plane_w)
+        flux = (0.5 * float(WEIGHT[i])) * (coef * plane_w)
+        flux_ref[i] = flux
+        fluxes.append(flux)
     kbar = jnp.sum(total) * (1.0 / (8 * ROWS * LANES))
-    stat[...] = lane_row([kbar, partition_total(b, zlo, zhi, ylo, yhi, near)])
-    tables = ((fyh, fyl), (fxh, fxl), (bxh, bxl), (byh, byl))
-    schwarz(b, zlo, zhi, ylo, yhi, tables, inv_den, near, w_ref, wlo, whi)
+    entries = [kbar, partition_total(b, zlo, zhi, ylo, yhi, near)] + [0.0] * 9
+    for first, second in ((0, 0), (0, 7), (7, 7)):
+        slopes = along_z(fluxes, (DERIV[:, first] * DERIV[:, second])[None, :])[0]
+        column = jnp.sum(slopes, axis=1, keepdims=True)
+        entries += [jnp.sum(column, axis=0, keepdims=True), column[0:1], column[ROWS - 1 : ROWS]]
+    inner = fluxes[0] + fluxes[1]
+    for i in range(2, 8):
+        inner = inner + fluxes[i]
+    for at, start in ((0, 0), (ROWS - 8, 8)):
+        square = packed[AT_SQUARE + start : AT_SQUARE + start + 8]
+        entries += [jnp.sum(square * plane[at : at + 8]) for plane in (inner, fluxes[0], fluxes[7])]
+    stat[...] = lane_row(entries)
 
 
 def schwarz_kernel(
@@ -483,29 +462,32 @@
     schwarz(b, zlo, zhi, ylo, yhi, tables, inv_den, near, w_ref, wlo, whi)
 
 
-def galerkin_kernel(zt, yt, wy, packed, stat_in, flux, w, zlo, zhi, zl_ref, stat):
+def galerkin_kernel(near, packed, stat_in, flux, w, zlo, zhi, zl_ref, stat):
     local = add_planes(w, zlo[...], zhi[...])
     zl_ref[...] = local
-    fluxes = flux[...]
-    applied = local_operator(local, fluxes, packed)
-
-    def combine(index, planes):
-        total = zt[index, 0] * planes[0]
-        for i in range(1, 8):
-            total = total + zt[index, i] * planes[i]
-        return jnp.sum(total, axis=1, keepdims=True)
-
-    total = jnp.zeros((ROWS, LANES), F32)
-    for a in range(3):
-        placed = pltpu.roll(yt[2], 2 + 3 * a, 1)
-        total = total + combine(12 + a, applied) * placed
-    for index in range(6):
-        shift = 11 + 9 * index
-        slope_z = combine(index, fluxes) + zt[15, index] * wy[...]
-        slope_y = combine(6 + index, fluxes)
-        total = total + slope_z * pltpu.roll(yt[0], shift, 1)
-        total = total + slope_y * pltpu.roll(yt[1], shift, 1)
-    stat[...] = stat_in[...] + jnp.sum(total, axis=0, keepdims=True)
+    applied = local_operator(local, flux[...], packed)
+    inner = near[0] * applied[0] + near[1] * applied[7]
+    for i in range(1, 7):
+        inner = inner + applied[i]
+    edge = edge_rows(ROWS, near[2], near[3])
+    entries = [0.0, 0.0]
+    for plane in ((1.0 - near[0]) * applied[0], inner, (1.0 - near[1]) * applied[7]):
+        entries += [
+            (1.0 - near[2]) * jnp.sum(plane[0:1]),
+            jnp.sum(edge * plane),
+            (1.0 - near[3]) * jnp.sum(plane[ROWS - 1 : ROWS]),
+        ]
+    stat[...] = jnp.broadcast_to(stat_in[...] + lane_row(entries), stat.shape)
+
+
+def turn_kernel(gathered, out_ref, wide):
+    count = gathered.shape[0]
+    wide[...] = jnp.zeros((LANES, LANES), F32)
+    wide[0:count] = gathered[...]
+    turned = wide[...].T
+    tile = turned[0:16] + pltpu.roll(turned[16:32], LANES // 2, 1)
+    for i in range(out_ref.shape[0]):
+        out_ref[i] = tile
 
 
 def invert(blocks, sub):
@@ -543,17 +525,68 @@
     return result
 
 
-def coarse_kernel(count, place, gathered, out_ref, wide, values):
+def coarse_operator(c, sums_z, sums_y, low_z, high_z, low_y, high_y):
+    result = [[None] * 3 for _ in range(3)]
+
+    def ends(values, low, high):
+        inside = values[1]
+        first = (1.0 - low) * inside + low * values[0]
+        last = (1.0 - high) * inside + high * values[2]
+        return inside, first, last
+
+    def tested(inside, first, last, low, high):
+        return (low * first, inside + (1.0 - low) * first + (1.0 - high) * last, high * last)
+
+    by_b = []
+    for b in range(3):
+        inside, first, last = ends([c[a][b] for a in range(3)], low_z, high_z)
+        end = float(WEIGHT[0])
+        by_b.append(tested((2.0 - 2.0 * end) * inside, end * first, end * last, low_z, high_z))
+    scale = HELM_COEF / 8.0 * float(np.sum(WX))
+    for a in range(3):
+        inside, first, last = ends([by_b[b][a] for b in range(3)], low_y, high_y)
+        end = scale * float(WEIGHT[0])
+        middle = scale * (2.0 * EY - 2.0 * float(WEIGHT[0]))
+        result[a] = list(tested(middle * inside, end * first, end * last, low_y, high_y))
+
+    slopes = []
+    for outer, factor in ((0, low_z), (2, high_z)):
+        slopes.append(ends([factor * (c[outer][b] - c[1][b]) for b in range(3)], low_y, high_y))
+    for s, (outer, factor) in enumerate(((0, low_z), (2, high_z))):
+        parts_y = []
+        for place in range(3):
+            total = None
+            for t in range(2):
+                whole, first, last = sums_z[s + t]
+                weight = (whole - first - last, first, last)[place]
+                term = weight * slopes[t][place]
+                total = term if total is None else total + term
+            parts_y.append(total)
+        for b, value in enumerate(tested(*parts_y, low_y, high_y)):
+            result[outer][b] = result[outer][b] + factor * value
+            result[1][b] = result[1][b] - factor * value
+
+    for s, (outer, factor) in enumerate(((0, low_y), (2, high_y))):
+        slope = ends([factor * (c[a][outer] - c[a][1]) for a in range(3)], low_z, high_z)
+        whole, first, last = sums_y[s]
+        pieces = ((whole - first - last) * slope[0], first * slope[1], last * slope[2])
+        for a, value in enumerate(tested(*pieces, low_z, high_z)):
+            result[a][outer] = result[a][outer] + factor * value
+            result[a][1] = result[a][1] - factor * value
+    return result
+
+
+def coarse_kernel(count, place, gathered, out_ref):
     lanes = LANES
-    wide[...] = jnp.zeros((LANES, LANES), F32)
-    for i in range(8):
-        wide[0:count] = gathered[count * i : count * (i + 1)]
-        values[i] = wide[...].T
     sub = lax.broadcasted_iota(jnp.int32, (8, lanes), 0)
     lane = lax.broadcasted_iota(jnp.int32, (8, lanes), 1)
 
     def value(index):
-        return jnp.concatenate([values[i, index : index + 1] for i in range(8)], axis=0)
+        row = index % 16
+        array = jnp.concatenate([gathered[i, row : row + 1] for i in range(8)], axis=0)
+        if index >= 16:
+            array = pltpu.roll(array, lanes // 2, 1)
+        return jnp.where(lane < count, array, 0.0)
 
     def move(array, dz, dy):
         if dz:
@@ -609,14 +642,17 @@
     offsets = [(a - 1, b - 1) for a in range(3) for b in range(3)]
     first = solve(value(1))
     near_first = [move(first, dz, dy) for dz, dy in offsets]
+    low_z = jnp.where(sub > 0, 0.5, 0.0)
+    high_z = jnp.where(sub < 7, 0.5, 0.0)
+    low_y = jnp.where(lane > 0, 0.5, 0.0)
+    high_y = jnp.where(lane < count - 1, 0.5, 0.0)
+    sums_z = [[value(11 + 3 * k + j) for j in range(3)] for k in range(3)]
+    sums_y = [[value(20 + 3 * k + j) for j in range(3)] for k in range(2)]
+    values = [near_first[0:3], near_first[3:6], near_first[6:9]]
+    tested = coarse_operator(values, sums_z, sums_y, low_z, high_z, low_y, high_y)
     totals = jnp.zeros((8, lanes), F32)
     for d, (dz, dy) in enumerate(offsets):
-        term = value(2 + d)
-        for e in range(9):
-            a, b, c, f = d // 3, d % 3, e // 3, e % 3
-            if a > c:
-                a, b, c, f = c, f, a, b
-            term = term + value(11 + 9 * PAIRS.index((a, c)) + 3 * b + f) * near_first[e]
+        term = jnp.where(lane < count, value(2 + d) + tested[d // 3][d % 3], 0.0)
         totals = totals + move(term, -dz, -dy)
     totals = jnp.where(lane < count, totals, 0.0)
     second = solve(totals)
@@ -629,29 +665,25 @@
         )
 
 
-def add_coarse(local, zt, yt, coarse, start):
+def add_coarse(local, near, coarse, start):
+    row = lax.broadcasted_iota(jnp.int32, (ROWS, LANES), 0)
+    edge = edge_rows(ROWS, near[2], near[3])
+    below = jnp.where(row == 0, 1.0 - near[2], 0.0)
+    above = jnp.where(row == ROWS - 1, 1.0 - near[3], 0.0)
     columns = []
     for a in range(3):
-        total = yt[2, :, 0:1] * coarse[start + 3 * a : start + 3 * a + 1]
-        for b in range(1, 3):
-            total = total + yt[2, :, b : b + 1] * coarse[start + 3 * a + b : start + 3 * a + b + 1]
-        columns.append(total)
-    planes = []
-    for i in range(8):
-        plane = local[i] + zt[13, i] * columns[1]
-        if i == 0:
-            plane = plane + zt[12, i] * columns[0]
-        if i == 7:
-            plane = plane + zt[14, i] * columns[2]
-        planes.append(plane)
+        at = start + 3 * a
+        columns.append(
+            below * coarse[at : at + 1] + edge * coarse[at + 1 : at + 2] + above * coarse[at + 2 : at + 3]
+        )
+    planes = [local[i] + columns[1] for i in range(8)]
+    planes[0] = planes[0] + (1.0 - near[0]) * (columns[0] - columns[1])
+    planes[7] = planes[7] + (1.0 - near[1]) * (columns[2] - columns[1])
     return stack(planes)
 
 
-def apply_kernel(
-    zt, yt, packed, coarse, flux, b, zl,
-    z_ref, y_ref, ylo, yhi, stat,
-):
-    field = add_coarse(zl[...], zt, yt, coarse, 0)
+def apply_kernel(near, packed, coarse, flux, b, zl, z_ref, y_ref, ylo, yhi, stat):
+    field = add_coarse(zl[...], near, coarse, 0)
     z_ref[...] = field
     applied = local_operator(field, flux[...], packed)
     y_ref[...] = applied
@@ -660,16 +692,13 @@
     stat[...] = lane_row([jnp.sum(b[...] * field), jnp.sum(field * applied)])
 
 
-def second_kernel(
-    zt, yt, packed, coarse, flux, b, y, w, zlo, zhi,
-    stat_in, q_ref, stat,
-):
+def second_kernel(near, packed, coarse, flux, b, y, w, zlo, zhi, stat_in, q_ref, stat):
     local = add_planes(w, zlo[...], zhi[...])
-    field = add_coarse(local, zt, yt, coarse, 16)
+    field = add_coarse(local, near, coarse, 16)
     q_ref[...] = field
     applied = local_operator(field, flux[...], packed)
     sums = [0.0, 0.0, jnp.sum(b[...] * field), jnp.sum(y[...] * field), jnp.sum(field * applied)]
-    stat[...] = stat_in[...] + lane_row(sums)
+    stat[...] = jnp.broadcast_to(stat_in[...] + lane_row(sums), stat.shape)
 
 
 def combine_kernel(sums, z, q, p_ref):
@@ -686,22 +715,18 @@
     p_ref[...] = on_z.reshape(1, 1, 1) * z[...] - on_q.reshape(1, 1, 1) * q[...]
 
 
-def call(kernel, outs, specs, args, scratch=(), flops=1000000):
+def run(kernel, outs, smem, args, scratch=(), flops=1000000, place=VMEM, limit=LIMIT):
     nbytes = sum(4 * int(np.prod(out)) for out in outs) * 2
     return pl.pallas_call(
         kernel,
         out_shape=[jax.ShapeDtypeStruct(out, F32) for out in outs],
-        in_specs=[pl.BlockSpec(memory_space=SMEM if spec else VMEM) for spec in specs],
+        in_specs=[pl.BlockSpec(memory_space=SMEM) for _ in smem]
+        + [pl.BlockSpec(memory_space=place) for _ in args],
         out_specs=[pl.BlockSpec(memory_space=VMEM) for _ in outs],
         scratch_shapes=list(scratch),
-        compiler_params=pltpu.CompilerParams(vmem_limit_bytes=LIMIT),
+        compiler_params=pltpu.CompilerParams(vmem_limit_bytes=limit),
         cost_estimate=pl.CostEstimate(flops=flops, bytes_accessed=nbytes, transcendentals=0),
-    )(*args)
-
-
-def run(kernel, outs, smem, args, scratch=(), flops=1000000):
-    specs = [True] * len(smem) + [False] * len(args)
-    return call(kernel, outs, specs, list(smem) + list(args), scratch, flops)
+    )(*smem, *args)
 
 
 def shift(axis, low_face, high_face):
@@ -721,15 +746,9 @@
     def ends(index, count):
         return [jnp.where(index > 0, 0.5, 1.0), jnp.where(index < count - 1, 0.5, 1.0)]
 
-    def case(index, count):
-        return jnp.where(index == 0, 0, jnp.where(index == count - 1, 2, 1))
-
     near = jnp.stack(ends(index_gx, count_gx) + ends(index_gy, count_gy)).astype(F32)
-    zt = lax.dynamic_index_in_dim(jnp.asarray(Z_TABLE), case(index_gx, count_gx), 0, False)
-    yt = lax.dynamic_index_in_dim(jnp.asarray(Y_TABLE), case(index_gy, count_gy), 0, False)
     place = jnp.stack([index_gx, index_gy]).astype(jnp.int32)
     packed = jnp.asarray(PACKED)
-    wy = jnp.asarray(WY.astype(np.float32)[:, None])
     solver = (INV_DEN, FY_H, FY_L, FX_H, FX_L, BX_H, BX_L, BY_H, BY_L)
     solver = tuple(jnp.asarray(table) for table in solver)
     face = (ROWS, LANES)
@@ -741,59 +760,62 @@
         [block, block, (3, *face), (3, *face)],
         [],
         [level_set, velocity, source, packed],
+        [VMEM(block, F32), VMEM((3, *block), F32), VMEM(block, F32), VMEM(PACKED.shape, F32)]
+        + [pltpu.SemaphoreType.DMA((4,))],
+        place=pl.ANY,
+        limit=56 * 1024 * 1024,
     )
     zlo, zhi = shift("gx", zlo, zhi)
     ylo, yhi = run(functools.partial(rim_kernel, 2), [rim, rim], [], [b, l, zlo, zhi])
     ylo, yhi = shift("gy", ylo, yhi)
-    level_new, flux, w, wlo, whi, stat = run(
+    w, wlo, whi = run(
+        schwarz_kernel, [block, face, face], [near], [*solver, b, zlo, zhi, ylo, yhi]
+    )
+    wlo, whi = shift("gx", wlo, whi)
+    level_new, flux, stat = run(
         level_kernel,
-        [block, block, block, face, face, (1, LANES)],
+        [block, block, (1, LANES)],
         [near],
         [
-            solid, jnp.asarray(SPREAD), jnp.asarray(INV_MASS), packed, *solver,
+            solid, jnp.asarray(SPREAD), jnp.asarray(INV_MASS), packed,
             b, l, zlo, zhi, ylo, yhi,
         ],
-    )
-    zlo, zhi = shift("gx", wlo, whi)
+        flops=20000000,
+    )
     zl, stat = run(
         galerkin_kernel,
-        [block, (1, LANES)],
-        [zt],
-        [yt, wy, packed, stat, flux, w, zlo, zhi],
-    )
-    wide = jnp.broadcast_to(stat, (count_gx * count_gy, LANES))
-    gathered = lax.all_to_all(wide, ("gx", "gy"), 0, 0, tiled=True)
+        [block, (count_gy, LANES)],
+        [near],
+        [packed, stat, flux, w, wlo, whi],
+    )
+    gathered = lax.all_to_all(stat, "gy", 0, 0, tiled=True)
+    (turned,) = run(
+        turn_kernel, [(count_gx, TILE, LANES)], [], [gathered], [VMEM((LANES, LANES), F32)]
+    )
+    gathered = lax.all_to_all(turned, "gx", 0, 0, tiled=True)
     (coarse,) = run(
-        functools.partial(coarse_kernel, count_gy),
-        [(32, LANES)],
-        [place],
-        [gathered],
-        [VMEM((LANES, LANES), F32), VMEM((8, LANES, LANES), F32)],
+        functools.partial(coarse_kernel, count_gy), [(32, LANES)], [place], [gathered]
     )
     z, y, zlo, zhi, sums = run(
         apply_kernel,
         [block, block, (2, *face), (2, *face), (1, LANES)],
-        [zt],
-        [yt, packed, coarse, flux, b, zl],
+        [near],
+        [packed, coarse, flux, b, zl],
     )
     zlo, zhi = shift("gx", zlo, zhi)
     ylo, yhi = run(functools.partial(rim_kernel, 1), [rim, rim], [], [y, zlo, zhi])
     ylo, yhi = shift("gy", ylo, yhi)
     w, wlo, whi = run(
-        schwarz_kernel,
-        [block, face, face],
-        [near],
-        [*solver, y, zlo, zhi, ylo, yhi],
+        schwarz_kernel, [block, face, face], [near], [*solver, y, zlo, zhi, ylo, yhi]
     )
     zlo, zhi = shift("gx", wlo, whi)
     q, sums = run(
         second_kernel,
-        [block, (1, LANES)],
-        [zt],
-        [yt, packed, coarse, flux, b, y, w, zlo, zhi, sums],
-    )
-    tile = jnp.broadcast_to(sums, (count_gx, LANES))
-    tile = lax.all_to_all(tile, "gx", 0, 0, tiled=True)
+        [block, (count_gx, LANES)],
+        [near],
+        [packed, coarse, flux, b, y, w, zlo, zhi, sums],
+    )
+    tile = lax.all_to_all(sums, "gx", 0, 0, tiled=True)
     wide = jnp.broadcast_to(jnp.sum(tile, axis=0, keepdims=True), (count_gy, LANES))
     wide = lax.all_to_all(wide, "gy", 0, 0, tiled=True)
     (pressure,) = run(combine_kernel, [block], [], [wide, z, q])

time: 140 us -> 139 us (level)
  blocking collectives: 28.3 us -> 49.2 us
  starting transfers between devices: 51.1 us -> 39.5 us
  waiting for transfers between devices: 38.4 us -> 29.2 us
  local copies, waits for them, and re-layouts: 6.94 us -> 1.91 us
  Pallas kernels: 13.7 us -> 16.8 us
    all_to_all x1 -> x2, blocking collectives: 11.1 us -> 31.5 us  [the longest x1 21.4 us: body(): gathered = lax.all_to_all(stat, 'gy', 0, 0, tiled=True)]
    all_to_all x1, starting transfers between devices: 19.1 us -> 6.54 us  [body(): gathered = lax.all_to_all(turned, 'gx', 0, 0, tiled=True)]
    all_to_all x1, waiting for transfers between devices: 17.4 us -> 7.16 us  [body(): gathered = lax.all_to_all(turned, 'gx', 0, 0, tiled=True)]
    pallas_call x10 -> x12, Pallas kernels: 13.7 us -> 16.8 us  [run(): pl.pallas_call(kernel, out_shape=[jax.ShapeDtypeStruct(out, F32) for out...]
    unnamed x36 -> x34, local copies, waits for them, and re-layouts: 4.46 us -> 1.89 us
    squeeze x3 -> x0, local copies, waits for them, and re-layouts: 1.62 us -> none  [the longest x1 0.85 us: body(): lax.dynamic_index_in_dim(jnp.asarray(Y_TABLE), case(index_gy, count_gy),...]
  transfers between devices with their start and end apart: 13 -> 13, of which waited for: 7 -> 8; matrix products, arithmetic and copies ran while one was open for 1% -> 0% of each run, Pallas kernels for 0% -> 1%
where the time goes in v3:
time: 139 us; the launch traced here: 138 us
  blocking collectives  49.2 us (35%)
  starting transfers between devices  39.5 us (28%)
  waiting for transfers between devices  29.2 us (21%)
  Pallas kernels  16.8 us (12%)
  local copies, waits for them, and re-layouts  1.91 us (1%)
    ppermute x6, starting transfers between devices, shift(): lax.ppermute(high_face, axis, forward)  23.7 us
    ppermute x6, waiting for transfers between devices, shift(): lax.ppermute(low_face, axis, backward)  21.9 us
    all_to_all x1, blocking collectives, body(): gathered = lax.all_to_all(stat, 'gy', 0, 0, tiled=True)  21.4 us
    all_to_all x1, blocking collectives, body(): wide = lax.all_to_all(wide, 'gy', 0, 0, tiled=True)  17.7 us
    pallas_call x12, Pallas kernels, run(): pl.pallas_call(kernel, out_shape=[jax.ShapeDtypeStruct(out, F32) for out...  16.8 us
    all_to_all x1, blocking collectives, body(): tile = lax.all_to_all(sums, 'gx', 0, 0, tiled=True)  10 us
    ppermute x6, starting transfers between devices, shift(): lax.ppermute(low_face, axis, backward)  9.31 us
    all_to_all x1, waiting for transfers between devices, body(): gathered = lax.all_to_all(turned, 'gx', 0, 0, tiled=True)  7.16 us
  transfers between devices with their start and end apart: 13, of which 8 were waited for; matrix products, arithmetic and copies ran while one was open for 0% of the time, Pallas kernels for 1%

profile of v3, /device:TPU:1, one launch (start us, length us, event | category | flops | bytes accessed | tf_op | source)
XLA Modules:
  0.0 137.9 jit_solution(7470137214481375839)
XLA Ops:
  0.6 0.0 copy-start.3
  0.6 2.5 %shard_map.167 = (f32[8,32,128]{2,1,0:T(8,128)}, f32[8,32,128]{2,1,0:T(8,128)}, f32[3,32,128]{2,1,0:T(8,128)}, f32[3,32,128]{2,1,0:T(8,128)}) custom-call(f32[8,32,128]{2,1,0:T(8,128)} %lev_in.1, f32[3,8,32,128]{3,2,1,0:T(8,128)} %vel_in.1, f32[8,32,128]{2,1,0:T(8,128)} %src_in.1, f32[432,128]{1,0:T(8,128)} %constant.45.clone.packed_in.packed), custom_call_target="tpu_custom_call" | custom-call | flops 1000000 | bytes 720896 | tf_op jit(solution)/shard_map/pallas_call | solution.py:720
  3.1 4.8 %collective-permute-start = (f32[3,32,128]{2,1,0:T(8,128)}, f32[3,32,128]{2,1,0:T(8,128)S(1)}, u32[]{:S(2)}, u32[]{:S(2)}) collective-permute-start(f32[3,32,128]{2,1,0:T(8,128)} %get-tuple-element.30), channel_id=1, source_target_pairs={{0,64},{64,128},{128,192},{192,256},{256,320},{320,384},{384,448},... | collective-permute-start | bytes 147464 | tf_op jit(solution)/shard_map/ppermute | solution.py:736
  8.0 1.3 collective-permute-start.1
  9.3 0.1 collective-permute-done.refs_2_.zlo
  9.5 4.2 %collective-permute-done.1.refs_3_.zhi = f32[3,32,128]{2,1,0:T(8,128)S(1)} collective-permute-done((f32[3,32,128]{2,1,0:T(8,128)}, f32[3,32,128]{2,1,0:T(8,128)S(1)}, u32[]{:S(2)}, u32[]{:S(2)}) %collective-permute-start.1) | collective-permute-done | bytes 49184 | tf_op jit(solution)/shard_map/ppermute | solution.py:736
  13.7 0.9 copy-done.1
  14.6 0.9 copy-done.4
  15.5 0.0 copy-start.10
  15.5 0.0 copy-start.11
  15.5 0.0 copy-start.13
  15.6 0.0 copy-start.12
  15.6 5.0 %collective-permute-start.2 = (f32[12,16,128]{2,1,0:T(8,128)S(1)}, f32[12,16,128]{2,1,0:T(8,128)S(1)}, u32[]{:S(2)}, u32[]{:S(2)}) collective-permute-start(f32[12,16,128]{2,1,0:T(8,128)S(1)} %get-tuple-element.32), channel_id=1, source_target_pairs={{0,1},{1,2},{2,3},{3,4},{4,5},{5,6},{6,7},{7,8},{8,9},{9,10},{10,1... | collective-permute-start | bytes 294920 | tf_op jit(solution)/shard_map/ppermute | solution.py:736
  20.5 2.2 %collective-permute-start.3 = (f32[12,16,128]{2,1,0:T(8,128)S(1)}, f32[12,16,128]{2,1,0:T(8,128)S(1)}, u32[]{:S(2)}, u32[]{:S(2)}) collective-permute-start(f32[12,16,128]{2,1,0:T(8,128)S(1)} %get-tuple-element.33), channel_id=1, source_target_pairs={{1,0},{2,1},{3,2},{4,3},{5,4},{6,5},{7,6},{8,7},{9,8},{10,9},{11,1... | collective-permute-start | bytes 294920 | tf_op jit(solution)/shard_map/ppermute | solution.py:736
  22.8 0.1 pad_maximum_fusion.near
  22.9 3.6 %collective-permute-done.3.yhi = f32[12,16,128]{2,1,0:T(8,128)S(1)} collective-permute-done((f32[12,16,128]{2,1,0:T(8,128)S(1)}, f32[12,16,128]{2,1,0:T(8,128)S(1)}, u32[]{:S(2)}, u32[]{:S(2)}) %collective-permute-start.3) | collective-permute-done | bytes 98336 | tf_op jit(solution)/shard_map/ppermute | solution.py:736
  26.5 0.0 copy-start.16
  26.6 0.0 copy-start.14
  26.6 2.2 %shard_map.170 = (f32[8,32,128]{2,1,0:T(8,128)S(1)}, f32[32,128]{1,0:T(8,128)S(1)}, f32[32,128]{1,0:T(8,128)S(1)}) custom-call(f32[4]{0:T(128)S(1)} %pad_maximum_fusion.near, f32[10,60,160]{2,1,0:T(8,128)S(1)} %copy-done.3, bf16[60,64]{1,0:T(8,128)(2,1)S(1)} %copy-done.11, bf16[60,64]{1,0:T(8,128)(2,1)S(1)} %copy-done.10, bf16[128,160]{1,0:T(8,128)(2,1)S(1)} %copy-done.7, ...), custom_call_target="tpu_custom_call" | custom-call | flops 1000000 | bytes 327680 | tf_op jit(solution)/shard_map/pallas_call | solution.py:720
  28.8 0.0 copy-start.15
  28.8 4.0 %collective-permute-start.4 = (f32[32,128]{1,0:T(8,128)S(1)}, f32[32,128]{1,0:T(8,128)S(1)}, u32[]{:S(2)}, u32[]{:S(2)}) collective-permute-start(f32[32,128]{1,0:T(8,128)S(1)} %get-tuple-element.38), channel_id=1, source_target_pairs={{0,64},{64,128},{128,192},{192,256},{256,320},{320,384},{384,448},... | collective-permute-start | bytes 49160 | tf_op jit(solution)/shard_map/ppermute | solution.py:736
  32.8 1.3 collective-permute-start.5
  34.2 1.4 %shard_map.169 = (f32[8,32,128]{2,1,0:T(8,128)}, f32[8,32,128]{2,1,0:T(8,128)S(1)}, f32[1,128]{1,0:T(1,128)S(1)}) custom-call(f32[4]{0:T(128)S(1)} %pad_maximum_fusion.near, f32[4,16]{1,0:T(4,128)S(1)} %convert_bitcast_fusion.solid, bf16[16,128]{1,0:T(8,128)(2,1)S(1)} %copy-done.15, f32[32,128]{1,0:T(8,128)S(1)} %copy-done.14, f32[432,128]{1,0:T(8,128)S(1)} %copy-done, ...), custom_call_target="tpu_custom_call" | custom-call | flops 20000000 | bytes 525312 | tf_op jit(solution)/shard_map/pallas_call | solution.py:720
  35.5 0.0 collective-permute-done.4.zlo
  35.5 3.6 %collective-permute-done.5.zhi = f32[32,128]{1,0:T(8,128)S(1)} collective-permute-done((f32[32,128]{1,0:T(8,128)S(1)}, f32[32,128]{1,0:T(8,128)S(1)}, u32[]{:S(2)}, u32[]{:S(2)}) %collective-permute-start.5) | collective-permute-done | bytes 16416 | tf_op jit(solution)/shard_map/ppermute | solution.py:736
  39.1 1.3 shard_map.171
  40.4 21.4 %all_to_all.33 = f32[64,1,128]{2,1,0:T(1,128)S(1)} all-to-all(f32[64,1,128]{2,1,0:T(1,128)S(1)} %bitcast.18), channel_id=1, replica_groups=mesh['gx'=8,'gy'=64] {'gy'}, dimensions={0} | all-to-all | bytes 65536 | tf_op jit(solution)/shard_map/all_to_all | solution.py:791
  61.9 0.8 shard_map.172
  62.6 6.5 %all-to-all-start.1 = ((f32[8,16,128]{2,1,0:T(8,128)}), f32[8,16,128]{2,1,0:T(8,128)S(1)}, u32[]{:S(2)}, u32[]{:S(2)}) async-start(f32[8,16,128]{2,1,0:T(8,128)} %shard_map.172), calls=%async_computation.1 | async-start | bytes 131072 | tf_op jit(solution)/shard_map/all_to_all | solution.py:795
  69.2 0.1 pad_add_fusion.place
  69.2 7.2 %all-to-all-done.1.gathered = f32[8,16,128]{2,1,0:T(8,128)S(1)} async-done(((f32[8,16,128]{2,1,0:T(8,128)}), f32[8,16,128]{2,1,0:T(8,128)S(1)}, u32[]{:S(2)}, u32[]{:S(2)}) %all-to-all-start.1) | async-done | bytes 65568 | tf_op jit(solution)/shard_map/all_to_all | solution.py:795
  76.4 3.1 %shard_map.173.coarse = f32[32,128]{1,0:T(8,128)S(1)} custom-call(s32[2]{0:T(128)S(1)} %pad_add_fusion.place, f32[8,16,128]{2,1,0:T(8,128)S(1)} %all-to-all-done.1.gathered), custom_call_target="tpu_custom_call" | custom-call | flops 1000000 | bytes 32768 | tf_op jit(solution)/shard_map/pallas_call | solution.py:720
  79.5 1.3 shard_map.174
  80.8 2.2 %collective-permute-start.6 = (f32[2,32,128]{2,1,0:T(8,128)S(1)}, f32[2,32,128]{2,1,0:T(8,128)S(1)}, u32[]{:S(2)}, u32[]{:S(2)}) collective-permute-start(f32[2,32,128]{2,1,0:T(8,128)S(1)} %get-tuple-element.43), channel_id=1, source_target_pairs={{0,64},{64,128},{128,192},{192,256},{256,320},{320,384},{384,448},... | collective-permute-start | bytes 98312 | tf_op jit(solution)/shard_map/ppermute | solution.py:736
  83.0 1.3 collective-permute-start.7
  84.3 3.3 %collective-permute-done.7.refs_2_.zhi = f32[2,32,128]{2,1,0:T(8,128)S(1)} collective-permute-done((f32[2,32,128]{2,1,0:T(8,128)S(1)}, f32[2,32,128]{2,1,0:T(8,128)S(1)}, u32[]{:S(2)}, u32[]{:S(2)}) %collective-permute-start.7) | collective-permute-done | bytes 32800 | tf_op jit(solution)/shard_map/ppermute | solution.py:736
  87.7 5.6 %collective-permute-start.8 = (f32[12,16,128]{2,1,0:T(8,128)S(1)}, f32[12,16,128]{2,1,0:T(8,128)S(1)}, u32[]{:S(2)}, u32[]{:S(2)}) collective-permute-start(f32[12,16,128]{2,1,0:T(8,128)S(1)} %get-tuple-element.45), channel_id=1, source_target_pairs={{0,1},{1,2},{2,3},{3,4},{4,5},{5,6},{6,7},{7,8},{8,9},{9,10},{10,1... | collective-permute-start | bytes 294920 | tf_op jit(solution)/shard_map/ppermute | solution.py:736
  93.3 1.9 %collective-permute-start.9 = (f32[12,16,128]{2,1,0:T(8,128)S(1)}, f32[12,16,128]{2,1,0:T(8,128)S(1)}, u32[]{:S(2)}, u32[]{:S(2)}) collective-permute-start(f32[12,16,128]{2,1,0:T(8,128)S(1)} %get-tuple-element.46), channel_id=1, source_target_pairs={{1,0},{2,1},{3,2},{4,3},{5,4},{6,5},{7,6},{8,7},{9,8},{10,9},{11,1... | collective-permute-start | bytes 294920 | tf_op jit(solution)/shard_map/ppermute | solution.py:736
  95.2 0.0 collective-permute-done.8.ylo
  95.2 4.0 %collective-permute-done.9.yhi = f32[12,16,128]{2,1,0:T(8,128)S(1)} collective-permute-done((f32[12,16,128]{2,1,0:T(8,128)S(1)}, f32[12,16,128]{2,1,0:T(8,128)S(1)}, u32[]{:S(2)}, u32[]{:S(2)}) %collective-permute-start.9) | collective-permute-done | bytes 98336 | tf_op jit(solution)/shard_map/ppermute | solution.py:736
  99.2 2.2 %shard_map.176 = (f32[8,32,128]{2,1,0:T(8,128)S(1)}, f32[32,128]{1,0:T(8,128)S(1)}, f32[32,128]{1,0:T(8,128)S(1)}) custom-call(f32[4]{0:T(128)S(1)} %pad_maximum_fusion.near, f32[10,60,160]{2,1,0:T(8,128)S(1)} %copy-done.3, bf16[60,64]{1,0:T(8,128)(2,1)S(1)} %copy-done.11, bf16[60,64]{1,0:T(8,128)(2,1)S(1)} %copy-done.10, bf16[128,160]{1,0:T(8,128)(2,1)S(1)} %copy-done.7, ...), custom_call_target="tpu_custom_call" | custom-call | flops 1000000 | bytes 327680 | tf_op jit(solution)/shard_map/pallas_call | solution.py:720
  101.4 2.1 %collective-permute-start.10 = (f32[32,128]{1,0:T(8,128)S(1)}, f32[32,128]{1,0:T(8,128)S(1)}, u32[]{:S(2)}, u32[]{:S(2)}) collective-permute-start(f32[32,128]{1,0:T(8,128)S(1)} %get-tuple-element.48), channel_id=1, source_target_pairs={{0,64},{64,128},{128,192},{192,256},{256,320},{320,384},{384,448},... | collective-permute-start | bytes 49160 | tf_op jit(solution)/shard_map/ppermute | solution.py:736
  103.5 1.3 collective-permute-start.11
  104.8 3.2 %collective-permute-done.11.zhi = f32[32,128]{1,0:T(8,128)S(1)} collective-permute-done((f32[32,128]{1,0:T(8,128)S(1)}, f32[32,128]{1,0:T(8,128)S(1)}, u32[]{:S(2)}, u32[]{:S(2)}) %collective-permute-start.11) | collective-permute-done | bytes 16416 | tf_op jit(solution)/shard_map/ppermute | solution.py:736
  108.0 1.3 shard_map.177
  109.3 10.0 %all_to_all.34 = f32[8,1,128]{2,1,0:T(1,128)S(1)} all-to-all(f32[8,1,128]{2,1,0:T(1,128)S(1)} %bitcast.19), channel_id=1, replica_groups=mesh['gx'=8,'gy'=64] {'gx'}, dimensions={0} | all-to-all | bytes 8192 | tf_op jit(solution)/shard_map/all_to_all | solution.py:818
  119.4 17.7 %all_to_all.35 = f32[64,1,128]{2,1,0:T(1,128)S(1)} all-to-all(f32[64,1,128]{2,1,0:T(1,128)S(1)} %broadcast_in_dim.2), channel_id=1, replica_groups=mesh['gx'=8,'gy'=64] {'gy'}, dimensions={0} | all-to-all | bytes 65536 | tf_op jit(solution)/shard_map/all_to_all | solution.py:820
  137.1 0.8 shard_map.178
  (32 shorter events, 0.1 us)
Async XLA Ops:
  0.6 25.8 %copy-start.3 = (f32[10,60,160]{2,1,0:T(8,128)S(1)}, f32[10,60,160]{2,1,0:T(8,128)}, u32[]{:S(2)}) copy-start(f32[10,60,160]{2,1,0:T(8,128)} %constant.46.clone.inv_den) | copy-start | bytes 1152004
  3.1 6.3 %collective-permute-start = (f32[3,32,128]{2,1,0:T(8,128)}, f32[3,32,128]{2,1,0:T(8,128)S(1)}, u32[]{:S(2)}, u32[]{:S(2)}) collective-permute-start(f32[3,32,128]{2,1,0:T(8,128)} %get-tuple-element.30), channel_id=1, source_target_pairs={{0,64},{64,128},{128,192},{192,256},{256,320},{320,384},{384,448},... | collective-permute-start | bytes 147464 | tf_op jit(solution)/shard_map/ppermute | solution.py:736
  8.0 5.7 %collective-permute-start.1 = (f32[3,32,128]{2,1,0:T(8,128)}, f32[3,32,128]{2,1,0:T(8,128)S(1)}, u32[]{:S(2)}, u32[]{:S(2)}) collective-permute-start(f32[3,32,128]{2,1,0:T(8,128)} %get-tuple-element.31), channel_id=1, source_target_pairs={{64,0},{128,64},{192,128},{256,192},{320,256},{384,320},{448,384},... | collective-permute-start | bytes 147464 | tf_op jit(solution)/shard_map/ppermute | solution.py:736
  13.7 0.9 copy-start.1
  14.6 0.9 copy-start.4
  15.5 11.0 %copy-start.6 = (bf16[128,160]{1,0:T(8,128)(2,1)S(1)}, bf16[128,160]{1,0:T(8,128)(2,1)}, u32[]{:S(2)}) copy-start(bf16[128,160]{1,0:T(8,128)(2,1)} %constant.50.clone.fxl) | copy-start | bytes 122884
  15.5 11.0 %copy-start.7 = (bf16[128,160]{1,0:T(8,128)(2,1)S(1)}, bf16[128,160]{1,0:T(8,128)(2,1)}, u32[]{:S(2)}) copy-start(bf16[128,160]{1,0:T(8,128)(2,1)} %constant.49.clone.fxh) | copy-start | bytes 122884
  15.5 11.0 %copy-start.8 = (bf16[160,128]{1,0:T(8,128)(2,1)S(1)}, bf16[160,128]{1,0:T(8,128)(2,1)}, u32[]{:S(2)}) copy-start(bf16[160,128]{1,0:T(8,128)(2,1)} %constant.52.clone.bxl) | copy-start | bytes 122884
  15.5 11.0 %copy-start.9 = (bf16[160,128]{1,0:T(8,128)(2,1)S(1)}, bf16[160,128]{1,0:T(8,128)(2,1)}, u32[]{:S(2)}) copy-start(bf16[160,128]{1,0:T(8,128)(2,1)} %constant.51.clone.bxh) | copy-start | bytes 122884
  15.5 11.0 %copy-start.10 = (bf16[60,64]{1,0:T(8,128)(2,1)S(1)}, bf16[60,64]{1,0:T(8,128)(2,1)}, u32[]{:S(2)}) copy-start(bf16[60,64]{1,0:T(8,128)(2,1)} %constant.48.clone.fyl) | copy-start | bytes 23044
  15.5 11.0 %copy-start.11 = (bf16[60,64]{1,0:T(8,128)(2,1)S(1)}, bf16[60,64]{1,0:T(8,128)(2,1)}, u32[]{:S(2)}) copy-start(bf16[60,64]{1,0:T(8,128)(2,1)} %constant.47.clone.fyh) | copy-start | bytes 23044
  15.5 11.0 %copy-start.13 = (bf16[40,60]{1,0:T(8,128)(2,1)S(1)}, bf16[40,60]{1,0:T(8,128)(2,1)}, u32[]{:S(2)}) copy-start(bf16[40,60]{1,0:T(8,128)(2,1)} %constant.53.clone.byh) | copy-start | bytes 14404
  15.6 11.0 %copy-start.12 = (bf16[40,60]{1,0:T(8,128)(2,1)S(1)}, bf16[40,60]{1,0:T(8,128)(2,1)}, u32[]{:S(2)}) copy-start(bf16[40,60]{1,0:T(8,128)(2,1)} %constant.54.clone.byl) | copy-start | bytes 14404
  15.6 7.3 %collective-permute-start.2 = (f32[12,16,128]{2,1,0:T(8,128)S(1)}, f32[12,16,128]{2,1,0:T(8,128)S(1)}, u32[]{:S(2)}, u32[]{:S(2)}) collective-permute-start(f32[12,16,128]{2,1,0:T(8,128)S(1)} %get-tuple-element.32), channel_id=1, source_target_pairs={{0,1},{1,2},{2,3},{3,4},{4,5},{5,6},{6,7},{7,8},{8,9},{9,10},{10,1... | collective-permute-start | bytes 294920 | tf_op jit(solution)/shard_map/ppermute | solution.py:736
  20.5 5.9 %collective-permute-start.3 = (f32[12,16,128]{2,1,0:T(8,128)S(1)}, f32[12,16,128]{2,1,0:T(8,128)S(1)}, u32[]{:S(2)}, u32[]{:S(2)}) collective-permute-start(f32[12,16,128]{2,1,0:T(8,128)S(1)} %get-tuple-element.33), channel_id=1, source_target_pairs={{1,0},{2,1},{3,2},{4,3},{5,4},{6,5},{7,6},{8,7},{9,8},{10,9},{11,1... | collective-permute-start | bytes 294920 | tf_op jit(solution)/shard_map/ppermute | solution.py:736
  22.9 11.3 %copy-start = (f32[432,128]{1,0:T(8,128)S(1)}, f32[432,128]{1,0:T(8,128)}, u32[]{:S(2)}) copy-start(f32[432,128]{1,0:T(8,128)} %constant.45.clone.packed_in.packed) | copy-start | bytes 663556
  22.9 11.3 %copy-start.5 = (f32[8,32,128]{2,1,0:T(8,128)S(1)}, f32[8,32,128]{2,1,0:T(8,128)}, u32[]{:S(2)}) copy-start(f32[8,32,128]{2,1,0:T(8,128)} %get-tuple-element.29.refs_1_.l) | copy-start | bytes 393220
  26.5 7.5 %copy-start.16 = (s32[1,4,16]{2,1,0:T(4,128)S(1)}, s32[1,4,16]{2,1,0:T(4,128)}, u32[]{:S(2)}) copy-start(s32[1,4,16]{2,1,0:T(4,128)} %param.19) | copy-start | bytes 772
  26.6 7.6 %copy-start.14 = (f32[32,128]{1,0:T(8,128)S(1)}, f32[32,128]{1,0:T(8,128)}, u32[]{:S(2)}) copy-start(f32[32,128]{1,0:T(8,128)} %constant.56.clone.inv_mass) | copy-start | bytes 49156
  28.8 5.4 %copy-start.15 = (bf16[16,128]{1,0:T(8,128)(2,1)S(1)}, bf16[16,128]{1,0:T(8,128)(2,1)}, u32[]{:S(2)}) copy-start(bf16[16,128]{1,0:T(8,128)(2,1)} %constant.55.clone.spread) | copy-start | bytes 12292
  28.8 6.8 %collective-permute-start.4 = (f32[32,128]{1,0:T(8,128)S(1)}, f32[32,128]{1,0:T(8,128)S(1)}, u32[]{:S(2)}, u32[]{:S(2)}) collective-permute-start(f32[32,128]{1,0:T(8,128)S(1)} %get-tuple-element.38), channel_id=1, source_target_pairs={{0,64},{64,128},{128,192},{192,256},{256,320},{320,384},{384,448},... | collective-permute-start | bytes 49160 | tf_op jit(solution)/shard_map/ppermute | solution.py:736
  32.8 6.3 %collective-permute-start.5 = (f32[32,128]{1,0:T(8,128)S(1)}, f32[32,128]{1,0:T(8,128)S(1)}, u32[]{:S(2)}, u32[]{:S(2)}) collective-permute-start(f32[32,128]{1,0:T(8,128)S(1)} %get-tuple-element.39), channel_id=1, source_target_pairs={{64,0},{128,64},{192,128},{256,192},{320,256},{384,320},{448,384},... | collective-permute-start | bytes 49160 | tf_op jit(solution)/shard_map/ppermute | solution.py:736
  62.6 16.9 %copy-start.2 = (f32[8,32,128]{2,1,0:T(8,128)S(1)}, f32[8,32,128]{2,1,0:T(8,128)}, u32[]{:S(2)}) copy-start(f32[8,32,128]{2,1,0:T(8,128)} %get-tuple-element.28.refs_0_.b) | copy-start | bytes 393220
  62.6 13.8 %all-to-all-start.1 = ((f32[8,16,128]{2,1,0:T(8,128)}), f32[8,16,128]{2,1,0:T(8,128)S(1)}, u32[]{:S(2)}, u32[]{:S(2)}) async-start(f32[8,16,128]{2,1,0:T(8,128)} %shard_map.172), calls=%async_computation.1 | async-start | bytes 131072 | tf_op jit(solution)/shard_map/all_to_all | solution.py:795
  80.8 3.5 %collective-permute-start.6 = (f32[2,32,128]{2,1,0:T(8,128)S(1)}, f32[2,32,128]{2,1,0:T(8,128)S(1)}, u32[]{:S(2)}, u32[]{:S(2)}) collective-permute-start(f32[2,32,128]{2,1,0:T(8,128)S(1)} %get-tuple-element.43), channel_id=1, source_target_pairs={{0,64},{64,128},{128,192},{192,256},{256,320},{320,384},{384,448},... | collective-permute-start | bytes 98312 | tf_op jit(solution)/shard_map/ppermute | solution.py:736
  83.0 4.7 %collective-permute-start.7 = (f32[2,32,128]{2,1,0:T(8,128)S(1)}, f32[2,32,128]{2,1,0:T(8,128)S(1)}, u32[]{:S(2)}, u32[]{:S(2)}) collective-permute-start(f32[2,32,128]{2,1,0:T(8,128)S(1)} %get-tuple-element.44), channel_id=1, source_target_pairs={{64,0},{128,64},{192,128},{256,192},{320,256},{384,320},{448,384},... | collective-permute-start | bytes 98312 | tf_op jit(solution)/shard_map/ppermute | solution.py:736
  87.7 7.6 %collective-permute-start.8 = (f32[12,16,128]{2,1,0:T(8,128)S(1)}, f32[12,16,128]{2,1,0:T(8,128)S(1)}, u32[]{:S(2)}, u32[]{:S(2)}) collective-permute-start(f32[12,16,128]{2,1,0:T(8,128)S(1)} %get-tuple-element.45), channel_id=1, source_target_pairs={{0,1},{1,2},{2,3},{3,4},{4,5},{5,6},{6,7},{7,8},{8,9},{9,10},{10,1... | collective-permute-start | bytes 294920 | tf_op jit(solution)/shard_map/ppermute | solution.py:736
  93.3 5.9 %collective-permute-start.9 = (f32[12,16,128]{2,1,0:T(8,128)S(1)}, f32[12,16,128]{2,1,0:T(8,128)S(1)}, u32[]{:S(2)}, u32[]{:S(2)}) collective-permute-start(f32[12,16,128]{2,1,0:T(8,128)S(1)} %get-tuple-element.46), channel_id=1, source_target_pairs={{1,0},{2,1},{3,2},{4,3},{5,4},{6,5},{7,6},{8,7},{9,8},{10,9},{11,1... | collective-permute-start | bytes 294920 | tf_op jit(solution)/shard_map/ppermute | solution.py:736
  101.4 3.4 %collective-permute-start.10 = (f32[32,128]{1,0:T(8,128)S(1)}, f32[32,128]{1,0:T(8,128)S(1)}, u32[]{:S(2)}, u32[]{:S(2)}) collective-permute-start(f32[32,128]{1,0:T(8,128)S(1)} %get-tuple-element.48), channel_id=1, source_target_pairs={{0,64},{64,128},{128,192},{192,256},{256,320},{320,384},{384,448},... | collective-permute-start | bytes 49160 | tf_op jit(solution)/shard_map/ppermute | solution.py:736
  103.5 4.5 %collective-permute-start.11 = (f32[32,128]{1,0:T(8,128)S(1)}, f32[32,128]{1,0:T(8,128)S(1)}, u32[]{:S(2)}, u32[]{:S(2)}) collective-permute-start(f32[32,128]{1,0:T(8,128)S(1)} %get-tuple-element.49), channel_id=1, source_target_pairs={{64,0},{128,64},{192,128},{256,192},{320,256},{384,320},{448,384},... | collective-permute-start | bytes 49160 | tf_op jit(solution)/shard_map/ppermute | solution.py:736

commit v4 on v3

--- a/solution.py
+++ b/solution.py
@@ -139,6 +139,9 @@
 TILE = 16
 FZ, BZ = line_maps(1)
 FY, BY = wide_maps()
+SPECTRAL_Y = 64
+FY = np.pad(FY, ((0, SPECTRAL_Y - FY.shape[0]), (0, 0)))
+BY = np.pad(BY, ((0, 0), (0, SPECTRAL_Y - BY.shape[1])))
 FX, BX = line_maps(EX)
 FX = FX[:, :LANES]
 
@@ -147,14 +150,24 @@
     lam_y = np.tile(EIGEN, EY + 2)
     lam_x = np.tile(EIGEN, EX)
     total = EIGEN[:, None, None] + lam_y[None, :, None] + lam_x[None, None, :]
-    return (1.0 / (SCHWARZ_SCALE * total + SCHWARZ_SHIFT)).astype(np.float32)
+    inverse = 1.0 / (SCHWARZ_SCALE * total + SCHWARZ_SHIFT)
+    inverse = np.pad(inverse, ((0, 0), (0, SPECTRAL_Y - inverse.shape[1]), (0, 0)))
+    return inverse.reshape(10 * SPECTRAL_Y, 10 * EX).astype(np.float32)
 
 
 INV_DEN = denominators()
-FY_H, FY_L = split_const(FY)
-BY_H, BY_L = split_const(BY)
 FX_H, FX_L = split_const(FX.T.copy())
 BX_H, BX_L = split_const(BX.T.copy())
+
+
+def wide_const(table):
+    high, low = split_const(table)
+    return np.concatenate([high, high, low], axis=1)
+
+
+FY_W = wide_const(FY)
+BY_W = wide_const(BY)
+FX_HH = np.concatenate([FX_H, FX_H], axis=0)
 
 
 def roll_table():
@@ -208,14 +221,13 @@
     return jnp.dot(left, right, preferred_element_type=F32)
 
 
-def left_table(table, values):
-    high, low = parts(values)
-    return dot(table[0][...], high) + dot(table[0][...], low) + dot(table[1][...], high)
-
-
-def right_table(values, table):
-    high, low = parts(values)
-    return dot(high, table[0][...]) + dot(low, table[0][...]) + dot(high, table[1][...])
+def left_pairs(table, planes):
+    results = []
+    for i in range(0, len(planes), 2):
+        high, low = parts(jnp.concatenate([planes[i], planes[i + 1]], axis=1))
+        both = dot(table[...], jnp.concatenate([high, low, high], axis=0))
+        results += [both[:, 0:LANES], both[:, LANES : 2 * LANES]]
+    return results
 
 
 def along_z(values, matrix):
@@ -232,19 +244,22 @@
 
 
 def along_y(values, packed, kind):
-    grouped = values.reshape(8 * EY, 8, LANES)
+    count = values.shape[0]
+    grouped = values.reshape(count * EY, 8, LANES)
     start = AT_ROLLS + 64 * kind
     total = packed[start : start + 8][None] * grouped
     for k in range(1, 8):
         total = total + packed[start + 8 * k : start + 8 * k + 8][None] * pltpu.roll(grouped, 8 - k, 1)
-    return total.reshape(8, ROWS, LANES)
+    return total.reshape(count, ROWS, LANES)
 
 
 def along_x(values, packed, kind):
     start = AT_DXT if kind else AT_DX
     high, low = parts(packed[start : start + LANES])
     first, rest = parts(values.reshape(8 * ROWS, LANES))
-    total = dot(first, high) + dot(rest, high) + dot(first, low)
+    total = dot(
+        jnp.concatenate([first, rest], axis=1), jnp.concatenate([high, high], axis=0)
+    ) + dot(first, low)
     return total.reshape(8, ROWS, LANES)
 
 
@@ -278,18 +293,19 @@
 
 
 def schwarz(own, low_z, high_z, low_y, high_y, tables, inv_den, near, out_ref, low_ref, high_ref):
-    fy, fx, bx, by = tables
+    fy, fxhh, fxl, bxh, bxl, by = tables
     middle = along_z([own[i] for i in range(8)] + [low_z[0], low_z[1], high_z[0], high_z[1]], FZ)
     below = along_z([low_y[i] for i in range(12)], FZ)
     above = along_z([high_y[i] for i in range(12)], FZ)
-    spectral = [
-        left_table(fy, jnp.concatenate([middle[i], below[i], above[i]], axis=0)) for i in range(10)
-    ]
-    step = 10 * (EY + 2)
-    wide = right_table(jnp.concatenate(spectral, axis=0), fx)
-    wide = wide * inv_den[...].reshape(10 * step, 10 * EX)
-    back = right_table(wide, bx)
-    back = [left_table(by, back[step * i : step * (i + 1)]) for i in range(10)]
+    spectral = left_pairs(
+        fy, [jnp.concatenate([middle[i], below[i], above[i]], axis=0) for i in range(10)]
+    )
+    high, low = parts(jnp.concatenate(spectral, axis=0))
+    wide = dot(jnp.concatenate([high, low], axis=1), fxhh[...]) + dot(high, fxl[...])
+    high, low = parts(wide * inv_den[...])
+    back = dot(high, bxh[...]) + dot(low, bxh[...]) + dot(high, bxl[...])
+    step = SPECTRAL_Y
+    back = left_pairs(by, [back[step * i : step * (i + 1)] for i in range(10)])
     planes = along_z(back, BZ)
     edge = edge_rows(ROWS, near[2], near[3])
     row = lax.broadcasted_iota(jnp.int32, (ROWS, LANES), 0)
@@ -455,17 +471,17 @@
 
 
 def schwarz_kernel(
-    near, inv_den, fyh, fyl, fxh, fxl, bxh, bxl, byh, byl, b, zlo, zhi, ylo, yhi,
-    w_ref, wlo, whi,
+    near, inv_den, fy, fxhh, fxl, bxh, bxl, by, b, zlo, zhi, ylo, yhi, w_ref, wlo, whi
 ):
-    tables = ((fyh, fyl), (fxh, fxl), (bxh, bxl), (byh, byl))
+    tables = (fy, fxhh, fxl, bxh, bxl, by)
     schwarz(b, zlo, zhi, ylo, yhi, tables, inv_den, near, w_ref, wlo, whi)
 
 
-def galerkin_kernel(near, packed, stat_in, flux, w, zlo, zhi, zl_ref, stat):
+def galerkin_kernel(near, packed, stat_in, flux, w, zlo, zhi, zl_ref, y_ref, stat):
     local = add_planes(w, zlo[...], zhi[...])
     zl_ref[...] = local
     applied = local_operator(local, flux[...], packed)
+    y_ref[...] = applied
     inner = near[0] * applied[0] + near[1] * applied[7]
     for i in range(1, 7):
         inner = inner + applied[i]
@@ -665,7 +681,7 @@
         )
 
 
-def add_coarse(local, near, coarse, start):
+def coarse_columns(near, coarse, start):
     row = lax.broadcasted_iota(jnp.int32, (ROWS, LANES), 0)
     edge = edge_rows(ROWS, near[2], near[3])
     below = jnp.where(row == 0, 1.0 - near[2], 0.0)
@@ -676,16 +692,43 @@
         columns.append(
             below * coarse[at : at + 1] + edge * coarse[at + 1 : at + 2] + above * coarse[at + 2 : at + 3]
         )
-    planes = [local[i] + columns[1] for i in range(8)]
-    planes[0] = planes[0] + (1.0 - near[0]) * (columns[0] - columns[1])
-    planes[7] = planes[7] + (1.0 - near[1]) * (columns[2] - columns[1])
+    first = (1.0 - near[0]) * (columns[0] - columns[1])
+    last = (1.0 - near[1]) * (columns[2] - columns[1])
+    return columns[1], first, last
+
+
+def add_coarse(local, columns):
+    inside, first, last = columns
+    planes = [local[i] + inside for i in range(8)]
+    planes[0] = planes[0] + first
+    planes[7] = planes[7] + last
     return stack(planes)
 
 
-def apply_kernel(near, packed, coarse, flux, b, zl, z_ref, y_ref, ylo, yhi, stat):
-    field = add_coarse(zl[...], near, coarse, 0)
+def coarse_applied(columns, flux, packed):
+    inside, first, last = columns
+    slopes = [
+        flux[i] * (float(DERIV[i, 0]) * first + float(DERIV[i, 7]) * last) for i in range(8)
+    ]
+    fz = along_z(slopes, DERIV.T)
+    three = stack([inside + first, inside, inside + last])
+    gy = along_y(three, packed, 0)
+    fy = along_y(
+        stack([flux[i] * gy[0 if i == 0 else 2 if i == 7 else 1] for i in range(8)]), packed, 1
+    )
+    plane_w = packed[0:ROWS]
+    planes = []
+    for i in range(8):
+        plane = three[0 if i == 0 else 2 if i == 7 else 1]
+        planes.append(fz[i] + fy[i] + (HELM_COEF * 0.125 * float(WEIGHT[i])) * (plane_w * plane))
+    return stack(planes)
+
+
+def apply_kernel(near, packed, coarse, flux, b, zl, yl, z_ref, y_ref, ylo, yhi, stat):
+    columns = coarse_columns(near, coarse, 0)
+    field = add_coarse(zl[...], columns)
     z_ref[...] = field
-    applied = local_operator(field, flux[...], packed)
+    applied = yl[...] + coarse_applied(columns, flux[...], packed)
     y_ref[...] = applied
     ylo[...] = applied[0:2]
     yhi[...] = applied[6:8]
@@ -694,7 +737,7 @@
 
 def second_kernel(near, packed, coarse, flux, b, y, w, zlo, zhi, stat_in, q_ref, stat):
     local = add_planes(w, zlo[...], zhi[...])
-    field = add_coarse(local, near, coarse, 16)
+    field = add_coarse(local, coarse_columns(near, coarse, 16))
     q_ref[...] = field
     applied = local_operator(field, flux[...], packed)
     sums = [0.0, 0.0, jnp.sum(b[...] * field), jnp.sum(y[...] * field), jnp.sum(field * applied)]
@@ -749,7 +792,7 @@
     near = jnp.stack(ends(index_gx, count_gx) + ends(index_gy, count_gy)).astype(F32)
     place = jnp.stack([index_gx, index_gy]).astype(jnp.int32)
     packed = jnp.asarray(PACKED)
-    solver = (INV_DEN, FY_H, FY_L, FX_H, FX_L, BX_H, BX_L, BY_H, BY_L)
+    solver = (INV_DEN, FY_W, FX_HH, FX_L, BX_H, BX_L, BY_W)
     solver = tuple(jnp.asarray(table) for table in solver)
     face = (ROWS, LANES)
     rim = (12, TILE, LANES)
@@ -759,11 +802,13 @@
         advect_kernel,
         [block, block, (3, *face), (3, *face)],
         [],
-        [level_set, velocity, source, packed],
+        [
+            pltpu.with_memory_space_constraint(array, pltpu.HBM)
+            for array in (level_set, velocity, source, packed)
+        ],
         [VMEM(block, F32), VMEM((3, *block), F32), VMEM(block, F32), VMEM(PACKED.shape, F32)]
         + [pltpu.SemaphoreType.DMA((4,))],
-        place=pl.ANY,
-        limit=56 * 1024 * 1024,
+        place=pltpu.HBM,
     )
     zlo, zhi = shift("gx", zlo, zhi)
     ylo, yhi = run(functools.partial(rim_kernel, 2), [rim, rim], [], [b, l, zlo, zhi])
@@ -782,9 +827,9 @@
         ],
         flops=20000000,
     )
-    zl, stat = run(
+    zl, yl, stat = run(
         galerkin_kernel,
-        [block, (count_gy, LANES)],
+        [block, block, (count_gy, LANES)],
         [near],
         [packed, stat, flux, w, wlo, whi],
     )
@@ -800,7 +845,7 @@
         apply_kernel,
         [block, block, (2, *face), (2, *face), (1, LANES)],
         [near],
-        [packed, coarse, flux, b, zl],
+        [packed, coarse, flux, b, zl, yl],
     )
     zlo, zhi = shift("gx", zlo, zhi)
     ylo, yhi = run(functools.partial(rim_kernel, 1), [rim, rim], [], [y, zlo, zhi])

time: 139 us -> 135 us (0.971)
  local copies, waits for them, and re-layouts: 1.91 us -> 0.08 us
  Pallas kernels: 16.8 us -> 15.1 us
    unnamed x34 -> x22, local copies, waits for them, and re-layouts: 1.89 us -> 0.06 us
    pallas_call x12, Pallas kernels: 16.8 us -> 15.1 us  [run(): pl.pallas_call(kernel, out_shape=[jax.ShapeDtypeStruct(out, F32) for out...]
  transfers between devices with their start and end apart: 13 -> 13, of which waited for: 8 -> 7; matrix products, arithmetic and copies ran while one was open for 0% -> 0% of each run, Pallas kernels for 1% -> 1%
where the time goes in v4:
time: 135 us; the launch traced here: 134 us
  blocking collectives  49.2 us (36%)
  starting transfers between devices  39.4 us (29%)
  waiting for transfers between devices  29 us (21%)
  Pallas kernels  15.1 us (11%)
    ppermute x6, starting transfers between devices, shift(): lax.ppermute(high_face, axis, forward)  23.7 us
    ppermute x6, waiting for transfers between devices, shift(): lax.ppermute(low_face, axis, backward)  21.8 us
    all_to_all x1, blocking collectives, body(): gathered = lax.all_to_all(stat, 'gy', 0, 0, tiled=True)  21.4 us
    all_to_all x1, blocking collectives, body(): wide = lax.all_to_all(wide, 'gy', 0, 0, tiled=True)  17.7 us
    pallas_call x12, Pallas kernels, run(): pl.pallas_call(kernel, out_shape=[jax.ShapeDtypeStruct(out, F32) for out...  15.1 us
    all_to_all x1, blocking collectives, body(): tile = lax.all_to_all(sums, 'gx', 0, 0, tiled=True)  10 us
    ppermute x6, starting transfers between devices, shift(): lax.ppermute(low_face, axis, backward)  9.32 us
    all_to_all x1, waiting for transfers between devices, body(): gathered = lax.all_to_all(turned, 'gx', 0, 0, tiled=True)  7.16 us
  transfers between devices with their start and end apart: 13, of which 7 were waited for; matrix products, arithmetic and copies ran while one was open for 0% of the time, Pallas kernels for 1%

profile of v4, /device:TPU:1, one launch (start us, length us, event | category | flops | bytes accessed | tf_op | source)
XLA Modules:
  0.0 133.9 jit_solution(11316050350200145596)
XLA Ops:
  0.6 0.0 copy-start.1
  0.6 1.8 %shard_map.149 = (f32[8,32,128]{2,1,0:T(8,128)S(1)}, f32[8,32,128]{2,1,0:T(8,128)S(1)}, f32[3,32,128]{2,1,0:T(8,128)S(1)}, f32[3,32,128]{2,1,0:T(8,128)S(1)}) custom-call(f32[8,32,128]{2,1,0:T(8,128)} %lev_in.1, f32[3,8,32,128]{3,2,1,0:T(8,128)} %vel_in.1, f32[8,32,128]{2,1,0:T(8,128)} %src_in.1, f32[432,128]{1,0:T(8,128)} %constant.41.clone.packed_in.packed), custom_call_target="tpu_custom_call" | custom-call | flops 1000000 | bytes 720896 | tf_op jit(solution)/shard_map/pallas_call | solution.py:763
  2.4 4.8 %collective-permute-start = (f32[3,32,128]{2,1,0:T(8,128)S(1)}, f32[3,32,128]{2,1,0:T(8,128)S(1)}, u32[]{:S(2)}, u32[]{:S(2)}) collective-permute-start(f32[3,32,128]{2,1,0:T(8,128)S(1)} %get-tuple-element.31), channel_id=1, source_target_pairs={{0,64},{64,128},{128,192},{192,256},{256,320},{320,384},{384,448},... | collective-permute-start | bytes 147464 | tf_op jit(solution)/shard_map/ppermute | solution.py:779
  7.3 1.3 collective-permute-start.1
  8.6 0.0 collective-permute-done.refs_2_.zlo
  8.6 4.1 %collective-permute-done.1.refs_3_.zhi = f32[3,32,128]{2,1,0:T(8,128)S(1)} collective-permute-done((f32[3,32,128]{2,1,0:T(8,128)S(1)}, f32[3,32,128]{2,1,0:T(8,128)S(1)}, u32[]{:S(2)}, u32[]{:S(2)}) %collective-permute-start.1) | collective-permute-done | bytes 49184 | tf_op jit(solution)/shard_map/ppermute | solution.py:779
  12.7 0.0 copy-start.6
  12.8 0.0 copy-start.7
  12.8 5.0 %collective-permute-start.2 = (f32[12,16,128]{2,1,0:T(8,128)S(1)}, f32[12,16,128]{2,1,0:T(8,128)S(1)}, u32[]{:S(2)}, u32[]{:S(2)}) collective-permute-start(f32[12,16,128]{2,1,0:T(8,128)S(1)} %get-tuple-element.33), channel_id=1, source_target_pairs={{0,1},{1,2},{2,3},{3,4},{4,5},{5,6},{6,7},{7,8},{8,9},{9,10},{10,1... | collective-permute-start | bytes 294920 | tf_op jit(solution)/shard_map/ppermute | solution.py:779
  17.8 2.2 %collective-permute-start.3 = (f32[12,16,128]{2,1,0:T(8,128)S(1)}, f32[12,16,128]{2,1,0:T(8,128)S(1)}, u32[]{:S(2)}, u32[]{:S(2)}) collective-permute-start(f32[12,16,128]{2,1,0:T(8,128)S(1)} %get-tuple-element.34), channel_id=1, source_target_pairs={{1,0},{2,1},{3,2},{4,3},{5,4},{6,5},{7,6},{8,7},{9,8},{10,9},{11,1... | collective-permute-start | bytes 294920 | tf_op jit(solution)/shard_map/ppermute | solution.py:779
  20.0 0.1 pad_maximum_fusion.near
  20.1 0.0 collective-permute-done.2.ylo
  20.1 3.6 %collective-permute-done.3.yhi = f32[12,16,128]{2,1,0:T(8,128)S(1)} collective-permute-done((f32[12,16,128]{2,1,0:T(8,128)S(1)}, f32[12,16,128]{2,1,0:T(8,128)S(1)}, u32[]{:S(2)}, u32[]{:S(2)}) %collective-permute-start.3) | collective-permute-done | bytes 98336 | tf_op jit(solution)/shard_map/ppermute | solution.py:779
  23.7 0.0 copy-done.1
  23.8 0.0 copy-start.10
  23.8 0.0 copy-start.8
  23.8 1.9 %shard_map.152 = (f32[8,32,128]{2,1,0:T(8,128)S(1)}, f32[32,128]{1,0:T(8,128)S(1)}, f32[32,128]{1,0:T(8,128)S(1)}) custom-call(f32[4]{0:T(128)S(1)} %pad_maximum_fusion.near, f32[640,160]{1,0:T(8,128)S(1)} %copy-done.1, bf16[64,192]{1,0:T(8,128)(2,1)S(1)} %copy-done.6, bf16[256,160]{1,0:T(8,128)(2,1)S(1)} %copy-done.2, bf16[128,160]{1,0:T(8,128)(2,1)S(1)} %copy-done.3, ...), custom_call_target="tpu_custom_call" | custom-call | flops 1000000 | bytes 327680 | tf_op jit(solution)/shard_map/pallas_call | solution.py:763
  25.7 0.0 copy-start.9
  25.7 4.0 %collective-permute-start.4 = (f32[32,128]{1,0:T(8,128)S(1)}, f32[32,128]{1,0:T(8,128)S(1)}, u32[]{:S(2)}, u32[]{:S(2)}) collective-permute-start(f32[32,128]{1,0:T(8,128)S(1)} %get-tuple-element.39), channel_id=1, source_target_pairs={{0,64},{64,128},{128,192},{192,256},{256,320},{320,384},{384,448},... | collective-permute-start | bytes 49160 | tf_op jit(solution)/shard_map/ppermute | solution.py:779
  29.7 1.3 collective-permute-start.5
  31.1 1.4 %shard_map.151 = (f32[8,32,128]{2,1,0:T(8,128)}, f32[8,32,128]{2,1,0:T(8,128)S(1)}, f32[1,128]{1,0:T(1,128)S(1)}) custom-call(f32[4]{0:T(128)S(1)} %pad_maximum_fusion.near, f32[4,16]{1,0:T(4,128)S(1)} %convert_bitcast_fusion.solid, bf16[16,128]{1,0:T(8,128)(2,1)S(1)} %copy-done.9, f32[32,128]{1,0:T(8,128)S(1)} %copy-done.8, f32[432,128]{1,0:T(8,128)S(1)} %copy-done, ...), custom_call_target="tpu_custom_call" | custom-call | flops 20000000 | bytes 525312 | tf_op jit(solution)/shard_map/pallas_call | solution.py:763
  32.4 0.0 collective-permute-done.4.zlo
  32.4 3.6 %collective-permute-done.5.zhi = f32[32,128]{1,0:T(8,128)S(1)} collective-permute-done((f32[32,128]{1,0:T(8,128)S(1)}, f32[32,128]{1,0:T(8,128)S(1)}, u32[]{:S(2)}, u32[]{:S(2)}) %collective-permute-start.5) | collective-permute-done | bytes 16416 | tf_op jit(solution)/shard_map/ppermute | solution.py:779
  36.0 1.2 shard_map.153
  37.3 21.4 %all_to_all.33 = f32[64,1,128]{2,1,0:T(1,128)S(1)} all-to-all(f32[64,1,128]{2,1,0:T(1,128)S(1)} %bitcast.18), channel_id=1, replica_groups=mesh['gx'=8,'gy'=64] {'gy'}, dimensions={0} | all-to-all | bytes 65536 | tf_op jit(solution)/shard_map/all_to_all | solution.py:836
  58.7 0.8 shard_map.154
  59.5 6.4 %all-to-all-start.1 = ((f32[8,16,128]{2,1,0:T(8,128)}), f32[8,16,128]{2,1,0:T(8,128)S(1)}, u32[]{:S(2)}, u32[]{:S(2)}) async-start(f32[8,16,128]{2,1,0:T(8,128)} %shard_map.154), calls=%async_computation.1 | async-start | bytes 131072 | tf_op jit(solution)/shard_map/all_to_all | solution.py:840
  65.9 0.1 pad_add_fusion.place
  66.0 7.2 %all-to-all-done.1.gathered = f32[8,16,128]{2,1,0:T(8,128)S(1)} async-done(((f32[8,16,128]{2,1,0:T(8,128)}), f32[8,16,128]{2,1,0:T(8,128)S(1)}, u32[]{:S(2)}, u32[]{:S(2)}) %all-to-all-start.1) | async-done | bytes 65568 | tf_op jit(solution)/shard_map/all_to_all | solution.py:840
  73.1 3.1 %shard_map.155.coarse = f32[32,128]{1,0:T(8,128)S(1)} custom-call(s32[2]{0:T(128)S(1)} %pad_add_fusion.place, f32[8,16,128]{2,1,0:T(8,128)S(1)} %all-to-all-done.1.gathered), custom_call_target="tpu_custom_call" | custom-call | flops 1000000 | bytes 32768 | tf_op jit(solution)/shard_map/pallas_call | solution.py:763
  76.2 1.0 shard_map.156
  77.2 2.2 %collective-permute-start.6 = (f32[2,32,128]{2,1,0:T(8,128)S(1)}, f32[2,32,128]{2,1,0:T(8,128)S(1)}, u32[]{:S(2)}, u32[]{:S(2)}) collective-permute-start(f32[2,32,128]{2,1,0:T(8,128)S(1)} %get-tuple-element.45), channel_id=1, source_target_pairs={{0,64},{64,128},{128,192},{192,256},{256,320},{320,384},{384,448},... | collective-permute-start | bytes 98312 | tf_op jit(solution)/shard_map/ppermute | solution.py:779
  79.4 1.3 collective-permute-start.7
  80.7 0.0 collective-permute-done.6.refs_1_.zlo
  80.7 3.3 %collective-permute-done.7.refs_2_.zhi = f32[2,32,128]{2,1,0:T(8,128)S(1)} collective-permute-done((f32[2,32,128]{2,1,0:T(8,128)S(1)}, f32[2,32,128]{2,1,0:T(8,128)S(1)}, u32[]{:S(2)}, u32[]{:S(2)}) %collective-permute-start.7) | collective-permute-done | bytes 32800 | tf_op jit(solution)/shard_map/ppermute | solution.py:779
  84.0 5.6 %collective-permute-start.8 = (f32[12,16,128]{2,1,0:T(8,128)S(1)}, f32[12,16,128]{2,1,0:T(8,128)S(1)}, u32[]{:S(2)}, u32[]{:S(2)}) collective-permute-start(f32[12,16,128]{2,1,0:T(8,128)S(1)} %get-tuple-element.47), channel_id=1, source_target_pairs={{0,1},{1,2},{2,3},{3,4},{4,5},{5,6},{6,7},{7,8},{8,9},{9,10},{10,1... | collective-permute-start | bytes 294920 | tf_op jit(solution)/shard_map/ppermute | solution.py:779
  89.7 1.9 %collective-permute-start.9 = (f32[12,16,128]{2,1,0:T(8,128)S(1)}, f32[12,16,128]{2,1,0:T(8,128)S(1)}, u32[]{:S(2)}, u32[]{:S(2)}) collective-permute-start(f32[12,16,128]{2,1,0:T(8,128)S(1)} %get-tuple-element.48), channel_id=1, source_target_pairs={{1,0},{2,1},{3,2},{4,3},{5,4},{6,5},{7,6},{8,7},{9,8},{10,9},{11,1... | collective-permute-start | bytes 294920 | tf_op jit(solution)/shard_map/ppermute | solution.py:779
  91.6 0.0 collective-permute-done.8.ylo
  91.6 4.0 %collective-permute-done.9.yhi = f32[12,16,128]{2,1,0:T(8,128)S(1)} collective-permute-done((f32[12,16,128]{2,1,0:T(8,128)S(1)}, f32[12,16,128]{2,1,0:T(8,128)S(1)}, u32[]{:S(2)}, u32[]{:S(2)}) %collective-permute-start.9) | collective-permute-done | bytes 98336 | tf_op jit(solution)/shard_map/ppermute | solution.py:779
  95.6 1.9 %shard_map.158 = (f32[8,32,128]{2,1,0:T(8,128)S(1)}, f32[32,128]{1,0:T(8,128)S(1)}, f32[32,128]{1,0:T(8,128)S(1)}) custom-call(f32[4]{0:T(128)S(1)} %pad_maximum_fusion.near, f32[640,160]{1,0:T(8,128)S(1)} %copy-done.1, bf16[64,192]{1,0:T(8,128)(2,1)S(1)} %copy-done.6, bf16[256,160]{1,0:T(8,128)(2,1)S(1)} %copy-done.2, bf16[128,160]{1,0:T(8,128)(2,1)S(1)} %copy-done.3, ...), custom_call_target="tpu_custom_call" | custom-call | flops 1000000 | bytes 327680 | tf_op jit(solution)/shard_map/pallas_call | solution.py:763
  97.5 2.1 %collective-permute-start.10 = (f32[32,128]{1,0:T(8,128)S(1)}, f32[32,128]{1,0:T(8,128)S(1)}, u32[]{:S(2)}, u32[]{:S(2)}) collective-permute-start(f32[32,128]{1,0:T(8,128)S(1)} %get-tuple-element.50), channel_id=1, source_target_pairs={{0,64},{64,128},{128,192},{192,256},{256,320},{320,384},{384,448},... | collective-permute-start | bytes 49160 | tf_op jit(solution)/shard_map/ppermute | solution.py:779
  99.6 1.3 collective-permute-start.11
  100.9 0.0 collective-permute-done.10.zlo
  100.9 3.2 %collective-permute-done.11.zhi = f32[32,128]{1,0:T(8,128)S(1)} collective-permute-done((f32[32,128]{1,0:T(8,128)S(1)}, f32[32,128]{1,0:T(8,128)S(1)}, u32[]{:S(2)}, u32[]{:S(2)}) %collective-permute-start.11) | collective-permute-done | bytes 16416 | tf_op jit(solution)/shard_map/ppermute | solution.py:779
  104.1 1.2 shard_map.159
  105.3 10.0 %all_to_all.34 = f32[8,1,128]{2,1,0:T(1,128)S(1)} all-to-all(f32[8,1,128]{2,1,0:T(1,128)S(1)} %bitcast.19), channel_id=1, replica_groups=mesh['gx'=8,'gy'=64] {'gx'}, dimensions={0} | all-to-all | bytes 8192 | tf_op jit(solution)/shard_map/all_to_all | solution.py:863
  115.4 17.7 %all_to_all.35 = f32[64,1,128]{2,1,0:T(1,128)S(1)} all-to-all(f32[64,1,128]{2,1,0:T(1,128)S(1)} %broadcast_in_dim.2), channel_id=1, replica_groups=mesh['gx'=8,'gy'=64] {'gy'}, dimensions={0} | all-to-all | bytes 65536 | tf_op jit(solution)/shard_map/all_to_all | solution.py:865
  133.1 0.8 shard_map.160
  (20 shorter events, 0.1 us)
Async XLA Ops:
  0.6 23.1 %copy-start.1 = (f32[640,160]{1,0:T(8,128)S(1)}, f32[640,160]{1,0:T(8,128)}, u32[]{:S(2)}) copy-start(f32[640,160]{1,0:T(8,128)} %constant.42.clone.inv_den) | copy-start | bytes 1228804
  2.4 6.2 %collective-permute-start = (f32[3,32,128]{2,1,0:T(8,128)S(1)}, f32[3,32,128]{2,1,0:T(8,128)S(1)}, u32[]{:S(2)}, u32[]{:S(2)}) collective-permute-start(f32[3,32,128]{2,1,0:T(8,128)S(1)} %get-tuple-element.31), channel_id=1, source_target_pairs={{0,64},{64,128},{128,192},{192,256},{256,320},{320,384},{384,448},... | collective-permute-start | bytes 147464 | tf_op jit(solution)/shard_map/ppermute | solution.py:779
  7.3 5.5 %collective-permute-start.1 = (f32[3,32,128]{2,1,0:T(8,128)S(1)}, f32[3,32,128]{2,1,0:T(8,128)S(1)}, u32[]{:S(2)}, u32[]{:S(2)}) collective-permute-start(f32[3,32,128]{2,1,0:T(8,128)S(1)} %get-tuple-element.32), channel_id=1, source_target_pairs={{64,0},{128,64},{192,128},{256,192},{320,256},{384,320},{448,384},... | collective-permute-start | bytes 147464 | tf_op jit(solution)/shard_map/ppermute | solution.py:779
  12.7 11.0 %copy-start.2 = (bf16[256,160]{1,0:T(8,128)(2,1)S(1)}, bf16[256,160]{1,0:T(8,128)(2,1)}, u32[]{:S(2)}) copy-start(bf16[256,160]{1,0:T(8,128)(2,1)} %constant.44.clone.fxhh) | copy-start | bytes 245764
  12.7 11.0 %copy-start.3 = (bf16[128,160]{1,0:T(8,128)(2,1)S(1)}, bf16[128,160]{1,0:T(8,128)(2,1)}, u32[]{:S(2)}) copy-start(bf16[128,160]{1,0:T(8,128)(2,1)} %constant.45.clone.fxl) | copy-start | bytes 122884
  12.7 11.0 %copy-start.4 = (bf16[160,128]{1,0:T(8,128)(2,1)S(1)}, bf16[160,128]{1,0:T(8,128)(2,1)}, u32[]{:S(2)}) copy-start(bf16[160,128]{1,0:T(8,128)(2,1)} %constant.47.clone.bxl) | copy-start | bytes 122884
  12.7 11.0 %copy-start.5 = (bf16[160,128]{1,0:T(8,128)(2,1)S(1)}, bf16[160,128]{1,0:T(8,128)(2,1)}, u32[]{:S(2)}) copy-start(bf16[160,128]{1,0:T(8,128)(2,1)} %constant.46.clone.bxh) | copy-start | bytes 122884
  12.7 11.0 %copy-start.6 = (bf16[64,192]{1,0:T(8,128)(2,1)S(1)}, bf16[64,192]{1,0:T(8,128)(2,1)}, u32[]{:S(2)}) copy-start(bf16[64,192]{1,0:T(8,128)(2,1)} %constant.43.clone.fy) | copy-start | bytes 73732
  12.8 11.0 %copy-start.7 = (bf16[40,192]{1,0:T(8,128)(2,1)S(1)}, bf16[40,192]{1,0:T(8,128)(2,1)}, u32[]{:S(2)}) copy-start(bf16[40,192]{1,0:T(8,128)(2,1)} %constant.48.clone.by) | copy-start | bytes 46084
  12.8 7.3 %collective-permute-start.2 = (f32[12,16,128]{2,1,0:T(8,128)S(1)}, f32[12,16,128]{2,1,0:T(8,128)S(1)}, u32[]{:S(2)}, u32[]{:S(2)}) collective-permute-start(f32[12,16,128]{2,1,0:T(8,128)S(1)} %get-tuple-element.33), channel_id=1, source_target_pairs={{0,1},{1,2},{2,3},{3,4},{4,5},{5,6},{6,7},{7,8},{8,9},{9,10},{10,1... | collective-permute-start | bytes 294920 | tf_op jit(solution)/shard_map/ppermute | solution.py:779
  17.8 5.9 %collective-permute-start.3 = (f32[12,16,128]{2,1,0:T(8,128)S(1)}, f32[12,16,128]{2,1,0:T(8,128)S(1)}, u32[]{:S(2)}, u32[]{:S(2)}) collective-permute-start(f32[12,16,128]{2,1,0:T(8,128)S(1)} %get-tuple-element.34), channel_id=1, source_target_pairs={{1,0},{2,1},{3,2},{4,3},{5,4},{6,5},{7,6},{8,7},{9,8},{10,9},{11,1... | collective-permute-start | bytes 294920 | tf_op jit(solution)/shard_map/ppermute | solution.py:779
  20.1 10.9 %copy-start = (f32[432,128]{1,0:T(8,128)S(1)}, f32[432,128]{1,0:T(8,128)}, u32[]{:S(2)}) copy-start(f32[432,128]{1,0:T(8,128)} %constant.41.clone.packed_in.packed) | copy-start | bytes 663556
  23.8 7.2 %copy-start.10 = (s32[1,4,16]{2,1,0:T(4,128)S(1)}, s32[1,4,16]{2,1,0:T(4,128)}, u32[]{:S(2)}) copy-start(s32[1,4,16]{2,1,0:T(4,128)} %param.17) | copy-start | bytes 772
  23.8 7.3 %copy-start.8 = (f32[32,128]{1,0:T(8,128)S(1)}, f32[32,128]{1,0:T(8,128)}, u32[]{:S(2)}) copy-start(f32[32,128]{1,0:T(8,128)} %constant.50.clone.inv_mass) | copy-start | bytes 49156
  25.7 5.4 %copy-start.9 = (bf16[16,128]{1,0:T(8,128)(2,1)S(1)}, bf16[16,128]{1,0:T(8,128)(2,1)}, u32[]{:S(2)}) copy-start(bf16[16,128]{1,0:T(8,128)(2,1)} %constant.49.clone.spread) | copy-start | bytes 12292
  25.7 6.7 %collective-permute-start.4 = (f32[32,128]{1,0:T(8,128)S(1)}, f32[32,128]{1,0:T(8,128)S(1)}, u32[]{:S(2)}, u32[]{:S(2)}) collective-permute-start(f32[32,128]{1,0:T(8,128)S(1)} %get-tuple-element.39), channel_id=1, source_target_pairs={{0,64},{64,128},{128,192},{192,256},{256,320},{320,384},{384,448},... | collective-permute-start | bytes 49160 | tf_op jit(solution)/shard_map/ppermute | solution.py:779
  29.7 6.3 %collective-permute-start.5 = (f32[32,128]{1,0:T(8,128)S(1)}, f32[32,128]{1,0:T(8,128)S(1)}, u32[]{:S(2)}, u32[]{:S(2)}) collective-permute-start(f32[32,128]{1,0:T(8,128)S(1)} %get-tuple-element.40), channel_id=1, source_target_pairs={{64,0},{128,64},{192,128},{256,192},{320,256},{384,320},{448,384},... | collective-permute-start | bytes 49160 | tf_op jit(solution)/shard_map/ppermute | solution.py:779
  59.5 13.6 %all-to-all-start.1 = ((f32[8,16,128]{2,1,0:T(8,128)}), f32[8,16,128]{2,1,0:T(8,128)S(1)}, u32[]{:S(2)}, u32[]{:S(2)}) async-start(f32[8,16,128]{2,1,0:T(8,128)} %shard_map.154), calls=%async_computation.1 | async-start | bytes 131072 | tf_op jit(solution)/shard_map/all_to_all | solution.py:840
  77.2 3.5 %collective-permute-start.6 = (f32[2,32,128]{2,1,0:T(8,128)S(1)}, f32[2,32,128]{2,1,0:T(8,128)S(1)}, u32[]{:S(2)}, u32[]{:S(2)}) collective-permute-start(f32[2,32,128]{2,1,0:T(8,128)S(1)} %get-tuple-element.45), channel_id=1, source_target_pairs={{0,64},{64,128},{128,192},{192,256},{256,320},{320,384},{384,448},... | collective-permute-start | bytes 98312 | tf_op jit(solution)/shard_map/ppermute | solution.py:779
  79.4 4.7 %collective-permute-start.7 = (f32[2,32,128]{2,1,0:T(8,128)S(1)}, f32[2,32,128]{2,1,0:T(8,128)S(1)}, u32[]{:S(2)}, u32[]{:S(2)}) collective-permute-start(f32[2,32,128]{2,1,0:T(8,128)S(1)} %get-tuple-element.46), channel_id=1, source_target_pairs={{64,0},{128,64},{192,128},{256,192},{320,256},{384,320},{448,384},... | collective-permute-start | bytes 98312 | tf_op jit(solution)/shard_map/ppermute | solution.py:779
  84.0 7.6 %collective-permute-start.8 = (f32[12,16,128]{2,1,0:T(8,128)S(1)}, f32[12,16,128]{2,1,0:T(8,128)S(1)}, u32[]{:S(2)}, u32[]{:S(2)}) collective-permute-start(f32[12,16,128]{2,1,0:T(8,128)S(1)} %get-tuple-element.47), channel_id=1, source_target_pairs={{0,1},{1,2},{2,3},{3,4},{4,5},{5,6},{6,7},{7,8},{8,9},{9,10},{10,1... | collective-permute-start | bytes 294920 | tf_op jit(solution)/shard_map/ppermute | solution.py:779
  89.7 5.9 %collective-permute-start.9 = (f32[12,16,128]{2,1,0:T(8,128)S(1)}, f32[12,16,128]{2,1,0:T(8,128)S(1)}, u32[]{:S(2)}, u32[]{:S(2)}) collective-permute-start(f32[12,16,128]{2,1,0:T(8,128)S(1)} %get-tuple-element.48), channel_id=1, source_target_pairs={{1,0},{2,1},{3,2},{4,3},{5,4},{6,5},{7,6},{8,7},{9,8},{10,9},{11,1... | collective-permute-start | bytes 294920 | tf_op jit(solution)/shard_map/ppermute | solution.py:779
  97.5 3.4 %collective-permute-start.10 = (f32[32,128]{1,0:T(8,128)S(1)}, f32[32,128]{1,0:T(8,128)S(1)}, u32[]{:S(2)}, u32[]{:S(2)}) collective-permute-start(f32[32,128]{1,0:T(8,128)S(1)} %get-tuple-element.50), channel_id=1, source_target_pairs={{0,64},{64,128},{128,192},{192,256},{256,320},{320,384},{384,448},... | collective-permute-start | bytes 49160 | tf_op jit(solution)/shard_map/ppermute | solution.py:779
  99.6 4.5 %collective-permute-start.11 = (f32[32,128]{1,0:T(8,128)S(1)}, f32[32,128]{1,0:T(8,128)S(1)}, u32[]{:S(2)}, u32[]{:S(2)}) collective-permute-start(f32[32,128]{1,0:T(8,128)S(1)} %get-tuple-element.51), channel_id=1, source_target_pairs={{64,0},{128,64},{192,128},{256,192},{320,256},{384,320},{448,384},... | collective-permute-start | bytes 49160 | tf_op jit(solution)/shard_map/ppermute | solution.py:779

commit v5 on v4

--- a/solution.py
+++ b/solution.py
@@ -496,14 +496,40 @@
     stat[...] = jnp.broadcast_to(stat_in[...] + lane_row(entries), stat.shape)
 
 
-def turn_kernel(gathered, out_ref, wide):
-    count = gathered.shape[0]
-    wide[...] = jnp.zeros((LANES, LANES), F32)
-    wide[0:count] = gathered[...]
-    turned = wide[...].T
-    tile = turned[0:16] + pltpu.roll(turned[16:32], LANES // 2, 1)
-    for i in range(out_ref.shape[0]):
-        out_ref[i] = tile
+def column_kernel(gathered, out_ref):
+    values = gathered[...]
+    sub = lax.broadcasted_iota(jnp.int32, (8, LANES), 0)
+    lane = lax.broadcasted_iota(jnp.int32, (8, LANES), 1)
+    after = jnp.where(sub < 7, pltpu.roll(values, 7, 0), 0.0)
+    before = jnp.where(sub > 0, pltpu.roll(values, 1, 0), 0.0)
+    first = lax.broadcasted_iota(jnp.int32, (8, 1), 0) == 0
+    last = lax.broadcasted_iota(jnp.int32, (8, 1), 0) == 7
+
+    def column(array, index):
+        return array[:, index : index + 1]
+
+    def slopes(array, pair):
+        whole, low, high = (column(array, 11 + 3 * pair + k) for k in range(3))
+        return whole - low - high, low, high
+
+    merged = [column(values, 0), column(values, 1)]
+    for b in range(3):
+        merged.append(column(values, 5 + b) + column(after, 2 + b) + column(before, 8 + b))
+    merged += [own + other for own, other in zip(slopes(values, 0), slopes(before, 2), strict=True)]
+    merged += list(slopes(values, 1))
+    inside, interface = [], []
+    for side in range(2):
+        whole, low, high = (column(values, 20 + 3 * side + k) for k in range(3))
+        ends = jnp.where(first, low, 0.0) + jnp.where(last, high, 0.0)
+        inside.append(whole - low - high + ends)
+        interface.append(jnp.where(first, 0.0, low) + column(before, 22 + 3 * side))
+    rows = jnp.zeros((8, LANES), F32)
+    for index, value in enumerate(merged + inside + interface):
+        rows = jnp.where(lane == index, value, rows)
+    total = rows[0:1]
+    for i in range(1, 8):
+        total = total + pltpu.roll(rows[i : i + 1], 16 * i, 1)
+    out_ref[...] = jnp.broadcast_to(total, out_ref.shape)
 
 
 def invert(blocks, sub):
@@ -541,68 +567,63 @@
     return result
 
 
-def coarse_operator(c, sums_z, sums_y, low_z, high_z, low_y, high_y):
-    result = [[None] * 3 for _ in range(3)]
-
-    def ends(values, low, high):
-        inside = values[1]
-        first = (1.0 - low) * inside + low * values[0]
-        last = (1.0 - high) * inside + high * values[2]
-        return inside, first, last
-
-    def tested(inside, first, last, low, high):
-        return (low * first, inside + (1.0 - low) * first + (1.0 - high) * last, high * last)
-
-    by_b = []
-    for b in range(3):
-        inside, first, last = ends([c[a][b] for a in range(3)], low_z, high_z)
-        end = float(WEIGHT[0])
-        by_b.append(tested((2.0 - 2.0 * end) * inside, end * first, end * last, low_z, high_z))
-    scale = HELM_COEF / 8.0 * float(np.sum(WX))
-    for a in range(3):
-        inside, first, last = ends([by_b[b][a] for b in range(3)], low_y, high_y)
-        end = scale * float(WEIGHT[0])
-        middle = scale * (2.0 * EY - 2.0 * float(WEIGHT[0]))
-        result[a] = list(tested(middle * inside, end * first, end * last, low_y, high_y))
-
-    slopes = []
-    for outer, factor in ((0, low_z), (2, high_z)):
-        slopes.append(ends([factor * (c[outer][b] - c[1][b]) for b in range(3)], low_y, high_y))
-    for s, (outer, factor) in enumerate(((0, low_z), (2, high_z))):
-        parts_y = []
-        for place in range(3):
-            total = None
-            for t in range(2):
-                whole, first, last = sums_z[s + t]
-                weight = (whole - first - last, first, last)[place]
-                term = weight * slopes[t][place]
-                total = term if total is None else total + term
-            parts_y.append(total)
-        for b, value in enumerate(tested(*parts_y, low_y, high_y)):
-            result[outer][b] = result[outer][b] + factor * value
-            result[1][b] = result[1][b] - factor * value
-
-    for s, (outer, factor) in enumerate(((0, low_y), (2, high_y))):
-        slope = ends([factor * (c[a][outer] - c[a][1]) for a in range(3)], low_z, high_z)
-        whole, first, last = sums_y[s]
-        pieces = ((whole - first - last) * slope[0], first * slope[1], last * slope[2])
-        for a, value in enumerate(tested(*pieces, low_z, high_z)):
-            result[a][outer] = result[a][outer] + factor * value
-            result[a][1] = result[a][1] - factor * value
-    return result
-
-
-def coarse_kernel(count, place, gathered, out_ref):
+def coarse_operator(c, count, sums_z, couplings_z, inside_y, interface_y):
+    sub = lax.broadcasted_iota(jnp.int32, c.shape, 0)
+    lane = lax.broadcasted_iota(jnp.int32, c.shape, 1)
+    has_low = lane > 0
+    has_high = lane < count - 1
+
+    def after(array):
+        return jnp.where(sub < 7, pltpu.roll(array, 7, 0), 0.0)
+
+    def before(array):
+        return jnp.where(sub > 0, pltpu.roll(array, 1, 0), 0.0)
+
+    def right(array):
+        return jnp.where(has_high, pltpu.roll(array, LANES - 1, 1), 0.0)
+
+    def left(array):
+        return jnp.where(has_low, pltpu.roll(array, 1, 1), 0.0)
+
+    on_low = jnp.where(has_low, 0.5 * (c + left(c)), c)
+    on_high = jnp.where(has_high, 0.5 * (c + right(c)), c)
+    tested = []
+    for place, value in enumerate((c, on_low, on_high)):
+        slope = jnp.where(sub > 0, 0.5 * (value - before(value)), 0.0)
+        coupling = couplings_z[place]
+        force = sums_z[place] * slope - coupling * after(slope) - before(coupling * slope)
+        force = jnp.where(sub > 0, force, 0.0)
+        tested.append(0.5 * (force - after(force)))
+    result = tested[0] + jnp.where(has_low, 0.5, 1.0) * tested[1] + jnp.where(has_high, 0.5, 1.0) * tested[2]
+    result = result + 0.5 * right(tested[1]) + 0.5 * left(tested[2])
+
+    interface = jnp.where(sub > 0, 0.5 * (c + before(c)), 0.0)
+    for side, (move, there) in enumerate(((left, has_low), (right, has_high))):
+        force = inside_y[side] * jnp.where(there, 0.5 * (move(c) - c), 0.0)
+        face = interface_y[side] * jnp.where(there, 0.5 * (move(interface) - interface), 0.0)
+        force = force + 0.5 * (face + after(face))
+        back = right if side == 0 else left
+        result = result + 0.5 * (back(force) - force)
+
+    end = float(WEIGHT[0])
+    mass = (2.0 - 2.0 * end) * c + end * (interface + after(interface))
+    mass = mass + jnp.where((sub == 0) | (sub == 7), end * c, 0.0)
+    beside = jnp.where(has_low, 0.5 * (mass + left(mass)), 0.0)
+    scaled = (2.0 * EY - 2.0 * end) * mass + end * (beside + right(beside))
+    scaled = scaled + jnp.where(has_low, 0.0, end * mass) + jnp.where(has_high, 0.0, end * mass)
+    return result + HELM_COEF / 8.0 * float(np.sum(WX)) * scaled
+
+
+def coarse_kernel(count, place, gathered, out_ref, wide, turned):
     lanes = LANES
     sub = lax.broadcasted_iota(jnp.int32, (8, lanes), 0)
     lane = lax.broadcasted_iota(jnp.int32, (8, lanes), 1)
+    wide[...] = jnp.zeros((LANES, LANES), F32)
+    wide[0:count] = gathered[...]
+    turned[...] = wide[...].T
 
     def value(index):
-        row = index % 16
-        array = jnp.concatenate([gathered[i, row : row + 1] for i in range(8)], axis=0)
-        if index >= 16:
-            array = pltpu.roll(array, lanes // 2, 1)
-        return jnp.where(lane < count, array, 0.0)
+        return turned[pl.ds(index, 8, stride=16), :]
 
     def move(array, dz, dy):
         if dz:
@@ -658,18 +679,17 @@
     offsets = [(a - 1, b - 1) for a in range(3) for b in range(3)]
     first = solve(value(1))
     near_first = [move(first, dz, dy) for dz, dy in offsets]
-    low_z = jnp.where(sub > 0, 0.5, 0.0)
-    high_z = jnp.where(sub < 7, 0.5, 0.0)
-    low_y = jnp.where(lane > 0, 0.5, 0.0)
-    high_y = jnp.where(lane < count - 1, 0.5, 0.0)
-    sums_z = [[value(11 + 3 * k + j) for j in range(3)] for k in range(3)]
-    sums_y = [[value(20 + 3 * k + j) for j in range(3)] for k in range(2)]
-    values = [near_first[0:3], near_first[3:6], near_first[6:9]]
-    tested = coarse_operator(values, sums_z, sums_y, low_z, high_z, low_y, high_y)
-    totals = jnp.zeros((8, lanes), F32)
-    for d, (dz, dy) in enumerate(offsets):
-        term = jnp.where(lane < count, value(2 + d) + tested[d // 3][d % 3], 0.0)
-        totals = totals + move(term, -dz, -dy)
+    totals = coarse_operator(
+        first,
+        count,
+        [value(5 + k) for k in range(3)],
+        [value(8 + k) for k in range(3)],
+        [value(11), value(12)],
+        [value(13), value(14)],
+    )
+    totals = totals + value(3)
+    totals = totals + jnp.where(lane < count - 1, move(value(2), 0, 1), 0.0)
+    totals = totals + jnp.where(lane > 0, move(value(4), 0, -1), 0.0)
     totals = jnp.where(lane < count, totals, 0.0)
     second = solve(totals)
     near_second = [move(second, dz, dy) for dz, dy in offsets]
@@ -829,17 +849,19 @@
     )
     zl, yl, stat = run(
         galerkin_kernel,
-        [block, block, (count_gy, LANES)],
+        [block, block, (count_gx, LANES)],
         [near],
         [packed, stat, flux, w, wlo, whi],
     )
-    gathered = lax.all_to_all(stat, "gy", 0, 0, tiled=True)
-    (turned,) = run(
-        turn_kernel, [(count_gx, TILE, LANES)], [], [gathered], [VMEM((LANES, LANES), F32)]
-    )
-    gathered = lax.all_to_all(turned, "gx", 0, 0, tiled=True)
+    gathered = lax.all_to_all(stat, "gx", 0, 0, tiled=True)
+    (column,) = run(column_kernel, [(count_gy, LANES)], [], [gathered])
+    gathered = lax.all_to_all(column, "gy", 0, 0, tiled=True)
     (coarse,) = run(
-        functools.partial(coarse_kernel, count_gy), [(32, LANES)], [place], [gathered]
+        functools.partial(coarse_kernel, count_gy),
+        [(32, LANES)],
+        [place],
+        [gathered],
+        [VMEM((LANES, LANES), F32), VMEM((LANES, LANES), F32)],
     )
     z, y, zlo, zhi, sums = run(
         apply_kernel,

time: 135 us -> 133 us (0.985)
  blocking collectives: 49.2 us -> 40.4 us
  starting transfers between devices: 39.4 us -> 44.2 us
  waiting for transfers between devices: 29 us -> 31.1 us
    all_to_all x1, blocking collectives: 21.4 us -> 12.7 us  [body(): gathered = lax.all_to_all(stat, 'gx', 0, 0, tiled=True)]
    all_to_all x1, starting transfers between devices: 6.39 us -> 12.6 us  [body(): gathered = lax.all_to_all(column, 'gy', 0, 0, tiled=True)]
    all_to_all x1, waiting for transfers between devices: 7.16 us -> 9.22 us  [body(): gathered = lax.all_to_all(column, 'gy', 0, 0, tiled=True)]
where the time goes in v5:
time: 133 us; the launch traced here: 132 us
  starting transfers between devices  44.2 us (33%)
  blocking collectives  40.4 us (30%)
  waiting for transfers between devices  31.1 us (23%)
  Pallas kernels  15.4 us (12%)
    ppermute x6, starting transfers between devices, shift(): lax.ppermute(high_face, axis, forward)  22.4 us
    ppermute x6, waiting for transfers between devices, shift(): lax.ppermute(low_face, axis, backward)  21.8 us
    all_to_all x1, blocking collectives, body(): wide = lax.all_to_all(wide, 'gy', 0, 0, tiled=True)  17.7 us
    pallas_call x12, Pallas kernels, run(): pl.pallas_call(kernel, out_shape=[jax.ShapeDtypeStruct(out, F32) for out...  15.4 us
    all_to_all x1, blocking collectives, body(): gathered = lax.all_to_all(stat, 'gx', 0, 0, tiled=True)  12.7 us
    all_to_all x1, starting transfers between devices, body(): gathered = lax.all_to_all(column, 'gy', 0, 0, tiled=True)  12.6 us
    all_to_all x1, blocking collectives, body(): tile = lax.all_to_all(sums, 'gx', 0, 0, tiled=True)  10 us
    ppermute x6, starting transfers between devices, shift(): lax.ppermute(low_face, axis, backward)  9.32 us
  transfers between devices with their start and end apart: 13, of which 7 were waited for; matrix products, arithmetic and copies ran while one was open for 0% of the time, Pallas kernels for 1%

profile of v5, /device:TPU:1, one launch (start us, length us, event | category | flops | bytes accessed | tf_op | source)
XLA Modules:
  0.0 132.4 jit_solution(1140556244779399191)
XLA Ops:
  0.6 0.0 copy-start.1
  0.6 1.8 %shard_map.149 = (f32[8,32,128]{2,1,0:T(8,128)S(1)}, f32[8,32,128]{2,1,0:T(8,128)S(1)}, f32[3,32,128]{2,1,0:T(8,128)S(1)}, f32[3,32,128]{2,1,0:T(8,128)S(1)}) custom-call(f32[8,32,128]{2,1,0:T(8,128)} %lev_in.1, f32[3,8,32,128]{3,2,1,0:T(8,128)} %vel_in.1, f32[8,32,128]{2,1,0:T(8,128)} %src_in.1, f32[432,128]{1,0:T(8,128)} %constant.41.clone.packed_in.packed), custom_call_target="tpu_custom_call" | custom-call | flops 1000000 | bytes 720896 | tf_op jit(solution)/shard_map/pallas_call | solution.py:783
  2.4 4.8 %collective-permute-start = (f32[3,32,128]{2,1,0:T(8,128)S(1)}, f32[3,32,128]{2,1,0:T(8,128)S(1)}, u32[]{:S(2)}, u32[]{:S(2)}) collective-permute-start(f32[3,32,128]{2,1,0:T(8,128)S(1)} %get-tuple-element.31), channel_id=1, source_target_pairs={{0,64},{64,128},{128,192},{192,256},{256,320},{320,384},{384,448},... | collective-permute-start | bytes 147464 | tf_op jit(solution)/shard_map/ppermute | solution.py:799
  7.3 1.3 collective-permute-start.1
  8.6 0.0 collective-permute-done.refs_2_.zlo
  8.6 4.1 %collective-permute-done.1.refs_3_.zhi = f32[3,32,128]{2,1,0:T(8,128)S(1)} collective-permute-done((f32[3,32,128]{2,1,0:T(8,128)S(1)}, f32[3,32,128]{2,1,0:T(8,128)S(1)}, u32[]{:S(2)}, u32[]{:S(2)}) %collective-permute-start.1) | collective-permute-done | bytes 49184 | tf_op jit(solution)/shard_map/ppermute | solution.py:799
  12.7 0.0 copy-start.6
  12.8 0.0 copy-start.7
  12.8 5.0 %collective-permute-start.2 = (f32[12,16,128]{2,1,0:T(8,128)S(1)}, f32[12,16,128]{2,1,0:T(8,128)S(1)}, u32[]{:S(2)}, u32[]{:S(2)}) collective-permute-start(f32[12,16,128]{2,1,0:T(8,128)S(1)} %get-tuple-element.33), channel_id=1, source_target_pairs={{0,1},{1,2},{2,3},{3,4},{4,5},{5,6},{6,7},{7,8},{8,9},{9,10},{10,1... | collective-permute-start | bytes 294920 | tf_op jit(solution)/shard_map/ppermute | solution.py:799
  17.8 2.2 %collective-permute-start.3 = (f32[12,16,128]{2,1,0:T(8,128)S(1)}, f32[12,16,128]{2,1,0:T(8,128)S(1)}, u32[]{:S(2)}, u32[]{:S(2)}) collective-permute-start(f32[12,16,128]{2,1,0:T(8,128)S(1)} %get-tuple-element.34), channel_id=1, source_target_pairs={{1,0},{2,1},{3,2},{4,3},{5,4},{6,5},{7,6},{8,7},{9,8},{10,9},{11,1... | collective-permute-start | bytes 294920 | tf_op jit(solution)/shard_map/ppermute | solution.py:799
  20.0 0.1 pad_maximum_fusion.near
  20.1 0.0 collective-permute-done.2.ylo
  20.1 3.6 %collective-permute-done.3.yhi = f32[12,16,128]{2,1,0:T(8,128)S(1)} collective-permute-done((f32[12,16,128]{2,1,0:T(8,128)S(1)}, f32[12,16,128]{2,1,0:T(8,128)S(1)}, u32[]{:S(2)}, u32[]{:S(2)}) %collective-permute-start.3) | collective-permute-done | bytes 98336 | tf_op jit(solution)/shard_map/ppermute | solution.py:799
  23.7 0.0 copy-done.1
  23.8 0.0 copy-start.10
  23.8 0.0 copy-start.8
  23.8 1.9 %shard_map.152 = (f32[8,32,128]{2,1,0:T(8,128)S(1)}, f32[32,128]{1,0:T(8,128)S(1)}, f32[32,128]{1,0:T(8,128)S(1)}) custom-call(f32[4]{0:T(128)S(1)} %pad_maximum_fusion.near, f32[640,160]{1,0:T(8,128)S(1)} %copy-done.1, bf16[64,192]{1,0:T(8,128)(2,1)S(1)} %copy-done.6, bf16[256,160]{1,0:T(8,128)(2,1)S(1)} %copy-done.2, bf16[128,160]{1,0:T(8,128)(2,1)S(1)} %copy-done.3, ...), custom_call_target="tpu_custom_call" | custom-call | flops 1000000 | bytes 327680 | tf_op jit(solution)/shard_map/pallas_call | solution.py:783
  25.7 0.0 copy-start.9
  25.7 4.0 %collective-permute-start.4 = (f32[32,128]{1,0:T(8,128)S(1)}, f32[32,128]{1,0:T(8,128)S(1)}, u32[]{:S(2)}, u32[]{:S(2)}) collective-permute-start(f32[32,128]{1,0:T(8,128)S(1)} %get-tuple-element.39), channel_id=1, source_target_pairs={{0,64},{64,128},{128,192},{192,256},{256,320},{320,384},{384,448},... | collective-permute-start | bytes 49160 | tf_op jit(solution)/shard_map/ppermute | solution.py:799
  29.7 1.3 collective-permute-start.5
  31.1 1.4 %shard_map.151 = (f32[8,32,128]{2,1,0:T(8,128)}, f32[8,32,128]{2,1,0:T(8,128)S(1)}, f32[1,128]{1,0:T(1,128)S(1)}) custom-call(f32[4]{0:T(128)S(1)} %pad_maximum_fusion.near, f32[4,16]{1,0:T(4,128)S(1)} %convert_bitcast_fusion.solid, bf16[16,128]{1,0:T(8,128)(2,1)S(1)} %copy-done.9, f32[32,128]{1,0:T(8,128)S(1)} %copy-done.8, f32[432,128]{1,0:T(8,128)S(1)} %copy-done, ...), custom_call_target="tpu_custom_call" | custom-call | flops 20000000 | bytes 525312 | tf_op jit(solution)/shard_map/pallas_call | solution.py:783
  32.4 0.0 collective-permute-done.4.zlo
  32.4 3.6 %collective-permute-done.5.zhi = f32[32,128]{1,0:T(8,128)S(1)} collective-permute-done((f32[32,128]{1,0:T(8,128)S(1)}, f32[32,128]{1,0:T(8,128)S(1)}, u32[]{:S(2)}, u32[]{:S(2)}) %collective-permute-start.5) | collective-permute-done | bytes 16416 | tf_op jit(solution)/shard_map/ppermute | solution.py:799
  36.0 1.2 shard_map.153
  37.3 12.7 %all_to_all.39 = f32[8,1,128]{2,1,0:T(1,128)S(1)} all-to-all(f32[8,1,128]{2,1,0:T(1,128)S(1)} %bitcast.24), channel_id=1, replica_groups=mesh['gx'=8,'gy'=64] {'gx'}, dimensions={0} | all-to-all | bytes 8192 | tf_op jit(solution)/shard_map/all_to_all | solution.py:856
  50.0 0.9 shard_map.154
  50.9 12.6 %all-to-all-start.1 = ((f32[64,1,128]{2,1,0:T(1,128)}), f32[64,1,128]{2,1,0:T(1,128)S(1)}, u32[]{:S(2)}, u32[]{:S(2)}) async-start(f32[64,1,128]{2,1,0:T(1,128)} %bitcast.11), calls=%async_computation.1 | async-start | bytes 65536 | tf_op jit(solution)/shard_map/all_to_all | solution.py:858
  63.5 0.1 pad_add_fusion.place
  63.5 9.2 %all-to-all-done.1 = f32[64,1,128]{2,1,0:T(1,128)S(1)} async-done(((f32[64,1,128]{2,1,0:T(1,128)}), f32[64,1,128]{2,1,0:T(1,128)S(1)}, u32[]{:S(2)}, u32[]{:S(2)}) %all-to-all-start.1) | async-done | bytes 32800 | tf_op jit(solution)/shard_map/all_to_all | solution.py:858
  72.8 3.3 %shard_map.155.coarse = f32[32,128]{1,0:T(8,128)S(1)} custom-call(s32[2]{0:T(128)S(1)} %pad_add_fusion.place, f32[64,128]{1,0:T(8,128)S(1)} %bitcast.20), custom_call_target="tpu_custom_call" | custom-call | flops 1000000 | bytes 32768 | tf_op jit(solution)/shard_map/pallas_call | solution.py:783
  76.0 1.0 shard_map.156
  77.0 2.2 %collective-permute-start.6 = (f32[2,32,128]{2,1,0:T(8,128)S(1)}, f32[2,32,128]{2,1,0:T(8,128)S(1)}, u32[]{:S(2)}, u32[]{:S(2)}) collective-permute-start(f32[2,32,128]{2,1,0:T(8,128)S(1)} %get-tuple-element.45), channel_id=1, source_target_pairs={{0,64},{64,128},{128,192},{192,256},{256,320},{320,384},{384,448},... | collective-permute-start | bytes 98312 | tf_op jit(solution)/shard_map/ppermute | solution.py:799
  79.2 1.3 collective-permute-start.7
  80.5 0.0 collective-permute-done.6.refs_1_.zlo
  80.5 3.3 %collective-permute-done.7.refs_2_.zhi = f32[2,32,128]{2,1,0:T(8,128)S(1)} collective-permute-done((f32[2,32,128]{2,1,0:T(8,128)S(1)}, f32[2,32,128]{2,1,0:T(8,128)S(1)}, u32[]{:S(2)}, u32[]{:S(2)}) %collective-permute-start.7) | collective-permute-done | bytes 32800 | tf_op jit(solution)/shard_map/ppermute | solution.py:799
  83.9 4.2 %collective-permute-start.8 = (f32[12,16,128]{2,1,0:T(8,128)S(1)}, f32[12,16,128]{2,1,0:T(8,128)S(1)}, u32[]{:S(2)}, u32[]{:S(2)}) collective-permute-start(f32[12,16,128]{2,1,0:T(8,128)S(1)} %get-tuple-element.47), channel_id=1, source_target_pairs={{0,1},{1,2},{2,3},{3,4},{4,5},{5,6},{6,7},{7,8},{8,9},{9,10},{10,1... | collective-permute-start | bytes 294920 | tf_op jit(solution)/shard_map/ppermute | solution.py:799
  88.1 1.9 %collective-permute-start.9 = (f32[12,16,128]{2,1,0:T(8,128)S(1)}, f32[12,16,128]{2,1,0:T(8,128)S(1)}, u32[]{:S(2)}, u32[]{:S(2)}) collective-permute-start(f32[12,16,128]{2,1,0:T(8,128)S(1)} %get-tuple-element.48), channel_id=1, source_target_pairs={{1,0},{2,1},{3,2},{4,3},{5,4},{6,5},{7,6},{8,7},{9,8},{10,9},{11,1... | collective-permute-start | bytes 294920 | tf_op jit(solution)/shard_map/ppermute | solution.py:799
  90.0 0.0 collective-permute-done.8.ylo
  90.0 4.0 %collective-permute-done.9.yhi = f32[12,16,128]{2,1,0:T(8,128)S(1)} collective-permute-done((f32[12,16,128]{2,1,0:T(8,128)S(1)}, f32[12,16,128]{2,1,0:T(8,128)S(1)}, u32[]{:S(2)}, u32[]{:S(2)}) %collective-permute-start.9) | collective-permute-done | bytes 98336 | tf_op jit(solution)/shard_map/ppermute | solution.py:799
  94.0 1.9 %shard_map.158 = (f32[8,32,128]{2,1,0:T(8,128)S(1)}, f32[32,128]{1,0:T(8,128)S(1)}, f32[32,128]{1,0:T(8,128)S(1)}) custom-call(f32[4]{0:T(128)S(1)} %pad_maximum_fusion.near, f32[640,160]{1,0:T(8,128)S(1)} %copy-done.1, bf16[64,192]{1,0:T(8,128)(2,1)S(1)} %copy-done.6, bf16[256,160]{1,0:T(8,128)(2,1)S(1)} %copy-done.2, bf16[128,160]{1,0:T(8,128)(2,1)S(1)} %copy-done.3, ...), custom_call_target="tpu_custom_call" | custom-call | flops 1000000 | bytes 327680 | tf_op jit(solution)/shard_map/pallas_call | solution.py:783
  95.9 2.2 %collective-permute-start.10 = (f32[32,128]{1,0:T(8,128)S(1)}, f32[32,128]{1,0:T(8,128)S(1)}, u32[]{:S(2)}, u32[]{:S(2)}) collective-permute-start(f32[32,128]{1,0:T(8,128)S(1)} %get-tuple-element.50), channel_id=1, source_target_pairs={{0,64},{64,128},{128,192},{192,256},{256,320},{320,384},{384,448},... | collective-permute-start | bytes 49160 | tf_op jit(solution)/shard_map/ppermute | solution.py:799
  98.1 1.3 collective-permute-start.11
  99.4 0.0 collective-permute-done.10.zlo
  99.4 3.2 %collective-permute-done.11.zhi = f32[32,128]{1,0:T(8,128)S(1)} collective-permute-done((f32[32,128]{1,0:T(8,128)S(1)}, f32[32,128]{1,0:T(8,128)S(1)}, u32[]{:S(2)}, u32[]{:S(2)}) %collective-permute-start.11) | collective-permute-done | bytes 16416 | tf_op jit(solution)/shard_map/ppermute | solution.py:799
  102.6 1.2 shard_map.159
  103.8 10.0 %all_to_all.40 = f32[8,1,128]{2,1,0:T(1,128)S(1)} all-to-all(f32[8,1,128]{2,1,0:T(1,128)S(1)} %bitcast.23), channel_id=1, replica_groups=mesh['gx'=8,'gy'=64] {'gx'}, dimensions={0} | all-to-all | bytes 8192 | tf_op jit(solution)/shard_map/all_to_all | solution.py:885
  113.9 17.7 %all_to_all.41 = f32[64,1,128]{2,1,0:T(1,128)S(1)} all-to-all(f32[64,1,128]{2,1,0:T(1,128)S(1)} %broadcast_in_dim.2), channel_id=1, replica_groups=mesh['gx'=8,'gy'=64] {'gy'}, dimensions={0} | all-to-all | bytes 65536 | tf_op jit(solution)/shard_map/all_to_all | solution.py:887
  131.6 0.8 shard_map.160
  (20 shorter events, 0.1 us)
Async XLA Ops:
  0.6 23.1 %copy-start.1 = (f32[640,160]{1,0:T(8,128)S(1)}, f32[640,160]{1,0:T(8,128)}, u32[]{:S(2)}) copy-start(f32[640,160]{1,0:T(8,128)} %constant.42.clone.inv_den) | copy-start | bytes 1228804
  2.4 6.2 %collective-permute-start = (f32[3,32,128]{2,1,0:T(8,128)S(1)}, f32[3,32,128]{2,1,0:T(8,128)S(1)}, u32[]{:S(2)}, u32[]{:S(2)}) collective-permute-start(f32[3,32,128]{2,1,0:T(8,128)S(1)} %get-tuple-element.31), channel_id=1, source_target_pairs={{0,64},{64,128},{128,192},{192,256},{256,320},{320,384},{384,448},... | collective-permute-start | bytes 147464 | tf_op jit(solution)/shard_map/ppermute | solution.py:799
  7.3 5.5 %collective-permute-start.1 = (f32[3,32,128]{2,1,0:T(8,128)S(1)}, f32[3,32,128]{2,1,0:T(8,128)S(1)}, u32[]{:S(2)}, u32[]{:S(2)}) collective-permute-start(f32[3,32,128]{2,1,0:T(8,128)S(1)} %get-tuple-element.32), channel_id=1, source_target_pairs={{64,0},{128,64},{192,128},{256,192},{320,256},{384,320},{448,384},... | collective-permute-start | bytes 147464 | tf_op jit(solution)/shard_map/ppermute | solution.py:799
  12.7 11.0 %copy-start.2 = (bf16[256,160]{1,0:T(8,128)(2,1)S(1)}, bf16[256,160]{1,0:T(8,128)(2,1)}, u32[]{:S(2)}) copy-start(bf16[256,160]{1,0:T(8,128)(2,1)} %constant.44.clone.fxhh) | copy-start | bytes 245764
  12.7 11.0 %copy-start.3 = (bf16[128,160]{1,0:T(8,128)(2,1)S(1)}, bf16[128,160]{1,0:T(8,128)(2,1)}, u32[]{:S(2)}) copy-start(bf16[128,160]{1,0:T(8,128)(2,1)} %constant.45.clone.fxl) | copy-start | bytes 122884
  12.7 11.0 %copy-start.4 = (bf16[160,128]{1,0:T(8,128)(2,1)S(1)}, bf16[160,128]{1,0:T(8,128)(2,1)}, u32[]{:S(2)}) copy-start(bf16[160,128]{1,0:T(8,128)(2,1)} %constant.47.clone.bxl) | copy-start | bytes 122884
  12.7 11.0 %copy-start.5 = (bf16[160,128]{1,0:T(8,128)(2,1)S(1)}, bf16[160,128]{1,0:T(8,128)(2,1)}, u32[]{:S(2)}) copy-start(bf16[160,128]{1,0:T(8,128)(2,1)} %constant.46.clone.bxh) | copy-start | bytes 122884
  12.7 11.0 %copy-start.6 = (bf16[64,192]{1,0:T(8,128)(2,1)S(1)}, bf16[64,192]{1,0:T(8,128)(2,1)}, u32[]{:S(2)}) copy-start(bf16[64,192]{1,0:T(8,128)(2,1)} %constant.43.clone.fy) | copy-start | bytes 73732
  12.8 11.0 %copy-start.7 = (bf16[40,192]{1,0:T(8,128)(2,1)S(1)}, bf16[40,192]{1,0:T(8,128)(2,1)}, u32[]{:S(2)}) copy-start(bf16[40,192]{1,0:T(8,128)(2,1)} %constant.48.clone.by) | copy-start | bytes 46084
  12.8 7.3 %collective-permute-start.2 = (f32[12,16,128]{2,1,0:T(8,128)S(1)}, f32[12,16,128]{2,1,0:T(8,128)S(1)}, u32[]{:S(2)}, u32[]{:S(2)}) collective-permute-start(f32[12,16,128]{2,1,0:T(8,128)S(1)} %get-tuple-element.33), channel_id=1, source_target_pairs={{0,1},{1,2},{2,3},{3,4},{4,5},{5,6},{6,7},{7,8},{8,9},{9,10},{10,1... | collective-permute-start | bytes 294920 | tf_op jit(solution)/shard_map/ppermute | solution.py:799
  17.8 5.9 %collective-permute-start.3 = (f32[12,16,128]{2,1,0:T(8,128)S(1)}, f32[12,16,128]{2,1,0:T(8,128)S(1)}, u32[]{:S(2)}, u32[]{:S(2)}) collective-permute-start(f32[12,16,128]{2,1,0:T(8,128)S(1)} %get-tuple-element.34), channel_id=1, source_target_pairs={{1,0},{2,1},{3,2},{4,3},{5,4},{6,5},{7,6},{8,7},{9,8},{10,9},{11,1... | collective-permute-start | bytes 294920 | tf_op jit(solution)/shard_map/ppermute | solution.py:799
  20.1 10.9 %copy-start = (f32[432,128]{1,0:T(8,128)S(1)}, f32[432,128]{1,0:T(8,128)}, u32[]{:S(2)}) copy-start(f32[432,128]{1,0:T(8,128)} %constant.41.clone.packed_in.packed) | copy-start | bytes 663556
  23.8 7.2 %copy-start.10 = (s32[1,4,16]{2,1,0:T(4,128)S(1)}, s32[1,4,16]{2,1,0:T(4,128)}, u32[]{:S(2)}) copy-start(s32[1,4,16]{2,1,0:T(4,128)} %param.17) | copy-start | bytes 772
  23.8 7.3 %copy-start.8 = (f32[32,128]{1,0:T(8,128)S(1)}, f32[32,128]{1,0:T(8,128)}, u32[]{:S(2)}) copy-start(f32[32,128]{1,0:T(8,128)} %constant.50.clone.inv_mass) | copy-start | bytes 49156
  25.7 5.4 %copy-start.9 = (bf16[16,128]{1,0:T(8,128)(2,1)S(1)}, bf16[16,128]{1,0:T(8,128)(2,1)}, u32[]{:S(2)}) copy-start(bf16[16,128]{1,0:T(8,128)(2,1)} %constant.49.clone.spread) | copy-start | bytes 12292
  25.7 6.7 %collective-permute-start.4 = (f32[32,128]{1,0:T(8,128)S(1)}, f32[32,128]{1,0:T(8,128)S(1)}, u32[]{:S(2)}, u32[]{:S(2)}) collective-permute-start(f32[32,128]{1,0:T(8,128)S(1)} %get-tuple-element.39), channel_id=1, source_target_pairs={{0,64},{64,128},{128,192},{192,256},{256,320},{320,384},{384,448},... | collective-permute-start | bytes 49160 | tf_op jit(solution)/shard_map/ppermute | solution.py:799
  29.7 6.3 %collective-permute-start.5 = (f32[32,128]{1,0:T(8,128)S(1)}, f32[32,128]{1,0:T(8,128)S(1)}, u32[]{:S(2)}, u32[]{:S(2)}) collective-permute-start(f32[32,128]{1,0:T(8,128)S(1)} %get-tuple-element.40), channel_id=1, source_target_pairs={{64,0},{128,64},{192,128},{256,192},{320,256},{384,320},{448,384},... | collective-permute-start | bytes 49160 | tf_op jit(solution)/shard_map/ppermute | solution.py:799
  50.9 21.9 %all-to-all-start.1 = ((f32[64,1,128]{2,1,0:T(1,128)}), f32[64,1,128]{2,1,0:T(1,128)S(1)}, u32[]{:S(2)}, u32[]{:S(2)}) async-start(f32[64,1,128]{2,1,0:T(1,128)} %bitcast.11), calls=%async_computation.1 | async-start | bytes 65536 | tf_op jit(solution)/shard_map/all_to_all | solution.py:858
  77.0 3.5 %collective-permute-start.6 = (f32[2,32,128]{2,1,0:T(8,128)S(1)}, f32[2,32,128]{2,1,0:T(8,128)S(1)}, u32[]{:S(2)}, u32[]{:S(2)}) collective-permute-start(f32[2,32,128]{2,1,0:T(8,128)S(1)} %get-tuple-element.45), channel_id=1, source_target_pairs={{0,64},{64,128},{128,192},{192,256},{256,320},{320,384},{384,448},... | collective-permute-start | bytes 98312 | tf_op jit(solution)/shard_map/ppermute | solution.py:799
  79.2 4.7 %collective-permute-start.7 = (f32[2,32,128]{2,1,0:T(8,128)S(1)}, f32[2,32,128]{2,1,0:T(8,128)S(1)}, u32[]{:S(2)}, u32[]{:S(2)}) collective-permute-start(f32[2,32,128]{2,1,0:T(8,128)S(1)} %get-tuple-element.46), channel_id=1, source_target_pairs={{64,0},{128,64},{192,128},{256,192},{320,256},{384,320},{448,384},... | collective-permute-start | bytes 98312 | tf_op jit(solution)/shard_map/ppermute | solution.py:799
  83.9 6.1 %collective-permute-start.8 = (f32[12,16,128]{2,1,0:T(8,128)S(1)}, f32[12,16,128]{2,1,0:T(8,128)S(1)}, u32[]{:S(2)}, u32[]{:S(2)}) collective-permute-start(f32[12,16,128]{2,1,0:T(8,128)S(1)} %get-tuple-element.47), channel_id=1, source_target_pairs={{0,1},{1,2},{2,3},{3,4},{4,5},{5,6},{6,7},{7,8},{8,9},{9,10},{10,1... | collective-permute-start | bytes 294920 | tf_op jit(solution)/shard_map/ppermute | solution.py:799
  88.1 5.9 %collective-permute-start.9 = (f32[12,16,128]{2,1,0:T(8,128)S(1)}, f32[12,16,128]{2,1,0:T(8,128)S(1)}, u32[]{:S(2)}, u32[]{:S(2)}) collective-permute-start(f32[12,16,128]{2,1,0:T(8,128)S(1)} %get-tuple-element.48), channel_id=1, source_target_pairs={{1,0},{2,1},{3,2},{4,3},{5,4},{6,5},{7,6},{8,7},{9,8},{10,9},{11,1... | collective-permute-start | bytes 294920 | tf_op jit(solution)/shard_map/ppermute | solution.py:799
  95.9 3.5 %collective-permute-start.10 = (f32[32,128]{1,0:T(8,128)S(1)}, f32[32,128]{1,0:T(8,128)S(1)}, u32[]{:S(2)}, u32[]{:S(2)}) collective-permute-start(f32[32,128]{1,0:T(8,128)S(1)} %get-tuple-element.50), channel_id=1, source_target_pairs={{0,64},{64,128},{128,192},{192,256},{256,320},{320,384},{384,448},... | collective-permute-start | bytes 49160 | tf_op jit(solution)/shard_map/ppermute | solution.py:799
  98.1 4.5 %collective-permute-start.11 = (f32[32,128]{1,0:T(8,128)S(1)}, f32[32,128]{1,0:T(8,128)S(1)}, u32[]{:S(2)}, u32[]{:S(2)}) collective-permute-start(f32[32,128]{1,0:T(8,128)S(1)} %get-tuple-element.51), channel_id=1, source_target_pairs={{64,0},{128,64},{192,128},{256,192},{320,256},{384,320},{448,384},... | collective-permute-start | bytes 49160 | tf_op jit(solution)/shard_map/ppermute | solution.py:799

commit v6 on v5

--- a/solution.py
+++ b/solution.py
@@ -118,44 +118,66 @@
     return forward, backward
 
 
-def wide_maps():
-    count = EY + 2
-    forward, backward = line_maps(count)
+RING = 16
+WIDE = ROWS + 2 * RING
+REACH = 26
+TILE = 48
+TILE_B = 32
+
+
+def ring_maps(reach, depth, inside):
+    count = EY + 2 * depth
+    forward, _ = line_maps(count)
     length = 8 * count
-    columns = np.zeros((10 * count, ROWS + 2 * TILE))
-    columns[:, :ROWS] = forward[:, 8 : 8 + ROWS]
-    columns[:, ROWS : ROWS + 2] = forward[:, length : length + 2]
-    columns[:, ROWS + 2 : ROWS + 10] = forward[:, :8]
-    columns[:, ROWS + TILE : ROWS + TILE + 8] = forward[:, length - 8 : length]
-    columns[:, ROWS + TILE + 8 : ROWS + TILE + 10] = forward[:, length + 2 : length + 4]
-    _, own = line_maps(EY)
-    rows = np.zeros((ROWS + 8, 10 * count))
-    rows[:ROWS, 10 : 10 + 10 * EY] = own
-    rows[ROWS, :10] = SINE[8]
-    rows[ROWS + 1, 10 + 10 * EY :] = SINE[1]
+    columns = np.zeros((10 * count, len(inside)))
+    for at, position in enumerate(inside):
+        place = None if position is None else position + 8 * depth
+        if place is None or place < -2 or place > length + 1:
+            continue
+        source = place if 0 <= place < length else {-2: 0, -1: 1}.get(place, place - length + 2) + length
+        columns[:, at] = forward[:, source]
+    _, backward = line_maps(count)
+    own = 8 * depth
+    rows = np.concatenate(
+        [
+            backward[own - reach : own + ROWS + reach],
+            np.zeros((8, 10 * count)),
+        ]
+    )
+    rows[ROWS + 2 * reach, 10 * depth : 10 * depth + 10] = SINE[1]
+    rows[ROWS + 2 * reach + 1, 10 * (depth + EY - 1) : 10 * (depth + EY)] = SINE[8]
     return columns, rows
 
 
-TILE = 16
 FZ, BZ = line_maps(1)
-FY, BY = wide_maps()
-SPECTRAL_Y = 64
-FY = np.pad(FY, ((0, SPECTRAL_Y - FY.shape[0]), (0, 0)))
-BY = np.pad(BY, ((0, 0), (0, SPECTRAL_Y - BY.shape[1])))
+TILES = list(range(-REACH, 0)) + [None] * (TILE_B - REACH) + list(range(ROWS))
+TILES += list(range(ROWS, ROWS + REACH)) + [None] * (TILE_B - REACH)
+FY_A, BY_A = ring_maps(RING, 3, TILES)
+FY_B, BY_B = ring_maps(0, 1, list(range(-RING, ROWS + RING)))
+STEP_A = 112
+STEP_B = 64
+
+
+def padded(forward, backward, step):
+    forward = np.pad(forward, ((0, step - forward.shape[0]), (0, 0)))
+    return forward, np.pad(backward, ((0, 0), (0, step - backward.shape[1])))
+
+
+FY_A, BY_A = padded(FY_A, BY_A, STEP_A)
+FY_B, BY_B = padded(FY_B, BY_B, STEP_B)
 FX, BX = line_maps(EX)
 FX = FX[:, :LANES]
 
 
-def denominators():
-    lam_y = np.tile(EIGEN, EY + 2)
+def denominators(step):
+    lam_y = np.tile(EIGEN, step // 10)
     lam_x = np.tile(EIGEN, EX)
     total = EIGEN[:, None, None] + lam_y[None, :, None] + lam_x[None, None, :]
     inverse = 1.0 / (SCHWARZ_SCALE * total + SCHWARZ_SHIFT)
-    inverse = np.pad(inverse, ((0, 0), (0, SPECTRAL_Y - inverse.shape[1]), (0, 0)))
-    return inverse.reshape(10 * SPECTRAL_Y, 10 * EX).astype(np.float32)
-
-
-INV_DEN = denominators()
+    inverse = np.pad(inverse, ((0, 0), (0, step - inverse.shape[1]), (0, 0)))
+    return inverse.reshape(10 * step, 10 * EX).astype(np.float32)
+
+
 FX_H, FX_L = split_const(FX.T.copy())
 BX_H, BX_L = split_const(BX.T.copy())
 
@@ -165,9 +187,9 @@
     return np.concatenate([high, high, low], axis=1)
 
 
-FY_W = wide_const(FY)
-BY_W = wide_const(BY)
 FX_HH = np.concatenate([FX_H, FX_H], axis=0)
+SOLVER_A = (denominators(STEP_A), wide_const(FY_A), FX_HH, FX_L, BX_H, BX_L, wide_const(BY_A))
+SOLVER_B = (denominators(STEP_B), wide_const(FY_B), FX_HH, FX_L, BX_H, BX_L, wide_const(BY_B))
 
 
 def roll_table():
@@ -179,9 +201,9 @@
     return table.reshape(2 * 64, LANES)
 
 
-WY = np.tile(WEIGHT, EY)
+WY = np.tile(WEIGHT, WIDE // 8)
 WX = np.tile(WEIGHT, EX)
-AT_ROLLS = ROWS
+AT_ROLLS = WIDE
 AT_DX = AT_ROLLS + 128
 AT_DXT = AT_DX + LANES
 AT_SQUARE = AT_DXT + LANES
@@ -205,9 +227,8 @@
     return mult
 
 
-INV_MASS = (8.0 / (WY * inner_count(EY))[:, None] / (WX * inner_count(EX))[None, :]).astype(
-    np.float32
-)
+END_MASS = np.where(np.arange(WIDE) % 8 % 7 == 0, 2.0, 1.0)
+INV_MASS = (8.0 / (WY * END_MASS)[:, None] / (WX * inner_count(EX))[None, :]).astype(np.float32)
 SPREAD = np.kron(np.eye(EX), np.ones((1, 8))).astype(jnp.bfloat16)
 
 
@@ -244,23 +265,23 @@
 
 
 def along_y(values, packed, kind):
-    count = values.shape[0]
-    grouped = values.reshape(count * EY, 8, LANES)
+    count, rows = values.shape[:2]
+    grouped = values.reshape(count * rows // 8, 8, LANES)
     start = AT_ROLLS + 64 * kind
     total = packed[start : start + 8][None] * grouped
     for k in range(1, 8):
         total = total + packed[start + 8 * k : start + 8 * k + 8][None] * pltpu.roll(grouped, 8 - k, 1)
-    return total.reshape(count, ROWS, LANES)
+    return total.reshape(count, rows, LANES)
 
 
 def along_x(values, packed, kind):
     start = AT_DXT if kind else AT_DX
     high, low = parts(packed[start : start + LANES])
-    first, rest = parts(values.reshape(8 * ROWS, LANES))
+    first, rest = parts(values.reshape(8 * values.shape[1], LANES))
     total = dot(
         jnp.concatenate([first, rest], axis=1), jnp.concatenate([high, high], axis=0)
     ) + dot(first, low)
-    return total.reshape(8, ROWS, LANES)
+    return total.reshape(values.shape)
 
 
 def stack(planes):
@@ -273,7 +294,7 @@
 
 
 def local_operator(values, flux, packed):
-    plane_w = packed[0:ROWS]
+    plane_w = packed[0 : values.shape[1]]
     gz = along_z([values[i] for i in range(8)], DERIV)
     fz = along_z([flux[i] * gz[i] for i in range(8)], DERIV.T)
     total = along_y(flux * along_y(values, packed, 0), packed, 1)
@@ -292,28 +313,19 @@
     return stack(planes)
 
 
-def schwarz(own, low_z, high_z, low_y, high_y, tables, inv_den, near, out_ref, low_ref, high_ref):
-    fy, fxhh, fxl, bxh, bxl, by = tables
-    middle = along_z([own[i] for i in range(8)] + [low_z[0], low_z[1], high_z[0], high_z[1]], FZ)
-    below = along_z([low_y[i] for i in range(12)], FZ)
-    above = along_z([high_y[i] for i in range(12)], FZ)
-    spectral = left_pairs(
-        fy, [jnp.concatenate([middle[i], below[i], above[i]], axis=0) for i in range(10)]
-    )
+def solve_elements(planes, tables):
+    inv_den, fy, fxhh, fxl, bxh, bxl, by = tables
+    spectral = left_pairs(fy, along_z(planes, FZ))
     high, low = parts(jnp.concatenate(spectral, axis=0))
     wide = dot(jnp.concatenate([high, low], axis=1), fxhh[...]) + dot(high, fxl[...])
     high, low = parts(wide * inv_den[...])
     back = dot(high, bxh[...]) + dot(low, bxh[...]) + dot(high, bxl[...])
-    step = SPECTRAL_Y
+    step = fy.shape[0]
     back = left_pairs(by, [back[step * i : step * (i + 1)] for i in range(10)])
-    planes = along_z(back, BZ)
-    edge = edge_rows(ROWS, near[2], near[3])
-    row = lax.broadcasted_iota(jnp.int32, (ROWS, LANES), 0)
-    for i in range(8):
-        first = (1.0 - near[2]) * planes[i][ROWS : ROWS + 1]
-        last = (1.0 - near[3]) * planes[i][ROWS + 1 : ROWS + 2]
-        other = jnp.where(row == 0, first, jnp.where(row == ROWS - 1, last, 0.0))
-        planes[i] = planes[i][0:ROWS] * edge + other
+    return along_z(back, BZ)
+
+
+def store_faces(planes, near, out_ref, low_ref, high_ref):
     planes[0] = planes[0] * near[0]
     planes[7] = planes[7] * near[1]
     for i in range(8):
@@ -322,6 +334,11 @@
     high_ref[...] = planes[7]
 
 
+def ring_rows(near):
+    row = lax.broadcasted_iota(jnp.int32, (WIDE, LANES), 0)
+    return row, 2.0 - 2.0 * near[2], 2.0 - 2.0 * near[3]
+
+
 def partition_total(own, low_z, high_z, low_y, high_y, near):
     def planes(array):
         total = near[0] * array[0] + near[1] * array[7]
@@ -332,7 +349,7 @@
     total = planes(own) + 0.5 * (low_z[1] + high_z[0])
     below = planes(low_y) + 0.5 * (low_y[9] + low_y[10])
     above = planes(high_y) + 0.5 * (high_y[9] + high_y[10])
-    faces = 0.5 * (below[9:10] + above[0:1])
+    faces = 0.5 * (below[REACH - 1 : REACH] + above[0:1])
     return jnp.sum(total * edge_rows(ROWS, near[2], near[3])) + jnp.sum(faces)
 
 
@@ -382,63 +399,78 @@
             zhi[2] = moved_i
 
 
-def rim_kernel(count, *refs):
-    own = refs[:count]
-    low_z, high_z, low_y, high_y = refs[count:]
-    zeros = jnp.zeros((TILE - 10 - (count - 1), LANES), F32)
-
-    def rows(planes, level, at, far):
-        pieces = [planes[at, ROWS - 10 : ROWS] if far else planes[at, 0:10]]
-        if count == 2:
-            if level is None:
-                pieces.append(jnp.zeros((1, LANES), F32))
-            else:
-                array, index = level
-                pieces.append(array[index, ROWS - 1 : ROWS] if far else array[index, 0:1])
-        return jnp.concatenate(pieces + [zeros], axis=0)
+def rim_kernel(solid, spread, b, l, low_z, high_z, low_y, high_y):
+    in_solid = dot(solid[...].astype(BF16), spread[...])
+    rest = TILE - REACH - RING - 1
+
+    def rows(planes, at, level, far, extra=None):
+        start = ROWS - REACH if far else 0
+        pieces = [planes[at, start : start + REACH]]
+        if level is None:
+            pieces.append(jnp.zeros((RING + 1, LANES), F32))
+        else:
+            array, index = level
+            start = ROWS - RING - 1 if far else 0
+            pieces.append(array[index, start : start + RING + 1])
+        if extra is None:
+            pieces.append(jnp.zeros((rest, LANES), F32))
+        else:
+            pieces += [extra, jnp.zeros((rest - 2, LANES), F32)]
+        return jnp.concatenate(pieces, axis=0)
 
     for far, out in ((False, low_y), (True, high_y)):
+        extra = in_solid[EY - 2 : EY] if far else in_solid[0:2]
         for i in range(8):
-            out[i] = rows(own[0], (own[-1], i), i, far)
+            out[i] = rows(b, i, (l, i), far, extra if i == 0 else None)
         for i in range(2):
-            out[8 + i] = rows(low_z, (low_z, 2) if i == 1 else None, i, far)
-            out[10 + i] = rows(high_z, (high_z, 2) if i == 0 else None, i, far)
+            out[8 + i] = rows(low_z, i, (low_z, 2) if i == 1 else None, far)
+            out[10 + i] = rows(high_z, i, (high_z, 2) if i == 0 else None, far)
 
 
 def level_kernel(
     near, solid, spread, inv_mass, packed, b, l, zlo, zhi, ylo, yhi, level_ref, flux_ref, stat
 ):
-    row = lax.broadcasted_iota(jnp.int32, (ROWS, LANES), 0)
+    row, has_low, has_high = ring_rows(near)
+    at = REACH
+
+    def wide_rows(slot, own):
+        return jnp.concatenate(
+            [ylo[slot, at + 1 : at + 1 + RING], own, yhi[slot, at : at + RING]], axis=0
+        )
+
     planes = []
     for i in range(8):
-        plane = l[i]
-        first = ylo[i, 10:11]
-        last = yhi[i, 10:11]
+        plane = wide_rows(i, l[i])
+        first = ylo[i, at : at + 1]
+        last = yhi[i, at + RING : at + RING + 1]
         if i == 0:
-            plane = plane + zlo[2]
-            first = first + ylo[9, 10:11]
-            last = last + yhi[9, 10:11]
+            plane = plane + wide_rows(9, zlo[2])
+            first = first + ylo[9, at : at + 1]
+            last = last + yhi[9, at + RING : at + RING + 1]
         if i == 7:
-            plane = plane + zhi[2]
-            first = first + ylo[10, 10:11]
-            last = last + yhi[10, 10:11]
-        planes.append(plane + jnp.where(row == 0, first, jnp.where(row == ROWS - 1, last, 0.0)))
+            plane = plane + wide_rows(10, zhi[2])
+            first = first + ylo[10, at : at + 1]
+            last = last + yhi[10, at + RING : at + RING + 1]
+        before = jnp.where(row == 0, first, pltpu.roll(plane, 1, 0))
+        after = jnp.where(row == WIDE - 1, last, pltpu.roll(plane, WIDE - 1, 0))
+        plane = plane + jnp.where(row % 8 == 0, before, jnp.where(row % 8 == 7, after, 0.0))
+        planes.append(plane)
     own = stack(planes)
-    row = lax.broadcasted_iota(jnp.int32, (8, ROWS, LANES), 1)
-    lane = lax.broadcasted_iota(jnp.int32, (8, ROWS, LANES), 2)
-    before = jnp.where((row % 8 == 0) & (row > 0), pltpu.roll(own, 1, 1), 0.0)
-    after = jnp.where((row % 8 == 7) & (row < ROWS - 1), pltpu.roll(own, ROWS - 1, 1), 0.0)
-    own = own + before + after
+    lane = lax.broadcasted_iota(jnp.int32, (8, WIDE, LANES), 2)
     before = jnp.where((lane % 8 == 0) & (lane > 0), pltpu.roll(own, 1, 2), 0.0)
     after = jnp.where((lane % 8 == 7) & (lane < LANES - 1), pltpu.roll(own, LANES - 1, 2), 0.0)
     own = own + before + after
-    inverse = inv_mass[...] * edge_rows(ROWS, near[2], near[3])
+    ends = jnp.where(row == RING, 2.0 * near[2], jnp.where(row == RING + ROWS - 1, 2.0 * near[3], 1.0))
+    inverse = inv_mass[...] * ends
     in_solid = dot(solid[...].astype(BF16), spread[...])
+    solids = [ylo[0, at + RING + 1 + k : at + RING + 2 + k] for k in range(2)]
+    solids += [in_solid[e : e + 1] for e in range(EY)]
+    solids += [yhi[0, at + RING + 1 + k : at + RING + 2 + k] for k in range(2)]
     open_part = jnp.concatenate(
-        [jnp.broadcast_to(1.0 - (1.0 - SOLID_FACTOR) * in_solid[e : e + 1], (8, LANES)) for e in range(EY)],
-        axis=0,
-    )
-    plane_w = packed[0:ROWS]
+        [jnp.broadcast_to(1.0 - (1.0 - SOLID_FACTOR) * rows, (8, LANES)) for rows in solids], axis=0
+    )
+    in_grid = jnp.where(row < RING, has_low, jnp.where(row >= RING + ROWS, has_high, 1.0))
+    flux_w = packed[0:WIDE] * in_grid
     total = jnp.zeros((ROWS, LANES), F32)
     fluxes = []
     for i in range(8):
@@ -448,13 +480,13 @@
             plane = plane * near[0]
         if i == 7:
             plane = plane * near[1]
-        level_ref[i] = plane
+        level_ref[i] = plane[RING : RING + ROWS]
         liquid = jax.nn.sigmoid(plane * (1.0 / LEVEL_WIDTH))
         coef = (GAS_RATIO - (GAS_RATIO - 1.0) * liquid) * open_part
-        total = total + coef
-        flux = (0.5 * float(WEIGHT[i])) * (coef * plane_w)
+        total = total + coef[RING : RING + ROWS]
+        flux = (0.5 * float(WEIGHT[i])) * (coef * flux_w)
         flux_ref[i] = flux
-        fluxes.append(flux)
+        fluxes.append(flux[RING : RING + ROWS])
     kbar = jnp.sum(total) * (1.0 / (8 * ROWS * LANES))
     entries = [kbar, partition_total(b, zlo, zhi, ylo, yhi, near)] + [0.0] * 9
     for first, second in ((0, 0), (0, 7), (7, 7)):
@@ -464,17 +496,47 @@
     inner = fluxes[0] + fluxes[1]
     for i in range(2, 8):
         inner = inner + fluxes[i]
-    for at, start in ((0, 0), (ROWS - 8, 8)):
+    for at_row, start in ((0, 0), (ROWS - 8, 8)):
         square = packed[AT_SQUARE + start : AT_SQUARE + start + 8]
-        entries += [jnp.sum(square * plane[at : at + 8]) for plane in (inner, fluxes[0], fluxes[7])]
+        entries += [
+            jnp.sum(square * plane[at_row : at_row + 8]) for plane in (inner, fluxes[0], fluxes[7])
+        ]
     stat[...] = lane_row(entries)
 
 
-def schwarz_kernel(
+def first_schwarz_kernel(
     near, inv_den, fy, fxhh, fxl, bxh, bxl, by, b, zlo, zhi, ylo, yhi, w_ref, wlo, whi
 ):
-    tables = (fy, fxhh, fxl, bxh, bxl, by)
-    schwarz(b, zlo, zhi, ylo, yhi, tables, inv_den, near, w_ref, wlo, whi)
+    own = [b[i] for i in range(8)] + [zlo[0], zlo[1], zhi[0], zhi[1]]
+    planes = [
+        jnp.concatenate([ylo[i, 0:TILE_B], own[i], yhi[i, 0:TILE_B]], axis=0) for i in range(12)
+    ]
+    planes = solve_elements(planes, (inv_den, fy, fxhh, fxl, bxh, bxl, by))
+    row, has_low, has_high = ring_rows(near)
+    in_grid = jnp.where(row < RING, has_low, jnp.where(row >= RING + ROWS, has_high, 1.0))
+    in_grid = jnp.where(row == RING, has_low, jnp.where(row == RING + ROWS - 1, has_high, in_grid))
+    for i in range(8):
+        first = (1.0 - has_low) * planes[i][WIDE : WIDE + 1]
+        last = (1.0 - has_high) * planes[i][WIDE + 1 : WIDE + 2]
+        alone = jnp.where(row == RING, first, jnp.where(row == RING + ROWS - 1, last, 0.0))
+        planes[i] = planes[i][0:WIDE] * in_grid + alone
+    store_faces(planes, near, w_ref, wlo, whi)
+
+
+def second_schwarz_kernel(
+    near, inv_den, fy, fxhh, fxl, bxh, bxl, by, y, zlo, zhi, w_ref, wlo, whi
+):
+    planes = [y[i] for i in range(8)] + [zlo[0], zlo[1], zhi[0], zhi[1]]
+    planes = solve_elements(planes, (inv_den, fy, fxhh, fxl, bxh, bxl, by))
+    row = lax.broadcasted_iota(jnp.int32, (ROWS, LANES), 0)
+    _, has_low, has_high = ring_rows(near)
+    in_grid = jnp.where(row == 0, has_low, jnp.where(row == ROWS - 1, has_high, 1.0))
+    for i in range(8):
+        first = (1.0 - has_low) * planes[i][ROWS : ROWS + 1]
+        last = (1.0 - has_high) * planes[i][ROWS + 1 : ROWS + 2]
+        alone = jnp.where(row == 0, first, jnp.where(row == ROWS - 1, last, 0.0))
+        planes[i] = planes[i][0:ROWS] * in_grid + alone
+    store_faces(planes, near, w_ref, wlo, whi)
 
 
 def galerkin_kernel(near, packed, stat_in, flux, w, zlo, zhi, zl_ref, y_ref, stat):
@@ -482,6 +544,7 @@
     zl_ref[...] = local
     applied = local_operator(local, flux[...], packed)
     y_ref[...] = applied
+    applied = applied[:, RING : RING + ROWS]
     inner = near[0] * applied[0] + near[1] * applied[7]
     for i in range(1, 7):
         inner = inner + applied[i]
@@ -702,10 +765,13 @@
 
 
 def coarse_columns(near, coarse, start):
-    row = lax.broadcasted_iota(jnp.int32, (ROWS, LANES), 0)
-    edge = edge_rows(ROWS, near[2], near[3])
-    below = jnp.where(row == 0, 1.0 - near[2], 0.0)
-    above = jnp.where(row == ROWS - 1, 1.0 - near[3], 0.0)
+    row, has_low, has_high = ring_rows(near)
+    below = jnp.where(row < RING - 1, 1.0, jnp.where(row <= RING, 0.5, 0.0)) * has_low
+    above = jnp.where(row > RING + ROWS, 1.0, jnp.where(row >= RING + ROWS - 1, 0.5, 0.0)) * has_high
+    edge = jnp.where((row > RING) & (row < RING + ROWS - 1), 1.0, 0.0)
+    edge = jnp.where(row == RING, near[2], jnp.where(row == RING + ROWS - 1, near[3], edge))
+    edge = jnp.where(row == RING - 1, 0.5 * has_low, edge)
+    edge = jnp.where(row == RING + ROWS, 0.5 * has_high, edge)
     columns = []
     for a in range(3):
         at = start + 3 * a
@@ -736,7 +802,7 @@
     fy = along_y(
         stack([flux[i] * gy[0 if i == 0 else 2 if i == 7 else 1] for i in range(8)]), packed, 1
     )
-    plane_w = packed[0:ROWS]
+    plane_w = packed[0:WIDE]
     planes = []
     for i in range(8):
         plane = three[0 if i == 0 else 2 if i == 7 else 1]
@@ -746,21 +812,24 @@
 
 def apply_kernel(near, packed, coarse, flux, b, zl, yl, z_ref, y_ref, ylo, yhi, stat):
     columns = coarse_columns(near, coarse, 0)
-    field = add_coarse(zl[...], columns)
+    field = add_coarse(zl[...], columns)[:, RING : RING + ROWS]
     z_ref[...] = field
     applied = yl[...] + coarse_applied(columns, flux[...], packed)
     y_ref[...] = applied
     ylo[...] = applied[0:2]
     yhi[...] = applied[6:8]
-    stat[...] = lane_row([jnp.sum(b[...] * field), jnp.sum(field * applied)])
+    own = applied[:, RING : RING + ROWS]
+    stat[...] = lane_row([jnp.sum(b[...] * field), jnp.sum(field * own)])
 
 
 def second_kernel(near, packed, coarse, flux, b, y, w, zlo, zhi, stat_in, q_ref, stat):
     local = add_planes(w, zlo[...], zhi[...])
-    field = add_coarse(local, coarse_columns(near, coarse, 16))
+    columns = [column[RING : RING + ROWS] for column in coarse_columns(near, coarse, 16)]
+    field = add_coarse(local, columns)
     q_ref[...] = field
-    applied = local_operator(field, flux[...], packed)
-    sums = [0.0, 0.0, jnp.sum(b[...] * field), jnp.sum(y[...] * field), jnp.sum(field * applied)]
+    applied = local_operator(field, flux[:, RING : RING + ROWS], packed)
+    own = y[:, RING : RING + ROWS]
+    sums = [0.0, 0.0, jnp.sum(b[...] * field), jnp.sum(own * field), jnp.sum(field * applied)]
     stat[...] = jnp.broadcast_to(stat_in[...] + lane_row(sums), stat.shape)
 
 
@@ -812,9 +881,12 @@
     near = jnp.stack(ends(index_gx, count_gx) + ends(index_gy, count_gy)).astype(F32)
     place = jnp.stack([index_gx, index_gy]).astype(jnp.int32)
     packed = jnp.asarray(PACKED)
-    solver = (INV_DEN, FY_W, FX_HH, FX_L, BX_H, BX_L, BY_W)
-    solver = tuple(jnp.asarray(table) for table in solver)
+    solver_a = tuple(jnp.asarray(table) for table in SOLVER_A)
+    solver_b = tuple(jnp.asarray(table) for table in SOLVER_B)
+    spread = jnp.asarray(SPREAD)
     face = (ROWS, LANES)
+    wide_block = (8, WIDE, LANES)
+    wide_face = (WIDE, LANES)
     rim = (12, TILE, LANES)
     solid = wick_solid.reshape(EY, EX).astype(F32)
 
@@ -831,25 +903,25 @@
         place=pltpu.HBM,
     )
     zlo, zhi = shift("gx", zlo, zhi)
-    ylo, yhi = run(functools.partial(rim_kernel, 2), [rim, rim], [], [b, l, zlo, zhi])
+    ylo, yhi = run(rim_kernel, [rim, rim], [], [solid, spread, b, l, zlo, zhi])
     ylo, yhi = shift("gy", ylo, yhi)
     w, wlo, whi = run(
-        schwarz_kernel, [block, face, face], [near], [*solver, b, zlo, zhi, ylo, yhi]
+        first_schwarz_kernel,
+        [wide_block, wide_face, wide_face],
+        [near],
+        [*solver_a, b, zlo, zhi, ylo, yhi],
     )
     wlo, whi = shift("gx", wlo, whi)
     level_new, flux, stat = run(
         level_kernel,
-        [block, block, (1, LANES)],
+        [block, wide_block, (1, LANES)],
         [near],
-        [
-            solid, jnp.asarray(SPREAD), jnp.asarray(INV_MASS), packed,
-            b, l, zlo, zhi, ylo, yhi,
-        ],
+        [solid, spread, jnp.asarray(INV_MASS), packed, b, l, zlo, zhi, ylo, yhi],
         flops=20000000,
     )
     zl, yl, stat = run(
         galerkin_kernel,
-        [block, block, (count_gx, LANES)],
+        [wide_block, wide_block, (count_gx, LANES)],
         [near],
         [packed, stat, flux, w, wlo, whi],
     )
@@ -865,15 +937,13 @@
     )
     z, y, zlo, zhi, sums = run(
         apply_kernel,
-        [block, block, (2, *face), (2, *face), (1, LANES)],
+        [block, wide_block, (2, *wide_face), (2, *wide_face), (1, LANES)],
         [near],
         [packed, coarse, flux, b, zl, yl],
     )
     zlo, zhi = shift("gx", zlo, zhi)
-    ylo, yhi = run(functools.partial(rim_kernel, 1), [rim, rim], [], [y, zlo, zhi])
-    ylo, yhi = shift("gy", ylo, yhi)
     w, wlo, whi = run(
-        schwarz_kernel, [block, face, face], [near], [*solver, y, zlo, zhi, ylo, yhi]
+        second_schwarz_kernel, [block, face, face], [near], [*solver_b, y, zlo, zhi]
     )
     zlo, zhi = shift("gx", wlo, whi)
     q, sums = run(

time: 133 us -> 131 us (0.985)
  starting transfers between devices: 44.2 us -> 37.9 us
  local copies, waits for them, and re-layouts: 0.08 us -> 4.08 us
  waiting for transfers between devices: 31.1 us -> 28.9 us
  Pallas kernels: 15.4 us -> 17.1 us
    ppermute x6 -> x5, starting transfers between devices: 22.4 us -> 18 us  [shift(): lax.ppermute(high_face, axis, forward)]
    unnamed x22 -> x32, local copies, waits for them, and re-layouts: 0.06 us -> 4.05 us
    ppermute x6 -> x5, waiting for transfers between devices: 21.8 us -> 18.4 us  [shift(): lax.ppermute(low_face, axis, backward)]
    ppermute x6 -> x5, starting transfers between devices: 9.32 us -> 7.41 us  [shift(): lax.ppermute(low_face, axis, backward)]
    pallas_call x12 -> x11, Pallas kernels: 15.4 us -> 17.1 us  [run(): pl.pallas_call(kernel, out_shape=[jax.ShapeDtypeStruct(out, F32) for out...]
  transfers between devices with their start and end apart: 13 -> 11, of which waited for: 7 -> 7; matrix products, arithmetic and copies ran while one was open for 0% -> 1% of each run, Pallas kernels for 1% -> 1%
where the time goes in v6:
time: 131 us; the launch traced here: 130 us
  blocking collectives  40.4 us (31%)
  starting transfers between devices  37.9 us (29%)
  waiting for transfers between devices  28.9 us (22%)
  Pallas kernels  17.1 us (13%)
  local copies, waits for them, and re-layouts  4.08 us (3%)
    ppermute x5, waiting for transfers between devices, shift(): lax.ppermute(low_face, axis, backward)  18.4 us
    ppermute x5, starting transfers between devices, shift(): lax.ppermute(high_face, axis, forward)  18 us
    all_to_all x1, blocking collectives, body(): wide = lax.all_to_all(wide, 'gy', 0, 0, tiled=True)  17.7 us
    pallas_call x11, Pallas kernels, run(): pl.pallas_call(kernel, out_shape=[jax.ShapeDtypeStruct(out, F32) for out...  17.1 us
    all_to_all x1, blocking collectives, body(): gathered = lax.all_to_all(stat, 'gx', 0, 0, tiled=True)  12.7 us
    all_to_all x1, starting transfers between devices, body(): gathered = lax.all_to_all(column, 'gy', 0, 0, tiled=True)  12.5 us
    all_to_all x1, blocking collectives, body(): tile = lax.all_to_all(sums, 'gx', 0, 0, tiled=True)  10 us
    all_to_all x1, waiting for transfers between devices, body(): gathered = lax.all_to_all(column, 'gy', 0, 0, tiled=True)  9.22 us
  transfers between devices with their start and end apart: 11, of which 7 were waited for; matrix products, arithmetic and copies ran while one was open for 1% of the time, Pallas kernels for 1%

profile of v6, /device:TPU:1, one launch (start us, length us, event | category | flops | bytes accessed | tf_op | source)
XLA Modules:
  0.0 130.2 jit_solution(15760807260966514364)
XLA Ops:
  0.6 0.0 copy-start.6
  0.6 0.0 copy-start.3
  0.7 0.0 copy-start.1
  0.7 1.8 %shard_map.176 = (f32[8,32,128]{2,1,0:T(8,128)S(1)}, f32[8,32,128]{2,1,0:T(8,128)S(1)}, f32[3,32,128]{2,1,0:T(8,128)S(1)}, f32[3,32,128]{2,1,0:T(8,128)S(1)}) custom-call(f32[8,32,128]{2,1,0:T(8,128)} %lev_in.1, f32[3,8,32,128]{3,2,1,0:T(8,128)} %vel_in.1, f32[8,32,128]{2,1,0:T(8,128)} %src_in.1, f32[464,128]{1,0:T(8,128)} %constant.47.clone.packed_in.packed), custom_call_target="tpu_custom_call" | custom-call | flops 1000000 | bytes 720896 | tf_op jit(solution)/shard_map/pallas_call | solution.py:852
  2.5 4.8 %collective-permute-start = (f32[3,32,128]{2,1,0:T(8,128)S(1)}, f32[3,32,128]{2,1,0:T(8,128)S(1)}, u32[]{:S(2)}, u32[]{:S(2)}) collective-permute-start(f32[3,32,128]{2,1,0:T(8,128)S(1)} %get-tuple-element.29), channel_id=1, source_target_pairs={{0,64},{64,128},{128,192},{192,256},{256,320},{320,384},{384,448},... | collective-permute-start | bytes 147464 | tf_op jit(solution)/shard_map/ppermute | solution.py:868
  7.3 1.3 collective-permute-start.1
  8.6 0.7 convert_bitcast_fusion.solid
  9.3 0.0 collective-permute-done.low_z.zlo
  9.3 3.5 %collective-permute-done.1.high_z.zhi = f32[3,32,128]{2,1,0:T(8,128)S(1)} collective-permute-done((f32[3,32,128]{2,1,0:T(8,128)S(1)}, f32[3,32,128]{2,1,0:T(8,128)S(1)}, u32[]{:S(2)}, u32[]{:S(2)}) %collective-permute-start.1) | collective-permute-done | bytes 49184 | tf_op jit(solution)/shard_map/ppermute | solution.py:868
  12.8 0.7 copy-done.14
  13.5 0.1 shard_map.177
  13.6 4.8 %collective-permute-start.2 = (f32[12,48,128]{2,1,0:T(8,128)S(1)}, f32[12,48,128]{2,1,0:T(8,128)S(1)}, u32[]{:S(2)}, u32[]{:S(2)}) collective-permute-start(f32[12,48,128]{2,1,0:T(8,128)S(1)} %get-tuple-element.31), channel_id=1, source_target_pairs={{0,1},{1,2},{2,3},{3,4},{4,5},{5,6},{6,7},{7,8},{8,9},{9,10},{10,1... | collective-permute-start | bytes 884744 | tf_op jit(solution)/shard_map/ppermute | solution.py:868
  18.4 2.2 %collective-permute-start.3 = (f32[12,48,128]{2,1,0:T(8,128)S(1)}, f32[12,48,128]{2,1,0:T(8,128)S(1)}, u32[]{:S(2)}, u32[]{:S(2)}) collective-permute-start(f32[12,48,128]{2,1,0:T(8,128)S(1)} %get-tuple-element.32), channel_id=1, source_target_pairs={{1,0},{2,1},{3,2},{4,3},{5,4},{6,5},{7,6},{8,7},{9,8},{10,9},{11,1... | collective-permute-start | bytes 884744 | tf_op jit(solution)/shard_map/ppermute | solution.py:868
  20.7 0.1 pad_maximum_fusion.near
  20.8 1.3 collective-permute-done.2.ylo
  22.1 4.4 %collective-permute-done.3.yhi = f32[12,48,128]{2,1,0:T(8,128)S(1)} collective-permute-done((f32[12,48,128]{2,1,0:T(8,128)S(1)}, f32[12,48,128]{2,1,0:T(8,128)S(1)}, u32[]{:S(2)}, u32[]{:S(2)}) %collective-permute-start.3) | collective-permute-done | bytes 294944 | tf_op jit(solution)/shard_map/ppermute | solution.py:868
  26.5 0.0 copy-start.4
  26.5 0.8 copy-done.4
  27.3 0.8 copy-done.7
  28.1 0.9 copy-done.9
  29.0 0.8 copy-done.10
  29.8 2.7 %shard_map.179 = (f32[8,64,128]{2,1,0:T(8,128)S(1)}, f32[64,128]{1,0:T(8,128)S(1)}, f32[64,128]{1,0:T(8,128)S(1)}) custom-call(f32[4]{0:T(128)S(1)} %pad_maximum_fusion.near, f32[1120,160]{1,0:T(8,128)S(1)} %copy-done.1, bf16[112,288]{1,0:T(8,128)(2,1)S(1)} %copy-done.9, bf16[256,160]{1,0:T(8,128)(2,1)S(1)} %copy-done.3, bf16[128,160]{1,0:T(8,128)(2,1)S(1)} %copy-done.4, ...), custom_call_target="tpu_custom_call" | custom-call | flops 1000000 | bytes 655360 | tf_op jit(solution)/shard_map/pallas_call | solution.py:852
  32.5 4.0 %collective-permute-start.4 = (f32[64,128]{1,0:T(8,128)S(1)}, f32[64,128]{1,0:T(8,128)S(1)}, u32[]{:S(2)}, u32[]{:S(2)}) collective-permute-start(f32[64,128]{1,0:T(8,128)S(1)} %get-tuple-element.37), channel_id=1, source_target_pairs={{0,64},{64,128},{128,192},{192,256},{256,320},{320,384},{384,448},... | collective-permute-start | bytes 98312 | tf_op jit(solution)/shard_map/ppermute | solution.py:868
  36.5 1.3 collective-permute-start.5
  37.9 1.5 %shard_map.178 = (f32[8,32,128]{2,1,0:T(8,128)}, f32[8,64,128]{2,1,0:T(8,128)S(1)}, f32[1,128]{1,0:T(1,128)S(1)}) custom-call(f32[4]{0:T(128)S(1)} %pad_maximum_fusion.near, f32[4,16]{1,0:T(4,128)S(1)} %convert_bitcast_fusion.solid, bf16[16,128]{1,0:T(8,128)(2,1)S(1)} %copy-done.15, f32[64,128]{1,0:T(8,128)S(1)} %copy-done.12, f32[464,128]{1,0:T(8,128)S(1)} %copy-done, ...), custom_call_target="tpu_custom_call" | custom-call | flops 20000000 | bytes 787456 | tf_op jit(solution)/shard_map/pallas_call | solution.py:852
  39.4 0.0 copy-start.13
  39.4 0.0 collective-permute-done.4.zlo
  39.4 3.6 %collective-permute-done.5.zhi = f32[64,128]{1,0:T(8,128)S(1)} collective-permute-done((f32[64,128]{1,0:T(8,128)S(1)}, f32[64,128]{1,0:T(8,128)S(1)}, u32[]{:S(2)}, u32[]{:S(2)}) %collective-permute-start.5) | collective-permute-done | bytes 32800 | tf_op jit(solution)/shard_map/ppermute | solution.py:868
  43.0 1.6 %shard_map.180 = (f32[8,64,128]{2,1,0:T(8,128)S(1)}, f32[8,64,128]{2,1,0:T(8,128)S(1)}, f32[8,128]{1,0:T(8,128)S(1)}) custom-call(f32[4]{0:T(128)S(1)} %pad_maximum_fusion.near, f32[464,128]{1,0:T(8,128)S(1)} %copy-done, f32[1,128]{1,0:T(1,128)S(1)} %get-tuple-element.34.stat_in, f32[8,64,128]{2,1,0:T(8,128)S(1)} %get-tuple-element.35.flux, ...), custom_call_target="tpu_custom_call" | custom-call | flops 1000000 | bytes 1056768 | tf_op jit(solution)/shard_map/pallas_call | solution.py:852
  44.7 12.7 %all_to_all.39 = f32[8,1,128]{2,1,0:T(1,128)S(1)} all-to-all(f32[8,1,128]{2,1,0:T(1,128)S(1)} %bitcast.24), channel_id=1, replica_groups=mesh['gx'=8,'gy'=64] {'gx'}, dimensions={0} | all-to-all | bytes 8192 | tf_op jit(solution)/shard_map/all_to_all | solution.py:928
  57.4 0.9 shard_map.181
  58.3 12.5 %all-to-all-start.1 = ((f32[64,1,128]{2,1,0:T(1,128)}), f32[64,1,128]{2,1,0:T(1,128)S(1)}, u32[]{:S(2)}, u32[]{:S(2)}) async-start(f32[64,1,128]{2,1,0:T(1,128)} %bitcast.11), calls=%async_computation.1 | async-start | bytes 65536 | tf_op jit(solution)/shard_map/all_to_all | solution.py:930
  70.8 0.1 pad_add_fusion.place
  70.9 9.2 %all-to-all-done.1 = f32[64,1,128]{2,1,0:T(1,128)S(1)} async-done(((f32[64,1,128]{2,1,0:T(1,128)}), f32[64,1,128]{2,1,0:T(1,128)S(1)}, u32[]{:S(2)}, u32[]{:S(2)}) %all-to-all-start.1) | async-done | bytes 32800 | tf_op jit(solution)/shard_map/all_to_all | solution.py:930
  80.1 3.3 %shard_map.182.coarse = f32[32,128]{1,0:T(8,128)S(1)} custom-call(s32[2]{0:T(128)S(1)} %pad_add_fusion.place, f32[64,128]{1,0:T(8,128)S(1)} %bitcast.20), custom_call_target="tpu_custom_call" | custom-call | flops 1000000 | bytes 32768 | tf_op jit(solution)/shard_map/pallas_call | solution.py:852
  83.4 1.1 shard_map.183
  84.6 2.2 %collective-permute-start.6 = (f32[2,64,128]{2,1,0:T(8,128)S(1)}, f32[2,64,128]{2,1,0:T(8,128)S(1)}, u32[]{:S(2)}, u32[]{:S(2)}) collective-permute-start(f32[2,64,128]{2,1,0:T(8,128)S(1)} %get-tuple-element.43), channel_id=1, source_target_pairs={{0,64},{64,128},{128,192},{192,256},{256,320},{320,384},{384,448},... | collective-permute-start | bytes 196616 | tf_op jit(solution)/shard_map/ppermute | solution.py:868
  86.8 1.3 collective-permute-start.7
  88.1 0.0 collective-permute-done.6.zlo
  88.1 3.7 %collective-permute-done.7.zhi = f32[2,64,128]{2,1,0:T(8,128)S(1)} collective-permute-done((f32[2,64,128]{2,1,0:T(8,128)S(1)}, f32[2,64,128]{2,1,0:T(8,128)S(1)}, u32[]{:S(2)}, u32[]{:S(2)}) %collective-permute-start.7) | collective-permute-done | bytes 65568 | tf_op jit(solution)/shard_map/ppermute | solution.py:868
  91.8 1.9 %shard_map.184 = (f32[8,32,128]{2,1,0:T(8,128)S(1)}, f32[32,128]{1,0:T(8,128)S(1)}, f32[32,128]{1,0:T(8,128)S(1)}) custom-call(f32[4]{0:T(128)S(1)} %pad_maximum_fusion.near, f32[640,160]{1,0:T(8,128)S(1)} %copy-done.2, bf16[64,192]{1,0:T(8,128)(2,1)S(1)} %copy-done.11, bf16[256,160]{1,0:T(8,128)(2,1)S(1)} %copy-done.3, bf16[128,160]{1,0:T(8,128)(2,1)S(1)} %copy-done.5, ...), custom_call_target="tpu_custom_call" | custom-call | flops 1000000 | bytes 327680 | tf_op jit(solution)/shard_map/pallas_call | solution.py:852
  93.7 2.2 %collective-permute-start.8 = (f32[32,128]{1,0:T(8,128)S(1)}, f32[32,128]{1,0:T(8,128)S(1)}, u32[]{:S(2)}, u32[]{:S(2)}) collective-permute-start(f32[32,128]{1,0:T(8,128)S(1)} %get-tuple-element.46), channel_id=1, source_target_pairs={{0,64},{64,128},{128,192},{192,256},{256,320},{320,384},{384,448},... | collective-permute-start | bytes 49160 | tf_op jit(solution)/shard_map/ppermute | solution.py:868
  95.9 1.3 collective-permute-start.9
  97.2 3.2 %collective-permute-done.9.zhi = f32[32,128]{1,0:T(8,128)S(1)} collective-permute-done((f32[32,128]{1,0:T(8,128)S(1)}, f32[32,128]{1,0:T(8,128)S(1)}, u32[]{:S(2)}, u32[]{:S(2)}) %collective-permute-start.9) | collective-permute-done | bytes 16416 | tf_op jit(solution)/shard_map/ppermute | solution.py:868
  100.4 1.2 shard_map.185
  101.6 10.0 %all_to_all.40 = f32[8,1,128]{2,1,0:T(1,128)S(1)} all-to-all(f32[8,1,128]{2,1,0:T(1,128)S(1)} %bitcast.23), channel_id=1, replica_groups=mesh['gx'=8,'gy'=64] {'gx'}, dimensions={0} | all-to-all | bytes 8192 | tf_op jit(solution)/shard_map/all_to_all | solution.py:955
  111.7 17.7 %all_to_all.41 = f32[64,1,128]{2,1,0:T(1,128)S(1)} all-to-all(f32[64,1,128]{2,1,0:T(1,128)S(1)} %broadcast_in_dim.2), channel_id=1, replica_groups=mesh['gx'=8,'gy'=64] {'gy'}, dimensions={0} | all-to-all | bytes 65536 | tf_op jit(solution)/shard_map/all_to_all | solution.py:957
  129.4 0.8 shard_map.186
  (25 shorter events, 0.1 us)
Async XLA Ops:
  0.6 25.8 %copy-start.6 = (bf16[160,128]{1,0:T(8,128)(2,1)S(1)}, bf16[160,128]{1,0:T(8,128)(2,1)}, u32[]{:S(2)}) copy-start(bf16[160,128]{1,0:T(8,128)(2,1)} %constant.53.clone.bxl) | copy-start | bytes 122884
  0.6 25.8 %copy-start.3 = (bf16[256,160]{1,0:T(8,128)(2,1)S(1)}, bf16[256,160]{1,0:T(8,128)(2,1)}, u32[]{:S(2)}) copy-start(bf16[256,160]{1,0:T(8,128)(2,1)} %constant.50.clone.fxhh) | copy-start | bytes 245764
  0.7 25.8 %copy-start.1 = (f32[1120,160]{1,0:T(8,128)S(1)}, f32[1120,160]{1,0:T(8,128)}, u32[]{:S(2)}) copy-start(f32[1120,160]{1,0:T(8,128)} %constant.48.clone.inv_den) | copy-start | bytes 2150404
  2.5 6.8 %collective-permute-start = (f32[3,32,128]{2,1,0:T(8,128)S(1)}, f32[3,32,128]{2,1,0:T(8,128)S(1)}, u32[]{:S(2)}, u32[]{:S(2)}) collective-permute-start(f32[3,32,128]{2,1,0:T(8,128)S(1)} %get-tuple-element.29), channel_id=1, source_target_pairs={{0,64},{64,128},{128,192},{192,256},{256,320},{320,384},{384,448},... | collective-permute-start | bytes 147464 | tf_op jit(solution)/shard_map/ppermute | solution.py:868
  7.3 5.5 %collective-permute-start.1 = (f32[3,32,128]{2,1,0:T(8,128)S(1)}, f32[3,32,128]{2,1,0:T(8,128)S(1)}, u32[]{:S(2)}, u32[]{:S(2)}) collective-permute-start(f32[3,32,128]{2,1,0:T(8,128)S(1)} %get-tuple-element.30), channel_id=1, source_target_pairs={{64,0},{128,64},{192,128},{256,192},{320,256},{384,320},{448,384},... | collective-permute-start | bytes 147464 | tf_op jit(solution)/shard_map/ppermute | solution.py:868
  12.8 0.7 copy-start.14
  13.6 8.5 %collective-permute-start.2 = (f32[12,48,128]{2,1,0:T(8,128)S(1)}, f32[12,48,128]{2,1,0:T(8,128)S(1)}, u32[]{:S(2)}, u32[]{:S(2)}) collective-permute-start(f32[12,48,128]{2,1,0:T(8,128)S(1)} %get-tuple-element.31), channel_id=1, source_target_pairs={{0,1},{1,2},{2,3},{3,4},{4,5},{5,6},{6,7},{7,8},{8,9},{9,10},{10,1... | collective-permute-start | bytes 884744 | tf_op jit(solution)/shard_map/ppermute | solution.py:868
  18.4 8.0 %collective-permute-start.3 = (f32[12,48,128]{2,1,0:T(8,128)S(1)}, f32[12,48,128]{2,1,0:T(8,128)S(1)}, u32[]{:S(2)}, u32[]{:S(2)}) collective-permute-start(f32[12,48,128]{2,1,0:T(8,128)S(1)} %get-tuple-element.32), channel_id=1, source_target_pairs={{1,0},{2,1},{3,2},{4,3},{5,4},{6,5},{7,6},{8,7},{9,8},{10,9},{11,1... | collective-permute-start | bytes 884744 | tf_op jit(solution)/shard_map/ppermute | solution.py:868
  20.8 17.1 %copy-start = (f32[464,128]{1,0:T(8,128)S(1)}, f32[464,128]{1,0:T(8,128)}, u32[]{:S(2)}) copy-start(f32[464,128]{1,0:T(8,128)} %constant.47.clone.packed_in.packed) | copy-start | bytes 712708
  26.5 0.8 copy-start.4
  27.3 0.8 copy-start.7
  28.1 0.9 copy-start.9
  29.0 0.8 copy-start.10
  29.8 8.0 %copy-start.12 = (f32[64,128]{1,0:T(8,128)S(1)}, f32[64,128]{1,0:T(8,128)}, u32[]{:S(2)}) copy-start(f32[64,128]{1,0:T(8,128)} %constant.59.clone.inv_mass) | copy-start | bytes 98308
  29.8 8.1 %copy-start.15 = (bf16[16,128]{1,0:T(8,128)(2,1)S(1)}, bf16[16,128]{1,0:T(8,128)(2,1)}, u32[]{:S(2)}) copy-start(bf16[16,128]{1,0:T(8,128)(2,1)} %constant.58.clone.spread) | copy-start | bytes 12292
  32.5 6.9 %collective-permute-start.4 = (f32[64,128]{1,0:T(8,128)S(1)}, f32[64,128]{1,0:T(8,128)S(1)}, u32[]{:S(2)}, u32[]{:S(2)}) collective-permute-start(f32[64,128]{1,0:T(8,128)S(1)} %get-tuple-element.37), channel_id=1, source_target_pairs={{0,64},{64,128},{128,192},{192,256},{256,320},{320,384},{384,448},... | collective-permute-start | bytes 98312 | tf_op jit(solution)/shard_map/ppermute | solution.py:868
  36.5 6.5 %collective-permute-start.5 = (f32[64,128]{1,0:T(8,128)S(1)}, f32[64,128]{1,0:T(8,128)S(1)}, u32[]{:S(2)}, u32[]{:S(2)}) collective-permute-start(f32[64,128]{1,0:T(8,128)S(1)} %get-tuple-element.38), channel_id=1, source_target_pairs={{64,0},{128,64},{192,128},{256,192},{320,256},{384,320},{448,384},... | collective-permute-start | bytes 98312 | tf_op jit(solution)/shard_map/ppermute | solution.py:868
  39.4 52.4 %copy-start.2 = (f32[640,160]{1,0:T(8,128)S(1)}, f32[640,160]{1,0:T(8,128)}, u32[]{:S(2)}) copy-start(f32[640,160]{1,0:T(8,128)} %constant.55.clone.inv_den) | copy-start | bytes 1228804
  39.4 52.4 %copy-start.5 = (bf16[128,160]{1,0:T(8,128)(2,1)S(1)}, bf16[128,160]{1,0:T(8,128)(2,1)}, u32[]{:S(2)}) copy-start(bf16[128,160]{1,0:T(8,128)(2,1)} %constant.51.clone.fxl) | copy-start | bytes 122884
  39.4 52.4 %copy-start.8 = (bf16[160,128]{1,0:T(8,128)(2,1)S(1)}, bf16[160,128]{1,0:T(8,128)(2,1)}, u32[]{:S(2)}) copy-start(bf16[160,128]{1,0:T(8,128)(2,1)} %constant.52.clone.bxh) | copy-start | bytes 122884
  39.4 52.4 %copy-start.11 = (bf16[64,192]{1,0:T(8,128)(2,1)S(1)}, bf16[64,192]{1,0:T(8,128)(2,1)}, u32[]{:S(2)}) copy-start(bf16[64,192]{1,0:T(8,128)(2,1)} %constant.56.clone.fy) | copy-start | bytes 73732
  39.4 52.4 %copy-start.13 = (bf16[40,192]{1,0:T(8,128)(2,1)S(1)}, bf16[40,192]{1,0:T(8,128)(2,1)}, u32[]{:S(2)}) copy-start(bf16[40,192]{1,0:T(8,128)(2,1)} %constant.57.clone.by) | copy-start | bytes 46084
  58.3 21.8 %all-to-all-start.1 = ((f32[64,1,128]{2,1,0:T(1,128)}), f32[64,1,128]{2,1,0:T(1,128)S(1)}, u32[]{:S(2)}, u32[]{:S(2)}) async-start(f32[64,1,128]{2,1,0:T(1,128)} %bitcast.11), calls=%async_computation.1 | async-start | bytes 65536 | tf_op jit(solution)/shard_map/all_to_all | solution.py:930
  84.6 3.5 %collective-permute-start.6 = (f32[2,64,128]{2,1,0:T(8,128)S(1)}, f32[2,64,128]{2,1,0:T(8,128)S(1)}, u32[]{:S(2)}, u32[]{:S(2)}) collective-permute-start(f32[2,64,128]{2,1,0:T(8,128)S(1)} %get-tuple-element.43), channel_id=1, source_target_pairs={{0,64},{64,128},{128,192},{192,256},{256,320},{320,384},{384,448},... | collective-permute-start | bytes 196616 | tf_op jit(solution)/shard_map/ppermute | solution.py:868
  86.8 5.0 %collective-permute-start.7 = (f32[2,64,128]{2,1,0:T(8,128)S(1)}, f32[2,64,128]{2,1,0:T(8,128)S(1)}, u32[]{:S(2)}, u32[]{:S(2)}) collective-permute-start(f32[2,64,128]{2,1,0:T(8,128)S(1)} %get-tuple-element.44), channel_id=1, source_target_pairs={{64,0},{128,64},{192,128},{256,192},{320,256},{384,320},{448,384},... | collective-permute-start | bytes 196616 | tf_op jit(solution)/shard_map/ppermute | solution.py:868
  93.7 3.5 %collective-permute-start.8 = (f32[32,128]{1,0:T(8,128)S(1)}, f32[32,128]{1,0:T(8,128)S(1)}, u32[]{:S(2)}, u32[]{:S(2)}) collective-permute-start(f32[32,128]{1,0:T(8,128)S(1)} %get-tuple-element.46), channel_id=1, source_target_pairs={{0,64},{64,128},{128,192},{192,256},{256,320},{320,384},{384,448},... | collective-permute-start | bytes 49160 | tf_op jit(solution)/shard_map/ppermute | solution.py:868
  95.9 4.5 %collective-permute-start.9 = (f32[32,128]{1,0:T(8,128)S(1)}, f32[32,128]{1,0:T(8,128)S(1)}, u32[]{:S(2)}, u32[]{:S(2)}) collective-permute-start(f32[32,128]{1,0:T(8,128)S(1)} %get-tuple-element.47), channel_id=1, source_target_pairs={{64,0},{128,64},{192,128},{256,192},{320,256},{384,320},{448,384},... | collective-permute-start | bytes 49160 | tf_op jit(solution)/shard_map/ppermute | solution.py:868

commit v7 on v6

--- a/solution.py
+++ b/solution.py
@@ -187,9 +187,31 @@
     return np.concatenate([high, high, low], axis=1)
 
 
-FX_HH = np.concatenate([FX_H, FX_H], axis=0)
-SOLVER_A = (denominators(STEP_A), wide_const(FY_A), FX_HH, FX_L, BX_H, BX_L, wide_const(BY_A))
-SOLVER_B = (denominators(STEP_B), wide_const(FY_B), FX_HH, FX_L, BX_H, BX_L, wide_const(BY_B))
+def pack_tables(tables):
+    places, pieces, at = [], [], 0
+    for table in tables:
+        rows = -(-table.shape[0] // 16) * 16
+        extra = ((0, rows - table.shape[0]), (0, 384 - table.shape[1]))
+        pieces.append(np.pad(table.astype(np.float32), extra))
+        places.append((at, rows, table.shape[1]))
+        at += rows
+    return np.concatenate(pieces).astype(jnp.bfloat16), places
+
+
+TABLES, PLACES = pack_tables(
+    [
+        np.concatenate([FX_H, FX_H], axis=0),
+        FX_L,
+        BX_H,
+        BX_L,
+        wide_const(FY_A),
+        wide_const(BY_A),
+        wide_const(FY_B),
+        wide_const(BY_B),
+    ]
+)
+DEN_A = denominators(STEP_A)
+DEN_B = denominators(STEP_B)
 
 
 def roll_table():
@@ -203,10 +225,25 @@
 
 WY = np.tile(WEIGHT, WIDE // 8)
 WX = np.tile(WEIGHT, EX)
+
+
+def inner_count(count):
+    mult = np.ones(8 * count)
+    position = np.arange(8 * count)
+    mult[(position % 8 == 0) & (position > 0)] += 1.0
+    mult[(position % 8 == 7) & (position < 8 * count - 1)] += 1.0
+    return mult
+
+
+END_MASS = np.where(np.arange(WIDE) % 8 % 7 == 0, 2.0, 1.0)
+INV_MASS = (8.0 / (WY * END_MASS)[:, None] / (WX * inner_count(EX))[None, :]).astype(np.float32)
+
 AT_ROLLS = WIDE
 AT_DX = AT_ROLLS + 128
 AT_DXT = AT_DX + LANES
 AT_SQUARE = AT_DXT + LANES
+AT_MASS = AT_SQUARE + 16
+AT_SPREAD = AT_MASS + WIDE
 PACKED = np.concatenate(
     [
         WY[:, None] * WX[None, :],
@@ -215,21 +252,10 @@
         np.kron(np.eye(EX), DERIV),
         np.repeat(DERIV[:, :1] ** 2, LANES, axis=1),
         np.repeat(DERIV[:, 7:] ** 2, LANES, axis=1),
+        INV_MASS,
+        np.kron(np.eye(EX), np.ones((1, 8))),
     ]
 ).astype(np.float32)
-
-
-def inner_count(count):
-    mult = np.ones(8 * count)
-    position = np.arange(8 * count)
-    mult[(position % 8 == 0) & (position > 0)] += 1.0
-    mult[(position % 8 == 7) & (position < 8 * count - 1)] += 1.0
-    return mult
-
-
-END_MASS = np.where(np.arange(WIDE) % 8 % 7 == 0, 2.0, 1.0)
-INV_MASS = (8.0 / (WY * END_MASS)[:, None] / (WX * inner_count(EX))[None, :]).astype(np.float32)
-SPREAD = np.kron(np.eye(EX), np.ones((1, 8))).astype(jnp.bfloat16)
 
 
 def parts(values):
@@ -246,7 +272,7 @@
     results = []
     for i in range(0, len(planes), 2):
         high, low = parts(jnp.concatenate([planes[i], planes[i + 1]], axis=1))
-        both = dot(table[...], jnp.concatenate([high, low, high], axis=0))
+        both = dot(table, jnp.concatenate([high, low, high], axis=0))
         results += [both[:, 0:LANES], both[:, LANES : 2 * LANES]]
     return results
 
@@ -313,15 +339,19 @@
     return stack(planes)
 
 
-def solve_elements(planes, tables):
-    inv_den, fy, fxhh, fxl, bxh, bxl, by = tables
-    spectral = left_pairs(fy, along_z(planes, FZ))
+def solve_elements(planes, inv_den, tables, kind):
+    def table(index):
+        at, rows, width = PLACES[index]
+        return tables[at : at + rows, 0:width]
+
+    fxhh, fxl, bxh, bxl = (table(index) for index in range(4))
+    spectral = left_pairs(table(4 + 2 * kind), along_z(planes, FZ))
     high, low = parts(jnp.concatenate(spectral, axis=0))
-    wide = dot(jnp.concatenate([high, low], axis=1), fxhh[...]) + dot(high, fxl[...])
+    wide = dot(jnp.concatenate([high, low], axis=1), fxhh) + dot(high, fxl)
     high, low = parts(wide * inv_den[...])
-    back = dot(high, bxh[...]) + dot(low, bxh[...]) + dot(high, bxl[...])
-    step = fy.shape[0]
-    back = left_pairs(by, [back[step * i : step * (i + 1)] for i in range(10)])
+    back = dot(high, bxh) + dot(low, bxh) + dot(high, bxl)
+    step = PLACES[4 + 2 * kind][1]
+    back = left_pairs(table(5 + 2 * kind), [back[step * i : step * (i + 1)] for i in range(10)])
     return along_z(back, BZ)
 
 
@@ -362,18 +392,24 @@
 
 
 def advect_kernel(
-    lev_in, vel_in, src_in, packed_in, b_ref, l_ref, zlo, zhi, lev, vel, src, packed, sems
+    lev_in, vel_in, src_in, packed_in, solid_in, b_ref, l_ref, zlo, zhi, solid_ref,
+    lev, vel, src, packed, solid, sems,
 ):
     copies = [
         pltpu.make_async_copy(source, target, sems.at[index])
         for index, (source, target) in enumerate(
-            ((vel_in, vel), (lev_in, lev), (packed_in, packed), (src_in, src))
+            (
+                (vel_in, vel), (lev_in, lev), (packed_in, packed), (src_in, src), (solid_in, solid),
+            )
         )
     ]
     for copy in copies:
         copy.start()
     for copy in copies:
         copy.wait()
+    spread = packed[AT_SPREAD : AT_SPREAD + EX].astype(BF16)
+    in_solid = dot(solid[...].astype(F32).astype(BF16), spread)
+    solid_ref[...] = jnp.concatenate([in_solid, jnp.zeros((8 - EY, LANES), F32)], axis=0)
     level = lev[...]
     v0, v1, v2 = vel[0], vel[1], vel[2]
     gz = stack(along_z([level[i] for i in range(8)], DERIV))
@@ -399,8 +435,8 @@
             zhi[2] = moved_i
 
 
-def rim_kernel(solid, spread, b, l, low_z, high_z, low_y, high_y):
-    in_solid = dot(solid[...].astype(BF16), spread[...])
+def rim_kernel(solid, b, l, low_z, high_z, low_y, high_y):
+    in_solid = solid[...]
     rest = TILE - REACH - RING - 1
 
     def rows(planes, at, level, far, extra=None):
@@ -428,7 +464,7 @@
 
 
 def level_kernel(
-    near, solid, spread, inv_mass, packed, b, l, zlo, zhi, ylo, yhi, level_ref, flux_ref, stat
+    near, solid, packed, b, l, zlo, zhi, ylo, yhi, level_ref, flux_ref, stat
 ):
     row, has_low, has_high = ring_rows(near)
     at = REACH
@@ -461,8 +497,8 @@
     after = jnp.where((lane % 8 == 7) & (lane < LANES - 1), pltpu.roll(own, LANES - 1, 2), 0.0)
     own = own + before + after
     ends = jnp.where(row == RING, 2.0 * near[2], jnp.where(row == RING + ROWS - 1, 2.0 * near[3], 1.0))
-    inverse = inv_mass[...] * ends
-    in_solid = dot(solid[...].astype(BF16), spread[...])
+    inverse = packed[AT_MASS : AT_MASS + WIDE] * ends
+    in_solid = solid[...]
     solids = [ylo[0, at + RING + 1 + k : at + RING + 2 + k] for k in range(2)]
     solids += [in_solid[e : e + 1] for e in range(EY)]
     solids += [yhi[0, at + RING + 1 + k : at + RING + 2 + k] for k in range(2)]
@@ -505,13 +541,13 @@
 
 
 def first_schwarz_kernel(
-    near, inv_den, fy, fxhh, fxl, bxh, bxl, by, b, zlo, zhi, ylo, yhi, w_ref, wlo, whi
+    near, inv_den, tables, b, zlo, zhi, ylo, yhi, w_ref, wlo, whi
 ):
     own = [b[i] for i in range(8)] + [zlo[0], zlo[1], zhi[0], zhi[1]]
     planes = [
         jnp.concatenate([ylo[i, 0:TILE_B], own[i], yhi[i, 0:TILE_B]], axis=0) for i in range(12)
     ]
-    planes = solve_elements(planes, (inv_den, fy, fxhh, fxl, bxh, bxl, by))
+    planes = solve_elements(planes, inv_den, tables, 0)
     row, has_low, has_high = ring_rows(near)
     in_grid = jnp.where(row < RING, has_low, jnp.where(row >= RING + ROWS, has_high, 1.0))
     in_grid = jnp.where(row == RING, has_low, jnp.where(row == RING + ROWS - 1, has_high, in_grid))
@@ -523,11 +559,9 @@
     store_faces(planes, near, w_ref, wlo, whi)
 
 
-def second_schwarz_kernel(
-    near, inv_den, fy, fxhh, fxl, bxh, bxl, by, y, zlo, zhi, w_ref, wlo, whi
-):
+def second_schwarz_kernel(near, inv_den, tables, y, zlo, zhi, w_ref, wlo, whi):
     planes = [y[i] for i in range(8)] + [zlo[0], zlo[1], zhi[0], zhi[1]]
-    planes = solve_elements(planes, (inv_den, fy, fxhh, fxl, bxh, bxl, by))
+    planes = solve_elements(planes, inv_den, tables, 1)
     row = lax.broadcasted_iota(jnp.int32, (ROWS, LANES), 0)
     _, has_low, has_high = ring_rows(near)
     in_grid = jnp.where(row == 0, has_low, jnp.where(row == ROWS - 1, has_high, 1.0))
@@ -677,7 +711,7 @@
     return result + HELM_COEF / 8.0 * float(np.sum(WX)) * scaled
 
 
-def coarse_kernel(count, place, gathered, out_ref, wide, turned):
+def coarse_kernel(count, near, gathered, out_ref, wide, turned):
     lanes = LANES
     sub = lax.broadcasted_iota(jnp.int32, (8, lanes), 0)
     lane = lax.broadcasted_iota(jnp.int32, (8, lanes), 1)
@@ -705,39 +739,49 @@
     back_z = move(link_z, -1, 0)
     back_y = move(link_y, 0, -1)
     diagonal = HELM_COEF * EZ * EY * EX + link_z + back_z + link_y + back_y
-    blocks, lower, upper = [], [], []
+    half = lanes // 2
+    low_half = lane < half
+
+    def twice(array):
+        return jnp.where(low_half, array, pltpu.roll(array, half, 1))
+
+    def swap(array):
+        return pltpu.roll(array, half, 1)
+
+    def beside_rows(rows, distance):
+        return [
+            jnp.where(low_half, pltpu.roll(row, distance, 1), pltpu.roll(row, lanes - distance, 1))
+            for row in rows
+        ]
+
+    diagonal, link_z, back_z = twice(diagonal), twice(link_z), twice(back_z)
+    link = jnp.where(low_half, back_y, swap(link_y))
+    blocks, sides = [], []
     for r in range(8):
         row = jnp.where(sub == r, diagonal, 0.0)
         row = jnp.where(sub == r + 1, -back_z, row)
         row = jnp.where(sub == r - 1, -link_z, row)
         blocks.append(row)
-        lower.append(jnp.where(sub == r, -back_y, 0.0))
-        upper.append(jnp.where(sub == r, -link_y, 0.0))
+        sides.append(jnp.where(sub == r, -link, 0.0))
     levels = []
     step = 1
     while step < count:
-        inverse = invert(blocks, sub)
-        down = multiply(lower, [move(row, 0, -step) for row in inverse])
-        up = multiply(upper, [move(row, 0, step) for row in inverse])
-        levels.append((step, down, up))
-        before_u = multiply(down, [move(row, 0, -step) for row in upper])
-        after_l = multiply(up, [move(row, 0, step) for row in lower])
+        factors = multiply(sides, beside_rows(invert(blocks, sub), step))
+        levels.append((step, factors))
+        terms = multiply(factors, beside_rows([swap(row) for row in sides], step))
+        blocks = [blocks[r] - terms[r] - swap(terms[r]) for r in range(8)]
         if 2 * step < count:
-            new_lower = multiply(down, [move(row, 0, -step) for row in lower])
-            new_upper = multiply(up, [move(row, 0, step) for row in upper])
-            lower = [-row for row in new_lower]
-            upper = [-row for row in new_upper]
-        blocks = [blocks[r] - before_u[r] - after_l[r] for r in range(8)]
+            sides = [-row for row in multiply(factors, beside_rows(sides, step))]
         step *= 2
     inverse = invert(blocks, sub)
 
     def solve(column):
-        for distance, down, up in levels:
-            pulled = matvec(
-                [(down, move(column, 0, -distance)), (up, move(column, 0, distance))], sub
-            )
-            column = column - pulled
-        return matvec([(inverse, column)], sub)
+        column = twice(column)
+        for distance, factors in levels:
+            pulled = matvec([(factors, beside_rows([column], distance)[0])], sub)
+            column = column - pulled - swap(pulled)
+        solved = matvec([(inverse, column)], sub)
+        return jnp.where(lane < count, solved, 0.0)
 
     offsets = [(a - 1, b - 1) for a in range(3) for b in range(3)]
     first = solve(value(1))
@@ -756,7 +800,7 @@
     totals = jnp.where(lane < count, totals, 0.0)
     second = solve(totals)
     near_second = [move(second, dz, dy) for dz, dy in offsets]
-    mine = (sub == place[0]) & (lane == place[1])
+    mine = (sub.astype(F32) == near[4]) & (lane.astype(F32) == near[5])
     for d in range(9):
         out_ref[d : d + 1] = jnp.full((1, lanes), jnp.sum(jnp.where(mine, near_first[d], 0.0)))
         out_ref[16 + d : 17 + d] = jnp.full(
@@ -878,45 +922,42 @@
     def ends(index, count):
         return [jnp.where(index > 0, 0.5, 1.0), jnp.where(index < count - 1, 0.5, 1.0)]
 
-    near = jnp.stack(ends(index_gx, count_gx) + ends(index_gy, count_gy)).astype(F32)
-    place = jnp.stack([index_gx, index_gy]).astype(jnp.int32)
+    place = [index_gx.astype(F32), index_gy.astype(F32)]
+    near = jnp.stack(ends(index_gx, count_gx) + ends(index_gy, count_gy) + place).astype(F32)
     packed = jnp.asarray(PACKED)
-    solver_a = tuple(jnp.asarray(table) for table in SOLVER_A)
-    solver_b = tuple(jnp.asarray(table) for table in SOLVER_B)
-    spread = jnp.asarray(SPREAD)
+    tables = jnp.asarray(TABLES)
     face = (ROWS, LANES)
     wide_block = (8, WIDE, LANES)
     wide_face = (WIDE, LANES)
     rim = (12, TILE, LANES)
-    solid = wick_solid.reshape(EY, EX).astype(F32)
-
-    b, l, zlo, zhi = run(
+
+    b, l, zlo, zhi, solid = run(
         advect_kernel,
-        [block, block, (3, *face), (3, *face)],
+        [block, block, (3, *face), (3, *face), (8, LANES)],
         [],
         [
             pltpu.with_memory_space_constraint(array, pltpu.HBM)
-            for array in (level_set, velocity, source, packed)
+            for array in (level_set, velocity, source, packed, wick_solid.reshape(EY, EX))
         ],
         [VMEM(block, F32), VMEM((3, *block), F32), VMEM(block, F32), VMEM(PACKED.shape, F32)]
-        + [pltpu.SemaphoreType.DMA((4,))],
+        + [VMEM((EY, EX), jnp.int32), pltpu.SemaphoreType.DMA((5,))],
         place=pltpu.HBM,
     )
     zlo, zhi = shift("gx", zlo, zhi)
-    ylo, yhi = run(rim_kernel, [rim, rim], [], [solid, spread, b, l, zlo, zhi])
+    ylo, yhi = run(rim_kernel, [rim, rim], [], [solid, b, l, zlo, zhi])
     ylo, yhi = shift("gy", ylo, yhi)
     w, wlo, whi = run(
         first_schwarz_kernel,
         [wide_block, wide_face, wide_face],
         [near],
-        [*solver_a, b, zlo, zhi, ylo, yhi],
+        [jnp.asarray(DEN_A), tables, b, zlo, zhi, ylo, yhi],
     )
     wlo, whi = shift("gx", wlo, whi)
     level_new, flux, stat = run(
         level_kernel,
         [block, wide_block, (1, LANES)],
         [near],
-        [solid, spread, jnp.asarray(INV_MASS), packed, b, l, zlo, zhi, ylo, yhi],
+        [solid, packed, b, l, zlo, zhi, ylo, yhi],
         flops=20000000,
     )
     zl, yl, stat = run(
@@ -931,7 +972,7 @@
     (coarse,) = run(
         functools.partial(coarse_kernel, count_gy),
         [(32, LANES)],
-        [place],
+        [near],
         [gathered],
         [VMEM((LANES, LANES), F32), VMEM((LANES, LANES), F32)],
     )
@@ -943,7 +984,7 @@
     )
     zlo, zhi = shift("gx", zlo, zhi)
     w, wlo, whi = run(
-        second_schwarz_kernel, [block, face, face], [near], [*solver_b, y, zlo, zhi]
+        second_schwarz_kernel, [block, face, face], [near], [jnp.asarray(DEN_B), tables, y, zlo, zhi]
     )
     zlo, zhi = shift("gx", wlo, whi)
     q, sums = run(

time: 131 us -> 128 us (0.977)
  blocking collectives: 40.4 us -> 62.1 us
  starting transfers between devices: 37.9 us -> 25.4 us
  waiting for transfers between devices: 28.9 us -> 20.4 us
  local copies, waits for them, and re-layouts: 4.08 us -> 1.38 us
    all_to_all x0 -> x1, blocking collectives: none -> 21.7 us  [body(): gathered = lax.all_to_all(column, 'gy', 0, 0, tiled=True)]
    all_to_all x1 -> x0, starting transfers between devices: 12.5 us -> none  [body(): gathered = lax.all_to_all(column, 'gy', 0, 0, tiled=True)]
    all_to_all x1 -> x0, waiting for transfers between devices: 9.22 us -> none  [body(): gathered = lax.all_to_all(column, 'gy', 0, 0, tiled=True)]
    unnamed x32 -> x8, local copies, waits for them, and re-layouts: 4.05 us -> 1.27 us
  transfers between devices with their start and end apart: 11 -> 10, of which waited for: 7 -> 6; matrix products, arithmetic and copies ran while one was open for 1% -> 0% of each run, Pallas kernels for 1% -> 1%
where the time goes in v7:
time: 128 us; the launch traced here: 127 us
  blocking collectives  62.1 us (49%)
  starting transfers between devices  25.4 us (20%)
  waiting for transfers between devices  20.4 us (16%)
  Pallas kernels  17.3 us (14%)
  local copies, waits for them, and re-layouts  1.38 us (1%)
    all_to_all x1, blocking collectives, body(): gathered = lax.all_to_all(column, 'gy', 0, 0, tiled=True)  21.7 us
    ppermute x5, waiting for transfers between devices, shift(): lax.ppermute(low_face, axis, backward)  19.1 us
    ppermute x5, starting transfers between devices, shift(): lax.ppermute(high_face, axis, forward)  18 us
    all_to_all x1, blocking collectives, body(): wide = lax.all_to_all(wide, 'gy', 0, 0, tiled=True)  17.7 us
    pallas_call x11, Pallas kernels, run(): pl.pallas_call(kernel, out_shape=[jax.ShapeDtypeStruct(out, F32) for out...  17.3 us
    all_to_all x1, blocking collectives, body(): gathered = lax.all_to_all(stat, 'gx', 0, 0, tiled=True)  12.7 us
    all_to_all x1, blocking collectives, body(): tile = lax.all_to_all(sums, 'gx', 0, 0, tiled=True)  10 us
    ppermute x5, starting transfers between devices, shift(): lax.ppermute(low_face, axis, backward)  7.4 us
  transfers between devices with their start and end apart: 10, of which 6 were waited for; matrix products, arithmetic and copies ran while one was open for 0% of the time, Pallas kernels for 1%

profile of v7, /device:TPU:1, one launch (start us, length us, event | category | flops | bytes accessed | tf_op | source)
XLA Modules:
  0.0 127.5 jit_solution(18045717072017169751)
XLA Ops:
  0.6 0.0 copy-start.1
  0.6 1.8 %shard_map.95 = (f32[8,32,128]{2,1,0:T(8,128)S(1)}, f32[8,32,128]{2,1,0:T(8,128)S(1)}, f32[3,32,128]{2,1,0:T(8,128)S(1)}, f32[3,32,128]{2,1,0:T(8,128)S(1)}, f32[8,128]{1,0:T(8,128)S(1)}) custom-call(f32[8,32,128]{2,1,0:T(8,128)} %lev_in.1, f32[3,8,32,128]{3,2,1,0:T(8,128)} %vel_in.1, f32[8,32,128]{2,1,0:T(8,128)} %src_in.1, ...), custom_call_target="tpu_custom_call" | custom-call | flops 1000000 | bytes 729088 | tf_op jit(solution)/shard_map/pallas_call | solution.py:896
  2.5 4.8 %collective-permute-start = (f32[3,32,128]{2,1,0:T(8,128)S(1)}, f32[3,32,128]{2,1,0:T(8,128)S(1)}, u32[]{:S(2)}, u32[]{:S(2)}) collective-permute-start(f32[3,32,128]{2,1,0:T(8,128)S(1)} %get-tuple-element.31), channel_id=1, source_target_pairs={{0,64},{64,128},{128,192},{192,256},{256,320},{320,384},{384,448},... | collective-permute-start | bytes 147464 | tf_op jit(solution)/shard_map/ppermute | solution.py:912
  7.3 1.3 %collective-permute-start.1 = (f32[3,32,128]{2,1,0:T(8,128)S(1)}, f32[3,32,128]{2,1,0:T(8,128)S(1)}, u32[]{:S(2)}, u32[]{:S(2)}) collective-permute-start(f32[3,32,128]{2,1,0:T(8,128)S(1)} %get-tuple-element.32), channel_id=1, source_target_pairs={{64,0},{128,64},{192,128},{256,192},{320,256},{384,320},{448,384},... | collective-permute-start | bytes 147464 | tf_op jit(solution)/shard_map/ppermute | solution.py:912
  8.6 0.0 collective-permute-done.low_z.zlo
  8.6 4.2 %collective-permute-done.1.high_z.zhi = f32[3,32,128]{2,1,0:T(8,128)S(1)} collective-permute-done((f32[3,32,128]{2,1,0:T(8,128)S(1)}, f32[3,32,128]{2,1,0:T(8,128)S(1)}, u32[]{:S(2)}, u32[]{:S(2)}) %collective-permute-start.1) | collective-permute-done | bytes 49184 | tf_op jit(solution)/shard_map/ppermute | solution.py:912
  12.8 4.8 %collective-permute-start.2 = (f32[12,48,128]{2,1,0:T(8,128)S(1)}, f32[12,48,128]{2,1,0:T(8,128)S(1)}, u32[]{:S(2)}, u32[]{:S(2)}) collective-permute-start(f32[12,48,128]{2,1,0:T(8,128)S(1)} %get-tuple-element.33), channel_id=1, source_target_pairs={{0,1},{1,2},{2,3},{3,4},{4,5},{5,6},{6,7},{7,8},{8,9},{9,10},{10,1... | collective-permute-start | bytes 884744 | tf_op jit(solution)/shard_map/ppermute | solution.py:912
  17.7 2.2 %collective-permute-start.3 = (f32[12,48,128]{2,1,0:T(8,128)S(1)}, f32[12,48,128]{2,1,0:T(8,128)S(1)}, u32[]{:S(2)}, u32[]{:S(2)}) collective-permute-start(f32[12,48,128]{2,1,0:T(8,128)S(1)} %get-tuple-element.34), channel_id=1, source_target_pairs={{1,0},{2,1},{3,2},{4,3},{5,4},{6,5},{7,6},{8,7},{9,8},{10,9},{11,1... | collective-permute-start | bytes 884744 | tf_op jit(solution)/shard_map/ppermute | solution.py:912
  19.9 0.1 stack.27.near
  20.0 0.0 copy-start
  20.0 1.3 %collective-permute-done.2.ylo = f32[12,48,128]{2,1,0:T(8,128)S(1)} collective-permute-done((f32[12,48,128]{2,1,0:T(8,128)S(1)}, f32[12,48,128]{2,1,0:T(8,128)S(1)}, u32[]{:S(2)}, u32[]{:S(2)}) %collective-permute-start.2) | collective-permute-done | bytes 294944 | tf_op jit(solution)/shard_map/ppermute | solution.py:912
  21.3 4.4 %collective-permute-done.3.yhi = f32[12,48,128]{2,1,0:T(8,128)S(1)} collective-permute-done((f32[12,48,128]{2,1,0:T(8,128)S(1)}, f32[12,48,128]{2,1,0:T(8,128)S(1)}, u32[]{:S(2)}, u32[]{:S(2)}) %collective-permute-start.3) | collective-permute-done | bytes 294944 | tf_op jit(solution)/shard_map/ppermute | solution.py:912
  25.7 0.0 copy-done.1
  25.7 0.0 copy-start.2
  25.7 1.3 copy-done.2
  27.0 2.7 %shard_map.98 = (f32[8,64,128]{2,1,0:T(8,128)S(1)}, f32[64,128]{1,0:T(8,128)S(1)}, f32[64,128]{1,0:T(8,128)S(1)}) custom-call(f32[6]{0:T(128)S(1)} %stack.27.near, f32[1120,160]{1,0:T(8,128)S(1)} %copy-done.2, bf16[1008,384]{1,0:T(8,128)(2,1)S(1)} %copy-done.1, f32[8,32,128]{2,1,0:T(8,128)S(1)} %get-tuple-element.29.b, ...), custom_call_target="tpu_custom_call" | custom-call | flops 1000000 | bytes 655360 | tf_op jit(solution)/shard_map/pallas_call | solution.py:896
  29.7 4.0 %collective-permute-start.4 = (f32[64,128]{1,0:T(8,128)S(1)}, f32[64,128]{1,0:T(8,128)S(1)}, u32[]{:S(2)}, u32[]{:S(2)}) collective-permute-start(f32[64,128]{1,0:T(8,128)S(1)} %get-tuple-element.39), channel_id=1, source_target_pairs={{0,64},{64,128},{128,192},{192,256},{256,320},{320,384},{384,448},... | collective-permute-start | bytes 98312 | tf_op jit(solution)/shard_map/ppermute | solution.py:912
  33.7 1.3 %collective-permute-start.5 = (f32[64,128]{1,0:T(8,128)S(1)}, f32[64,128]{1,0:T(8,128)S(1)}, u32[]{:S(2)}, u32[]{:S(2)}) collective-permute-start(f32[64,128]{1,0:T(8,128)S(1)} %get-tuple-element.40), channel_id=1, source_target_pairs={{64,0},{128,64},{192,128},{256,192},{320,256},{384,320},{448,384},... | collective-permute-start | bytes 98312 | tf_op jit(solution)/shard_map/ppermute | solution.py:912
  35.0 0.0 copy-done
  35.0 1.5 %shard_map.97 = (f32[8,32,128]{2,1,0:T(8,128)}, f32[8,64,128]{2,1,0:T(8,128)S(1)}, f32[1,128]{1,0:T(1,128)S(1)}) custom-call(f32[6]{0:T(128)S(1)} %stack.27.near, f32[8,128]{1,0:T(8,128)S(1)} %get-tuple-element.28.solid, f32[544,128]{1,0:T(8,128)S(1)} %copy-done, f32[8,32,128]{2,1,0:T(8,128)S(1)} %get-tuple-element.29.b, ...), custom_call_target="tpu_custom_call" | custom-call | flops 20000000 | bytes 787456 | tf_op jit(solution)/shard_map/pallas_call | solution.py:896
  36.5 0.0 copy-start.3
  36.5 0.0 collective-permute-done.4.zlo
  36.5 3.7 %collective-permute-done.5.zhi = f32[64,128]{1,0:T(8,128)S(1)} collective-permute-done((f32[64,128]{1,0:T(8,128)S(1)}, f32[64,128]{1,0:T(8,128)S(1)}, u32[]{:S(2)}, u32[]{:S(2)}) %collective-permute-start.5) | collective-permute-done | bytes 32800 | tf_op jit(solution)/shard_map/ppermute | solution.py:912
  40.2 1.7 %shard_map.99 = (f32[8,64,128]{2,1,0:T(8,128)S(1)}, f32[8,64,128]{2,1,0:T(8,128)S(1)}, f32[8,128]{1,0:T(8,128)S(1)}) custom-call(f32[6]{0:T(128)S(1)} %stack.27.near, f32[544,128]{1,0:T(8,128)S(1)} %copy-done, f32[1,128]{1,0:T(1,128)S(1)} %get-tuple-element.36.stat_in, f32[8,64,128]{2,1,0:T(8,128)S(1)} %get-tuple-element.37.flux, ...), custom_call_target="tpu_custom_call" | custom-call | flops 1000000 | bytes 1056768 | tf_op jit(solution)/shard_map/pallas_call | solution.py:896
  41.9 12.7 %all_to_all.39 = f32[8,1,128]{2,1,0:T(1,128)S(1)} all-to-all(f32[8,1,128]{2,1,0:T(1,128)S(1)} %bitcast.24), channel_id=1, replica_groups=mesh['gx'=8,'gy'=64] {'gx'}, dimensions={0} | all-to-all | bytes 8192 | tf_op jit(solution)/shard_map/all_to_all | solution.py:969
  54.5 0.3 shard_map.100
  54.8 21.7 %all_to_all.40 = f32[64,1,128]{2,1,0:T(1,128)S(1)} all-to-all(f32[64,1,128]{2,1,0:T(1,128)S(1)} %bitcast.19), channel_id=1, replica_groups=mesh['gx'=8,'gy'=64] {'gy'}, dimensions={0} | all-to-all | bytes 65536 | tf_op jit(solution)/shard_map/all_to_all | solution.py:971
  76.5 4.2 %shard_map.101.coarse = f32[32,128]{1,0:T(8,128)S(1)} custom-call(f32[6]{0:T(128)S(1)} %stack.27.near, f32[64,128]{1,0:T(8,128)S(1)} %bitcast.20), custom_call_target="tpu_custom_call" | custom-call | flops 1000000 | bytes 32768 | tf_op jit(solution)/shard_map/pallas_call | solution.py:896
  80.7 1.2 shard_map.102
  81.9 2.2 %collective-permute-start.6 = (f32[2,64,128]{2,1,0:T(8,128)S(1)}, f32[2,64,128]{2,1,0:T(8,128)S(1)}, u32[]{:S(2)}, u32[]{:S(2)}) collective-permute-start(f32[2,64,128]{2,1,0:T(8,128)S(1)} %get-tuple-element.45), channel_id=1, source_target_pairs={{0,64},{64,128},{128,192},{192,256},{256,320},{320,384},{384,448},... | collective-permute-start | bytes 196616 | tf_op jit(solution)/shard_map/ppermute | solution.py:912
  84.1 1.3 %collective-permute-start.7 = (f32[2,64,128]{2,1,0:T(8,128)S(1)}, f32[2,64,128]{2,1,0:T(8,128)S(1)}, u32[]{:S(2)}, u32[]{:S(2)}) collective-permute-start(f32[2,64,128]{2,1,0:T(8,128)S(1)} %get-tuple-element.46), channel_id=1, source_target_pairs={{64,0},{128,64},{192,128},{256,192},{320,256},{384,320},{448,384},... | collective-permute-start | bytes 196616 | tf_op jit(solution)/shard_map/ppermute | solution.py:912
  85.4 0.0 collective-permute-done.6.zlo
  85.4 3.7 %collective-permute-done.7.zhi = f32[2,64,128]{2,1,0:T(8,128)S(1)} collective-permute-done((f32[2,64,128]{2,1,0:T(8,128)S(1)}, f32[2,64,128]{2,1,0:T(8,128)S(1)}, u32[]{:S(2)}, u32[]{:S(2)}) %collective-permute-start.7) | collective-permute-done | bytes 65568 | tf_op jit(solution)/shard_map/ppermute | solution.py:912
  89.1 0.0 copy-done.3
  89.1 1.9 %shard_map.103 = (f32[8,32,128]{2,1,0:T(8,128)S(1)}, f32[32,128]{1,0:T(8,128)S(1)}, f32[32,128]{1,0:T(8,128)S(1)}) custom-call(f32[6]{0:T(128)S(1)} %stack.27.near, f32[640,160]{1,0:T(8,128)S(1)} %copy-done.3, bf16[1008,384]{1,0:T(8,128)(2,1)S(1)} %copy-done.1, f32[8,64,128]{2,1,0:T(8,128)S(1)} %get-tuple-element.44.y, ...), custom_call_target="tpu_custom_call" | custom-call | flops 1000000 | bytes 327680 | tf_op jit(solution)/shard_map/pallas_call | solution.py:896
  91.0 2.2 %collective-permute-start.8 = (f32[32,128]{1,0:T(8,128)S(1)}, f32[32,128]{1,0:T(8,128)S(1)}, u32[]{:S(2)}, u32[]{:S(2)}) collective-permute-start(f32[32,128]{1,0:T(8,128)S(1)} %get-tuple-element.48), channel_id=1, source_target_pairs={{0,64},{64,128},{128,192},{192,256},{256,320},{320,384},{384,448},... | collective-permute-start | bytes 49160 | tf_op jit(solution)/shard_map/ppermute | solution.py:912
  93.2 1.3 %collective-permute-start.9 = (f32[32,128]{1,0:T(8,128)S(1)}, f32[32,128]{1,0:T(8,128)S(1)}, u32[]{:S(2)}, u32[]{:S(2)}) collective-permute-start(f32[32,128]{1,0:T(8,128)S(1)} %get-tuple-element.49), channel_id=1, source_target_pairs={{64,0},{128,64},{192,128},{256,192},{320,256},{384,320},{448,384},... | collective-permute-start | bytes 49160 | tf_op jit(solution)/shard_map/ppermute | solution.py:912
  94.5 0.0 collective-permute-done.8.zlo
  94.5 3.2 %collective-permute-done.9.zhi = f32[32,128]{1,0:T(8,128)S(1)} collective-permute-done((f32[32,128]{1,0:T(8,128)S(1)}, f32[32,128]{1,0:T(8,128)S(1)}, u32[]{:S(2)}, u32[]{:S(2)}) %collective-permute-start.9) | collective-permute-done | bytes 16416 | tf_op jit(solution)/shard_map/ppermute | solution.py:912
  97.6 1.2 shard_map.104
  98.9 10.0 %all_to_all.41 = f32[8,1,128]{2,1,0:T(1,128)S(1)} all-to-all(f32[8,1,128]{2,1,0:T(1,128)S(1)} %bitcast.23), channel_id=1, replica_groups=mesh['gx'=8,'gy'=64] {'gx'}, dimensions={0} | all-to-all | bytes 8192 | tf_op jit(solution)/shard_map/all_to_all | solution.py:996
  109.0 17.7 %all_to_all.42 = f32[64,1,128]{2,1,0:T(1,128)S(1)} all-to-all(f32[64,1,128]{2,1,0:T(1,128)S(1)} %broadcast_in_dim.2), channel_id=1, replica_groups=mesh['gx'=8,'gy'=64] {'gy'}, dimensions={0} | all-to-all | bytes 65536 | tf_op jit(solution)/shard_map/all_to_all | solution.py:998
  126.6 0.8 shard_map.105
  (3 shorter events, 0.1 us)
Async XLA Ops:
  0.6 25.1 %copy-start.1 = (bf16[1008,384]{1,0:T(8,128)(2,1)S(1)}, bf16[1008,384]{1,0:T(8,128)(2,1)}, u32[]{:S(2)}) copy-start(bf16[1008,384]{1,0:T(8,128)(2,1)} %constant.30.clone.tables) | copy-start | bytes 2322436
  2.5 6.1 %collective-permute-start = (f32[3,32,128]{2,1,0:T(8,128)S(1)}, f32[3,32,128]{2,1,0:T(8,128)S(1)}, u32[]{:S(2)}, u32[]{:S(2)}) collective-permute-start(f32[3,32,128]{2,1,0:T(8,128)S(1)} %get-tuple-element.31), channel_id=1, source_target_pairs={{0,64},{64,128},{128,192},{192,256},{256,320},{320,384},{384,448},... | collective-permute-start | bytes 147464 | tf_op jit(solution)/shard_map/ppermute | solution.py:912
  7.3 5.5 %collective-permute-start.1 = (f32[3,32,128]{2,1,0:T(8,128)S(1)}, f32[3,32,128]{2,1,0:T(8,128)S(1)}, u32[]{:S(2)}, u32[]{:S(2)}) collective-permute-start(f32[3,32,128]{2,1,0:T(8,128)S(1)} %get-tuple-element.32), channel_id=1, source_target_pairs={{64,0},{128,64},{192,128},{256,192},{320,256},{384,320},{448,384},... | collective-permute-start | bytes 147464 | tf_op jit(solution)/shard_map/ppermute | solution.py:912
  12.8 8.5 %collective-permute-start.2 = (f32[12,48,128]{2,1,0:T(8,128)S(1)}, f32[12,48,128]{2,1,0:T(8,128)S(1)}, u32[]{:S(2)}, u32[]{:S(2)}) collective-permute-start(f32[12,48,128]{2,1,0:T(8,128)S(1)} %get-tuple-element.33), channel_id=1, source_target_pairs={{0,1},{1,2},{2,3},{3,4},{4,5},{5,6},{6,7},{7,8},{8,9},{9,10},{10,1... | collective-permute-start | bytes 884744 | tf_op jit(solution)/shard_map/ppermute | solution.py:912
  17.7 8.0 %collective-permute-start.3 = (f32[12,48,128]{2,1,0:T(8,128)S(1)}, f32[12,48,128]{2,1,0:T(8,128)S(1)}, u32[]{:S(2)}, u32[]{:S(2)}) collective-permute-start(f32[12,48,128]{2,1,0:T(8,128)S(1)} %get-tuple-element.34), channel_id=1, source_target_pairs={{1,0},{2,1},{3,2},{4,3},{5,4},{6,5},{7,6},{8,7},{9,8},{10,9},{11,1... | collective-permute-start | bytes 884744 | tf_op jit(solution)/shard_map/ppermute | solution.py:912
  20.0 15.0 %copy-start = (f32[544,128]{1,0:T(8,128)S(1)}, f32[544,128]{1,0:T(8,128)}, u32[]{:S(2)}) copy-start(f32[544,128]{1,0:T(8,128)} %constant.29.clone.packed_in.packed) | copy-start | bytes 835588
  25.7 1.3 copy-start.2
  29.7 6.8 %collective-permute-start.4 = (f32[64,128]{1,0:T(8,128)S(1)}, f32[64,128]{1,0:T(8,128)S(1)}, u32[]{:S(2)}, u32[]{:S(2)}) collective-permute-start(f32[64,128]{1,0:T(8,128)S(1)} %get-tuple-element.39), channel_id=1, source_target_pairs={{0,64},{64,128},{128,192},{192,256},{256,320},{320,384},{384,448},... | collective-permute-start | bytes 98312 | tf_op jit(solution)/shard_map/ppermute | solution.py:912
  33.7 6.5 %collective-permute-start.5 = (f32[64,128]{1,0:T(8,128)S(1)}, f32[64,128]{1,0:T(8,128)S(1)}, u32[]{:S(2)}, u32[]{:S(2)}) collective-permute-start(f32[64,128]{1,0:T(8,128)S(1)} %get-tuple-element.40), channel_id=1, source_target_pairs={{64,0},{128,64},{192,128},{256,192},{320,256},{384,320},{448,384},... | collective-permute-start | bytes 98312 | tf_op jit(solution)/shard_map/ppermute | solution.py:912
  36.5 52.6 %copy-start.3 = (f32[640,160]{1,0:T(8,128)S(1)}, f32[640,160]{1,0:T(8,128)}, u32[]{:S(2)}) copy-start(f32[640,160]{1,0:T(8,128)} %constant.32.clone.inv_den) | copy-start | bytes 1228804
  81.9 3.5 %collective-permute-start.6 = (f32[2,64,128]{2,1,0:T(8,128)S(1)}, f32[2,64,128]{2,1,0:T(8,128)S(1)}, u32[]{:S(2)}, u32[]{:S(2)}) collective-permute-start(f32[2,64,128]{2,1,0:T(8,128)S(1)} %get-tuple-element.45), channel_id=1, source_target_pairs={{0,64},{64,128},{128,192},{192,256},{256,320},{320,384},{384,448},... | collective-permute-start | bytes 196616 | tf_op jit(solution)/shard_map/ppermute | solution.py:912
  84.1 5.0 %collective-permute-start.7 = (f32[2,64,128]{2,1,0:T(8,128)S(1)}, f32[2,64,128]{2,1,0:T(8,128)S(1)}, u32[]{:S(2)}, u32[]{:S(2)}) collective-permute-start(f32[2,64,128]{2,1,0:T(8,128)S(1)} %get-tuple-element.46), channel_id=1, source_target_pairs={{64,0},{128,64},{192,128},{256,192},{320,256},{384,320},{448,384},... | collective-permute-start | bytes 196616 | tf_op jit(solution)/shard_map/ppermute | solution.py:912
  91.0 3.5 %collective-permute-start.8 = (f32[32,128]{1,0:T(8,128)S(1)}, f32[32,128]{1,0:T(8,128)S(1)}, u32[]{:S(2)}, u32[]{:S(2)}) collective-permute-start(f32[32,128]{1,0:T(8,128)S(1)} %get-tuple-element.48), channel_id=1, source_target_pairs={{0,64},{64,128},{128,192},{192,256},{256,320},{320,384},{384,448},... | collective-permute-start | bytes 49160 | tf_op jit(solution)/shard_map/ppermute | solution.py:912
  93.2 4.5 %collective-permute-start.9 = (f32[32,128]{1,0:T(8,128)S(1)}, f32[32,128]{1,0:T(8,128)S(1)}, u32[]{:S(2)}, u32[]{:S(2)}) collective-permute-start(f32[32,128]{1,0:T(8,128)S(1)} %get-tuple-element.49), channel_id=1, source_target_pairs={{64,0},{128,64},{192,128},{256,192},{320,256},{384,320},{448,384},... | collective-permute-start | bytes 49160 | tf_op jit(solution)/shard_map/ppermute | solution.py:912

commit v8 on v7

--- a/solution.py
+++ b/solution.py
@@ -169,15 +169,6 @@
 FX = FX[:, :LANES]
 
 
-def denominators(step):
-    lam_y = np.tile(EIGEN, step // 10)
-    lam_x = np.tile(EIGEN, EX)
-    total = EIGEN[:, None, None] + lam_y[None, :, None] + lam_x[None, None, :]
-    inverse = 1.0 / (SCHWARZ_SCALE * total + SCHWARZ_SHIFT)
-    inverse = np.pad(inverse, ((0, 0), (0, step - inverse.shape[1]), (0, 0)))
-    return inverse.reshape(10 * step, 10 * EX).astype(np.float32)
-
-
 FX_H, FX_L = split_const(FX.T.copy())
 BX_H, BX_L = split_const(BX.T.copy())
 
@@ -210,8 +201,6 @@
         wide_const(BY_B),
     ]
 )
-DEN_A = denominators(STEP_A)
-DEN_B = denominators(STEP_B)
 
 
 def roll_table():
@@ -244,6 +233,10 @@
 AT_SQUARE = AT_DXT + LANES
 AT_MASS = AT_SQUARE + 16
 AT_SPREAD = AT_MASS + WIDE
+AT_EIGEN_Y = AT_SPREAD + EX
+AT_EIGEN_X = AT_EIGEN_Y + STEP_A
+LAM_Y = np.resize(EIGEN, STEP_A)
+LAM_X = np.resize(EIGEN, 8 * LANES).reshape(8, LANES)
 PACKED = np.concatenate(
     [
         WY[:, None] * WX[None, :],
@@ -254,6 +247,8 @@
         np.repeat(DERIV[:, 7:] ** 2, LANES, axis=1),
         INV_MASS,
         np.kron(np.eye(EX), np.ones((1, 8))),
+        np.repeat(LAM_Y[:, None], LANES, axis=1),
+        LAM_X,
     ]
 ).astype(np.float32)
 
@@ -339,7 +334,7 @@
     return stack(planes)
 
 
-def solve_elements(planes, inv_den, tables, kind):
+def solve_elements(planes, packed, tables, kind):
     def table(index):
         at, rows, width = PLACES[index]
         return tables[at : at + rows, 0:width]
@@ -348,9 +343,23 @@
     spectral = left_pairs(table(4 + 2 * kind), along_z(planes, FZ))
     high, low = parts(jnp.concatenate(spectral, axis=0))
     wide = dot(jnp.concatenate([high, low], axis=1), fxhh) + dot(high, fxl)
-    high, low = parts(wide * inv_den[...])
+    step = PLACES[4 + 2 * kind][1]
+    column = packed[AT_EIGEN_Y : AT_EIGEN_Y + step]
+    rest = 10 * EX - LANES
+    lam = jnp.concatenate(
+        [
+            column + packed[AT_EIGEN_X : AT_EIGEN_X + 1],
+            column[:, 0:rest] + packed[AT_EIGEN_X + 1 : AT_EIGEN_X + 2, 0:rest],
+        ],
+        axis=1,
+    )
+    scaled = [
+        wide[step * i : step * (i + 1)]
+        / (SCHWARZ_SCALE * lam + float(SCHWARZ_SCALE * EIGEN[i] + SCHWARZ_SHIFT))
+        for i in range(10)
+    ]
+    high, low = parts(jnp.concatenate(scaled, axis=0))
     back = dot(high, bxh) + dot(low, bxh) + dot(high, bxl)
-    step = PLACES[4 + 2 * kind][1]
     back = left_pairs(table(5 + 2 * kind), [back[step * i : step * (i + 1)] for i in range(10)])
     return along_z(back, BZ)
 
@@ -541,13 +550,13 @@
 
 
 def first_schwarz_kernel(
-    near, inv_den, tables, b, zlo, zhi, ylo, yhi, w_ref, wlo, whi
+    near, packed, tables, b, zlo, zhi, ylo, yhi, w_ref, wlo, whi
 ):
     own = [b[i] for i in range(8)] + [zlo[0], zlo[1], zhi[0], zhi[1]]
     planes = [
         jnp.concatenate([ylo[i, 0:TILE_B], own[i], yhi[i, 0:TILE_B]], axis=0) for i in range(12)
     ]
-    planes = solve_elements(planes, inv_den, tables, 0)
+    planes = solve_elements(planes, packed, tables, 0)
     row, has_low, has_high = ring_rows(near)
     in_grid = jnp.where(row < RING, has_low, jnp.where(row >= RING + ROWS, has_high, 1.0))
     in_grid = jnp.where(row == RING, has_low, jnp.where(row == RING + ROWS - 1, has_high, in_grid))
@@ -559,9 +568,9 @@
     store_faces(planes, near, w_ref, wlo, whi)
 
 
-def second_schwarz_kernel(near, inv_den, tables, y, zlo, zhi, w_ref, wlo, whi):
+def second_schwarz_kernel(near, packed, tables, y, zlo, zhi, w_ref, wlo, whi):
     planes = [y[i] for i in range(8)] + [zlo[0], zlo[1], zhi[0], zhi[1]]
-    planes = solve_elements(planes, inv_den, tables, 1)
+    planes = solve_elements(planes, packed, tables, 1)
     row = lax.broadcasted_iota(jnp.int32, (ROWS, LANES), 0)
     _, has_low, has_high = ring_rows(near)
     in_grid = jnp.where(row == 0, has_low, jnp.where(row == ROWS - 1, has_high, 1.0))
@@ -739,49 +748,39 @@
     back_z = move(link_z, -1, 0)
     back_y = move(link_y, 0, -1)
     diagonal = HELM_COEF * EZ * EY * EX + link_z + back_z + link_y + back_y
-    half = lanes // 2
-    low_half = lane < half
-
-    def twice(array):
-        return jnp.where(low_half, array, pltpu.roll(array, half, 1))
-
-    def swap(array):
-        return pltpu.roll(array, half, 1)
-
-    def beside_rows(rows, distance):
-        return [
-            jnp.where(low_half, pltpu.roll(row, distance, 1), pltpu.roll(row, lanes - distance, 1))
-            for row in rows
-        ]
-
-    diagonal, link_z, back_z = twice(diagonal), twice(link_z), twice(back_z)
-    link = jnp.where(low_half, back_y, swap(link_y))
-    blocks, sides = [], []
+    blocks, lower, upper = [], [], []
     for r in range(8):
         row = jnp.where(sub == r, diagonal, 0.0)
         row = jnp.where(sub == r + 1, -back_z, row)
         row = jnp.where(sub == r - 1, -link_z, row)
         blocks.append(row)
-        sides.append(jnp.where(sub == r, -link, 0.0))
+        lower.append(jnp.where(sub == r, -back_y, 0.0))
+        upper.append(jnp.where(sub == r, -link_y, 0.0))
     levels = []
     step = 1
     while step < count:
-        factors = multiply(sides, beside_rows(invert(blocks, sub), step))
-        levels.append((step, factors))
-        terms = multiply(factors, beside_rows([swap(row) for row in sides], step))
-        blocks = [blocks[r] - terms[r] - swap(terms[r]) for r in range(8)]
+        inverse = invert(blocks, sub)
+        down = multiply(lower, [move(row, 0, -step) for row in inverse])
+        up = multiply(upper, [move(row, 0, step) for row in inverse])
+        levels.append((step, down, up))
+        before_u = multiply(down, [move(row, 0, -step) for row in upper])
+        after_l = multiply(up, [move(row, 0, step) for row in lower])
         if 2 * step < count:
-            sides = [-row for row in multiply(factors, beside_rows(sides, step))]
+            new_lower = multiply(down, [move(row, 0, -step) for row in lower])
+            new_upper = multiply(up, [move(row, 0, step) for row in upper])
+            lower = [-row for row in new_lower]
+            upper = [-row for row in new_upper]
+        blocks = [blocks[r] - before_u[r] - after_l[r] for r in range(8)]
         step *= 2
     inverse = invert(blocks, sub)
 
     def solve(column):
-        column = twice(column)
-        for distance, factors in levels:
-            pulled = matvec([(factors, beside_rows([column], distance)[0])], sub)
-            column = column - pulled - swap(pulled)
-        solved = matvec([(inverse, column)], sub)
-        return jnp.where(lane < count, solved, 0.0)
+        for distance, down, up in levels:
+            pulled = matvec(
+                [(down, move(column, 0, -distance)), (up, move(column, 0, distance))], sub
+            )
+            column = column - pulled
+        return matvec([(inverse, column)], sub)
 
     offsets = [(a - 1, b - 1) for a in range(3) for b in range(3)]
     first = solve(value(1))
@@ -950,7 +949,7 @@
         first_schwarz_kernel,
         [wide_block, wide_face, wide_face],
         [near],
-        [jnp.asarray(DEN_A), tables, b, zlo, zhi, ylo, yhi],
+        [packed, tables, b, zlo, zhi, ylo, yhi],
     )
     wlo, whi = shift("gx", wlo, whi)
     level_new, flux, stat = run(
@@ -984,7 +983,7 @@
     )
     zlo, zhi = shift("gx", zlo, zhi)
     w, wlo, whi = run(
-        second_schwarz_kernel, [block, face, face], [near], [jnp.asarray(DEN_B), tables, y, zlo, zhi]
+        second_schwarz_kernel, [block, face, face], [near], [packed, tables, y, zlo, zhi]
     )
     zlo, zhi = shift("gx", wlo, whi)
     q, sums = run(

time: 128 us -> 126 us (0.984)
  no operation moved by 1% of the time
where the time goes in v8:
time: 126 us; the launch traced here: 125 us
  blocking collectives  62.1 us (49%)
  starting transfers between devices  25.6 us (20%)
  waiting for transfers between devices  20.5 us (16%)
  Pallas kernels  16.4 us (13%)
    all_to_all x1, blocking collectives, body(): gathered = lax.all_to_all(column, 'gy', 0, 0, tiled=True)  21.7 us
    ppermute x5, waiting for transfers between devices, shift(): lax.ppermute(low_face, axis, backward)  19.1 us
    ppermute x5, starting transfers between devices, shift(): lax.ppermute(high_face, axis, forward)  18.2 us
    all_to_all x1, blocking collectives, body(): wide = lax.all_to_all(wide, 'gy', 0, 0, tiled=True)  17.6 us
    pallas_call x11, Pallas kernels, run(): pl.pallas_call(kernel, out_shape=[jax.ShapeDtypeStruct(out, F32) for out...  16.4 us
    all_to_all x1, blocking collectives, body(): gathered = lax.all_to_all(stat, 'gx', 0, 0, tiled=True)  12.7 us
    all_to_all x1, blocking collectives, body(): tile = lax.all_to_all(sums, 'gx', 0, 0, tiled=True)  10 us
    ppermute x5, starting transfers between devices, shift(): lax.ppermute(low_face, axis, backward)  7.4 us
  transfers between devices with their start and end apart: 10, of which 6 were waited for; matrix products, arithmetic and copies ran while one was open for 0% of the time, Pallas kernels for 1%

profile of v8, /device:TPU:1, one launch (start us, length us, event | category | flops | bytes accessed | tf_op | source)
XLA Modules:
  0.0 125.5 jit_solution(14309062489653536501)
XLA Ops:
  0.6 0.0 copy-start.1
  0.6 1.8 %shard_map.77 = (f32[8,32,128]{2,1,0:T(8,128)S(1)}, f32[8,32,128]{2,1,0:T(8,128)S(1)}, f32[3,32,128]{2,1,0:T(8,128)S(1)}, f32[3,32,128]{2,1,0:T(8,128)S(1)}, f32[8,128]{1,0:T(8,128)S(1)}) custom-call(f32[8,32,128]{2,1,0:T(8,128)} %lev_in.1, f32[3,8,32,128]{3,2,1,0:T(8,128)} %vel_in.1, f32[8,32,128]{2,1,0:T(8,128)} %src_in.1, ...), custom_call_target="tpu_custom_call" | custom-call | flops 1000000 | bytes 729088 | tf_op jit(solution)/shard_map/pallas_call | solution.py:895
  2.5 0.0 copy-start
  2.5 5.0 %collective-permute-start = (f32[3,32,128]{2,1,0:T(8,128)S(1)}, f32[3,32,128]{2,1,0:T(8,128)S(1)}, u32[]{:S(2)}, u32[]{:S(2)}) collective-permute-start(f32[3,32,128]{2,1,0:T(8,128)S(1)} %get-tuple-element.31), channel_id=1, source_target_pairs={{0,64},{64,128},{128,192},{192,256},{256,320},{320,384},{384,448},... | collective-permute-start | bytes 147464 | tf_op jit(solution)/shard_map/ppermute | solution.py:911
  7.5 1.3 %collective-permute-start.1 = (f32[3,32,128]{2,1,0:T(8,128)S(1)}, f32[3,32,128]{2,1,0:T(8,128)S(1)}, u32[]{:S(2)}, u32[]{:S(2)}) collective-permute-start(f32[3,32,128]{2,1,0:T(8,128)S(1)} %get-tuple-element.32), channel_id=1, source_target_pairs={{64,0},{128,64},{192,128},{256,192},{320,256},{384,320},{448,384},... | collective-permute-start | bytes 147464 | tf_op jit(solution)/shard_map/ppermute | solution.py:911
  8.8 0.0 collective-permute-done.low_z.zlo
  8.8 4.2 %collective-permute-done.1.high_z.zhi = f32[3,32,128]{2,1,0:T(8,128)S(1)} collective-permute-done((f32[3,32,128]{2,1,0:T(8,128)S(1)}, f32[3,32,128]{2,1,0:T(8,128)S(1)}, u32[]{:S(2)}, u32[]{:S(2)}) %collective-permute-start.1) | collective-permute-done | bytes 49184 | tf_op jit(solution)/shard_map/ppermute | solution.py:911
  13.0 4.8 %collective-permute-start.2 = (f32[12,48,128]{2,1,0:T(8,128)S(1)}, f32[12,48,128]{2,1,0:T(8,128)S(1)}, u32[]{:S(2)}, u32[]{:S(2)}) collective-permute-start(f32[12,48,128]{2,1,0:T(8,128)S(1)} %get-tuple-element.33), channel_id=1, source_target_pairs={{0,1},{1,2},{2,3},{3,4},{4,5},{5,6},{6,7},{7,8},{8,9},{9,10},{10,1... | collective-permute-start | bytes 884744 | tf_op jit(solution)/shard_map/ppermute | solution.py:911
  17.8 2.2 %collective-permute-start.3 = (f32[12,48,128]{2,1,0:T(8,128)S(1)}, f32[12,48,128]{2,1,0:T(8,128)S(1)}, u32[]{:S(2)}, u32[]{:S(2)}) collective-permute-start(f32[12,48,128]{2,1,0:T(8,128)S(1)} %get-tuple-element.34), channel_id=1, source_target_pairs={{1,0},{2,1},{3,2},{4,3},{5,4},{6,5},{7,6},{8,7},{9,8},{10,9},{11,1... | collective-permute-start | bytes 884744 | tf_op jit(solution)/shard_map/ppermute | solution.py:911
  20.1 0.1 stack.27.near
  20.2 1.3 %collective-permute-done.2.ylo = f32[12,48,128]{2,1,0:T(8,128)S(1)} collective-permute-done((f32[12,48,128]{2,1,0:T(8,128)S(1)}, f32[12,48,128]{2,1,0:T(8,128)S(1)}, u32[]{:S(2)}, u32[]{:S(2)}) %collective-permute-start.2) | collective-permute-done | bytes 294944 | tf_op jit(solution)/shard_map/ppermute | solution.py:911
  21.5 4.4 %collective-permute-done.3.yhi = f32[12,48,128]{2,1,0:T(8,128)S(1)} collective-permute-done((f32[12,48,128]{2,1,0:T(8,128)S(1)}, f32[12,48,128]{2,1,0:T(8,128)S(1)}, u32[]{:S(2)}, u32[]{:S(2)}) %collective-permute-start.3) | collective-permute-done | bytes 294944 | tf_op jit(solution)/shard_map/ppermute | solution.py:911
  25.9 0.0 copy-done.1
  25.9 0.0 copy-done
  25.9 2.7 %shard_map.80 = (f32[8,64,128]{2,1,0:T(8,128)S(1)}, f32[64,128]{1,0:T(8,128)S(1)}, f32[64,128]{1,0:T(8,128)S(1)}) custom-call(f32[6]{0:T(128)S(1)} %stack.27.near, f32[664,128]{1,0:T(8,128)S(1)} %copy-done, bf16[1008,384]{1,0:T(8,128)(2,1)S(1)} %copy-done.1, f32[8,32,128]{2,1,0:T(8,128)S(1)} %get-tuple-element.29.b, ...), custom_call_target="tpu_custom_call" | custom-call | flops 1000000 | bytes 655360 | tf_op jit(solution)/shard_map/pallas_call | solution.py:895
  28.6 4.0 %collective-permute-start.4 = (f32[64,128]{1,0:T(8,128)S(1)}, f32[64,128]{1,0:T(8,128)S(1)}, u32[]{:S(2)}, u32[]{:S(2)}) collective-permute-start(f32[64,128]{1,0:T(8,128)S(1)} %get-tuple-element.39), channel_id=1, source_target_pairs={{0,64},{64,128},{128,192},{192,256},{256,320},{320,384},{384,448},... | collective-permute-start | bytes 98312 | tf_op jit(solution)/shard_map/ppermute | solution.py:911
  32.6 1.3 %collective-permute-start.5 = (f32[64,128]{1,0:T(8,128)S(1)}, f32[64,128]{1,0:T(8,128)S(1)}, u32[]{:S(2)}, u32[]{:S(2)}) collective-permute-start(f32[64,128]{1,0:T(8,128)S(1)} %get-tuple-element.40), channel_id=1, source_target_pairs={{64,0},{128,64},{192,128},{256,192},{320,256},{384,320},{448,384},... | collective-permute-start | bytes 98312 | tf_op jit(solution)/shard_map/ppermute | solution.py:911
  33.9 1.5 %shard_map.79 = (f32[8,32,128]{2,1,0:T(8,128)}, f32[8,64,128]{2,1,0:T(8,128)S(1)}, f32[1,128]{1,0:T(1,128)S(1)}) custom-call(f32[6]{0:T(128)S(1)} %stack.27.near, f32[8,128]{1,0:T(8,128)S(1)} %get-tuple-element.28.solid, f32[664,128]{1,0:T(8,128)S(1)} %copy-done, f32[8,32,128]{2,1,0:T(8,128)S(1)} %get-tuple-element.29.b, ...), custom_call_target="tpu_custom_call" | custom-call | flops 20000000 | bytes 787456 | tf_op jit(solution)/shard_map/pallas_call | solution.py:895
  35.4 0.0 collective-permute-done.4.zlo
  35.4 3.7 %collective-permute-done.5.zhi = f32[64,128]{1,0:T(8,128)S(1)} collective-permute-done((f32[64,128]{1,0:T(8,128)S(1)}, f32[64,128]{1,0:T(8,128)S(1)}, u32[]{:S(2)}, u32[]{:S(2)}) %collective-permute-start.5) | collective-permute-done | bytes 32800 | tf_op jit(solution)/shard_map/ppermute | solution.py:911
  39.1 1.6 %shard_map.81 = (f32[8,64,128]{2,1,0:T(8,128)S(1)}, f32[8,64,128]{2,1,0:T(8,128)S(1)}, f32[8,128]{1,0:T(8,128)S(1)}) custom-call(f32[6]{0:T(128)S(1)} %stack.27.near, f32[664,128]{1,0:T(8,128)S(1)} %copy-done, f32[1,128]{1,0:T(1,128)S(1)} %get-tuple-element.36.stat_in, f32[8,64,128]{2,1,0:T(8,128)S(1)} %get-tuple-element.37.flux, ...), custom_call_target="tpu_custom_call" | custom-call | flops 1000000 | bytes 1056768 | tf_op jit(solution)/shard_map/pallas_call | solution.py:895
  40.8 12.7 %all_to_all.39 = f32[8,1,128]{2,1,0:T(1,128)S(1)} all-to-all(f32[8,1,128]{2,1,0:T(1,128)S(1)} %bitcast.24), channel_id=1, replica_groups=mesh['gx'=8,'gy'=64] {'gx'}, dimensions={0} | all-to-all | bytes 8192 | tf_op jit(solution)/shard_map/all_to_all | solution.py:968
  53.4 0.3 shard_map.82
  53.7 21.7 %all_to_all.40 = f32[64,1,128]{2,1,0:T(1,128)S(1)} all-to-all(f32[64,1,128]{2,1,0:T(1,128)S(1)} %bitcast.19), channel_id=1, replica_groups=mesh['gx'=8,'gy'=64] {'gy'}, dimensions={0} | all-to-all | bytes 65536 | tf_op jit(solution)/shard_map/all_to_all | solution.py:970
  75.4 3.3 %shard_map.83.coarse = f32[32,128]{1,0:T(8,128)S(1)} custom-call(f32[6]{0:T(128)S(1)} %stack.27.near, f32[64,128]{1,0:T(8,128)S(1)} %bitcast.20), custom_call_target="tpu_custom_call" | custom-call | flops 1000000 | bytes 32768 | tf_op jit(solution)/shard_map/pallas_call | solution.py:895
  78.7 1.2 shard_map.84
  79.9 2.2 %collective-permute-start.6 = (f32[2,64,128]{2,1,0:T(8,128)S(1)}, f32[2,64,128]{2,1,0:T(8,128)S(1)}, u32[]{:S(2)}, u32[]{:S(2)}) collective-permute-start(f32[2,64,128]{2,1,0:T(8,128)S(1)} %get-tuple-element.45), channel_id=1, source_target_pairs={{0,64},{64,128},{128,192},{192,256},{256,320},{320,384},{384,448},... | collective-permute-start | bytes 196616 | tf_op jit(solution)/shard_map/ppermute | solution.py:911
  82.1 1.3 %collective-permute-start.7 = (f32[2,64,128]{2,1,0:T(8,128)S(1)}, f32[2,64,128]{2,1,0:T(8,128)S(1)}, u32[]{:S(2)}, u32[]{:S(2)}) collective-permute-start(f32[2,64,128]{2,1,0:T(8,128)S(1)} %get-tuple-element.46), channel_id=1, source_target_pairs={{64,0},{128,64},{192,128},{256,192},{320,256},{384,320},{448,384},... | collective-permute-start | bytes 196616 | tf_op jit(solution)/shard_map/ppermute | solution.py:911
  83.4 0.0 collective-permute-done.6.zlo
  83.4 3.7 %collective-permute-done.7.zhi = f32[2,64,128]{2,1,0:T(8,128)S(1)} collective-permute-done((f32[2,64,128]{2,1,0:T(8,128)S(1)}, f32[2,64,128]{2,1,0:T(8,128)S(1)}, u32[]{:S(2)}, u32[]{:S(2)}) %collective-permute-start.7) | collective-permute-done | bytes 65568 | tf_op jit(solution)/shard_map/ppermute | solution.py:911
  87.1 1.9 %shard_map.85 = (f32[8,32,128]{2,1,0:T(8,128)S(1)}, f32[32,128]{1,0:T(8,128)S(1)}, f32[32,128]{1,0:T(8,128)S(1)}) custom-call(f32[6]{0:T(128)S(1)} %stack.27.near, f32[664,128]{1,0:T(8,128)S(1)} %copy-done, bf16[1008,384]{1,0:T(8,128)(2,1)S(1)} %copy-done.1, f32[8,64,128]{2,1,0:T(8,128)S(1)} %get-tuple-element.44.y, ...), custom_call_target="tpu_custom_call" | custom-call | flops 1000000 | bytes 327680 | tf_op jit(solution)/shard_map/pallas_call | solution.py:895
  89.0 2.2 %collective-permute-start.8 = (f32[32,128]{1,0:T(8,128)S(1)}, f32[32,128]{1,0:T(8,128)S(1)}, u32[]{:S(2)}, u32[]{:S(2)}) collective-permute-start(f32[32,128]{1,0:T(8,128)S(1)} %get-tuple-element.48), channel_id=1, source_target_pairs={{0,64},{64,128},{128,192},{192,256},{256,320},{320,384},{384,448},... | collective-permute-start | bytes 49160 | tf_op jit(solution)/shard_map/ppermute | solution.py:911
  91.2 1.3 %collective-permute-start.9 = (f32[32,128]{1,0:T(8,128)S(1)}, f32[32,128]{1,0:T(8,128)S(1)}, u32[]{:S(2)}, u32[]{:S(2)}) collective-permute-start(f32[32,128]{1,0:T(8,128)S(1)} %get-tuple-element.49), channel_id=1, source_target_pairs={{64,0},{128,64},{192,128},{256,192},{320,256},{384,320},{448,384},... | collective-permute-start | bytes 49160 | tf_op jit(solution)/shard_map/ppermute | solution.py:911
  92.5 0.0 collective-permute-done.8.zlo
  92.5 3.2 %collective-permute-done.9.zhi = f32[32,128]{1,0:T(8,128)S(1)} collective-permute-done((f32[32,128]{1,0:T(8,128)S(1)}, f32[32,128]{1,0:T(8,128)S(1)}, u32[]{:S(2)}, u32[]{:S(2)}) %collective-permute-start.9) | collective-permute-done | bytes 16416 | tf_op jit(solution)/shard_map/ppermute | solution.py:911
  95.7 1.2 shard_map.86
  96.9 10.0 %all_to_all.41 = f32[8,1,128]{2,1,0:T(1,128)S(1)} all-to-all(f32[8,1,128]{2,1,0:T(1,128)S(1)} %bitcast.23), channel_id=1, replica_groups=mesh['gx'=8,'gy'=64] {'gx'}, dimensions={0} | all-to-all | bytes 8192 | tf_op jit(solution)/shard_map/all_to_all | solution.py:995
  107.0 17.6 %all_to_all.42 = f32[64,1,128]{2,1,0:T(1,128)S(1)} all-to-all(f32[64,1,128]{2,1,0:T(1,128)S(1)} %broadcast_in_dim.2), channel_id=1, replica_groups=mesh['gx'=8,'gy'=64] {'gy'}, dimensions={0} | all-to-all | bytes 65536 | tf_op jit(solution)/shard_map/all_to_all | solution.py:997
  124.6 0.8 shard_map.87
  (3 shorter events, 0.1 us)
Async XLA Ops:
  0.6 25.2 %copy-start.1 = (bf16[1008,384]{1,0:T(8,128)(2,1)S(1)}, bf16[1008,384]{1,0:T(8,128)(2,1)}, u32[]{:S(2)}) copy-start(bf16[1008,384]{1,0:T(8,128)(2,1)} %constant.26.clone.tables) | copy-start | bytes 2322436
  2.5 23.4 %copy-start = (f32[664,128]{1,0:T(8,128)S(1)}, f32[664,128]{1,0:T(8,128)}, u32[]{:S(2)}) copy-start(f32[664,128]{1,0:T(8,128)} %constant.25.clone.packed_in.packed) | copy-start | bytes 1019908
  2.5 6.3 %collective-permute-start = (f32[3,32,128]{2,1,0:T(8,128)S(1)}, f32[3,32,128]{2,1,0:T(8,128)S(1)}, u32[]{:S(2)}, u32[]{:S(2)}) collective-permute-start(f32[3,32,128]{2,1,0:T(8,128)S(1)} %get-tuple-element.31), channel_id=1, source_target_pairs={{0,64},{64,128},{128,192},{192,256},{256,320},{320,384},{384,448},... | collective-permute-start | bytes 147464 | tf_op jit(solution)/shard_map/ppermute | solution.py:911
  7.5 5.5 %collective-permute-start.1 = (f32[3,32,128]{2,1,0:T(8,128)S(1)}, f32[3,32,128]{2,1,0:T(8,128)S(1)}, u32[]{:S(2)}, u32[]{:S(2)}) collective-permute-start(f32[3,32,128]{2,1,0:T(8,128)S(1)} %get-tuple-element.32), channel_id=1, source_target_pairs={{64,0},{128,64},{192,128},{256,192},{320,256},{384,320},{448,384},... | collective-permute-start | bytes 147464 | tf_op jit(solution)/shard_map/ppermute | solution.py:911
  13.0 8.5 %collective-permute-start.2 = (f32[12,48,128]{2,1,0:T(8,128)S(1)}, f32[12,48,128]{2,1,0:T(8,128)S(1)}, u32[]{:S(2)}, u32[]{:S(2)}) collective-permute-start(f32[12,48,128]{2,1,0:T(8,128)S(1)} %get-tuple-element.33), channel_id=1, source_target_pairs={{0,1},{1,2},{2,3},{3,4},{4,5},{5,6},{6,7},{7,8},{8,9},{9,10},{10,1... | collective-permute-start | bytes 884744 | tf_op jit(solution)/shard_map/ppermute | solution.py:911
  17.8 8.0 %collective-permute-start.3 = (f32[12,48,128]{2,1,0:T(8,128)S(1)}, f32[12,48,128]{2,1,0:T(8,128)S(1)}, u32[]{:S(2)}, u32[]{:S(2)}) collective-permute-start(f32[12,48,128]{2,1,0:T(8,128)S(1)} %get-tuple-element.34), channel_id=1, source_target_pairs={{1,0},{2,1},{3,2},{4,3},{5,4},{6,5},{7,6},{8,7},{9,8},{10,9},{11,1... | collective-permute-start | bytes 884744 | tf_op jit(solution)/shard_map/ppermute | solution.py:911
  28.6 6.8 %collective-permute-start.4 = (f32[64,128]{1,0:T(8,128)S(1)}, f32[64,128]{1,0:T(8,128)S(1)}, u32[]{:S(2)}, u32[]{:S(2)}) collective-permute-start(f32[64,128]{1,0:T(8,128)S(1)} %get-tuple-element.39), channel_id=1, source_target_pairs={{0,64},{64,128},{128,192},{192,256},{256,320},{320,384},{384,448},... | collective-permute-start | bytes 98312 | tf_op jit(solution)/shard_map/ppermute | solution.py:911
  32.6 6.5 %collective-permute-start.5 = (f32[64,128]{1,0:T(8,128)S(1)}, f32[64,128]{1,0:T(8,128)S(1)}, u32[]{:S(2)}, u32[]{:S(2)}) collective-permute-start(f32[64,128]{1,0:T(8,128)S(1)} %get-tuple-element.40), channel_id=1, source_target_pairs={{64,0},{128,64},{192,128},{256,192},{320,256},{384,320},{448,384},... | collective-permute-start | bytes 98312 | tf_op jit(solution)/shard_map/ppermute | solution.py:911
  79.9 3.5 %collective-permute-start.6 = (f32[2,64,128]{2,1,0:T(8,128)S(1)}, f32[2,64,128]{2,1,0:T(8,128)S(1)}, u32[]{:S(2)}, u32[]{:S(2)}) collective-permute-start(f32[2,64,128]{2,1,0:T(8,128)S(1)} %get-tuple-element.45), channel_id=1, source_target_pairs={{0,64},{64,128},{128,192},{192,256},{256,320},{320,384},{384,448},... | collective-permute-start | bytes 196616 | tf_op jit(solution)/shard_map/ppermute | solution.py:911
  82.1 5.0 %collective-permute-start.7 = (f32[2,64,128]{2,1,0:T(8,128)S(1)}, f32[2,64,128]{2,1,0:T(8,128)S(1)}, u32[]{:S(2)}, u32[]{:S(2)}) collective-permute-start(f32[2,64,128]{2,1,0:T(8,128)S(1)} %get-tuple-element.46), channel_id=1, source_target_pairs={{64,0},{128,64},{192,128},{256,192},{320,256},{384,320},{448,384},... | collective-permute-start | bytes 196616 | tf_op jit(solution)/shard_map/ppermute | solution.py:911
  89.0 3.5 %collective-permute-start.8 = (f32[32,128]{1,0:T(8,128)S(1)}, f32[32,128]{1,0:T(8,128)S(1)}, u32[]{:S(2)}, u32[]{:S(2)}) collective-permute-start(f32[32,128]{1,0:T(8,128)S(1)} %get-tuple-element.48), channel_id=1, source_target_pairs={{0,64},{64,128},{128,192},{192,256},{256,320},{320,384},{384,448},... | collective-permute-start | bytes 49160 | tf_op jit(solution)/shard_map/ppermute | solution.py:911
  91.2 4.5 %collective-permute-start.9 = (f32[32,128]{1,0:T(8,128)S(1)}, f32[32,128]{1,0:T(8,128)S(1)}, u32[]{:S(2)}, u32[]{:S(2)}) collective-permute-start(f32[32,128]{1,0:T(8,128)S(1)} %get-tuple-element.49), channel_id=1, source_target_pairs={{64,0},{128,64},{192,128},{256,192},{320,256},{384,320},{448,384},... | collective-permute-start | bytes 49160 | tf_op jit(solution)/shard_map/ppermute | solution.py:911

commit v9 on v8

--- a/solution.py
+++ b/solution.py
@@ -568,25 +568,18 @@
     store_faces(planes, near, w_ref, wlo, whi)
 
 
-def second_schwarz_kernel(near, packed, tables, y, zlo, zhi, w_ref, wlo, whi):
-    planes = [y[i] for i in range(8)] + [zlo[0], zlo[1], zhi[0], zhi[1]]
-    planes = solve_elements(planes, packed, tables, 1)
-    row = lax.broadcasted_iota(jnp.int32, (ROWS, LANES), 0)
-    _, has_low, has_high = ring_rows(near)
-    in_grid = jnp.where(row == 0, has_low, jnp.where(row == ROWS - 1, has_high, 1.0))
-    for i in range(8):
-        first = (1.0 - has_low) * planes[i][ROWS : ROWS + 1]
-        last = (1.0 - has_high) * planes[i][ROWS + 1 : ROWS + 2]
-        alone = jnp.where(row == 0, first, jnp.where(row == ROWS - 1, last, 0.0))
-        planes[i] = planes[i][0:ROWS] * in_grid + alone
-    store_faces(planes, near, w_ref, wlo, whi)
-
-
-def galerkin_kernel(near, packed, stat_in, flux, w, zlo, zhi, zl_ref, y_ref, stat):
+def galerkin_kernel(near, packed, stat_in, flux, w, zlo, zhi, zl_ref, y_ref, ylo, yhi, stat):
     local = add_planes(w, zlo[...], zhi[...])
     zl_ref[...] = local
     applied = local_operator(local, flux[...], packed)
     y_ref[...] = applied
+    fluxes = [flux[i] for i in range(8)]
+    for out, rows in ((ylo, (0, 1)), (yhi, (6, 7))):
+        for k, i in enumerate(rows):
+            out[k] = applied[i]
+            for t, end in enumerate((0, 7)):
+                out[2 + 2 * t + k] = along_z(fluxes, (DERIV[:, i] * DERIV[:, end])[None, :])[0]
+            out[6 + k] = fluxes[i]
     applied = applied[:, RING : RING + ROWS]
     inner = near[0] * applied[0] + near[1] * applied[7]
     for i in range(1, 7):
@@ -782,9 +775,7 @@
             column = column - pulled
         return matvec([(inverse, column)], sub)
 
-    offsets = [(a - 1, b - 1) for a in range(3) for b in range(3)]
     first = solve(value(1))
-    near_first = [move(first, dz, dy) for dz, dy in offsets]
     totals = coarse_operator(
         first,
         count,
@@ -798,16 +789,20 @@
     totals = totals + jnp.where(lane > 0, move(value(4), 0, -1), 0.0)
     totals = jnp.where(lane < count, totals, 0.0)
     second = solve(totals)
-    near_second = [move(second, dz, dy) for dz, dy in offsets]
     mine = (sub.astype(F32) == near[4]) & (lane.astype(F32) == near[5])
-    for d in range(9):
-        out_ref[d : d + 1] = jnp.full((1, lanes), jnp.sum(jnp.where(mine, near_first[d], 0.0)))
-        out_ref[16 + d : 17 + d] = jnp.full(
-            (1, lanes), jnp.sum(jnp.where(mine, near_second[d], 0.0))
-        )
-
-
-def coarse_columns(near, coarse, start):
+
+    def store(at, solved, reach):
+        for a in range(-reach, reach + 1):
+            for b in range(-1, 2):
+                picked = jnp.sum(jnp.where(mine, move(solved, a, b), 0.0))
+                row = at + 3 * (a + reach) + b + 1
+                out_ref[row : row + 1] = jnp.full((1, lanes), picked)
+
+    store(0, first, 2)
+    store(16, second, 1)
+
+
+def coarse_columns(near, coarse, start, count):
     row, has_low, has_high = ring_rows(near)
     below = jnp.where(row < RING - 1, 1.0, jnp.where(row <= RING, 0.5, 0.0)) * has_low
     above = jnp.where(row > RING + ROWS, 1.0, jnp.where(row >= RING + ROWS - 1, 0.5, 0.0)) * has_high
@@ -816,14 +811,17 @@
     edge = jnp.where(row == RING - 1, 0.5 * has_low, edge)
     edge = jnp.where(row == RING + ROWS, 0.5 * has_high, edge)
     columns = []
-    for a in range(3):
+    for a in range(count):
         at = start + 3 * a
         columns.append(
             below * coarse[at : at + 1] + edge * coarse[at + 1 : at + 2] + above * coarse[at + 2 : at + 3]
         )
-    first = (1.0 - near[0]) * (columns[0] - columns[1])
-    last = (1.0 - near[1]) * (columns[2] - columns[1])
-    return columns[1], first, last
+    return columns
+
+
+def coarse_planes(columns, low, high):
+    before, inside, after = columns
+    return inside, low * (before - inside), high * (after - inside)
 
 
 def add_coarse(local, columns):
@@ -853,26 +851,56 @@
     return stack(planes)
 
 
-def apply_kernel(near, packed, coarse, flux, b, zl, yl, z_ref, y_ref, ylo, yhi, stat):
-    columns = coarse_columns(near, coarse, 0)
-    field = add_coarse(zl[...], columns)[:, RING : RING + ROWS]
+def face_applied(planes, payload, packed, rows, in_grid):
+    inside, first, last = planes
+    fields = [inside + (first if i == 0 else last if i == 7 else 0.0) for i in rows]
+    gy = along_y(stack(fields), packed, 0)
+    fy = along_y(stack([payload[6 + k] * gy[k] for k in range(2)]), packed, 1)
+    plane_w = packed[0:WIDE]
+    result = []
+    for k, i in enumerate(rows):
+        slopes = payload[2 + k] * first + payload[4 + k] * last
+        mass = (HELM_COEF * 0.125 * float(WEIGHT[i])) * in_grid * (plane_w * fields[k])
+        result.append(payload[k] + slopes + fy[k] + mass)
+    return result
+
+
+def apply_kernel(
+    near, packed, tables, coarse, flux, b, zl, yl, ylo, yhi,
+    z_ref, y_ref, w_ref, wlo, whi, stat,
+):
+    columns = coarse_columns(near, coarse, 0, 5)
+    own = coarse_planes(columns[1:4], 1.0 - near[0], 1.0 - near[1])
+    field = add_coarse(zl[...], own)[:, RING : RING + ROWS]
     z_ref[...] = field
-    applied = yl[...] + coarse_applied(columns, flux[...], packed)
-    y_ref[...] = applied
-    ylo[...] = applied[0:2]
-    yhi[...] = applied[6:8]
-    own = applied[:, RING : RING + ROWS]
-    stat[...] = lane_row([jnp.sum(b[...] * field), jnp.sum(field * own)])
+    applied = yl[...] + coarse_applied(own, flux[...], packed)
+    kept = applied[:, RING : RING + ROWS]
+    y_ref[...] = kept
+    stat[...] = lane_row([jnp.sum(b[...] * field), jnp.sum(field * kept)])
+    lower = coarse_planes(columns[0:3], 1.0 - near[7], 0.5)
+    upper = coarse_planes(columns[2:5], 0.5, 1.0 - near[6])
+    planes = [applied[i] for i in range(8)]
+    planes += face_applied(lower, ylo, packed, (6, 7), 2.0 - 2.0 * near[0])
+    planes += face_applied(upper, yhi, packed, (0, 1), 2.0 - 2.0 * near[1])
+    planes = solve_elements(planes, packed, tables, 1)
+    row = lax.broadcasted_iota(jnp.int32, (ROWS, LANES), 0)
+    _, has_low, has_high = ring_rows(near)
+    in_grid = jnp.where(row == 0, has_low, jnp.where(row == ROWS - 1, has_high, 1.0))
+    for i in range(8):
+        first = (1.0 - has_low) * planes[i][ROWS : ROWS + 1]
+        last = (1.0 - has_high) * planes[i][ROWS + 1 : ROWS + 2]
+        alone = jnp.where(row == 0, first, jnp.where(row == ROWS - 1, last, 0.0))
+        planes[i] = planes[i][0:ROWS] * in_grid + alone
+    store_faces(planes, near, w_ref, wlo, whi)
 
 
 def second_kernel(near, packed, coarse, flux, b, y, w, zlo, zhi, stat_in, q_ref, stat):
     local = add_planes(w, zlo[...], zhi[...])
-    columns = [column[RING : RING + ROWS] for column in coarse_columns(near, coarse, 16)]
-    field = add_coarse(local, columns)
+    columns = [column[RING : RING + ROWS] for column in coarse_columns(near, coarse, 16, 3)]
+    field = add_coarse(local, coarse_planes(columns, 1.0 - near[0], 1.0 - near[1]))
     q_ref[...] = field
     applied = local_operator(field, flux[:, RING : RING + ROWS], packed)
-    own = y[:, RING : RING + ROWS]
-    sums = [0.0, 0.0, jnp.sum(b[...] * field), jnp.sum(own * field), jnp.sum(field * applied)]
+    sums = [0.0, 0.0, jnp.sum(b[...] * field), jnp.sum(y[...] * field), jnp.sum(field * applied)]
     stat[...] = jnp.broadcast_to(stat_in[...] + lane_row(sums), stat.shape)
 
 
@@ -922,7 +950,12 @@
         return [jnp.where(index > 0, 0.5, 1.0), jnp.where(index < count - 1, 0.5, 1.0)]
 
     place = [index_gx.astype(F32), index_gy.astype(F32)]
-    near = jnp.stack(ends(index_gx, count_gx) + ends(index_gy, count_gy) + place).astype(F32)
+    beyond = [
+        jnp.where(index_gx < count_gx - 2, 0.5, 1.0),
+        jnp.where(index_gx > 1, 0.5, 1.0),
+    ]
+    near = jnp.stack(ends(index_gx, count_gx) + ends(index_gy, count_gy) + place + beyond)
+    near = near.astype(F32)
     packed = jnp.asarray(PACKED)
     tables = jnp.asarray(TABLES)
     face = (ROWS, LANES)
@@ -959,12 +992,13 @@
         [solid, packed, b, l, zlo, zhi, ylo, yhi],
         flops=20000000,
     )
-    zl, yl, stat = run(
+    zl, yl, zlo, zhi, stat = run(
         galerkin_kernel,
-        [wide_block, wide_block, (count_gx, LANES)],
+        [wide_block, wide_block, wide_block, wide_block, (count_gx, LANES)],
         [near],
         [packed, stat, flux, w, wlo, whi],
     )
+    zlo, zhi = shift("gx", zlo, zhi)
     gathered = lax.all_to_all(stat, "gx", 0, 0, tiled=True)
     (column,) = run(column_kernel, [(count_gy, LANES)], [], [gathered])
     gathered = lax.all_to_all(column, "gy", 0, 0, tiled=True)
@@ -975,15 +1009,11 @@
         [gathered],
         [VMEM((LANES, LANES), F32), VMEM((LANES, LANES), F32)],
     )
-    z, y, zlo, zhi, sums = run(
+    z, y, w, wlo, whi, sums = run(
         apply_kernel,
-        [block, wide_block, (2, *wide_face), (2, *wide_face), (1, LANES)],
+        [block, block, block, face, face, (1, LANES)],
         [near],
-        [packed, coarse, flux, b, zl, yl],
-    )
-    zlo, zhi = shift("gx", zlo, zhi)
-    w, wlo, whi = run(
-        second_schwarz_kernel, [block, face, face], [near], [packed, tables, y, zlo, zhi]
+        [packed, tables, coarse, flux, b, zl, yl, zlo, zhi],
     )
     zlo, zhi = shift("gx", wlo, whi)
     q, sums = run(

time: 126 us -> 123 us (0.976)
  waiting for transfers between devices: 20.5 us -> 16.8 us
  starting transfers between devices: 25.6 us -> 28.3 us
  blocking collectives: 62.1 us -> 60.3 us
    ppermute x5, waiting for transfers between devices: 19.1 us -> 15.5 us  [shift(): lax.ppermute(low_face, axis, backward)]
    ppermute x5, starting transfers between devices: 18.2 us -> 20.8 us  [shift(): lax.ppermute(high_face, axis, forward)]
    all_to_all x1, blocking collectives: 17.6 us -> 16.3 us  [body(): wide = lax.all_to_all(wide, 'gy', 0, 0, tiled=True)]
    pallas_call x11 -> x10, Pallas kernels: 16.4 us -> 16.3 us  [run(): pl.pallas_call(kernel, out_shape=[jax.ShapeDtypeStruct(out, F32) for out...]
  transfers between devices with their start and end apart: 10 -> 10, of which waited for: 6 -> 5; matrix products, arithmetic and copies ran while one was open for 0% -> 0% of each run, Pallas kernels for 1% -> 4%
where the time goes in v9:
time: 123 us
  blocking collectives  60.3 us (49%)
  starting transfers between devices  28.3 us (23%)
  waiting for transfers between devices  16.8 us (14%)
  Pallas kernels  16.3 us (13%)
    all_to_all x1, blocking collectives, body(): gathered = lax.all_to_all(column, 'gy', 0, 0, tiled=True)  22 us
    ppermute x5, starting transfers between devices, shift(): lax.ppermute(high_face, axis, forward)  20.8 us
    pallas_call x10, Pallas kernels, run(): pl.pallas_call(kernel, out_shape=[jax.ShapeDtypeStruct(out, F32) for out...  16.3 us
    all_to_all x1, blocking collectives, body(): wide = lax.all_to_all(wide, 'gy', 0, 0, tiled=True)  16.3 us
    ppermute x5, waiting for transfers between devices, shift(): lax.ppermute(low_face, axis, backward)  15.5 us
    all_to_all x1, blocking collectives, body(): gathered = lax.all_to_all(stat, 'gx', 0, 0, tiled=True)  12.9 us
    all_to_all x1, blocking collectives, body(): tile = lax.all_to_all(sums, 'gx', 0, 0, tiled=True)  9.09 us
    ppermute x5, starting transfers between devices, shift(): lax.ppermute(low_face, axis, backward)  7.4 us
  transfers between devices with their start and end apart: 10, of which 5 were waited for; matrix products, arithmetic and copies ran while one was open for 0% of the time, Pallas kernels for 4%

profile of v9, /device:TPU:1, one launch (start us, length us, event | category | flops | bytes accessed | tf_op | source)
XLA Modules:
  0.0 122.6 jit_solution(4144574760470856585)
XLA Ops:
  0.6 0.0 copy-start.1
  0.6 1.8 %shard_map.77 = (f32[8,32,128]{2,1,0:T(8,128)S(1)}, f32[8,32,128]{2,1,0:T(8,128)S(1)}, f32[3,32,128]{2,1,0:T(8,128)S(1)}, f32[3,32,128]{2,1,0:T(8,128)S(1)}, f32[8,128]{1,0:T(8,128)S(1)}) custom-call(f32[8,32,128]{2,1,0:T(8,128)} %lev_in.1, f32[3,8,32,128]{3,2,1,0:T(8,128)} %vel_in.1, f32[8,32,128]{2,1,0:T(8,128)} %src_in.1, ...), custom_call_target="tpu_custom_call" | custom-call | flops 1000000 | bytes 729088 | tf_op jit(solution)/shard_map/pallas_call | solution.py:923
  2.5 0.0 copy-start
  2.5 5.0 %collective-permute-start = (f32[3,32,128]{2,1,0:T(8,128)S(1)}, f32[3,32,128]{2,1,0:T(8,128)S(1)}, u32[]{:S(2)}, u32[]{:S(2)}) collective-permute-start(f32[3,32,128]{2,1,0:T(8,128)S(1)} %get-tuple-element.31), channel_id=1, source_target_pairs={{0,64},{64,128},{128,192},{192,256},{256,320},{320,384},{384,448},... | collective-permute-start | bytes 147464 | tf_op jit(solution)/shard_map/ppermute | solution.py:939
  7.5 1.3 %collective-permute-start.1 = (f32[3,32,128]{2,1,0:T(8,128)S(1)}, f32[3,32,128]{2,1,0:T(8,128)S(1)}, u32[]{:S(2)}, u32[]{:S(2)}) collective-permute-start(f32[3,32,128]{2,1,0:T(8,128)S(1)} %get-tuple-element.32), channel_id=1, source_target_pairs={{64,0},{128,64},{192,128},{256,192},{320,256},{384,320},{448,384},... | collective-permute-start | bytes 147464 | tf_op jit(solution)/shard_map/ppermute | solution.py:939
  8.8 0.0 collective-permute-done.low_z.zlo
  8.8 4.2 %collective-permute-done.1.high_z.zhi = f32[3,32,128]{2,1,0:T(8,128)S(1)} collective-permute-done((f32[3,32,128]{2,1,0:T(8,128)S(1)}, f32[3,32,128]{2,1,0:T(8,128)S(1)}, u32[]{:S(2)}, u32[]{:S(2)}) %collective-permute-start.1) | collective-permute-done | bytes 49184 | tf_op jit(solution)/shard_map/ppermute | solution.py:939
  13.0 4.8 %collective-permute-start.2 = (f32[12,48,128]{2,1,0:T(8,128)S(1)}, f32[12,48,128]{2,1,0:T(8,128)S(1)}, u32[]{:S(2)}, u32[]{:S(2)}) collective-permute-start(f32[12,48,128]{2,1,0:T(8,128)S(1)} %get-tuple-element.33), channel_id=1, source_target_pairs={{0,1},{1,2},{2,3},{3,4},{4,5},{5,6},{6,7},{7,8},{8,9},{9,10},{10,1... | collective-permute-start | bytes 884744 | tf_op jit(solution)/shard_map/ppermute | solution.py:939
  17.8 2.2 %collective-permute-start.3 = (f32[12,48,128]{2,1,0:T(8,128)S(1)}, f32[12,48,128]{2,1,0:T(8,128)S(1)}, u32[]{:S(2)}, u32[]{:S(2)}) collective-permute-start(f32[12,48,128]{2,1,0:T(8,128)S(1)} %get-tuple-element.34), channel_id=1, source_target_pairs={{1,0},{2,1},{3,2},{4,3},{5,4},{6,5},{7,6},{8,7},{9,8},{10,9},{11,1... | collective-permute-start | bytes 884744 | tf_op jit(solution)/shard_map/ppermute | solution.py:939
  20.1 0.1 stack.35.near
  20.2 1.3 %collective-permute-done.2.ylo = f32[12,48,128]{2,1,0:T(8,128)S(1)} collective-permute-done((f32[12,48,128]{2,1,0:T(8,128)S(1)}, f32[12,48,128]{2,1,0:T(8,128)S(1)}, u32[]{:S(2)}, u32[]{:S(2)}) %collective-permute-start.2) | collective-permute-done | bytes 294944 | tf_op jit(solution)/shard_map/ppermute | solution.py:939
  21.5 4.4 %collective-permute-done.3.yhi = f32[12,48,128]{2,1,0:T(8,128)S(1)} collective-permute-done((f32[12,48,128]{2,1,0:T(8,128)S(1)}, f32[12,48,128]{2,1,0:T(8,128)S(1)}, u32[]{:S(2)}, u32[]{:S(2)}) %collective-permute-start.3) | collective-permute-done | bytes 294944 | tf_op jit(solution)/shard_map/ppermute | solution.py:939
  25.9 0.0 copy-done.1
  25.9 0.0 copy-done
  25.9 2.7 %shard_map.80 = (f32[8,64,128]{2,1,0:T(8,128)S(1)}, f32[64,128]{1,0:T(8,128)S(1)}, f32[64,128]{1,0:T(8,128)S(1)}) custom-call(f32[8]{0:T(128)S(1)} %stack.35.near, f32[664,128]{1,0:T(8,128)S(1)} %copy-done, bf16[1008,384]{1,0:T(8,128)(2,1)S(1)} %copy-done.1, f32[8,32,128]{2,1,0:T(8,128)S(1)} %get-tuple-element.29.b, ...), custom_call_target="tpu_custom_call" | custom-call | flops 1000000 | bytes 655360 | tf_op jit(solution)/shard_map/pallas_call | solution.py:923
  28.6 4.0 %collective-permute-start.4 = (f32[64,128]{1,0:T(8,128)S(1)}, f32[64,128]{1,0:T(8,128)S(1)}, u32[]{:S(2)}, u32[]{:S(2)}) collective-permute-start(f32[64,128]{1,0:T(8,128)S(1)} %get-tuple-element.39), channel_id=1, source_target_pairs={{0,64},{64,128},{128,192},{192,256},{256,320},{320,384},{384,448},... | collective-permute-start | bytes 98312 | tf_op jit(solution)/shard_map/ppermute | solution.py:939
  32.6 1.3 %collective-permute-start.5 = (f32[64,128]{1,0:T(8,128)S(1)}, f32[64,128]{1,0:T(8,128)S(1)}, u32[]{:S(2)}, u32[]{:S(2)}) collective-permute-start(f32[64,128]{1,0:T(8,128)S(1)} %get-tuple-element.40), channel_id=1, source_target_pairs={{64,0},{128,64},{192,128},{256,192},{320,256},{384,320},{448,384},... | collective-permute-start | bytes 98312 | tf_op jit(solution)/shard_map/ppermute | solution.py:939
  33.9 1.5 %shard_map.79 = (f32[8,32,128]{2,1,0:T(8,128)}, f32[8,64,128]{2,1,0:T(8,128)S(1)}, f32[1,128]{1,0:T(1,128)S(1)}) custom-call(f32[8]{0:T(128)S(1)} %stack.35.near, f32[8,128]{1,0:T(8,128)S(1)} %get-tuple-element.28.solid, f32[664,128]{1,0:T(8,128)S(1)} %copy-done, f32[8,32,128]{2,1,0:T(8,128)S(1)} %get-tuple-element.29.b, ...), custom_call_target="tpu_custom_call" | custom-call | flops 20000000 | bytes 787456 | tf_op jit(solution)/shard_map/pallas_call | solution.py:923
  35.4 0.0 collective-permute-done.4.zlo
  35.4 3.7 %collective-permute-done.5.zhi = f32[64,128]{1,0:T(8,128)S(1)} collective-permute-done((f32[64,128]{1,0:T(8,128)S(1)}, f32[64,128]{1,0:T(8,128)S(1)}, u32[]{:S(2)}, u32[]{:S(2)}) %collective-permute-start.5) | collective-permute-done | bytes 32800 | tf_op jit(solution)/shard_map/ppermute | solution.py:939
  39.1 1.8 %shard_map.81 = (f32[8,64,128]{2,1,0:T(8,128)S(1)}, f32[8,64,128]{2,1,0:T(8,128)S(1)}, f32[8,64,128]{2,1,0:T(8,128)S(1)}, f32[8,64,128]{2,1,0:T(8,128)S(1)}, f32[8,128]{1,0:T(8,128)S(1)}) custom-call(f32[8]{0:T(128)S(1)} %stack.35.near, f32[664,128]{1,0:T(8,128)S(1)} %copy-done, f32[1,128]{1,0:T(1,128)S(1)} %get-tuple-element.36.stat_in, ...), custom_call_target="tpu_custom_call" | custom-call | flops 1000000 | bytes 2105344 | tf_op jit(solution)/shard_map/pallas_call | solution.py:923
  40.9 4.9 %collective-permute-start.6 = (f32[8,64,128]{2,1,0:T(8,128)S(1)}, f32[8,64,128]{2,1,0:T(8,128)S(1)}, u32[]{:S(2)}, u32[]{:S(2)}) collective-permute-start(f32[8,64,128]{2,1,0:T(8,128)S(1)} %get-tuple-element.44), channel_id=1, source_target_pairs={{0,64},{64,128},{128,192},{192,256},{256,320},{320,384},{384,448},... | collective-permute-start | bytes 786440 | tf_op jit(solution)/shard_map/ppermute | solution.py:939
  45.8 1.3 %collective-permute-start.7 = (f32[8,64,128]{2,1,0:T(8,128)S(1)}, f32[8,64,128]{2,1,0:T(8,128)S(1)}, u32[]{:S(2)}, u32[]{:S(2)}) collective-permute-start(f32[8,64,128]{2,1,0:T(8,128)S(1)} %get-tuple-element.45), channel_id=1, source_target_pairs={{64,0},{128,64},{192,128},{256,192},{320,256},{384,320},{448,384},... | collective-permute-start | bytes 786440 | tf_op jit(solution)/shard_map/ppermute | solution.py:939
  47.1 12.9 %all_to_all.39 = f32[8,1,128]{2,1,0:T(1,128)S(1)} all-to-all(f32[8,1,128]{2,1,0:T(1,128)S(1)} %bitcast.25), channel_id=1, replica_groups=mesh['gx'=8,'gy'=64] {'gx'}, dimensions={0} | all-to-all | bytes 8192 | tf_op jit(solution)/shard_map/all_to_all | solution.py:1002
  60.0 0.3 shard_map.82
  60.3 22.0 %all_to_all.40 = f32[64,1,128]{2,1,0:T(1,128)S(1)} all-to-all(f32[64,1,128]{2,1,0:T(1,128)S(1)} %bitcast.21), channel_id=1, replica_groups=mesh['gx'=8,'gy'=64] {'gy'}, dimensions={0} | all-to-all | bytes 65536 | tf_op jit(solution)/shard_map/all_to_all | solution.py:1004
  82.3 3.5 %shard_map.83.coarse = f32[32,128]{1,0:T(8,128)S(1)} custom-call(f32[8]{0:T(128)S(1)} %stack.35.near, f32[64,128]{1,0:T(8,128)S(1)} %bitcast.22), custom_call_target="tpu_custom_call" | custom-call | flops 1000000 | bytes 32768 | tf_op jit(solution)/shard_map/pallas_call | solution.py:923
  85.8 0.0 collective-permute-done.6.ylo
  85.8 0.0 collective-permute-done.7.yhi
  85.8 2.6 %shard_map.84 = (f32[8,32,128]{2,1,0:T(8,128)S(1)}, f32[8,32,128]{2,1,0:T(8,128)S(1)}, f32[8,32,128]{2,1,0:T(8,128)S(1)}, f32[32,128]{1,0:T(8,128)S(1)}, f32[32,128]{1,0:T(8,128)S(1)}, /*index=5*/f32[1,128]{1,0:T(1,128)S(1)}) custom-call(f32[8]{0:T(128)S(1)} %stack.35.near, f32[664,128]{1,0:T(8,128)S(1)} %copy-done, bf16[1008,384]{1,0:T(8,128)(2,1)S(1)} %copy-done.1, ...), custom_call_target="tpu_custom_call" | custom-call | flops 1000000 | bytes 852992 | tf_op jit(solution)/shard_map/pallas_call | solution.py:923
  88.5 2.2 %collective-permute-start.8 = (f32[32,128]{1,0:T(8,128)S(1)}, f32[32,128]{1,0:T(8,128)S(1)}, u32[]{:S(2)}, u32[]{:S(2)}) collective-permute-start(f32[32,128]{1,0:T(8,128)S(1)} %get-tuple-element.48), channel_id=1, source_target_pairs={{0,64},{64,128},{128,192},{192,256},{256,320},{320,384},{384,448},... | collective-permute-start | bytes 49160 | tf_op jit(solution)/shard_map/ppermute | solution.py:939
  90.7 1.3 %collective-permute-start.9 = (f32[32,128]{1,0:T(8,128)S(1)}, f32[32,128]{1,0:T(8,128)S(1)}, u32[]{:S(2)}, u32[]{:S(2)}) collective-permute-start(f32[32,128]{1,0:T(8,128)S(1)} %get-tuple-element.49), channel_id=1, source_target_pairs={{64,0},{128,64},{192,128},{256,192},{320,256},{384,320},{448,384},... | collective-permute-start | bytes 49160 | tf_op jit(solution)/shard_map/ppermute | solution.py:939
  92.0 0.0 collective-permute-done.8.zlo
  92.0 3.2 %collective-permute-done.9.zhi = f32[32,128]{1,0:T(8,128)S(1)} collective-permute-done((f32[32,128]{1,0:T(8,128)S(1)}, f32[32,128]{1,0:T(8,128)S(1)}, u32[]{:S(2)}, u32[]{:S(2)}) %collective-permute-start.9) | collective-permute-done | bytes 16416 | tf_op jit(solution)/shard_map/ppermute | solution.py:939
  95.2 1.2 %shard_map.85 = (f32[8,32,128]{2,1,0:T(8,128)S(1)}, f32[8,128]{1,0:T(8,128)S(1)}) custom-call(f32[8]{0:T(128)S(1)} %stack.35.near, f32[664,128]{1,0:T(8,128)S(1)} %copy-done, f32[32,128]{1,0:T(8,128)S(1)} %shard_map.83.coarse, f32[8,64,128]{2,1,0:T(8,128)S(1)} %get-tuple-element.37.flux, f32[8,32,128]{2,1,0:T(8,128)S(1)} %get-tuple-element.29.b, ...), custom_call_target="tpu_custom_call" | custom-call | flops 1000000 | bytes 270336 | tf_op jit(solution)/shard_map/pallas_call | solution.py:923
  96.4 9.1 %all_to_all.41 = f32[8,1,128]{2,1,0:T(1,128)S(1)} all-to-all(f32[8,1,128]{2,1,0:T(1,128)S(1)} %bitcast.26), channel_id=1, replica_groups=mesh['gx'=8,'gy'=64] {'gx'}, dimensions={0} | all-to-all | bytes 8192 | tf_op jit(solution)/shard_map/all_to_all | solution.py:1025
  105.5 16.3 %all_to_all.42 = f32[64,1,128]{2,1,0:T(1,128)S(1)} all-to-all(f32[64,1,128]{2,1,0:T(1,128)S(1)} %broadcast_in_dim.2), channel_id=1, replica_groups=mesh['gx'=8,'gy'=64] {'gy'}, dimensions={0} | all-to-all | bytes 65536 | tf_op jit(solution)/shard_map/all_to_all | solution.py:1027
  121.8 0.8 shard_map.86
  (3 shorter events, 0.1 us)
Async XLA Ops:
  0.6 25.2 %copy-start.1 = (bf16[1008,384]{1,0:T(8,128)(2,1)S(1)}, bf16[1008,384]{1,0:T(8,128)(2,1)}, u32[]{:S(2)}) copy-start(bf16[1008,384]{1,0:T(8,128)(2,1)} %constant.30.clone.tables) | copy-start | bytes 2322436
  2.5 23.4 %copy-start = (f32[664,128]{1,0:T(8,128)S(1)}, f32[664,128]{1,0:T(8,128)}, u32[]{:S(2)}) copy-start(f32[664,128]{1,0:T(8,128)} %constant.29.clone.packed_in.packed) | copy-start | bytes 1019908
  2.5 6.3 %collective-permute-start = (f32[3,32,128]{2,1,0:T(8,128)S(1)}, f32[3,32,128]{2,1,0:T(8,128)S(1)}, u32[]{:S(2)}, u32[]{:S(2)}) collective-permute-start(f32[3,32,128]{2,1,0:T(8,128)S(1)} %get-tuple-element.31), channel_id=1, source_target_pairs={{0,64},{64,128},{128,192},{192,256},{256,320},{320,384},{384,448},... | collective-permute-start | bytes 147464 | tf_op jit(solution)/shard_map/ppermute | solution.py:939
  7.5 5.5 %collective-permute-start.1 = (f32[3,32,128]{2,1,0:T(8,128)S(1)}, f32[3,32,128]{2,1,0:T(8,128)S(1)}, u32[]{:S(2)}, u32[]{:S(2)}) collective-permute-start(f32[3,32,128]{2,1,0:T(8,128)S(1)} %get-tuple-element.32), channel_id=1, source_target_pairs={{64,0},{128,64},{192,128},{256,192},{320,256},{384,320},{448,384},... | collective-permute-start | bytes 147464 | tf_op jit(solution)/shard_map/ppermute | solution.py:939
  13.0 8.5 %collective-permute-start.2 = (f32[12,48,128]{2,1,0:T(8,128)S(1)}, f32[12,48,128]{2,1,0:T(8,128)S(1)}, u32[]{:S(2)}, u32[]{:S(2)}) collective-permute-start(f32[12,48,128]{2,1,0:T(8,128)S(1)} %get-tuple-element.33), channel_id=1, source_target_pairs={{0,1},{1,2},{2,3},{3,4},{4,5},{5,6},{6,7},{7,8},{8,9},{9,10},{10,1... | collective-permute-start | bytes 884744 | tf_op jit(solution)/shard_map/ppermute | solution.py:939
  17.8 8.0 %collective-permute-start.3 = (f32[12,48,128]{2,1,0:T(8,128)S(1)}, f32[12,48,128]{2,1,0:T(8,128)S(1)}, u32[]{:S(2)}, u32[]{:S(2)}) collective-permute-start(f32[12,48,128]{2,1,0:T(8,128)S(1)} %get-tuple-element.34), channel_id=1, source_target_pairs={{1,0},{2,1},{3,2},{4,3},{5,4},{6,5},{7,6},{8,7},{9,8},{10,9},{11,1... | collective-permute-start | bytes 884744 | tf_op jit(solution)/shard_map/ppermute | solution.py:939
  28.6 6.8 %collective-permute-start.4 = (f32[64,128]{1,0:T(8,128)S(1)}, f32[64,128]{1,0:T(8,128)S(1)}, u32[]{:S(2)}, u32[]{:S(2)}) collective-permute-start(f32[64,128]{1,0:T(8,128)S(1)} %get-tuple-element.39), channel_id=1, source_target_pairs={{0,64},{64,128},{128,192},{192,256},{256,320},{320,384},{384,448},... | collective-permute-start | bytes 98312 | tf_op jit(solution)/shard_map/ppermute | solution.py:939
  32.6 6.5 %collective-permute-start.5 = (f32[64,128]{1,0:T(8,128)S(1)}, f32[64,128]{1,0:T(8,128)S(1)}, u32[]{:S(2)}, u32[]{:S(2)}) collective-permute-start(f32[64,128]{1,0:T(8,128)S(1)} %get-tuple-element.40), channel_id=1, source_target_pairs={{64,0},{128,64},{192,128},{256,192},{320,256},{384,320},{448,384},... | collective-permute-start | bytes 98312 | tf_op jit(solution)/shard_map/ppermute | solution.py:939
  40.9 44.9 %collective-permute-start.6 = (f32[8,64,128]{2,1,0:T(8,128)S(1)}, f32[8,64,128]{2,1,0:T(8,128)S(1)}, u32[]{:S(2)}, u32[]{:S(2)}) collective-permute-start(f32[8,64,128]{2,1,0:T(8,128)S(1)} %get-tuple-element.44), channel_id=1, source_target_pairs={{0,64},{64,128},{128,192},{192,256},{256,320},{320,384},{384,448},... | collective-permute-start | bytes 786440 | tf_op jit(solution)/shard_map/ppermute | solution.py:939
  45.8 40.0 %collective-permute-start.7 = (f32[8,64,128]{2,1,0:T(8,128)S(1)}, f32[8,64,128]{2,1,0:T(8,128)S(1)}, u32[]{:S(2)}, u32[]{:S(2)}) collective-permute-start(f32[8,64,128]{2,1,0:T(8,128)S(1)} %get-tuple-element.45), channel_id=1, source_target_pairs={{64,0},{128,64},{192,128},{256,192},{320,256},{384,320},{448,384},... | collective-permute-start | bytes 786440 | tf_op jit(solution)/shard_map/ppermute | solution.py:939
  88.5 3.5 %collective-permute-start.8 = (f32[32,128]{1,0:T(8,128)S(1)}, f32[32,128]{1,0:T(8,128)S(1)}, u32[]{:S(2)}, u32[]{:S(2)}) collective-permute-start(f32[32,128]{1,0:T(8,128)S(1)} %get-tuple-element.48), channel_id=1, source_target_pairs={{0,64},{64,128},{128,192},{192,256},{256,320},{320,384},{384,448},... | collective-permute-start | bytes 49160 | tf_op jit(solution)/shard_map/ppermute | solution.py:939
  90.7 4.5 %collective-permute-start.9 = (f32[32,128]{1,0:T(8,128)S(1)}, f32[32,128]{1,0:T(8,128)S(1)}, u32[]{:S(2)}, u32[]{:S(2)}) collective-permute-start(f32[32,128]{1,0:T(8,128)S(1)} %get-tuple-element.49), channel_id=1, source_target_pairs={{64,0},{128,64},{192,128},{256,192},{320,256},{384,320},{448,384},... | collective-permute-start | bytes 49160 | tf_op jit(solution)/shard_map/ppermute | solution.py:939

commit v10 on v9

--- a/solution.py
+++ b/solution.py
@@ -298,7 +298,7 @@
 def along_x(values, packed, kind):
     start = AT_DXT if kind else AT_DX
     high, low = parts(packed[start : start + LANES])
-    first, rest = parts(values.reshape(8 * values.shape[1], LANES))
+    first, rest = parts(values.reshape(values.shape[0] * values.shape[1], LANES))
     total = dot(
         jnp.concatenate([first, rest], axis=1), jnp.concatenate([high, high], axis=0)
     ) + dot(first, low)
@@ -741,16 +741,21 @@
     back_z = move(link_z, -1, 0)
     back_y = move(link_y, 0, -1)
     diagonal = HELM_COEF * EZ * EY * EX + link_z + back_z + link_y + back_y
-    blocks, lower, upper = [], [], []
+    blocks = []
     for r in range(8):
         row = jnp.where(sub == r, diagonal, 0.0)
         row = jnp.where(sub == r + 1, -back_z, row)
         row = jnp.where(sub == r - 1, -link_z, row)
         blocks.append(row)
-        lower.append(jnp.where(sub == r, -back_y, 0.0))
-        upper.append(jnp.where(sub == r, -link_y, 0.0))
-    levels = []
-    step = 1
+    inverse = invert(blocks, sub)
+    down = [-back_y[r : r + 1] * move(inverse[r], 0, -1) for r in range(8)]
+    up = [-link_y[r : r + 1] * move(inverse[r], 0, 1) for r in range(8)]
+    levels = [(1, down, up)]
+    link_before, link_after = move(link_y, 0, -1), move(back_y, 0, 1)
+    blocks = [blocks[r] + down[r] * link_before + up[r] * link_after for r in range(8)]
+    lower = [row * move(back_y, 0, -1) for row in down]
+    upper = [row * move(link_y, 0, 1) for row in up]
+    step = 2
     while step < count:
         inverse = invert(blocks, sub)
         down = multiply(lower, [move(row, 0, -step) for row in inverse])
@@ -866,17 +871,15 @@
 
 
 def apply_kernel(
-    near, packed, tables, coarse, flux, b, zl, yl, ylo, yhi,
-    z_ref, y_ref, w_ref, wlo, whi, stat,
+    near, packed, tables, coarse, flux, zl, yl, ylo, yhi,
+    z_ref, y_ref, w_ref, wlo, whi,
 ):
     columns = coarse_columns(near, coarse, 0, 5)
     own = coarse_planes(columns[1:4], 1.0 - near[0], 1.0 - near[1])
     field = add_coarse(zl[...], own)[:, RING : RING + ROWS]
     z_ref[...] = field
     applied = yl[...] + coarse_applied(own, flux[...], packed)
-    kept = applied[:, RING : RING + ROWS]
-    y_ref[...] = kept
-    stat[...] = lane_row([jnp.sum(b[...] * field), jnp.sum(field * kept)])
+    y_ref[...] = applied[:, RING : RING + ROWS]
     lower = coarse_planes(columns[0:3], 1.0 - near[7], 0.5)
     upper = coarse_planes(columns[2:5], 0.5, 1.0 - near[6])
     planes = [applied[i] for i in range(8)]
@@ -894,17 +897,58 @@
     store_faces(planes, near, w_ref, wlo, whi)
 
 
-def second_kernel(near, packed, coarse, flux, b, y, w, zlo, zhi, stat_in, q_ref, stat):
-    local = add_planes(w, zlo[...], zhi[...])
+def second_kernel(near, packed, coarse, flux, b, y, z, w, x_ref, kx_ref, stat):
     columns = [column[RING : RING + ROWS] for column in coarse_columns(near, coarse, 16, 3)]
-    field = add_coarse(local, coarse_planes(columns, 1.0 - near[0], 1.0 - near[1]))
-    q_ref[...] = field
-    applied = local_operator(field, flux[:, RING : RING + ROWS], packed)
-    sums = [0.0, 0.0, jnp.sum(b[...] * field), jnp.sum(y[...] * field), jnp.sum(field * applied)]
+    field = add_coarse(w[...], coarse_planes(columns, 1.0 - near[0], 1.0 - near[1]))
+    x_ref[...] = field
+    fluxes = flux[:, RING : RING + ROWS]
+    gz = along_z([field[i] for i in range(8)], DERIV)
+    gy = along_y(field, packed, 0)
+    gx = along_x(field, packed, 0)
+    slopes = [fluxes[i] * gz[i] for i in range(8)]
+    ends = (0, 7)
+    back = along_z(slopes, DERIV.T[[0, 7]])
+    back_y = along_y(stack([fluxes[i] * gy[i] for i in ends]), packed, 1)
+    back_x = along_x(stack([fluxes[i] * gx[i] for i in ends]), packed, 1)
+    plane_w = packed[0:ROWS]
+    mass = HELM_COEF * 0.125
+    for k, i in enumerate(ends):
+        weighted = (mass * float(WEIGHT[i])) * (plane_w * field[i])
+        kx_ref[k] = back[k] + back_y[k] + back_x[k] + weighted
+    energy = None
+    for i in range(8):
+        term = slopes[i] * gz[i] + fluxes[i] * (gy[i] * gy[i] + gx[i] * gx[i])
+        term = term + (mass * float(WEIGHT[i])) * (plane_w * field[i] * field[i])
+        energy = term if energy is None else energy + term
+    first, right = z[...], b[...]
+    sums = [right * first, y[...] * first, right * field, y[...] * field]
+    stat[...] = lane_row([jnp.sum(term) for term in sums] + [jnp.sum(energy)])
+
+
+def face_kernel(packed, flux, b, y, kx, zlo, zhi, stat_in, stat):
+    faces = stack([zlo[...], zhi[...]])
+    fluxes = flux[:, RING : RING + ROWS]
+    gy = along_y(faces, packed, 0)
+    gx = along_x(faces, packed, 0)
+    plane_w = packed[0:ROWS]
+    energy = 2.0 * (kx[0] * faces[0] + kx[1] * faces[1])
+    for k, i in enumerate((0, 7)):
+        mass = (HELM_COEF * 0.125 * float(WEIGHT[i])) * (plane_w * faces[k] * faces[k])
+        energy = energy + mass + fluxes[i] * (gy[k] * gy[k] + gx[k] * gx[k])
+    for i in range(8):
+        slope = float(DERIV[i, 0]) * faces[0] + float(DERIV[i, 7]) * faces[1]
+        energy = energy + fluxes[i] * slope * slope
+    sums = [
+        0.0,
+        0.0,
+        jnp.sum(b[0] * faces[0] + b[7] * faces[1]),
+        jnp.sum(y[0] * faces[0] + y[7] * faces[1]),
+        jnp.sum(energy),
+    ]
     stat[...] = jnp.broadcast_to(stat_in[...] + lane_row(sums), stat.shape)
 
 
-def combine_kernel(sums, z, q, p_ref):
+def combine_kernel(sums, z, x, zlo, zhi, p_ref):
     total = jnp.sum(sums[...], axis=0, keepdims=True)
     rz, pap, rq, aq, qhq = (total[:, k : k + 1] for k in range(5))
     step = rz / pap
@@ -915,7 +959,13 @@
     step_next = rz_next / curved
     on_z = step + step_next * grown
     on_q = step_next * step
-    p_ref[...] = on_z.reshape(1, 1, 1) * z[...] - on_q.reshape(1, 1, 1) * q[...]
+    for i in range(8):
+        plane = x[i]
+        if i == 0:
+            plane = plane + zlo[...]
+        if i == 7:
+            plane = plane + zhi[...]
+        p_ref[i] = on_z * z[i] - on_q * plane
 
 
 def run(kernel, outs, smem, args, scratch=(), flops=1000000, place=VMEM, limit=LIMIT):
@@ -1009,23 +1059,27 @@
         [gathered],
         [VMEM((LANES, LANES), F32), VMEM((LANES, LANES), F32)],
     )
-    z, y, w, wlo, whi, sums = run(
+    z, y, w, wlo, whi = run(
         apply_kernel,
-        [block, block, block, face, face, (1, LANES)],
+        [block, block, block, face, face],
         [near],
-        [packed, tables, coarse, flux, b, zl, yl, zlo, zhi],
+        [packed, tables, coarse, flux, zl, yl, zlo, zhi],
     )
     zlo, zhi = shift("gx", wlo, whi)
-    q, sums = run(
+    x, kx, sums = run(
         second_kernel,
-        [block, (count_gx, LANES)],
+        [block, (2, *face), (1, LANES)],
         [near],
-        [packed, coarse, flux, b, y, w, zlo, zhi, sums],
+        [packed, coarse, flux, b, y, z, w],
+        flops=20000000,
+    )
+    (sums,) = run(
+        face_kernel, [(count_gx, LANES)], [], [packed, flux, b, y, kx, zlo, zhi, sums]
     )
     tile = lax.all_to_all(sums, "gx", 0, 0, tiled=True)
     wide = jnp.broadcast_to(jnp.sum(tile, axis=0, keepdims=True), (count_gy, LANES))
     wide = lax.all_to_all(wide, "gy", 0, 0, tiled=True)
-    (pressure,) = run(combine_kernel, [block], [], [wide, z, q])
+    (pressure,) = run(combine_kernel, [block], [], [wide, z, x, zlo, zhi])
     return (level_new, pressure)
 
 

time: 123 us -> 122 us (level)
    pallas_call x10 -> x11, Pallas kernels: 16.3 us -> 16.3 us  [run(): pl.pallas_call(kernel, out_shape=[jax.ShapeDtypeStruct(out, F32) for out...]
  transfers between devices with their start and end apart: 10 -> 10, of which waited for: 5 -> 5; matrix products, arithmetic and copies ran while one was open for 0% -> 0% of each run, Pallas kernels for 4% -> 5%
where the time goes in v10:
time: 122 us
  blocking collectives  60.3 us (49%)
  starting transfers between devices  28.2 us (23%)
  Pallas kernels  16.3 us (13%)
  waiting for transfers between devices  15.7 us (13%)
    all_to_all x1, blocking collectives, body(): gathered = lax.all_to_all(column, 'gy', 0, 0, tiled=True)  22 us
    ppermute x5, starting transfers between devices, shift(): lax.ppermute(high_face, axis, forward)  20.8 us
    pallas_call x11, Pallas kernels, run(): pl.pallas_call(kernel, out_shape=[jax.ShapeDtypeStruct(out, F32) for out...  16.3 us
    all_to_all x1, blocking collectives, body(): wide = lax.all_to_all(wide, 'gy', 0, 0, tiled=True)  16.3 us
    ppermute x5, waiting for transfers between devices, shift(): lax.ppermute(low_face, axis, backward)  14.4 us
    all_to_all x1, blocking collectives, body(): gathered = lax.all_to_all(stat, 'gx', 0, 0, tiled=True)  12.9 us
    all_to_all x1, blocking collectives, body(): tile = lax.all_to_all(sums, 'gx', 0, 0, tiled=True)  9.09 us
    ppermute x5, starting transfers between devices, shift(): lax.ppermute(low_face, axis, backward)  7.4 us
  transfers between devices with their start and end apart: 10, of which 5 were waited for; matrix products, arithmetic and copies ran while one was open for 0% of the time, Pallas kernels for 5%

profile of v10, /device:TPU:1, one launch (start us, length us, event | category | flops | bytes accessed | tf_op | source)
XLA Modules:
  0.0 121.6 jit_solution(4716217201932534175)
XLA Ops:
  0.6 0.0 copy-start.1
  0.6 1.8 %shard_map.77 = (f32[8,32,128]{2,1,0:T(8,128)S(1)}, f32[8,32,128]{2,1,0:T(8,128)S(1)}, f32[3,32,128]{2,1,0:T(8,128)S(1)}, f32[3,32,128]{2,1,0:T(8,128)S(1)}, f32[8,128]{1,0:T(8,128)S(1)}) custom-call(f32[8,32,128]{2,1,0:T(8,128)} %lev_in.1, f32[3,8,32,128]{3,2,1,0:T(8,128)} %vel_in.1, f32[8,32,128]{2,1,0:T(8,128)} %src_in.1, ...), custom_call_target="tpu_custom_call" | custom-call | flops 1000000 | bytes 729088 | tf_op jit(solution)/shard_map/pallas_call | solution.py:973
  2.5 0.0 copy-start
  2.5 5.0 %collective-permute-start = (f32[3,32,128]{2,1,0:T(8,128)S(1)}, f32[3,32,128]{2,1,0:T(8,128)S(1)}, u32[]{:S(2)}, u32[]{:S(2)}) collective-permute-start(f32[3,32,128]{2,1,0:T(8,128)S(1)} %get-tuple-element.31), channel_id=1, source_target_pairs={{0,64},{64,128},{128,192},{192,256},{256,320},{320,384},{384,448},... | collective-permute-start | bytes 147464 | tf_op jit(solution)/shard_map/ppermute | solution.py:989
  7.5 1.3 %collective-permute-start.1 = (f32[3,32,128]{2,1,0:T(8,128)S(1)}, f32[3,32,128]{2,1,0:T(8,128)S(1)}, u32[]{:S(2)}, u32[]{:S(2)}) collective-permute-start(f32[3,32,128]{2,1,0:T(8,128)S(1)} %get-tuple-element.32), channel_id=1, source_target_pairs={{64,0},{128,64},{192,128},{256,192},{320,256},{384,320},{448,384},... | collective-permute-start | bytes 147464 | tf_op jit(solution)/shard_map/ppermute | solution.py:989
  8.8 0.0 collective-permute-done.low_z.zlo
  8.8 4.2 %collective-permute-done.1.high_z.zhi = f32[3,32,128]{2,1,0:T(8,128)S(1)} collective-permute-done((f32[3,32,128]{2,1,0:T(8,128)S(1)}, f32[3,32,128]{2,1,0:T(8,128)S(1)}, u32[]{:S(2)}, u32[]{:S(2)}) %collective-permute-start.1) | collective-permute-done | bytes 49184 | tf_op jit(solution)/shard_map/ppermute | solution.py:989
  13.0 4.8 %collective-permute-start.2 = (f32[12,48,128]{2,1,0:T(8,128)S(1)}, f32[12,48,128]{2,1,0:T(8,128)S(1)}, u32[]{:S(2)}, u32[]{:S(2)}) collective-permute-start(f32[12,48,128]{2,1,0:T(8,128)S(1)} %get-tuple-element.33), channel_id=1, source_target_pairs={{0,1},{1,2},{2,3},{3,4},{4,5},{5,6},{6,7},{7,8},{8,9},{9,10},{10,1... | collective-permute-start | bytes 884744 | tf_op jit(solution)/shard_map/ppermute | solution.py:989
  17.8 2.2 %collective-permute-start.3 = (f32[12,48,128]{2,1,0:T(8,128)S(1)}, f32[12,48,128]{2,1,0:T(8,128)S(1)}, u32[]{:S(2)}, u32[]{:S(2)}) collective-permute-start(f32[12,48,128]{2,1,0:T(8,128)S(1)} %get-tuple-element.34), channel_id=1, source_target_pairs={{1,0},{2,1},{3,2},{4,3},{5,4},{6,5},{7,6},{8,7},{9,8},{10,9},{11,1... | collective-permute-start | bytes 884744 | tf_op jit(solution)/shard_map/ppermute | solution.py:989
  20.1 0.1 stack.35.near
  20.2 1.3 %collective-permute-done.2.ylo = f32[12,48,128]{2,1,0:T(8,128)S(1)} collective-permute-done((f32[12,48,128]{2,1,0:T(8,128)S(1)}, f32[12,48,128]{2,1,0:T(8,128)S(1)}, u32[]{:S(2)}, u32[]{:S(2)}) %collective-permute-start.2) | collective-permute-done | bytes 294944 | tf_op jit(solution)/shard_map/ppermute | solution.py:989
  21.5 4.4 %collective-permute-done.3.yhi = f32[12,48,128]{2,1,0:T(8,128)S(1)} collective-permute-done((f32[12,48,128]{2,1,0:T(8,128)S(1)}, f32[12,48,128]{2,1,0:T(8,128)S(1)}, u32[]{:S(2)}, u32[]{:S(2)}) %collective-permute-start.3) | collective-permute-done | bytes 294944 | tf_op jit(solution)/shard_map/ppermute | solution.py:989
  25.9 0.0 copy-done.1
  25.9 0.0 copy-done
  25.9 2.7 %shard_map.80 = (f32[8,64,128]{2,1,0:T(8,128)S(1)}, f32[64,128]{1,0:T(8,128)S(1)}, f32[64,128]{1,0:T(8,128)S(1)}) custom-call(f32[8]{0:T(128)S(1)} %stack.35.near, f32[664,128]{1,0:T(8,128)S(1)} %copy-done, bf16[1008,384]{1,0:T(8,128)(2,1)S(1)} %copy-done.1, f32[8,32,128]{2,1,0:T(8,128)S(1)} %get-tuple-element.29.b, ...), custom_call_target="tpu_custom_call" | custom-call | flops 1000000 | bytes 655360 | tf_op jit(solution)/shard_map/pallas_call | solution.py:973
  28.6 4.0 %collective-permute-start.4 = (f32[64,128]{1,0:T(8,128)S(1)}, f32[64,128]{1,0:T(8,128)S(1)}, u32[]{:S(2)}, u32[]{:S(2)}) collective-permute-start(f32[64,128]{1,0:T(8,128)S(1)} %get-tuple-element.39), channel_id=1, source_target_pairs={{0,64},{64,128},{128,192},{192,256},{256,320},{320,384},{384,448},... | collective-permute-start | bytes 98312 | tf_op jit(solution)/shard_map/ppermute | solution.py:989
  32.6 1.3 %collective-permute-start.5 = (f32[64,128]{1,0:T(8,128)S(1)}, f32[64,128]{1,0:T(8,128)S(1)}, u32[]{:S(2)}, u32[]{:S(2)}) collective-permute-start(f32[64,128]{1,0:T(8,128)S(1)} %get-tuple-element.40), channel_id=1, source_target_pairs={{64,0},{128,64},{192,128},{256,192},{320,256},{384,320},{448,384},... | collective-permute-start | bytes 98312 | tf_op jit(solution)/shard_map/ppermute | solution.py:989
  33.9 1.5 %shard_map.79 = (f32[8,32,128]{2,1,0:T(8,128)}, f32[8,64,128]{2,1,0:T(8,128)S(1)}, f32[1,128]{1,0:T(1,128)S(1)}) custom-call(f32[8]{0:T(128)S(1)} %stack.35.near, f32[8,128]{1,0:T(8,128)S(1)} %get-tuple-element.28.solid, f32[664,128]{1,0:T(8,128)S(1)} %copy-done, f32[8,32,128]{2,1,0:T(8,128)S(1)} %get-tuple-element.29.b, ...), custom_call_target="tpu_custom_call" | custom-call | flops 20000000 | bytes 787456 | tf_op jit(solution)/shard_map/pallas_call | solution.py:973
  35.4 0.0 collective-permute-done.4.zlo
  35.4 3.7 %collective-permute-done.5.zhi = f32[64,128]{1,0:T(8,128)S(1)} collective-permute-done((f32[64,128]{1,0:T(8,128)S(1)}, f32[64,128]{1,0:T(8,128)S(1)}, u32[]{:S(2)}, u32[]{:S(2)}) %collective-permute-start.5) | collective-permute-done | bytes 32800 | tf_op jit(solution)/shard_map/ppermute | solution.py:989
  39.1 1.8 %shard_map.81 = (f32[8,64,128]{2,1,0:T(8,128)S(1)}, f32[8,64,128]{2,1,0:T(8,128)S(1)}, f32[8,64,128]{2,1,0:T(8,128)S(1)}, f32[8,64,128]{2,1,0:T(8,128)S(1)}, f32[8,128]{1,0:T(8,128)S(1)}) custom-call(f32[8]{0:T(128)S(1)} %stack.35.near, f32[664,128]{1,0:T(8,128)S(1)} %copy-done, f32[1,128]{1,0:T(1,128)S(1)} %get-tuple-element.37.stat_in, ...), custom_call_target="tpu_custom_call" | custom-call | flops 1000000 | bytes 2105344 | tf_op jit(solution)/shard_map/pallas_call | solution.py:973
  40.9 4.9 %collective-permute-start.6 = (f32[8,64,128]{2,1,0:T(8,128)S(1)}, f32[8,64,128]{2,1,0:T(8,128)S(1)}, u32[]{:S(2)}, u32[]{:S(2)}) collective-permute-start(f32[8,64,128]{2,1,0:T(8,128)S(1)} %get-tuple-element.44), channel_id=1, source_target_pairs={{0,64},{64,128},{128,192},{192,256},{256,320},{320,384},{384,448},... | collective-permute-start | bytes 786440 | tf_op jit(solution)/shard_map/ppermute | solution.py:989
  45.8 1.3 %collective-permute-start.7 = (f32[8,64,128]{2,1,0:T(8,128)S(1)}, f32[8,64,128]{2,1,0:T(8,128)S(1)}, u32[]{:S(2)}, u32[]{:S(2)}) collective-permute-start(f32[8,64,128]{2,1,0:T(8,128)S(1)} %get-tuple-element.45), channel_id=1, source_target_pairs={{64,0},{128,64},{192,128},{256,192},{320,256},{384,320},{448,384},... | collective-permute-start | bytes 786440 | tf_op jit(solution)/shard_map/ppermute | solution.py:989
  47.1 12.9 %all_to_all.39 = f32[8,1,128]{2,1,0:T(1,128)S(1)} all-to-all(f32[8,1,128]{2,1,0:T(1,128)S(1)} %bitcast.26), channel_id=1, replica_groups=mesh['gx'=8,'gy'=64] {'gx'}, dimensions={0} | all-to-all | bytes 8192 | tf_op jit(solution)/shard_map/all_to_all | solution.py:1052
  60.0 0.3 shard_map.82
  60.3 22.0 %all_to_all.40 = f32[64,1,128]{2,1,0:T(1,128)S(1)} all-to-all(f32[64,1,128]{2,1,0:T(1,128)S(1)} %bitcast.22), channel_id=1, replica_groups=mesh['gx'=8,'gy'=64] {'gy'}, dimensions={0} | all-to-all | bytes 65536 | tf_op jit(solution)/shard_map/all_to_all | solution.py:1054
  82.3 3.4 %shard_map.83.coarse = f32[32,128]{1,0:T(8,128)S(1)} custom-call(f32[8]{0:T(128)S(1)} %stack.35.near, f32[64,128]{1,0:T(8,128)S(1)} %bitcast.23), custom_call_target="tpu_custom_call" | custom-call | flops 1000000 | bytes 32768 | tf_op jit(solution)/shard_map/pallas_call | solution.py:973
  85.8 0.0 collective-permute-done.6.ylo
  85.8 0.0 collective-permute-done.7.yhi
  85.8 2.6 %shard_map.84 = (f32[8,32,128]{2,1,0:T(8,128)S(1)}, f32[8,32,128]{2,1,0:T(8,128)S(1)}, f32[8,32,128]{2,1,0:T(8,128)S(1)}, f32[32,128]{1,0:T(8,128)S(1)}, f32[32,128]{1,0:T(8,128)S(1)}) custom-call(f32[8]{0:T(128)S(1)} %stack.35.near, f32[664,128]{1,0:T(8,128)S(1)} %copy-done, bf16[1008,384]{1,0:T(8,128)(2,1)S(1)} %copy-done.1, ...), custom_call_target="tpu_custom_call" | custom-call | flops 1000000 | bytes 851968 | tf_op jit(solution)/shard_map/pallas_call | solution.py:973
  88.4 2.2 %collective-permute-start.8 = (f32[32,128]{1,0:T(8,128)S(1)}, f32[32,128]{1,0:T(8,128)S(1)}, u32[]{:S(2)}, u32[]{:S(2)}) collective-permute-start(f32[32,128]{1,0:T(8,128)S(1)} %get-tuple-element.50), channel_id=1, source_target_pairs={{0,64},{64,128},{128,192},{192,256},{256,320},{320,384},{384,448},... | collective-permute-start | bytes 49160 | tf_op jit(solution)/shard_map/ppermute | solution.py:989
  90.6 1.3 %collective-permute-start.9 = (f32[32,128]{1,0:T(8,128)S(1)}, f32[32,128]{1,0:T(8,128)S(1)}, u32[]{:S(2)}, u32[]{:S(2)}) collective-permute-start(f32[32,128]{1,0:T(8,128)S(1)} %get-tuple-element.51), channel_id=1, source_target_pairs={{64,0},{128,64},{192,128},{256,192},{320,256},{384,320},{448,384},... | collective-permute-start | bytes 49160 | tf_op jit(solution)/shard_map/ppermute | solution.py:989
  91.9 1.0 shard_map.85
  93.0 0.0 collective-permute-done.8.zlo
  93.0 2.1 %collective-permute-done.9.zhi = f32[32,128]{1,0:T(8,128)S(1)} collective-permute-done((f32[32,128]{1,0:T(8,128)S(1)}, f32[32,128]{1,0:T(8,128)S(1)}, u32[]{:S(2)}, u32[]{:S(2)}) %collective-permute-start.9) | collective-permute-done | bytes 16416 | tf_op jit(solution)/shard_map/ppermute | solution.py:989
  95.1 0.3 shard_map.86
  95.4 9.1 %all_to_all.41 = f32[8,1,128]{2,1,0:T(1,128)S(1)} all-to-all(f32[8,1,128]{2,1,0:T(1,128)S(1)} %bitcast.24), channel_id=1, replica_groups=mesh['gx'=8,'gy'=64] {'gx'}, dimensions={0} | all-to-all | bytes 8192 | tf_op jit(solution)/shard_map/all_to_all | solution.py:1079
  104.5 16.3 %all_to_all.42 = f32[64,1,128]{2,1,0:T(1,128)S(1)} all-to-all(f32[64,1,128]{2,1,0:T(1,128)S(1)} %broadcast_in_dim.2), channel_id=1, replica_groups=mesh['gx'=8,'gy'=64] {'gy'}, dimensions={0} | all-to-all | bytes 65536 | tf_op jit(solution)/shard_map/all_to_all | solution.py:1081
  120.8 0.8 shard_map.87
  (3 shorter events, 0.1 us)
Async XLA Ops:
  0.6 25.2 %copy-start.1 = (bf16[1008,384]{1,0:T(8,128)(2,1)S(1)}, bf16[1008,384]{1,0:T(8,128)(2,1)}, u32[]{:S(2)}) copy-start(bf16[1008,384]{1,0:T(8,128)(2,1)} %constant.30.clone.tables) | copy-start | bytes 2322436
  2.5 23.4 %copy-start = (f32[664,128]{1,0:T(8,128)S(1)}, f32[664,128]{1,0:T(8,128)}, u32[]{:S(2)}) copy-start(f32[664,128]{1,0:T(8,128)} %constant.29.clone.packed_in.packed) | copy-start | bytes 1019908
  2.5 6.3 %collective-permute-start = (f32[3,32,128]{2,1,0:T(8,128)S(1)}, f32[3,32,128]{2,1,0:T(8,128)S(1)}, u32[]{:S(2)}, u32[]{:S(2)}) collective-permute-start(f32[3,32,128]{2,1,0:T(8,128)S(1)} %get-tuple-element.31), channel_id=1, source_target_pairs={{0,64},{64,128},{128,192},{192,256},{256,320},{320,384},{384,448},... | collective-permute-start | bytes 147464 | tf_op jit(solution)/shard_map/ppermute | solution.py:989
  7.5 5.5 %collective-permute-start.1 = (f32[3,32,128]{2,1,0:T(8,128)S(1)}, f32[3,32,128]{2,1,0:T(8,128)S(1)}, u32[]{:S(2)}, u32[]{:S(2)}) collective-permute-start(f32[3,32,128]{2,1,0:T(8,128)S(1)} %get-tuple-element.32), channel_id=1, source_target_pairs={{64,0},{128,64},{192,128},{256,192},{320,256},{384,320},{448,384},... | collective-permute-start | bytes 147464 | tf_op jit(solution)/shard_map/ppermute | solution.py:989
  13.0 8.5 %collective-permute-start.2 = (f32[12,48,128]{2,1,0:T(8,128)S(1)}, f32[12,48,128]{2,1,0:T(8,128)S(1)}, u32[]{:S(2)}, u32[]{:S(2)}) collective-permute-start(f32[12,48,128]{2,1,0:T(8,128)S(1)} %get-tuple-element.33), channel_id=1, source_target_pairs={{0,1},{1,2},{2,3},{3,4},{4,5},{5,6},{6,7},{7,8},{8,9},{9,10},{10,1... | collective-permute-start | bytes 884744 | tf_op jit(solution)/shard_map/ppermute | solution.py:989
  17.8 8.0 %collective-permute-start.3 = (f32[12,48,128]{2,1,0:T(8,128)S(1)}, f32[12,48,128]{2,1,0:T(8,128)S(1)}, u32[]{:S(2)}, u32[]{:S(2)}) collective-permute-start(f32[12,48,128]{2,1,0:T(8,128)S(1)} %get-tuple-element.34), channel_id=1, source_target_pairs={{1,0},{2,1},{3,2},{4,3},{5,4},{6,5},{7,6},{8,7},{9,8},{10,9},{11,1... | collective-permute-start | bytes 884744 | tf_op jit(solution)/shard_map/ppermute | solution.py:989
  28.6 6.8 %collective-permute-start.4 = (f32[64,128]{1,0:T(8,128)S(1)}, f32[64,128]{1,0:T(8,128)S(1)}, u32[]{:S(2)}, u32[]{:S(2)}) collective-permute-start(f32[64,128]{1,0:T(8,128)S(1)} %get-tuple-element.39), channel_id=1, source_target_pairs={{0,64},{64,128},{128,192},{192,256},{256,320},{320,384},{384,448},... | collective-permute-start | bytes 98312 | tf_op jit(solution)/shard_map/ppermute | solution.py:989
  32.6 6.5 %collective-permute-start.5 = (f32[64,128]{1,0:T(8,128)S(1)}, f32[64,128]{1,0:T(8,128)S(1)}, u32[]{:S(2)}, u32[]{:S(2)}) collective-permute-start(f32[64,128]{1,0:T(8,128)S(1)} %get-tuple-element.40), channel_id=1, source_target_pairs={{64,0},{128,64},{192,128},{256,192},{320,256},{384,320},{448,384},... | collective-permute-start | bytes 98312 | tf_op jit(solution)/shard_map/ppermute | solution.py:989
  40.9 44.8 %collective-permute-start.6 = (f32[8,64,128]{2,1,0:T(8,128)S(1)}, f32[8,64,128]{2,1,0:T(8,128)S(1)}, u32[]{:S(2)}, u32[]{:S(2)}) collective-permute-start(f32[8,64,128]{2,1,0:T(8,128)S(1)} %get-tuple-element.44), channel_id=1, source_target_pairs={{0,64},{64,128},{128,192},{192,256},{256,320},{320,384},{384,448},... | collective-permute-start | bytes 786440 | tf_op jit(solution)/shard_map/ppermute | solution.py:989
  45.8 40.0 %collective-permute-start.7 = (f32[8,64,128]{2,1,0:T(8,128)S(1)}, f32[8,64,128]{2,1,0:T(8,128)S(1)}, u32[]{:S(2)}, u32[]{:S(2)}) collective-permute-start(f32[8,64,128]{2,1,0:T(8,128)S(1)} %get-tuple-element.45), channel_id=1, source_target_pairs={{64,0},{128,64},{192,128},{256,192},{320,256},{384,320},{448,384},... | collective-permute-start | bytes 786440 | tf_op jit(solution)/shard_map/ppermute | solution.py:989
  88.4 4.6 %collective-permute-start.8 = (f32[32,128]{1,0:T(8,128)S(1)}, f32[32,128]{1,0:T(8,128)S(1)}, u32[]{:S(2)}, u32[]{:S(2)}) collective-permute-start(f32[32,128]{1,0:T(8,128)S(1)} %get-tuple-element.50), channel_id=1, source_target_pairs={{0,64},{64,128},{128,192},{192,256},{256,320},{320,384},{384,448},... | collective-permute-start | bytes 49160 | tf_op jit(solution)/shard_map/ppermute | solution.py:989
  90.6 4.5 %collective-permute-start.9 = (f32[32,128]{1,0:T(8,128)S(1)}, f32[32,128]{1,0:T(8,128)S(1)}, u32[]{:S(2)}, u32[]{:S(2)}) collective-permute-start(f32[32,128]{1,0:T(8,128)S(1)} %get-tuple-element.51), channel_id=1, source_target_pairs={{64,0},{128,64},{192,128},{256,192},{320,256},{384,320},{448,384},... | collective-permute-start | bytes 49160 | tf_op jit(solution)/shard_map/ppermute | solution.py:989

commit v11 on v10

--- a/solution.py
+++ b/solution.py
@@ -632,16 +632,25 @@
 
 
 def invert(blocks, sub):
-    for k in range(8):
-        pivot = 1.0 / blocks[k][k : k + 1]
-        scaled = jnp.where(sub == k, pivot, blocks[k] * pivot)
+    for k in range(0, 8, 2):
+        first, second = blocks[k], blocks[k + 1]
+        a, b = first[k : k + 1], first[k + 1 : k + 2]
+        c, d = second[k : k + 1], second[k + 1 : k + 2]
+        scale = 1.0 / (a * d - b * c)
+        first = jnp.where(sub == k, 1.0, jnp.where(sub == k + 1, 0.0, first))
+        second = jnp.where(sub == k + 1, 1.0, jnp.where(sub == k, 0.0, second))
+        low = (d * scale) * first - (b * scale) * second
+        high = (a * scale) * second - (c * scale) * first
+        pivots = (sub == k) | (sub == k + 1)
         rows = []
         for r in range(8):
             if r == k:
-                rows.append(scaled)
+                rows.append(low)
+            elif r == k + 1:
+                rows.append(high)
             else:
-                rest = jnp.where(sub == k, 0.0, blocks[r])
-                rows.append(rest - blocks[r][k : k + 1] * scaled)
+                rest = jnp.where(pivots, 0.0, blocks[r])
+                rows.append(rest - blocks[r][k : k + 1] * low - blocks[r][k + 1 : k + 2] * high)
         blocks = rows
     return blocks
 
@@ -1048,8 +1057,9 @@
         [near],
         [packed, stat, flux, w, wlo, whi],
     )
+    gathered = lax.all_to_all(stat, "gx", 0, 0, tiled=True)
+    gathered, zlo, zhi = lax.optimization_barrier((gathered, zlo, zhi))
     zlo, zhi = shift("gx", zlo, zhi)
-    gathered = lax.all_to_all(stat, "gx", 0, 0, tiled=True)
     (column,) = run(column_kernel, [(count_gy, LANES)], [], [gathered])
     gathered = lax.all_to_all(column, "gy", 0, 0, tiled=True)
     (coarse,) = run(

time: 122 us -> 122 us (level)
  no operation moved by 1% of the time
where the time goes in v11:
time: 122 us
  blocking collectives  61.2 us (50%)
  starting transfers between devices  27.7 us (23%)
  Pallas kernels  16.3 us (13%)
  waiting for transfers between devices  15.7 us (13%)
    all_to_all x1, blocking collectives, body(): gathered = lax.all_to_all(column, 'gy', 0, 0, tiled=True)  22 us
    ppermute x5, starting transfers between devices, shift(): lax.ppermute(high_face, axis, forward)  20.3 us
    pallas_call x11, Pallas kernels, run(): pl.pallas_call(kernel, out_shape=[jax.ShapeDtypeStruct(out, F32) for out...  16.3 us
    all_to_all x1, blocking collectives, body(): wide = lax.all_to_all(wide, 'gy', 0, 0, tiled=True)  16.3 us
    ppermute x5, waiting for transfers between devices, shift(): lax.ppermute(low_face, axis, backward)  14.4 us
    all_to_all x1, blocking collectives, body(): gathered = lax.all_to_all(stat, 'gx', 0, 0, tiled=True)  12.7 us
    all_to_all x1, blocking collectives, body(): tile = lax.all_to_all(sums, 'gx', 0, 0, tiled=True)  10.3 us
    ppermute x5, starting transfers between devices, shift(): lax.ppermute(low_face, axis, backward)  7.4 us
  transfers between devices with their start and end apart: 10, of which 5 were waited for; matrix products, arithmetic and copies ran while one was open for 0% of the time, Pallas kernels for 5%

profile of v11, /device:TPU:1, one launch (start us, length us, event | category | flops | bytes accessed | tf_op | source)
XLA Modules:
  0.0 121.8 jit_solution(7334233993774897190)
XLA Ops:
  0.6 0.0 copy-start.1
  0.6 1.8 %shard_map.77 = (f32[8,32,128]{2,1,0:T(8,128)S(1)}, f32[8,32,128]{2,1,0:T(8,128)S(1)}, f32[3,32,128]{2,1,0:T(8,128)S(1)}, f32[3,32,128]{2,1,0:T(8,128)S(1)}, f32[8,128]{1,0:T(8,128)S(1)}) custom-call(f32[8,32,128]{2,1,0:T(8,128)} %lev_in.1, f32[3,8,32,128]{3,2,1,0:T(8,128)} %vel_in.1, f32[8,32,128]{2,1,0:T(8,128)} %src_in.1, ...), custom_call_target="tpu_custom_call" | custom-call | flops 1000000 | bytes 729088 | tf_op jit(solution)/shard_map/pallas_call | solution.py:982
  2.5 0.0 copy-start
  2.5 5.0 %collective-permute-start = (f32[3,32,128]{2,1,0:T(8,128)S(1)}, f32[3,32,128]{2,1,0:T(8,128)S(1)}, u32[]{:S(2)}, u32[]{:S(2)}) collective-permute-start(f32[3,32,128]{2,1,0:T(8,128)S(1)} %get-tuple-element.34), channel_id=1, source_target_pairs={{0,64},{64,128},{128,192},{192,256},{256,320},{320,384},{384,448},... | collective-permute-start | bytes 147464 | tf_op jit(solution)/shard_map/ppermute | solution.py:998
  7.5 1.3 %collective-permute-start.1 = (f32[3,32,128]{2,1,0:T(8,128)S(1)}, f32[3,32,128]{2,1,0:T(8,128)S(1)}, u32[]{:S(2)}, u32[]{:S(2)}) collective-permute-start(f32[3,32,128]{2,1,0:T(8,128)S(1)} %get-tuple-element.35), channel_id=1, source_target_pairs={{64,0},{128,64},{192,128},{256,192},{320,256},{384,320},{448,384},... | collective-permute-start | bytes 147464 | tf_op jit(solution)/shard_map/ppermute | solution.py:998
  8.8 0.0 collective-permute-done.low_z.zlo
  8.8 4.2 %collective-permute-done.1.high_z.zhi = f32[3,32,128]{2,1,0:T(8,128)S(1)} collective-permute-done((f32[3,32,128]{2,1,0:T(8,128)S(1)}, f32[3,32,128]{2,1,0:T(8,128)S(1)}, u32[]{:S(2)}, u32[]{:S(2)}) %collective-permute-start.1) | collective-permute-done | bytes 49184 | tf_op jit(solution)/shard_map/ppermute | solution.py:998
  13.0 4.8 %collective-permute-start.2 = (f32[12,48,128]{2,1,0:T(8,128)S(1)}, f32[12,48,128]{2,1,0:T(8,128)S(1)}, u32[]{:S(2)}, u32[]{:S(2)}) collective-permute-start(f32[12,48,128]{2,1,0:T(8,128)S(1)} %get-tuple-element.36), channel_id=1, source_target_pairs={{0,1},{1,2},{2,3},{3,4},{4,5},{5,6},{6,7},{7,8},{8,9},{9,10},{10,1... | collective-permute-start | bytes 884744 | tf_op jit(solution)/shard_map/ppermute | solution.py:998
  17.8 2.2 %collective-permute-start.3 = (f32[12,48,128]{2,1,0:T(8,128)S(1)}, f32[12,48,128]{2,1,0:T(8,128)S(1)}, u32[]{:S(2)}, u32[]{:S(2)}) collective-permute-start(f32[12,48,128]{2,1,0:T(8,128)S(1)} %get-tuple-element.37), channel_id=1, source_target_pairs={{1,0},{2,1},{3,2},{4,3},{5,4},{6,5},{7,6},{8,7},{9,8},{10,9},{11,1... | collective-permute-start | bytes 884744 | tf_op jit(solution)/shard_map/ppermute | solution.py:998
  20.1 0.1 stack.35.near
  20.2 1.3 %collective-permute-done.2.ylo = f32[12,48,128]{2,1,0:T(8,128)S(1)} collective-permute-done((f32[12,48,128]{2,1,0:T(8,128)S(1)}, f32[12,48,128]{2,1,0:T(8,128)S(1)}, u32[]{:S(2)}, u32[]{:S(2)}) %collective-permute-start.2) | collective-permute-done | bytes 294944 | tf_op jit(solution)/shard_map/ppermute | solution.py:998
  21.5 4.4 %collective-permute-done.3.yhi = f32[12,48,128]{2,1,0:T(8,128)S(1)} collective-permute-done((f32[12,48,128]{2,1,0:T(8,128)S(1)}, f32[12,48,128]{2,1,0:T(8,128)S(1)}, u32[]{:S(2)}, u32[]{:S(2)}) %collective-permute-start.3) | collective-permute-done | bytes 294944 | tf_op jit(solution)/shard_map/ppermute | solution.py:998
  25.9 0.0 copy-done.1
  25.9 0.0 copy-done
  25.9 2.7 %shard_map.80 = (f32[8,64,128]{2,1,0:T(8,128)S(1)}, f32[64,128]{1,0:T(8,128)S(1)}, f32[64,128]{1,0:T(8,128)S(1)}) custom-call(f32[8]{0:T(128)S(1)} %stack.35.near, f32[664,128]{1,0:T(8,128)S(1)} %copy-done, bf16[1008,384]{1,0:T(8,128)(2,1)S(1)} %copy-done.1, f32[8,32,128]{2,1,0:T(8,128)S(1)} %get-tuple-element.32.b, ...), custom_call_target="tpu_custom_call" | custom-call | flops 1000000 | bytes 655360 | tf_op jit(solution)/shard_map/pallas_call | solution.py:982
  28.6 4.0 %collective-permute-start.4 = (f32[64,128]{1,0:T(8,128)S(1)}, f32[64,128]{1,0:T(8,128)S(1)}, u32[]{:S(2)}, u32[]{:S(2)}) collective-permute-start(f32[64,128]{1,0:T(8,128)S(1)} %get-tuple-element.42), channel_id=1, source_target_pairs={{0,64},{64,128},{128,192},{192,256},{256,320},{320,384},{384,448},... | collective-permute-start | bytes 98312 | tf_op jit(solution)/shard_map/ppermute | solution.py:998
  32.6 1.3 %collective-permute-start.5 = (f32[64,128]{1,0:T(8,128)S(1)}, f32[64,128]{1,0:T(8,128)S(1)}, u32[]{:S(2)}, u32[]{:S(2)}) collective-permute-start(f32[64,128]{1,0:T(8,128)S(1)} %get-tuple-element.43), channel_id=1, source_target_pairs={{64,0},{128,64},{192,128},{256,192},{320,256},{384,320},{448,384},... | collective-permute-start | bytes 98312 | tf_op jit(solution)/shard_map/ppermute | solution.py:998
  33.9 1.5 %shard_map.79 = (f32[8,32,128]{2,1,0:T(8,128)}, f32[8,64,128]{2,1,0:T(8,128)S(1)}, f32[1,128]{1,0:T(1,128)S(1)}) custom-call(f32[8]{0:T(128)S(1)} %stack.35.near, f32[8,128]{1,0:T(8,128)S(1)} %get-tuple-element.31.solid, f32[664,128]{1,0:T(8,128)S(1)} %copy-done, f32[8,32,128]{2,1,0:T(8,128)S(1)} %get-tuple-element.32.b, ...), custom_call_target="tpu_custom_call" | custom-call | flops 20000000 | bytes 787456 | tf_op jit(solution)/shard_map/pallas_call | solution.py:982
  35.4 0.0 collective-permute-done.4.zlo
  35.4 3.7 %collective-permute-done.5.zhi = f32[64,128]{1,0:T(8,128)S(1)} collective-permute-done((f32[64,128]{1,0:T(8,128)S(1)}, f32[64,128]{1,0:T(8,128)S(1)}, u32[]{:S(2)}, u32[]{:S(2)}) %collective-permute-start.5) | collective-permute-done | bytes 32800 | tf_op jit(solution)/shard_map/ppermute | solution.py:998
  39.1 1.8 %shard_map.81 = (f32[8,64,128]{2,1,0:T(8,128)S(1)}, f32[8,64,128]{2,1,0:T(8,128)S(1)}, f32[8,64,128]{2,1,0:T(8,128)S(1)}, f32[8,64,128]{2,1,0:T(8,128)S(1)}, f32[8,128]{1,0:T(8,128)S(1)}) custom-call(f32[8]{0:T(128)S(1)} %stack.35.near, f32[664,128]{1,0:T(8,128)S(1)} %copy-done, f32[1,128]{1,0:T(1,128)S(1)} %get-tuple-element.40.stat_in, ...), custom_call_target="tpu_custom_call" | custom-call | flops 1000000 | bytes 2105344 | tf_op jit(solution)/shard_map/pallas_call | solution.py:982
  40.9 12.7 %all_to_all.40 = f32[8,1,128]{2,1,0:T(1,128)S(1)} all-to-all(f32[8,1,128]{2,1,0:T(1,128)S(1)} %bitcast.26), channel_id=1, replica_groups=mesh['gx'=8,'gy'=64] {'gx'}, dimensions={0} | all-to-all | bytes 8192 | tf_op jit(solution)/shard_map/all_to_all | solution.py:1060
  53.6 2.2 %collective-permute-start.6 = (f32[8,64,128]{2,1,0:T(8,128)S(1)}, f32[8,64,128]{2,1,0:T(8,128)S(1)}, u32[]{:S(2)}, u32[]{:S(2)}) collective-permute-start(f32[8,64,128]{2,1,0:T(8,128)S(1)} %get-tuple-element.50), channel_id=1, source_target_pairs={{0,64},{64,128},{128,192},{192,256},{256,320},{320,384},{384,448},... | collective-permute-start | bytes 786440 | tf_op jit(solution)/shard_map/ppermute | solution.py:998
  55.8 1.3 %collective-permute-start.7 = (f32[8,64,128]{2,1,0:T(8,128)S(1)}, f32[8,64,128]{2,1,0:T(8,128)S(1)}, u32[]{:S(2)}, u32[]{:S(2)}) collective-permute-start(f32[8,64,128]{2,1,0:T(8,128)S(1)} %get-tuple-element.51), channel_id=1, source_target_pairs={{64,0},{128,64},{192,128},{256,192},{320,256},{384,320},{448,384},... | collective-permute-start | bytes 786440 | tf_op jit(solution)/shard_map/ppermute | solution.py:998
  57.1 0.3 shard_map.82
  57.4 22.0 %all_to_all.41 = f32[64,1,128]{2,1,0:T(1,128)S(1)} all-to-all(f32[64,1,128]{2,1,0:T(1,128)S(1)} %bitcast.22), channel_id=1, replica_groups=mesh['gx'=8,'gy'=64] {'gy'}, dimensions={0} | all-to-all | bytes 65536 | tf_op jit(solution)/shard_map/all_to_all | solution.py:1064
  79.4 3.3 %shard_map.83.coarse = f32[32,128]{1,0:T(8,128)S(1)} custom-call(f32[8]{0:T(128)S(1)} %stack.35.near, f32[64,128]{1,0:T(8,128)S(1)} %bitcast.23), custom_call_target="tpu_custom_call" | custom-call | flops 1000000 | bytes 32768 | tf_op jit(solution)/shard_map/pallas_call | solution.py:982
  82.7 0.0 collective-permute-done.6.ylo
  82.7 0.0 collective-permute-done.7.yhi
  82.7 2.6 %shard_map.84 = (f32[8,32,128]{2,1,0:T(8,128)S(1)}, f32[8,32,128]{2,1,0:T(8,128)S(1)}, f32[8,32,128]{2,1,0:T(8,128)S(1)}, f32[32,128]{1,0:T(8,128)S(1)}, f32[32,128]{1,0:T(8,128)S(1)}) custom-call(f32[8]{0:T(128)S(1)} %stack.35.near, f32[664,128]{1,0:T(8,128)S(1)} %copy-done, bf16[1008,384]{1,0:T(8,128)(2,1)S(1)} %copy-done.1, ...), custom_call_target="tpu_custom_call" | custom-call | flops 1000000 | bytes 851968 | tf_op jit(solution)/shard_map/pallas_call | solution.py:982
  85.4 4.3 %collective-permute-start.8 = (f32[32,128]{1,0:T(8,128)S(1)}, f32[32,128]{1,0:T(8,128)S(1)}, u32[]{:S(2)}, u32[]{:S(2)}) collective-permute-start(f32[32,128]{1,0:T(8,128)S(1)} %get-tuple-element.56), channel_id=1, source_target_pairs={{0,64},{64,128},{128,192},{192,256},{256,320},{320,384},{384,448},... | collective-permute-start | bytes 49160 | tf_op jit(solution)/shard_map/ppermute | solution.py:998
  89.6 1.3 %collective-permute-start.9 = (f32[32,128]{1,0:T(8,128)S(1)}, f32[32,128]{1,0:T(8,128)S(1)}, u32[]{:S(2)}, u32[]{:S(2)}) collective-permute-start(f32[32,128]{1,0:T(8,128)S(1)} %get-tuple-element.57), channel_id=1, source_target_pairs={{64,0},{128,64},{192,128},{256,192},{320,256},{384,320},{448,384},... | collective-permute-start | bytes 49160 | tf_op jit(solution)/shard_map/ppermute | solution.py:998
  90.9 1.0 shard_map.85
  92.0 0.0 collective-permute-done.8.zlo
  92.0 2.1 %collective-permute-done.9.zhi = f32[32,128]{1,0:T(8,128)S(1)} collective-permute-done((f32[32,128]{1,0:T(8,128)S(1)}, f32[32,128]{1,0:T(8,128)S(1)}, u32[]{:S(2)}, u32[]{:S(2)}) %collective-permute-start.9) | collective-permute-done | bytes 16416 | tf_op jit(solution)/shard_map/ppermute | solution.py:998
  94.1 0.3 shard_map.86
  94.4 10.3 %all_to_all.42 = f32[8,1,128]{2,1,0:T(1,128)S(1)} all-to-all(f32[8,1,128]{2,1,0:T(1,128)S(1)} %bitcast.24), channel_id=1, replica_groups=mesh['gx'=8,'gy'=64] {'gx'}, dimensions={0} | all-to-all | bytes 8192 | tf_op jit(solution)/shard_map/all_to_all | solution.py:1089
  104.8 16.3 %all_to_all.43 = f32[64,1,128]{2,1,0:T(1,128)S(1)} all-to-all(f32[64,1,128]{2,1,0:T(1,128)S(1)} %broadcast_in_dim.2), channel_id=1, replica_groups=mesh['gx'=8,'gy'=64] {'gy'}, dimensions={0} | all-to-all | bytes 65536 | tf_op jit(solution)/shard_map/all_to_all | solution.py:1091
  121.0 0.8 shard_map.87
  (3 shorter events, 0.1 us)
Async XLA Ops:
  0.6 25.2 %copy-start.1 = (bf16[1008,384]{1,0:T(8,128)(2,1)S(1)}, bf16[1008,384]{1,0:T(8,128)(2,1)}, u32[]{:S(2)}) copy-start(bf16[1008,384]{1,0:T(8,128)(2,1)} %constant.30.clone.tables) | copy-start | bytes 2322436
  2.5 23.4 %copy-start = (f32[664,128]{1,0:T(8,128)S(1)}, f32[664,128]{1,0:T(8,128)}, u32[]{:S(2)}) copy-start(f32[664,128]{1,0:T(8,128)} %constant.29.clone.packed_in.packed) | copy-start | bytes 1019908
  2.5 6.3 %collective-permute-start = (f32[3,32,128]{2,1,0:T(8,128)S(1)}, f32[3,32,128]{2,1,0:T(8,128)S(1)}, u32[]{:S(2)}, u32[]{:S(2)}) collective-permute-start(f32[3,32,128]{2,1,0:T(8,128)S(1)} %get-tuple-element.34), channel_id=1, source_target_pairs={{0,64},{64,128},{128,192},{192,256},{256,320},{320,384},{384,448},... | collective-permute-start | bytes 147464 | tf_op jit(solution)/shard_map/ppermute | solution.py:998
  7.5 5.5 %collective-permute-start.1 = (f32[3,32,128]{2,1,0:T(8,128)S(1)}, f32[3,32,128]{2,1,0:T(8,128)S(1)}, u32[]{:S(2)}, u32[]{:S(2)}) collective-permute-start(f32[3,32,128]{2,1,0:T(8,128)S(1)} %get-tuple-element.35), channel_id=1, source_target_pairs={{64,0},{128,64},{192,128},{256,192},{320,256},{384,320},{448,384},... | collective-permute-start | bytes 147464 | tf_op jit(solution)/shard_map/ppermute | solution.py:998
  13.0 8.5 %collective-permute-start.2 = (f32[12,48,128]{2,1,0:T(8,128)S(1)}, f32[12,48,128]{2,1,0:T(8,128)S(1)}, u32[]{:S(2)}, u32[]{:S(2)}) collective-permute-start(f32[12,48,128]{2,1,0:T(8,128)S(1)} %get-tuple-element.36), channel_id=1, source_target_pairs={{0,1},{1,2},{2,3},{3,4},{4,5},{5,6},{6,7},{7,8},{8,9},{9,10},{10,1... | collective-permute-start | bytes 884744 | tf_op jit(solution)/shard_map/ppermute | solution.py:998
  17.8 8.0 %collective-permute-start.3 = (f32[12,48,128]{2,1,0:T(8,128)S(1)}, f32[12,48,128]{2,1,0:T(8,128)S(1)}, u32[]{:S(2)}, u32[]{:S(2)}) collective-permute-start(f32[12,48,128]{2,1,0:T(8,128)S(1)} %get-tuple-element.37), channel_id=1, source_target_pairs={{1,0},{2,1},{3,2},{4,3},{5,4},{6,5},{7,6},{8,7},{9,8},{10,9},{11,1... | collective-permute-start | bytes 884744 | tf_op jit(solution)/shard_map/ppermute | solution.py:998
  28.6 6.8 %collective-permute-start.4 = (f32[64,128]{1,0:T(8,128)S(1)}, f32[64,128]{1,0:T(8,128)S(1)}, u32[]{:S(2)}, u32[]{:S(2)}) collective-permute-start(f32[64,128]{1,0:T(8,128)S(1)} %get-tuple-element.42), channel_id=1, source_target_pairs={{0,64},{64,128},{128,192},{192,256},{256,320},{320,384},{384,448},... | collective-permute-start | bytes 98312 | tf_op jit(solution)/shard_map/ppermute | solution.py:998
  32.6 6.5 %collective-permute-start.5 = (f32[64,128]{1,0:T(8,128)S(1)}, f32[64,128]{1,0:T(8,128)S(1)}, u32[]{:S(2)}, u32[]{:S(2)}) collective-permute-start(f32[64,128]{1,0:T(8,128)S(1)} %get-tuple-element.43), channel_id=1, source_target_pairs={{64,0},{128,64},{192,128},{256,192},{320,256},{384,320},{448,384},... | collective-permute-start | bytes 98312 | tf_op jit(solution)/shard_map/ppermute | solution.py:998
  53.6 29.1 %collective-permute-start.6 = (f32[8,64,128]{2,1,0:T(8,128)S(1)}, f32[8,64,128]{2,1,0:T(8,128)S(1)}, u32[]{:S(2)}, u32[]{:S(2)}) collective-permute-start(f32[8,64,128]{2,1,0:T(8,128)S(1)} %get-tuple-element.50), channel_id=1, source_target_pairs={{0,64},{64,128},{128,192},{192,256},{256,320},{320,384},{384,448},... | collective-permute-start | bytes 786440 | tf_op jit(solution)/shard_map/ppermute | solution.py:998
  55.8 26.9 %collective-permute-start.7 = (f32[8,64,128]{2,1,0:T(8,128)S(1)}, f32[8,64,128]{2,1,0:T(8,128)S(1)}, u32[]{:S(2)}, u32[]{:S(2)}) collective-permute-start(f32[8,64,128]{2,1,0:T(8,128)S(1)} %get-tuple-element.51), channel_id=1, source_target_pairs={{64,0},{128,64},{192,128},{256,192},{320,256},{384,320},{448,384},... | collective-permute-start | bytes 786440 | tf_op jit(solution)/shard_map/ppermute | solution.py:998
  85.4 6.6 %collective-permute-start.8 = (f32[32,128]{1,0:T(8,128)S(1)}, f32[32,128]{1,0:T(8,128)S(1)}, u32[]{:S(2)}, u32[]{:S(2)}) collective-permute-start(f32[32,128]{1,0:T(8,128)S(1)} %get-tuple-element.56), channel_id=1, source_target_pairs={{0,64},{64,128},{128,192},{192,256},{256,320},{320,384},{384,448},... | collective-permute-start | bytes 49160 | tf_op jit(solution)/shard_map/ppermute | solution.py:998
  89.6 4.5 %collective-permute-start.9 = (f32[32,128]{1,0:T(8,128)S(1)}, f32[32,128]{1,0:T(8,128)S(1)}, u32[]{:S(2)}, u32[]{:S(2)}) collective-permute-start(f32[32,128]{1,0:T(8,128)S(1)} %get-tuple-element.57), channel_id=1, source_target_pairs={{64,0},{128,64},{192,128},{256,192},{320,256},{384,320},{448,384},... | collective-permute-start | bytes 49160 | tf_op jit(solution)/shard_map/ppermute | solution.py:998

commit v12 on v11

--- a/solution.py
+++ b/solution.py
@@ -665,14 +665,21 @@
     return rows
 
 
-def matvec(terms, sub):
-    result = jnp.zeros_like(terms[0][1])
+def multiply_turned(left, right):
+    rows = []
     for r in range(8):
-        product = terms[0][0][r] * terms[0][1]
-        for blocks, column in terms[1:]:
-            product = product + blocks[r] * column
-        result = jnp.where(sub == r, jnp.sum(product, axis=0, keepdims=True), result)
-    return result
+        total = left[0][r : r + 1] * right[0]
+        for k in range(1, 8):
+            total = total + left[k][r : r + 1] * right[k]
+        rows.append(total)
+    return rows
+
+
+def apply_turned(blocks, column):
+    total = blocks[0] * column[0:1]
+    for k in range(1, 8):
+        total = total + blocks[k] * column[k : k + 1]
+    return total
 
 
 def coarse_operator(c, count, sums_z, couplings_z, inside_y, interface_y):
@@ -756,38 +763,42 @@
         row = jnp.where(sub == r + 1, -back_z, row)
         row = jnp.where(sub == r - 1, -link_z, row)
         blocks.append(row)
-    inverse = invert(blocks, sub)
-    down = [-back_y[r : r + 1] * move(inverse[r], 0, -1) for r in range(8)]
-    up = [-link_y[r : r + 1] * move(inverse[r], 0, 1) for r in range(8)]
-    levels = [(1, down, up)]
-    link_before, link_after = move(link_y, 0, -1), move(back_y, 0, 1)
-    blocks = [blocks[r] + down[r] * link_before + up[r] * link_after for r in range(8)]
-    lower = [row * move(back_y, 0, -1) for row in down]
-    upper = [row * move(link_y, 0, 1) for row in up]
-    step = 2
+
+    levels = []
+    step = 1
     while step < count:
         inverse = invert(blocks, sub)
-        down = multiply(lower, [move(row, 0, -step) for row in inverse])
-        up = multiply(upper, [move(row, 0, step) for row in inverse])
-        levels.append((step, down, up))
-        before_u = multiply(down, [move(row, 0, -step) for row in upper])
-        after_l = multiply(up, [move(row, 0, step) for row in lower])
+        if step == 1:
+            up, low = -link_y, -back_y
+            solved_up = [row * up for row in inverse]
+            solved_low = [row * low for row in inverse]
+            pull_up = [up[r : r + 1] * solved_up[r] for r in range(8)]
+            pull_low = [low[r : r + 1] * solved_low[r] for r in range(8)]
+            new_low = [up[r : r + 1] * solved_low[r] for r in range(8)]
+            new_up = [low[r : r + 1] * solved_up[r] for r in range(8)]
+        else:
+            solved_up, solved_low = multiply(inverse, upper), multiply(inverse, lower)
+            pull_up = multiply_turned(solved_up, upper)
+            pull_low = multiply_turned(solved_low, lower)
+            if 2 * step < count:
+                new_low = multiply_turned(solved_up, lower)
+                new_up = multiply_turned(solved_low, upper)
+        levels.append((step, solved_up, solved_low))
+        blocks = [
+            blocks[r] - move(pull_up[r], 0, -step) - move(pull_low[r], 0, step) for r in range(8)
+        ]
         if 2 * step < count:
-            new_lower = multiply(down, [move(row, 0, -step) for row in lower])
-            new_upper = multiply(up, [move(row, 0, step) for row in upper])
-            lower = [-row for row in new_lower]
-            upper = [-row for row in new_upper]
-        blocks = [blocks[r] - before_u[r] - after_l[r] for r in range(8)]
+            lower = [-move(row, 0, -step) for row in new_low]
+            upper = [-move(row, 0, step) for row in new_up]
         step *= 2
     inverse = invert(blocks, sub)
 
     def solve(column):
-        for distance, down, up in levels:
-            pulled = matvec(
-                [(down, move(column, 0, -distance)), (up, move(column, 0, distance))], sub
-            )
-            column = column - pulled
-        return matvec([(inverse, column)], sub)
+        for distance, solved_up, solved_low in levels:
+            before = move(apply_turned(solved_up, column), 0, -distance)
+            after = move(apply_turned(solved_low, column), 0, distance)
+            column = column - before - after
+        return apply_turned(inverse, column)
 
     first = solve(value(1))
     totals = coarse_operator(
@@ -803,17 +814,11 @@
     totals = totals + jnp.where(lane > 0, move(value(4), 0, -1), 0.0)
     totals = jnp.where(lane < count, totals, 0.0)
     second = solve(totals)
-    mine = (sub.astype(F32) == near[4]) & (lane.astype(F32) == near[5])
-
-    def store(at, solved, reach):
-        for a in range(-reach, reach + 1):
-            for b in range(-1, 2):
-                picked = jnp.sum(jnp.where(mine, move(solved, a, b), 0.0))
-                row = at + 3 * (a + reach) + b + 1
-                out_ref[row : row + 1] = jnp.full((1, lanes), picked)
-
-    store(0, first, 2)
-    store(16, second, 1)
+    gx = near[4].astype(jnp.int32)
+    gy = near[5].astype(jnp.int32)
+    for at, solved in ((0, first), (8, second)):
+        turned_z = pltpu.roll(solved, (10 - gx) % 8, 0)
+        out_ref[at : at + 8] = pltpu.roll(turned_z, (lanes + 1 - gy) % lanes, 1)
 
 
 def coarse_columns(near, coarse, start, count):
@@ -825,11 +830,9 @@
     edge = jnp.where(row == RING - 1, 0.5 * has_low, edge)
     edge = jnp.where(row == RING + ROWS, 0.5 * has_high, edge)
     columns = []
-    for a in range(count):
-        at = start + 3 * a
-        columns.append(
-            below * coarse[at : at + 1] + edge * coarse[at + 1 : at + 2] + above * coarse[at + 2 : at + 3]
-        )
+    for a in range(start, start + count):
+        low, own, high = (coarse[a : a + 1, b : b + 1] for b in range(3))
+        columns.append(below * low + edge * own + above * high)
     return columns
 
 
@@ -907,7 +910,7 @@
 
 
 def second_kernel(near, packed, coarse, flux, b, y, z, w, x_ref, kx_ref, stat):
-    columns = [column[RING : RING + ROWS] for column in coarse_columns(near, coarse, 16, 3)]
+    columns = [column[RING : RING + ROWS] for column in coarse_columns(near, coarse, 9, 3)]
     field = add_coarse(w[...], coarse_planes(columns, 1.0 - near[0], 1.0 - near[1]))
     x_ref[...] = field
     fluxes = flux[:, RING : RING + ROWS]
@@ -1057,14 +1060,13 @@
         [near],
         [packed, stat, flux, w, wlo, whi],
     )
+    zlo, zhi = shift("gx", zlo, zhi)
     gathered = lax.all_to_all(stat, "gx", 0, 0, tiled=True)
-    gathered, zlo, zhi = lax.optimization_barrier((gathered, zlo, zhi))
-    zlo, zhi = shift("gx", zlo, zhi)
     (column,) = run(column_kernel, [(count_gy, LANES)], [], [gathered])
     gathered = lax.all_to_all(column, "gy", 0, 0, tiled=True)
     (coarse,) = run(
         functools.partial(coarse_kernel, count_gy),
-        [(32, LANES)],
+        [(16, LANES)],
         [near],
         [gathered],
         [VMEM((LANES, LANES), F32), VMEM((LANES, LANES), F32)],

time: 122 us -> 122 us (level)
  no operation moved by 1% of the time
where the time goes in v12:
time: 122 us; the launch traced here: 121 us
  blocking collectives  60.3 us (49%)
  starting transfers between devices  28.3 us (23%)
  Pallas kernels  16 us (13%)
  waiting for transfers between devices  15.7 us (13%)
    all_to_all x1, blocking collectives, body(): gathered = lax.all_to_all(column, 'gy', 0, 0, tiled=True)  22 us
    ppermute x5, starting transfers between devices, shift(): lax.ppermute(high_face, axis, forward)  20.8 us
    all_to_all x1, blocking collectives, body(): wide = lax.all_to_all(wide, 'gy', 0, 0, tiled=True)  16.3 us
    pallas_call x11, Pallas kernels, run(): pl.pallas_call(kernel, out_shape=[jax.ShapeDtypeStruct(out, F32) for out...  16 us
    ppermute x5, waiting for transfers between devices, shift(): lax.ppermute(low_face, axis, backward)  14.4 us
    all_to_all x1, blocking collectives, body(): gathered = lax.all_to_all(stat, 'gx', 0, 0, tiled=True)  12.9 us
    all_to_all x1, blocking collectives, body(): tile = lax.all_to_all(sums, 'gx', 0, 0, tiled=True)  9.09 us
    ppermute x5, starting transfers between devices, shift(): lax.ppermute(low_face, axis, backward)  7.4 us
  transfers between devices with their start and end apart: 10, of which 5 were waited for; matrix products, arithmetic and copies ran while one was open for 0% of the time, Pallas kernels for 5%

profile of v12, /device:TPU:1, one launch (start us, length us, event | category | flops | bytes accessed | tf_op | source)
XLA Modules:
  0.0 121.2 jit_solution(4316803807506288583)
XLA Ops:
  0.6 0.0 copy-start.1
  0.6 1.8 %shard_map.77 = (f32[8,32,128]{2,1,0:T(8,128)S(1)}, f32[8,32,128]{2,1,0:T(8,128)S(1)}, f32[3,32,128]{2,1,0:T(8,128)S(1)}, f32[3,32,128]{2,1,0:T(8,128)S(1)}, f32[8,128]{1,0:T(8,128)S(1)}) custom-call(f32[8,32,128]{2,1,0:T(8,128)} %lev_in.1, f32[3,8,32,128]{3,2,1,0:T(8,128)} %vel_in.1, f32[8,32,128]{2,1,0:T(8,128)} %src_in.1, ...), custom_call_target="tpu_custom_call" | custom-call | flops 1000000 | bytes 729088 | tf_op jit(solution)/shard_map/pallas_call | solution.py:985
  2.5 0.0 copy-start
  2.5 5.0 %collective-permute-start = (f32[3,32,128]{2,1,0:T(8,128)S(1)}, f32[3,32,128]{2,1,0:T(8,128)S(1)}, u32[]{:S(2)}, u32[]{:S(2)}) collective-permute-start(f32[3,32,128]{2,1,0:T(8,128)S(1)} %get-tuple-element.31), channel_id=1, source_target_pairs={{0,64},{64,128},{128,192},{192,256},{256,320},{320,384},{384,448},... | collective-permute-start | bytes 147464 | tf_op jit(solution)/shard_map/ppermute | solution.py:1001
  7.5 1.3 %collective-permute-start.1 = (f32[3,32,128]{2,1,0:T(8,128)S(1)}, f32[3,32,128]{2,1,0:T(8,128)S(1)}, u32[]{:S(2)}, u32[]{:S(2)}) collective-permute-start(f32[3,32,128]{2,1,0:T(8,128)S(1)} %get-tuple-element.32), channel_id=1, source_target_pairs={{64,0},{128,64},{192,128},{256,192},{320,256},{384,320},{448,384},... | collective-permute-start | bytes 147464 | tf_op jit(solution)/shard_map/ppermute | solution.py:1001
  8.8 0.0 collective-permute-done.low_z.zlo
  8.8 4.2 %collective-permute-done.1.high_z.zhi = f32[3,32,128]{2,1,0:T(8,128)S(1)} collective-permute-done((f32[3,32,128]{2,1,0:T(8,128)S(1)}, f32[3,32,128]{2,1,0:T(8,128)S(1)}, u32[]{:S(2)}, u32[]{:S(2)}) %collective-permute-start.1) | collective-permute-done | bytes 49184 | tf_op jit(solution)/shard_map/ppermute | solution.py:1001
  13.0 4.8 %collective-permute-start.2 = (f32[12,48,128]{2,1,0:T(8,128)S(1)}, f32[12,48,128]{2,1,0:T(8,128)S(1)}, u32[]{:S(2)}, u32[]{:S(2)}) collective-permute-start(f32[12,48,128]{2,1,0:T(8,128)S(1)} %get-tuple-element.33), channel_id=1, source_target_pairs={{0,1},{1,2},{2,3},{3,4},{4,5},{5,6},{6,7},{7,8},{8,9},{9,10},{10,1... | collective-permute-start | bytes 884744 | tf_op jit(solution)/shard_map/ppermute | solution.py:1001
  17.8 2.2 %collective-permute-start.3 = (f32[12,48,128]{2,1,0:T(8,128)S(1)}, f32[12,48,128]{2,1,0:T(8,128)S(1)}, u32[]{:S(2)}, u32[]{:S(2)}) collective-permute-start(f32[12,48,128]{2,1,0:T(8,128)S(1)} %get-tuple-element.34), channel_id=1, source_target_pairs={{1,0},{2,1},{3,2},{4,3},{5,4},{6,5},{7,6},{8,7},{9,8},{10,9},{11,1... | collective-permute-start | bytes 884744 | tf_op jit(solution)/shard_map/ppermute | solution.py:1001
  20.1 0.1 stack.35.near
  20.2 1.3 %collective-permute-done.2.ylo = f32[12,48,128]{2,1,0:T(8,128)S(1)} collective-permute-done((f32[12,48,128]{2,1,0:T(8,128)S(1)}, f32[12,48,128]{2,1,0:T(8,128)S(1)}, u32[]{:S(2)}, u32[]{:S(2)}) %collective-permute-start.2) | collective-permute-done | bytes 294944 | tf_op jit(solution)/shard_map/ppermute | solution.py:1001
  21.5 4.4 %collective-permute-done.3.yhi = f32[12,48,128]{2,1,0:T(8,128)S(1)} collective-permute-done((f32[12,48,128]{2,1,0:T(8,128)S(1)}, f32[12,48,128]{2,1,0:T(8,128)S(1)}, u32[]{:S(2)}, u32[]{:S(2)}) %collective-permute-start.3) | collective-permute-done | bytes 294944 | tf_op jit(solution)/shard_map/ppermute | solution.py:1001
  25.9 0.0 copy-done.1
  25.9 0.0 copy-done
  25.9 2.7 %shard_map.80 = (f32[8,64,128]{2,1,0:T(8,128)S(1)}, f32[64,128]{1,0:T(8,128)S(1)}, f32[64,128]{1,0:T(8,128)S(1)}) custom-call(f32[8]{0:T(128)S(1)} %stack.35.near, f32[664,128]{1,0:T(8,128)S(1)} %copy-done, bf16[1008,384]{1,0:T(8,128)(2,1)S(1)} %copy-done.1, f32[8,32,128]{2,1,0:T(8,128)S(1)} %get-tuple-element.29.b, ...), custom_call_target="tpu_custom_call" | custom-call | flops 1000000 | bytes 655360 | tf_op jit(solution)/shard_map/pallas_call | solution.py:985
  28.6 4.0 %collective-permute-start.4 = (f32[64,128]{1,0:T(8,128)S(1)}, f32[64,128]{1,0:T(8,128)S(1)}, u32[]{:S(2)}, u32[]{:S(2)}) collective-permute-start(f32[64,128]{1,0:T(8,128)S(1)} %get-tuple-element.39), channel_id=1, source_target_pairs={{0,64},{64,128},{128,192},{192,256},{256,320},{320,384},{384,448},... | collective-permute-start | bytes 98312 | tf_op jit(solution)/shard_map/ppermute | solution.py:1001
  32.6 1.3 %collective-permute-start.5 = (f32[64,128]{1,0:T(8,128)S(1)}, f32[64,128]{1,0:T(8,128)S(1)}, u32[]{:S(2)}, u32[]{:S(2)}) collective-permute-start(f32[64,128]{1,0:T(8,128)S(1)} %get-tuple-element.40), channel_id=1, source_target_pairs={{64,0},{128,64},{192,128},{256,192},{320,256},{384,320},{448,384},... | collective-permute-start | bytes 98312 | tf_op jit(solution)/shard_map/ppermute | solution.py:1001
  33.9 1.5 %shard_map.79 = (f32[8,32,128]{2,1,0:T(8,128)}, f32[8,64,128]{2,1,0:T(8,128)S(1)}, f32[1,128]{1,0:T(1,128)S(1)}) custom-call(f32[8]{0:T(128)S(1)} %stack.35.near, f32[8,128]{1,0:T(8,128)S(1)} %get-tuple-element.28.solid, f32[664,128]{1,0:T(8,128)S(1)} %copy-done, f32[8,32,128]{2,1,0:T(8,128)S(1)} %get-tuple-element.29.b, ...), custom_call_target="tpu_custom_call" | custom-call | flops 20000000 | bytes 787456 | tf_op jit(solution)/shard_map/pallas_call | solution.py:985
  35.4 0.0 collective-permute-done.4.zlo
  35.4 3.7 %collective-permute-done.5.zhi = f32[64,128]{1,0:T(8,128)S(1)} collective-permute-done((f32[64,128]{1,0:T(8,128)S(1)}, f32[64,128]{1,0:T(8,128)S(1)}, u32[]{:S(2)}, u32[]{:S(2)}) %collective-permute-start.5) | collective-permute-done | bytes 32800 | tf_op jit(solution)/shard_map/ppermute | solution.py:1001
  39.1 1.8 %shard_map.81 = (f32[8,64,128]{2,1,0:T(8,128)S(1)}, f32[8,64,128]{2,1,0:T(8,128)S(1)}, f32[8,64,128]{2,1,0:T(8,128)S(1)}, f32[8,64,128]{2,1,0:T(8,128)S(1)}, f32[8,128]{1,0:T(8,128)S(1)}) custom-call(f32[8]{0:T(128)S(1)} %stack.35.near, f32[664,128]{1,0:T(8,128)S(1)} %copy-done, f32[1,128]{1,0:T(1,128)S(1)} %get-tuple-element.37.stat_in, ...), custom_call_target="tpu_custom_call" | custom-call | flops 1000000 | bytes 2105344 | tf_op jit(solution)/shard_map/pallas_call | solution.py:985
  40.9 4.9 %collective-permute-start.6 = (f32[8,64,128]{2,1,0:T(8,128)S(1)}, f32[8,64,128]{2,1,0:T(8,128)S(1)}, u32[]{:S(2)}, u32[]{:S(2)}) collective-permute-start(f32[8,64,128]{2,1,0:T(8,128)S(1)} %get-tuple-element.44), channel_id=1, source_target_pairs={{0,64},{64,128},{128,192},{192,256},{256,320},{320,384},{384,448},... | collective-permute-start | bytes 786440 | tf_op jit(solution)/shard_map/ppermute | solution.py:1001
  45.8 1.3 %collective-permute-start.7 = (f32[8,64,128]{2,1,0:T(8,128)S(1)}, f32[8,64,128]{2,1,0:T(8,128)S(1)}, u32[]{:S(2)}, u32[]{:S(2)}) collective-permute-start(f32[8,64,128]{2,1,0:T(8,128)S(1)} %get-tuple-element.45), channel_id=1, source_target_pairs={{64,0},{128,64},{192,128},{256,192},{320,256},{384,320},{448,384},... | collective-permute-start | bytes 786440 | tf_op jit(solution)/shard_map/ppermute | solution.py:1001
  47.1 12.9 %all_to_all.39 = f32[8,1,128]{2,1,0:T(1,128)S(1)} all-to-all(f32[8,1,128]{2,1,0:T(1,128)S(1)} %bitcast.26), channel_id=1, replica_groups=mesh['gx'=8,'gy'=64] {'gx'}, dimensions={0} | all-to-all | bytes 8192 | tf_op jit(solution)/shard_map/all_to_all | solution.py:1064
  60.0 0.3 shard_map.82
  60.3 22.0 %all_to_all.40 = f32[64,1,128]{2,1,0:T(1,128)S(1)} all-to-all(f32[64,1,128]{2,1,0:T(1,128)S(1)} %bitcast.22), channel_id=1, replica_groups=mesh['gx'=8,'gy'=64] {'gy'}, dimensions={0} | all-to-all | bytes 65536 | tf_op jit(solution)/shard_map/all_to_all | solution.py:1066
  82.3 2.9 %shard_map.83.coarse = f32[16,128]{1,0:T(8,128)S(1)} custom-call(f32[8]{0:T(128)S(1)} %stack.35.near, f32[64,128]{1,0:T(8,128)S(1)} %bitcast.23), custom_call_target="tpu_custom_call" | custom-call | flops 1000000 | bytes 16384 | tf_op jit(solution)/shard_map/pallas_call | solution.py:985
  85.2 0.0 collective-permute-done.6.ylo
  85.2 0.0 collective-permute-done.7.yhi
  85.2 2.7 %shard_map.84 = (f32[8,32,128]{2,1,0:T(8,128)S(1)}, f32[8,32,128]{2,1,0:T(8,128)S(1)}, f32[8,32,128]{2,1,0:T(8,128)S(1)}, f32[32,128]{1,0:T(8,128)S(1)}, f32[32,128]{1,0:T(8,128)S(1)}) custom-call(f32[8]{0:T(128)S(1)} %stack.35.near, f32[664,128]{1,0:T(8,128)S(1)} %copy-done, bf16[1008,384]{1,0:T(8,128)(2,1)S(1)} %copy-done.1, ...), custom_call_target="tpu_custom_call" | custom-call | flops 1000000 | bytes 851968 | tf_op jit(solution)/shard_map/pallas_call | solution.py:985
  88.0 2.2 %collective-permute-start.8 = (f32[32,128]{1,0:T(8,128)S(1)}, f32[32,128]{1,0:T(8,128)S(1)}, u32[]{:S(2)}, u32[]{:S(2)}) collective-permute-start(f32[32,128]{1,0:T(8,128)S(1)} %get-tuple-element.50), channel_id=1, source_target_pairs={{0,64},{64,128},{128,192},{192,256},{256,320},{320,384},{384,448},... | collective-permute-start | bytes 49160 | tf_op jit(solution)/shard_map/ppermute | solution.py:1001
  90.2 1.3 %collective-permute-start.9 = (f32[32,128]{1,0:T(8,128)S(1)}, f32[32,128]{1,0:T(8,128)S(1)}, u32[]{:S(2)}, u32[]{:S(2)}) collective-permute-start(f32[32,128]{1,0:T(8,128)S(1)} %get-tuple-element.51), channel_id=1, source_target_pairs={{64,0},{128,64},{192,128},{256,192},{320,256},{384,320},{448,384},... | collective-permute-start | bytes 49160 | tf_op jit(solution)/shard_map/ppermute | solution.py:1001
  91.5 1.1 shard_map.85
  92.6 0.0 collective-permute-done.8.zlo
  92.6 2.1 %collective-permute-done.9.zhi = f32[32,128]{1,0:T(8,128)S(1)} collective-permute-done((f32[32,128]{1,0:T(8,128)S(1)}, f32[32,128]{1,0:T(8,128)S(1)}, u32[]{:S(2)}, u32[]{:S(2)}) %collective-permute-start.9) | collective-permute-done | bytes 16416 | tf_op jit(solution)/shard_map/ppermute | solution.py:1001
  94.7 0.3 shard_map.86
  95.0 9.1 %all_to_all.41 = f32[8,1,128]{2,1,0:T(1,128)S(1)} all-to-all(f32[8,1,128]{2,1,0:T(1,128)S(1)} %bitcast.24), channel_id=1, replica_groups=mesh['gx'=8,'gy'=64] {'gx'}, dimensions={0} | all-to-all | bytes 8192 | tf_op jit(solution)/shard_map/all_to_all | solution.py:1091
  104.1 16.3 %all_to_all.42 = f32[64,1,128]{2,1,0:T(1,128)S(1)} all-to-all(f32[64,1,128]{2,1,0:T(1,128)S(1)} %broadcast_in_dim.2), channel_id=1, replica_groups=mesh['gx'=8,'gy'=64] {'gy'}, dimensions={0} | all-to-all | bytes 65536 | tf_op jit(solution)/shard_map/all_to_all | solution.py:1093
  120.4 0.8 shard_map.87
  (3 shorter events, 0.1 us)
Async XLA Ops:
  0.6 25.2 %copy-start.1 = (bf16[1008,384]{1,0:T(8,128)(2,1)S(1)}, bf16[1008,384]{1,0:T(8,128)(2,1)}, u32[]{:S(2)}) copy-start(bf16[1008,384]{1,0:T(8,128)(2,1)} %constant.30.clone.tables) | copy-start | bytes 2322436
  2.5 23.4 %copy-start = (f32[664,128]{1,0:T(8,128)S(1)}, f32[664,128]{1,0:T(8,128)}, u32[]{:S(2)}) copy-start(f32[664,128]{1,0:T(8,128)} %constant.29.clone.packed_in.packed) | copy-start | bytes 1019908
  2.5 6.3 %collective-permute-start = (f32[3,32,128]{2,1,0:T(8,128)S(1)}, f32[3,32,128]{2,1,0:T(8,128)S(1)}, u32[]{:S(2)}, u32[]{:S(2)}) collective-permute-start(f32[3,32,128]{2,1,0:T(8,128)S(1)} %get-tuple-element.31), channel_id=1, source_target_pairs={{0,64},{64,128},{128,192},{192,256},{256,320},{320,384},{384,448},... | collective-permute-start | bytes 147464 | tf_op jit(solution)/shard_map/ppermute | solution.py:1001
  7.5 5.5 %collective-permute-start.1 = (f32[3,32,128]{2,1,0:T(8,128)S(1)}, f32[3,32,128]{2,1,0:T(8,128)S(1)}, u32[]{:S(2)}, u32[]{:S(2)}) collective-permute-start(f32[3,32,128]{2,1,0:T(8,128)S(1)} %get-tuple-element.32), channel_id=1, source_target_pairs={{64,0},{128,64},{192,128},{256,192},{320,256},{384,320},{448,384},... | collective-permute-start | bytes 147464 | tf_op jit(solution)/shard_map/ppermute | solution.py:1001
  13.0 8.5 %collective-permute-start.2 = (f32[12,48,128]{2,1,0:T(8,128)S(1)}, f32[12,48,128]{2,1,0:T(8,128)S(1)}, u32[]{:S(2)}, u32[]{:S(2)}) collective-permute-start(f32[12,48,128]{2,1,0:T(8,128)S(1)} %get-tuple-element.33), channel_id=1, source_target_pairs={{0,1},{1,2},{2,3},{3,4},{4,5},{5,6},{6,7},{7,8},{8,9},{9,10},{10,1... | collective-permute-start | bytes 884744 | tf_op jit(solution)/shard_map/ppermute | solution.py:1001
  17.8 8.0 %collective-permute-start.3 = (f32[12,48,128]{2,1,0:T(8,128)S(1)}, f32[12,48,128]{2,1,0:T(8,128)S(1)}, u32[]{:S(2)}, u32[]{:S(2)}) collective-permute-start(f32[12,48,128]{2,1,0:T(8,128)S(1)} %get-tuple-element.34), channel_id=1, source_target_pairs={{1,0},{2,1},{3,2},{4,3},{5,4},{6,5},{7,6},{8,7},{9,8},{10,9},{11,1... | collective-permute-start | bytes 884744 | tf_op jit(solution)/shard_map/ppermute | solution.py:1001
  28.6 6.8 %collective-permute-start.4 = (f32[64,128]{1,0:T(8,128)S(1)}, f32[64,128]{1,0:T(8,128)S(1)}, u32[]{:S(2)}, u32[]{:S(2)}) collective-permute-start(f32[64,128]{1,0:T(8,128)S(1)} %get-tuple-element.39), channel_id=1, source_target_pairs={{0,64},{64,128},{128,192},{192,256},{256,320},{320,384},{384,448},... | collective-permute-start | bytes 98312 | tf_op jit(solution)/shard_map/ppermute | solution.py:1001
  32.6 6.5 %collective-permute-start.5 = (f32[64,128]{1,0:T(8,128)S(1)}, f32[64,128]{1,0:T(8,128)S(1)}, u32[]{:S(2)}, u32[]{:S(2)}) collective-permute-start(f32[64,128]{1,0:T(8,128)S(1)} %get-tuple-element.40), channel_id=1, source_target_pairs={{64,0},{128,64},{192,128},{256,192},{320,256},{384,320},{448,384},... | collective-permute-start | bytes 98312 | tf_op jit(solution)/shard_map/ppermute | solution.py:1001
  40.9 44.3 %collective-permute-start.6 = (f32[8,64,128]{2,1,0:T(8,128)S(1)}, f32[8,64,128]{2,1,0:T(8,128)S(1)}, u32[]{:S(2)}, u32[]{:S(2)}) collective-permute-start(f32[8,64,128]{2,1,0:T(8,128)S(1)} %get-tuple-element.44), channel_id=1, source_target_pairs={{0,64},{64,128},{128,192},{192,256},{256,320},{320,384},{384,448},... | collective-permute-start | bytes 786440 | tf_op jit(solution)/shard_map/ppermute | solution.py:1001
  45.8 39.5 %collective-permute-start.7 = (f32[8,64,128]{2,1,0:T(8,128)S(1)}, f32[8,64,128]{2,1,0:T(8,128)S(1)}, u32[]{:S(2)}, u32[]{:S(2)}) collective-permute-start(f32[8,64,128]{2,1,0:T(8,128)S(1)} %get-tuple-element.45), channel_id=1, source_target_pairs={{64,0},{128,64},{192,128},{256,192},{320,256},{384,320},{448,384},... | collective-permute-start | bytes 786440 | tf_op jit(solution)/shard_map/ppermute | solution.py:1001
  88.0 4.6 %collective-permute-start.8 = (f32[32,128]{1,0:T(8,128)S(1)}, f32[32,128]{1,0:T(8,128)S(1)}, u32[]{:S(2)}, u32[]{:S(2)}) collective-permute-start(f32[32,128]{1,0:T(8,128)S(1)} %get-tuple-element.50), channel_id=1, source_target_pairs={{0,64},{64,128},{128,192},{192,256},{256,320},{320,384},{384,448},... | collective-permute-start | bytes 49160 | tf_op jit(solution)/shard_map/ppermute | solution.py:1001
  90.2 4.5 %collective-permute-start.9 = (f32[32,128]{1,0:T(8,128)S(1)}, f32[32,128]{1,0:T(8,128)S(1)}, u32[]{:S(2)}, u32[]{:S(2)}) collective-permute-start(f32[32,128]{1,0:T(8,128)S(1)} %get-tuple-element.51), channel_id=1, source_target_pairs={{64,0},{128,64},{192,128},{256,192},{320,256},{384,320},{448,384},... | collective-permute-start | bytes 49160 | tf_op jit(solution)/shard_map/ppermute | solution.py:1001

commit v13 on v12

--- a/solution.py
+++ b/solution.py
@@ -154,8 +154,13 @@
 TILES += list(range(ROWS, ROWS + REACH)) + [None] * (TILE_B - REACH)
 FY_A, BY_A = ring_maps(RING, 3, TILES)
 FY_B, BY_B = ring_maps(0, 1, list(range(-RING, ROWS + RING)))
-STEP_A = 112
+INNER = np.arange(40, 60)
+OUTER = np.concatenate([np.arange(0, 40), np.arange(60, 100)])
+FY_I, BY_I = FY_A[INNER, TILE_B : TILE_B + ROWS], BY_A[RING : RING + ROWS, INNER]
+FY_A, BY_A = FY_A[OUTER], BY_A[:, OUTER]
+STEP_A = 80
 STEP_B = 64
+STEP_I = 32
 
 
 def padded(forward, backward, step):
@@ -165,6 +170,7 @@
 
 FY_A, BY_A = padded(FY_A, BY_A, STEP_A)
 FY_B, BY_B = padded(FY_B, BY_B, STEP_B)
+FY_I, BY_I = padded(FY_I, BY_I, STEP_I)
 FX, BX = line_maps(EX)
 FX = FX[:, :LANES]
 
@@ -199,6 +205,8 @@
         wide_const(BY_A),
         wide_const(FY_B),
         wide_const(BY_B),
+        wide_const(FY_I),
+        wide_const(BY_I),
     ]
 )
 
@@ -404,26 +412,26 @@
     lev_in, vel_in, src_in, packed_in, solid_in, b_ref, l_ref, zlo, zhi, solid_ref,
     lev, vel, src, packed, solid, sems,
 ):
+    pairs = ((lev_in, lev), (packed_in, packed), (vel_in, vel), (src_in, src), (solid_in, solid))
     copies = [
         pltpu.make_async_copy(source, target, sems.at[index])
-        for index, (source, target) in enumerate(
-            (
-                (vel_in, vel), (lev_in, lev), (packed_in, packed), (src_in, src), (solid_in, solid),
-            )
-        )
+        for index, (source, target) in enumerate(pairs)
     ]
     for copy in copies:
         copy.start()
-    for copy in copies:
+    copies[0].wait()
+    level = lev[...]
+    gz = stack(along_z([level[i] for i in range(8)], DERIV))
+    copies[1].wait()
+    gy = along_y(level, packed, 0)
+    gx = along_x(level, packed, 0)
+    for copy in copies[2:]:
         copy.wait()
     spread = packed[AT_SPREAD : AT_SPREAD + EX].astype(BF16)
     in_solid = dot(solid[...].astype(F32).astype(BF16), spread)
     solid_ref[...] = jnp.concatenate([in_solid, jnp.zeros((8 - EY, LANES), F32)], axis=0)
-    level = lev[...]
     v0, v1, v2 = vel[0], vel[1], vel[2]
-    gz = stack(along_z([level[i] for i in range(8)], DERIV))
-    advect = v0 * gz + v1 * along_y(level, packed, 0) + v2 * along_x(level, packed, 0)
-    moved = level - (2.0 * TIME_STEP) * advect
+    moved = level - (2.0 * TIME_STEP) * (v0 * gz + v1 * gy + v2 * gx)
     diverge = stack(along_z([v0[i] for i in range(8)], DERIV))
     diverge = diverge + along_y(v1, packed, 0) + along_x(v2, packed, 0)
     force = src[...] - (2.0 * TIME_STEP) * diverge
@@ -549,8 +557,15 @@
     stat[...] = lane_row(entries)
 
 
+def inner_schwarz_kernel(packed, tables, b, zlo, zhi, out_ref):
+    planes = [b[i] for i in range(8)] + [zlo[0], zlo[1], zhi[0], zhi[1]]
+    planes = solve_elements(planes, packed, tables, 2)
+    for i in range(8):
+        out_ref[i] = planes[i]
+
+
 def first_schwarz_kernel(
-    near, packed, tables, b, zlo, zhi, ylo, yhi, w_ref, wlo, whi
+    near, packed, tables, inner, b, zlo, zhi, ylo, yhi, w_ref, wlo, whi
 ):
     own = [b[i] for i in range(8)] + [zlo[0], zlo[1], zhi[0], zhi[1]]
     planes = [
@@ -560,11 +575,13 @@
     row, has_low, has_high = ring_rows(near)
     in_grid = jnp.where(row < RING, has_low, jnp.where(row >= RING + ROWS, has_high, 1.0))
     in_grid = jnp.where(row == RING, has_low, jnp.where(row == RING + ROWS - 1, has_high, in_grid))
+    rest = jnp.zeros((RING, LANES), F32)
     for i in range(8):
         first = (1.0 - has_low) * planes[i][WIDE : WIDE + 1]
         last = (1.0 - has_high) * planes[i][WIDE + 1 : WIDE + 2]
         alone = jnp.where(row == RING, first, jnp.where(row == RING + ROWS - 1, last, 0.0))
         planes[i] = planes[i][0:WIDE] * in_grid + alone
+        planes[i] = planes[i] + jnp.concatenate([rest, inner[i], rest], axis=0)
     store_faces(planes, near, w_ref, wlo, whi)
 
 
@@ -1040,11 +1057,14 @@
     zlo, zhi = shift("gx", zlo, zhi)
     ylo, yhi = run(rim_kernel, [rim, rim], [], [solid, b, l, zlo, zhi])
     ylo, yhi = shift("gy", ylo, yhi)
+    (inner,) = run(
+        inner_schwarz_kernel, [block], [], [packed, tables, b, zlo, zhi], flops=20000000
+    )
     w, wlo, whi = run(
         first_schwarz_kernel,
         [wide_block, wide_face, wide_face],
         [near],
-        [packed, tables, b, zlo, zhi, ylo, yhi],
+        [packed, tables, inner, b, zlo, zhi, ylo, yhi],
     )
     wlo, whi = shift("gx", wlo, whi)
     level_new, flux, stat = run(

time: 122 us -> 121 us (level)
    pallas_call x11 -> x12, Pallas kernels: 16 us -> 16.4 us  [run(): pl.pallas_call(kernel, out_shape=[jax.ShapeDtypeStruct(out, F32) for out...]
  transfers between devices with their start and end apart: 10 -> 10, of which waited for: 5 -> 5; matrix products, arithmetic and copies ran while one was open for 0% -> 0% of each run, Pallas kernels for 5% -> 6%
where the time goes in v13:
time: 121 us
  blocking collectives  60.3 us (50%)
  starting transfers between devices  28.2 us (23%)
  Pallas kernels  16.4 us (14%)
  waiting for transfers between devices  14.7 us (12%)
    all_to_all x1, blocking collectives, body(): gathered = lax.all_to_all(column, 'gy', 0, 0, tiled=True)  22 us
    ppermute x5, starting transfers between devices, shift(): lax.ppermute(high_face, axis, forward)  20.8 us
    pallas_call x12, Pallas kernels, run(): pl.pallas_call(kernel, out_shape=[jax.ShapeDtypeStruct(out, F32) for out...  16.4 us
    all_to_all x1, blocking collectives, body(): wide = lax.all_to_all(wide, 'gy', 0, 0, tiled=True)  16.3 us
    ppermute x5, waiting for transfers between devices, shift(): lax.ppermute(low_face, axis, backward)  14.3 us
    all_to_all x1, blocking collectives, body(): gathered = lax.all_to_all(stat, 'gx', 0, 0, tiled=True)  12.9 us
    all_to_all x1, blocking collectives, body(): tile = lax.all_to_all(sums, 'gx', 0, 0, tiled=True)  9.09 us
    ppermute x5, starting transfers between devices, shift(): lax.ppermute(low_face, axis, backward)  7.41 us
  transfers between devices with their start and end apart: 10, of which 5 were waited for; matrix products, arithmetic and copies ran while one was open for 0% of the time, Pallas kernels for 6%

profile of v13, /device:TPU:1, one launch (start us, length us, event | category | flops | bytes accessed | tf_op | source)
XLA Modules:
  0.0 120.7 jit_solution(6458007120105078978)
XLA Ops:
  0.6 0.0 copy-start.1
  0.6 1.8 %shard_map.77 = (f32[8,32,128]{2,1,0:T(8,128)S(1)}, f32[8,32,128]{2,1,0:T(8,128)S(1)}, f32[3,32,128]{2,1,0:T(8,128)S(1)}, f32[3,32,128]{2,1,0:T(8,128)S(1)}, f32[8,128]{1,0:T(8,128)S(1)}) custom-call(f32[8,32,128]{2,1,0:T(8,128)} %lev_in.1, f32[3,8,32,128]{3,2,1,0:T(8,128)} %vel_in.1, f32[8,32,128]{2,1,0:T(8,128)} %src_in.1, ...), custom_call_target="tpu_custom_call" | custom-call | flops 1000000 | bytes 729088 | tf_op jit(solution)/shard_map/pallas_call | solution.py:1002
  2.4 0.0 copy-start
  2.4 5.0 %collective-permute-start = (f32[3,32,128]{2,1,0:T(8,128)S(1)}, f32[3,32,128]{2,1,0:T(8,128)S(1)}, u32[]{:S(2)}, u32[]{:S(2)}) collective-permute-start(f32[3,32,128]{2,1,0:T(8,128)S(1)} %get-tuple-element.31), channel_id=1, source_target_pairs={{0,64},{64,128},{128,192},{192,256},{256,320},{320,384},{384,448},... | collective-permute-start | bytes 147464 | tf_op jit(solution)/shard_map/ppermute | solution.py:1018
  7.4 1.3 %collective-permute-start.1 = (f32[3,32,128]{2,1,0:T(8,128)S(1)}, f32[3,32,128]{2,1,0:T(8,128)S(1)}, u32[]{:S(2)}, u32[]{:S(2)}) collective-permute-start(f32[3,32,128]{2,1,0:T(8,128)S(1)} %get-tuple-element.32), channel_id=1, source_target_pairs={{64,0},{128,64},{192,128},{256,192},{320,256},{384,320},{448,384},... | collective-permute-start | bytes 147464 | tf_op jit(solution)/shard_map/ppermute | solution.py:1018
  8.7 0.0 collective-permute-done.low_z.zlo
  8.7 4.2 %collective-permute-done.1.high_z.zhi = f32[3,32,128]{2,1,0:T(8,128)S(1)} collective-permute-done((f32[3,32,128]{2,1,0:T(8,128)S(1)}, f32[3,32,128]{2,1,0:T(8,128)S(1)}, u32[]{:S(2)}, u32[]{:S(2)}) %collective-permute-start.1) | collective-permute-done | bytes 49184 | tf_op jit(solution)/shard_map/ppermute | solution.py:1018
  12.9 4.8 %collective-permute-start.2 = (f32[12,48,128]{2,1,0:T(8,128)S(1)}, f32[12,48,128]{2,1,0:T(8,128)S(1)}, u32[]{:S(2)}, u32[]{:S(2)}) collective-permute-start(f32[12,48,128]{2,1,0:T(8,128)S(1)} %get-tuple-element.33), channel_id=1, source_target_pairs={{0,1},{1,2},{2,3},{3,4},{4,5},{5,6},{6,7},{7,8},{8,9},{9,10},{10,1... | collective-permute-start | bytes 884744 | tf_op jit(solution)/shard_map/ppermute | solution.py:1018
  17.7 2.2 %collective-permute-start.3 = (f32[12,48,128]{2,1,0:T(8,128)S(1)}, f32[12,48,128]{2,1,0:T(8,128)S(1)}, u32[]{:S(2)}, u32[]{:S(2)}) collective-permute-start(f32[12,48,128]{2,1,0:T(8,128)S(1)} %get-tuple-element.34), channel_id=1, source_target_pairs={{1,0},{2,1},{3,2},{4,3},{5,4},{6,5},{7,6},{8,7},{9,8},{10,9},{11,1... | collective-permute-start | bytes 884744 | tf_op jit(solution)/shard_map/ppermute | solution.py:1018
  20.0 0.1 stack.35.near
  20.1 0.0 copy-done.1
  20.1 0.0 copy-done
  20.1 0.9 shard_map.80.inner
  21.0 0.4 collective-permute-done.2.ylo
  21.4 4.4 %collective-permute-done.3.yhi = f32[12,48,128]{2,1,0:T(8,128)S(1)} collective-permute-done((f32[12,48,128]{2,1,0:T(8,128)S(1)}, f32[12,48,128]{2,1,0:T(8,128)S(1)}, u32[]{:S(2)}, u32[]{:S(2)}) %collective-permute-start.3) | collective-permute-done | bytes 294944 | tf_op jit(solution)/shard_map/ppermute | solution.py:1018
  25.8 2.3 %shard_map.81 = (f32[8,64,128]{2,1,0:T(8,128)S(1)}, f32[64,128]{1,0:T(8,128)S(1)}, f32[64,128]{1,0:T(8,128)S(1)}) custom-call(f32[8]{0:T(128)S(1)} %stack.35.near, f32[632,128]{1,0:T(8,128)S(1)} %copy-done, bf16[1040,384]{1,0:T(8,128)(2,1)S(1)} %copy-done.1, f32[8,32,128]{2,1,0:T(8,128)S(1)} %shard_map.80.inner, f32[8,32,128]{2,1,0:T(8,128)S(1)} %get-tuple-element.29.b, ...), custom_call_target="tpu_custom_call" | custom-call | flops 1000000 | bytes 655360 | tf_op jit(solution)/shard_map/pallas_call | solution.py:1002
  28.1 4.0 %collective-permute-start.4 = (f32[64,128]{1,0:T(8,128)S(1)}, f32[64,128]{1,0:T(8,128)S(1)}, u32[]{:S(2)}, u32[]{:S(2)}) collective-permute-start(f32[64,128]{1,0:T(8,128)S(1)} %get-tuple-element.39), channel_id=1, source_target_pairs={{0,64},{64,128},{128,192},{192,256},{256,320},{320,384},{384,448},... | collective-permute-start | bytes 98312 | tf_op jit(solution)/shard_map/ppermute | solution.py:1018
  32.1 1.3 %collective-permute-start.5 = (f32[64,128]{1,0:T(8,128)S(1)}, f32[64,128]{1,0:T(8,128)S(1)}, u32[]{:S(2)}, u32[]{:S(2)}) collective-permute-start(f32[64,128]{1,0:T(8,128)S(1)} %get-tuple-element.40), channel_id=1, source_target_pairs={{64,0},{128,64},{192,128},{256,192},{320,256},{384,320},{448,384},... | collective-permute-start | bytes 98312 | tf_op jit(solution)/shard_map/ppermute | solution.py:1018
  33.4 1.5 %shard_map.79 = (f32[8,32,128]{2,1,0:T(8,128)}, f32[8,64,128]{2,1,0:T(8,128)S(1)}, f32[1,128]{1,0:T(1,128)S(1)}) custom-call(f32[8]{0:T(128)S(1)} %stack.35.near, f32[8,128]{1,0:T(8,128)S(1)} %get-tuple-element.28.solid, f32[632,128]{1,0:T(8,128)S(1)} %copy-done, f32[8,32,128]{2,1,0:T(8,128)S(1)} %get-tuple-element.29.b, ...), custom_call_target="tpu_custom_call" | custom-call | flops 20000000 | bytes 787456 | tf_op jit(solution)/shard_map/pallas_call | solution.py:1002
  34.9 0.0 collective-permute-done.4.zlo
  34.9 3.7 %collective-permute-done.5.zhi = f32[64,128]{1,0:T(8,128)S(1)} collective-permute-done((f32[64,128]{1,0:T(8,128)S(1)}, f32[64,128]{1,0:T(8,128)S(1)}, u32[]{:S(2)}, u32[]{:S(2)}) %collective-permute-start.5) | collective-permute-done | bytes 32800 | tf_op jit(solution)/shard_map/ppermute | solution.py:1018
  38.6 1.8 %shard_map.82 = (f32[8,64,128]{2,1,0:T(8,128)S(1)}, f32[8,64,128]{2,1,0:T(8,128)S(1)}, f32[8,64,128]{2,1,0:T(8,128)S(1)}, f32[8,64,128]{2,1,0:T(8,128)S(1)}, f32[8,128]{1,0:T(8,128)S(1)}) custom-call(f32[8]{0:T(128)S(1)} %stack.35.near, f32[632,128]{1,0:T(8,128)S(1)} %copy-done, f32[1,128]{1,0:T(1,128)S(1)} %get-tuple-element.37.stat_in, ...), custom_call_target="tpu_custom_call" | custom-call | flops 1000000 | bytes 2105344 | tf_op jit(solution)/shard_map/pallas_call | solution.py:1002
  40.4 4.9 %collective-permute-start.6 = (f32[8,64,128]{2,1,0:T(8,128)S(1)}, f32[8,64,128]{2,1,0:T(8,128)S(1)}, u32[]{:S(2)}, u32[]{:S(2)}) collective-permute-start(f32[8,64,128]{2,1,0:T(8,128)S(1)} %get-tuple-element.44), channel_id=1, source_target_pairs={{0,64},{64,128},{128,192},{192,256},{256,320},{320,384},{384,448},... | collective-permute-start | bytes 786440 | tf_op jit(solution)/shard_map/ppermute | solution.py:1018
  45.3 1.3 %collective-permute-start.7 = (f32[8,64,128]{2,1,0:T(8,128)S(1)}, f32[8,64,128]{2,1,0:T(8,128)S(1)}, u32[]{:S(2)}, u32[]{:S(2)}) collective-permute-start(f32[8,64,128]{2,1,0:T(8,128)S(1)} %get-tuple-element.45), channel_id=1, source_target_pairs={{64,0},{128,64},{192,128},{256,192},{320,256},{384,320},{448,384},... | collective-permute-start | bytes 786440 | tf_op jit(solution)/shard_map/ppermute | solution.py:1018
  46.6 12.9 %all_to_all.39 = f32[8,1,128]{2,1,0:T(1,128)S(1)} all-to-all(f32[8,1,128]{2,1,0:T(1,128)S(1)} %bitcast.26), channel_id=1, replica_groups=mesh['gx'=8,'gy'=64] {'gx'}, dimensions={0} | all-to-all | bytes 8192 | tf_op jit(solution)/shard_map/all_to_all | solution.py:1084
  59.5 0.3 shard_map.83
  59.8 22.0 %all_to_all.40 = f32[64,1,128]{2,1,0:T(1,128)S(1)} all-to-all(f32[64,1,128]{2,1,0:T(1,128)S(1)} %bitcast.22), channel_id=1, replica_groups=mesh['gx'=8,'gy'=64] {'gy'}, dimensions={0} | all-to-all | bytes 65536 | tf_op jit(solution)/shard_map/all_to_all | solution.py:1086
  81.8 2.9 %shard_map.84.coarse = f32[16,128]{1,0:T(8,128)S(1)} custom-call(f32[8]{0:T(128)S(1)} %stack.35.near, f32[64,128]{1,0:T(8,128)S(1)} %bitcast.23), custom_call_target="tpu_custom_call" | custom-call | flops 1000000 | bytes 16384 | tf_op jit(solution)/shard_map/pallas_call | solution.py:1002
  84.7 0.0 collective-permute-done.6.ylo
  84.7 0.0 collective-permute-done.7.yhi
  84.7 2.7 %shard_map.85 = (f32[8,32,128]{2,1,0:T(8,128)S(1)}, f32[8,32,128]{2,1,0:T(8,128)S(1)}, f32[8,32,128]{2,1,0:T(8,128)S(1)}, f32[32,128]{1,0:T(8,128)S(1)}, f32[32,128]{1,0:T(8,128)S(1)}) custom-call(f32[8]{0:T(128)S(1)} %stack.35.near, f32[632,128]{1,0:T(8,128)S(1)} %copy-done, bf16[1040,384]{1,0:T(8,128)(2,1)S(1)} %copy-done.1, ...), custom_call_target="tpu_custom_call" | custom-call | flops 1000000 | bytes 851968 | tf_op jit(solution)/shard_map/pallas_call | solution.py:1002
  87.5 2.2 %collective-permute-start.8 = (f32[32,128]{1,0:T(8,128)S(1)}, f32[32,128]{1,0:T(8,128)S(1)}, u32[]{:S(2)}, u32[]{:S(2)}) collective-permute-start(f32[32,128]{1,0:T(8,128)S(1)} %get-tuple-element.50), channel_id=1, source_target_pairs={{0,64},{64,128},{128,192},{192,256},{256,320},{320,384},{384,448},... | collective-permute-start | bytes 49160 | tf_op jit(solution)/shard_map/ppermute | solution.py:1018
  89.7 1.3 %collective-permute-start.9 = (f32[32,128]{1,0:T(8,128)S(1)}, f32[32,128]{1,0:T(8,128)S(1)}, u32[]{:S(2)}, u32[]{:S(2)}) collective-permute-start(f32[32,128]{1,0:T(8,128)S(1)} %get-tuple-element.51), channel_id=1, source_target_pairs={{64,0},{128,64},{192,128},{256,192},{320,256},{384,320},{448,384},... | collective-permute-start | bytes 49160 | tf_op jit(solution)/shard_map/ppermute | solution.py:1018
  91.0 1.1 shard_map.86
  92.1 0.0 collective-permute-done.8.zlo
  92.1 2.1 %collective-permute-done.9.zhi = f32[32,128]{1,0:T(8,128)S(1)} collective-permute-done((f32[32,128]{1,0:T(8,128)S(1)}, f32[32,128]{1,0:T(8,128)S(1)}, u32[]{:S(2)}, u32[]{:S(2)}) %collective-permute-start.9) | collective-permute-done | bytes 16416 | tf_op jit(solution)/shard_map/ppermute | solution.py:1018
  94.2 0.3 shard_map.87
  94.4 9.1 %all_to_all.41 = f32[8,1,128]{2,1,0:T(1,128)S(1)} all-to-all(f32[8,1,128]{2,1,0:T(1,128)S(1)} %bitcast.24), channel_id=1, replica_groups=mesh['gx'=8,'gy'=64] {'gx'}, dimensions={0} | all-to-all | bytes 8192 | tf_op jit(solution)/shard_map/all_to_all | solution.py:1111
  103.6 16.3 %all_to_all.42 = f32[64,1,128]{2,1,0:T(1,128)S(1)} all-to-all(f32[64,1,128]{2,1,0:T(1,128)S(1)} %broadcast_in_dim.2), channel_id=1, replica_groups=mesh['gx'=8,'gy'=64] {'gy'}, dimensions={0} | all-to-all | bytes 65536 | tf_op jit(solution)/shard_map/all_to_all | solution.py:1113
  119.8 0.8 shard_map.88
  (3 shorter events, 0.1 us)
Async XLA Ops:
  0.6 19.5 %copy-start.1 = (bf16[1040,384]{1,0:T(8,128)(2,1)S(1)}, bf16[1040,384]{1,0:T(8,128)(2,1)}, u32[]{:S(2)}) copy-start(bf16[1040,384]{1,0:T(8,128)(2,1)} %constant.30.clone.tables) | copy-start | bytes 2396164
  2.4 17.7 %copy-start = (f32[632,128]{1,0:T(8,128)S(1)}, f32[632,128]{1,0:T(8,128)}, u32[]{:S(2)}) copy-start(f32[632,128]{1,0:T(8,128)} %constant.29.clone.packed_in.packed) | copy-start | bytes 970756
  2.4 6.3 %collective-permute-start = (f32[3,32,128]{2,1,0:T(8,128)S(1)}, f32[3,32,128]{2,1,0:T(8,128)S(1)}, u32[]{:S(2)}, u32[]{:S(2)}) collective-permute-start(f32[3,32,128]{2,1,0:T(8,128)S(1)} %get-tuple-element.31), channel_id=1, source_target_pairs={{0,64},{64,128},{128,192},{192,256},{256,320},{320,384},{384,448},... | collective-permute-start | bytes 147464 | tf_op jit(solution)/shard_map/ppermute | solution.py:1018
  7.4 5.5 %collective-permute-start.1 = (f32[3,32,128]{2,1,0:T(8,128)S(1)}, f32[3,32,128]{2,1,0:T(8,128)S(1)}, u32[]{:S(2)}, u32[]{:S(2)}) collective-permute-start(f32[3,32,128]{2,1,0:T(8,128)S(1)} %get-tuple-element.32), channel_id=1, source_target_pairs={{64,0},{128,64},{192,128},{256,192},{320,256},{384,320},{448,384},... | collective-permute-start | bytes 147464 | tf_op jit(solution)/shard_map/ppermute | solution.py:1018
  12.9 8.5 %collective-permute-start.2 = (f32[12,48,128]{2,1,0:T(8,128)S(1)}, f32[12,48,128]{2,1,0:T(8,128)S(1)}, u32[]{:S(2)}, u32[]{:S(2)}) collective-permute-start(f32[12,48,128]{2,1,0:T(8,128)S(1)} %get-tuple-element.33), channel_id=1, source_target_pairs={{0,1},{1,2},{2,3},{3,4},{4,5},{5,6},{6,7},{7,8},{8,9},{9,10},{10,1... | collective-permute-start | bytes 884744 | tf_op jit(solution)/shard_map/ppermute | solution.py:1018
  17.7 8.0 %collective-permute-start.3 = (f32[12,48,128]{2,1,0:T(8,128)S(1)}, f32[12,48,128]{2,1,0:T(8,128)S(1)}, u32[]{:S(2)}, u32[]{:S(2)}) collective-permute-start(f32[12,48,128]{2,1,0:T(8,128)S(1)} %get-tuple-element.34), channel_id=1, source_target_pairs={{1,0},{2,1},{3,2},{4,3},{5,4},{6,5},{7,6},{8,7},{9,8},{10,9},{11,1... | collective-permute-start | bytes 884744 | tf_op jit(solution)/shard_map/ppermute | solution.py:1018
  28.1 6.8 %collective-permute-start.4 = (f32[64,128]{1,0:T(8,128)S(1)}, f32[64,128]{1,0:T(8,128)S(1)}, u32[]{:S(2)}, u32[]{:S(2)}) collective-permute-start(f32[64,128]{1,0:T(8,128)S(1)} %get-tuple-element.39), channel_id=1, source_target_pairs={{0,64},{64,128},{128,192},{192,256},{256,320},{320,384},{384,448},... | collective-permute-start | bytes 98312 | tf_op jit(solution)/shard_map/ppermute | solution.py:1018
  32.1 6.5 %collective-permute-start.5 = (f32[64,128]{1,0:T(8,128)S(1)}, f32[64,128]{1,0:T(8,128)S(1)}, u32[]{:S(2)}, u32[]{:S(2)}) collective-permute-start(f32[64,128]{1,0:T(8,128)S(1)} %get-tuple-element.40), channel_id=1, source_target_pairs={{64,0},{128,64},{192,128},{256,192},{320,256},{384,320},{448,384},... | collective-permute-start | bytes 98312 | tf_op jit(solution)/shard_map/ppermute | solution.py:1018
  40.4 44.3 %collective-permute-start.6 = (f32[8,64,128]{2,1,0:T(8,128)S(1)}, f32[8,64,128]{2,1,0:T(8,128)S(1)}, u32[]{:S(2)}, u32[]{:S(2)}) collective-permute-start(f32[8,64,128]{2,1,0:T(8,128)S(1)} %get-tuple-element.44), channel_id=1, source_target_pairs={{0,64},{64,128},{128,192},{192,256},{256,320},{320,384},{384,448},... | collective-permute-start | bytes 786440 | tf_op jit(solution)/shard_map/ppermute | solution.py:1018
  45.3 39.5 %collective-permute-start.7 = (f32[8,64,128]{2,1,0:T(8,128)S(1)}, f32[8,64,128]{2,1,0:T(8,128)S(1)}, u32[]{:S(2)}, u32[]{:S(2)}) collective-permute-start(f32[8,64,128]{2,1,0:T(8,128)S(1)} %get-tuple-element.45), channel_id=1, source_target_pairs={{64,0},{128,64},{192,128},{256,192},{320,256},{384,320},{448,384},... | collective-permute-start | bytes 786440 | tf_op jit(solution)/shard_map/ppermute | solution.py:1018
  87.5 4.6 %collective-permute-start.8 = (f32[32,128]{1,0:T(8,128)S(1)}, f32[32,128]{1,0:T(8,128)S(1)}, u32[]{:S(2)}, u32[]{:S(2)}) collective-permute-start(f32[32,128]{1,0:T(8,128)S(1)} %get-tuple-element.50), channel_id=1, source_target_pairs={{0,64},{64,128},{128,192},{192,256},{256,320},{320,384},{384,448},... | collective-permute-start | bytes 49160 | tf_op jit(solution)/shard_map/ppermute | solution.py:1018
  89.7 4.5 %collective-permute-start.9 = (f32[32,128]{1,0:T(8,128)S(1)}, f32[32,128]{1,0:T(8,128)S(1)}, u32[]{:S(2)}, u32[]{:S(2)}) collective-permute-start(f32[32,128]{1,0:T(8,128)S(1)} %get-tuple-element.51), channel_id=1, source_target_pairs={{64,0},{128,64},{192,128},{256,192},{320,256},{384,320},{448,384},... | collective-permute-start | bytes 49160 | tf_op jit(solution)/shard_map/ppermute | solution.py:1018

commit v14 on v13

--- a/solution.py
+++ b/solution.py
@@ -1106,11 +1106,19 @@
         flops=20000000,
     )
     (sums,) = run(
-        face_kernel, [(count_gx, LANES)], [], [packed, flux, b, y, kx, zlo, zhi, sums]
-    )
-    tile = lax.all_to_all(sums, "gx", 0, 0, tiled=True)
-    wide = jnp.broadcast_to(jnp.sum(tile, axis=0, keepdims=True), (count_gy, LANES))
-    wide = lax.all_to_all(wide, "gy", 0, 0, tiled=True)
+        face_kernel, [(2 * count_gx, LANES)], [], [packed, flux, b, y, kx, zlo, zhi, sums]
+    )
+    pairs = count_gy // 2
+    columns = [
+        [z * count_gy + 2 * m + c for z in range(count_gx) for c in range(2)] for m in range(pairs)
+    ]
+    layers = [
+        [z * count_gy + 2 * m + c for m in range(pairs)] for z in range(count_gx) for c in range(2)
+    ]
+    axes = ("gx", "gy")
+    tile = lax.all_to_all(sums, axes, 0, 0, axis_index_groups=columns, tiled=True)
+    wide = jnp.broadcast_to(jnp.sum(tile, axis=0, keepdims=True), (pairs, LANES))
+    wide = lax.all_to_all(wide, axes, 0, 0, axis_index_groups=layers, tiled=True)
     (pressure,) = run(combine_kernel, [block], [], [wide, z, x, zlo, zhi])
     return (level_new, pressure)
 

time: 121 us -> 119 us (0.983)
  blocking collectives: 60.3 us -> 58.5 us
    all_to_all x2, blocking collectives: 25.3 us -> 23.5 us  [the longest x1 12 us: body(): lax.all_to_all(sums, axes, 0, 0, axis_index_groups=columns, tiled=True)]
where the time goes in v14:
time: 119 us
  blocking collectives  58.5 us (49%)
  starting transfers between devices  28.2 us (24%)
  Pallas kernels  16.4 us (14%)
  waiting for transfers between devices  14.7 us (12%)
    all_to_all x1, blocking collectives, body(): gathered = lax.all_to_all(column, 'gy', 0, 0, tiled=True)  22 us
    ppermute x5, starting transfers between devices, shift(): lax.ppermute(high_face, axis, forward)  20.8 us
    pallas_call x12, Pallas kernels, run(): pl.pallas_call(kernel, out_shape=[jax.ShapeDtypeStruct(out, F32) for out...  16.4 us
    ppermute x5, waiting for transfers between devices, shift(): lax.ppermute(low_face, axis, backward)  14.3 us
    all_to_all x1, blocking collectives, body(): gathered = lax.all_to_all(stat, 'gx', 0, 0, tiled=True)  12.9 us
    all_to_all x1, blocking collectives, body(): lax.all_to_all(sums, axes, 0, 0, axis_index_groups=columns, tiled=True)  12 us
    all_to_all x1, blocking collectives, body(): lax.all_to_all(wide, axes, 0, 0, axis_index_groups=layers, tiled=True)  11.6 us
    ppermute x5, starting transfers between devices, shift(): lax.ppermute(low_face, axis, backward)  7.41 us
  transfers between devices with their start and end apart: 10, of which 5 were waited for; matrix products, arithmetic and copies ran while one was open for 0% of the time, Pallas kernels for 6%

profile of v14, /device:TPU:1, one launch (start us, length us, event | category | flops | bytes accessed | tf_op | source)
XLA Modules:
  0.0 118.8 jit_solution(1277411117899509161)
XLA Ops:
  0.6 0.0 copy-start.1
  0.6 1.8 %shard_map.77 = (f32[8,32,128]{2,1,0:T(8,128)S(1)}, f32[8,32,128]{2,1,0:T(8,128)S(1)}, f32[3,32,128]{2,1,0:T(8,128)S(1)}, f32[3,32,128]{2,1,0:T(8,128)S(1)}, f32[8,128]{1,0:T(8,128)S(1)}) custom-call(f32[8,32,128]{2,1,0:T(8,128)} %lev_in.1, f32[3,8,32,128]{3,2,1,0:T(8,128)} %vel_in.1, f32[8,32,128]{2,1,0:T(8,128)} %src_in.1, ...), custom_call_target="tpu_custom_call" | custom-call | flops 1000000 | bytes 729088 | tf_op jit(solution)/shard_map/pallas_call | solution.py:1002
  2.4 0.0 copy-start
  2.4 5.0 %collective-permute-start = (f32[3,32,128]{2,1,0:T(8,128)S(1)}, f32[3,32,128]{2,1,0:T(8,128)S(1)}, u32[]{:S(2)}, u32[]{:S(2)}) collective-permute-start(f32[3,32,128]{2,1,0:T(8,128)S(1)} %get-tuple-element.31), channel_id=1, source_target_pairs={{0,64},{64,128},{128,192},{192,256},{256,320},{320,384},{384,448},... | collective-permute-start | bytes 147464 | tf_op jit(solution)/shard_map/ppermute | solution.py:1018
  7.4 1.3 %collective-permute-start.1 = (f32[3,32,128]{2,1,0:T(8,128)S(1)}, f32[3,32,128]{2,1,0:T(8,128)S(1)}, u32[]{:S(2)}, u32[]{:S(2)}) collective-permute-start(f32[3,32,128]{2,1,0:T(8,128)S(1)} %get-tuple-element.32), channel_id=1, source_target_pairs={{64,0},{128,64},{192,128},{256,192},{320,256},{384,320},{448,384},... | collective-permute-start | bytes 147464 | tf_op jit(solution)/shard_map/ppermute | solution.py:1018
  8.7 0.0 collective-permute-done.low_z.zlo
  8.7 4.2 %collective-permute-done.1.high_z.zhi = f32[3,32,128]{2,1,0:T(8,128)S(1)} collective-permute-done((f32[3,32,128]{2,1,0:T(8,128)S(1)}, f32[3,32,128]{2,1,0:T(8,128)S(1)}, u32[]{:S(2)}, u32[]{:S(2)}) %collective-permute-start.1) | collective-permute-done | bytes 49184 | tf_op jit(solution)/shard_map/ppermute | solution.py:1018
  12.9 4.8 %collective-permute-start.2 = (f32[12,48,128]{2,1,0:T(8,128)S(1)}, f32[12,48,128]{2,1,0:T(8,128)S(1)}, u32[]{:S(2)}, u32[]{:S(2)}) collective-permute-start(f32[12,48,128]{2,1,0:T(8,128)S(1)} %get-tuple-element.33), channel_id=1, source_target_pairs={{0,1},{1,2},{2,3},{3,4},{4,5},{5,6},{6,7},{7,8},{8,9},{9,10},{10,1... | collective-permute-start | bytes 884744 | tf_op jit(solution)/shard_map/ppermute | solution.py:1018
  17.7 2.2 %collective-permute-start.3 = (f32[12,48,128]{2,1,0:T(8,128)S(1)}, f32[12,48,128]{2,1,0:T(8,128)S(1)}, u32[]{:S(2)}, u32[]{:S(2)}) collective-permute-start(f32[12,48,128]{2,1,0:T(8,128)S(1)} %get-tuple-element.34), channel_id=1, source_target_pairs={{1,0},{2,1},{3,2},{4,3},{5,4},{6,5},{7,6},{8,7},{9,8},{10,9},{11,1... | collective-permute-start | bytes 884744 | tf_op jit(solution)/shard_map/ppermute | solution.py:1018
  20.0 0.1 stack.35.near
  20.1 0.0 copy-done.1
  20.1 0.0 copy-done
  20.1 0.9 shard_map.80.inner
  21.0 0.4 collective-permute-done.2.ylo
  21.4 4.4 %collective-permute-done.3.yhi = f32[12,48,128]{2,1,0:T(8,128)S(1)} collective-permute-done((f32[12,48,128]{2,1,0:T(8,128)S(1)}, f32[12,48,128]{2,1,0:T(8,128)S(1)}, u32[]{:S(2)}, u32[]{:S(2)}) %collective-permute-start.3) | collective-permute-done | bytes 294944 | tf_op jit(solution)/shard_map/ppermute | solution.py:1018
  25.8 2.3 %shard_map.81 = (f32[8,64,128]{2,1,0:T(8,128)S(1)}, f32[64,128]{1,0:T(8,128)S(1)}, f32[64,128]{1,0:T(8,128)S(1)}) custom-call(f32[8]{0:T(128)S(1)} %stack.35.near, f32[632,128]{1,0:T(8,128)S(1)} %copy-done, bf16[1040,384]{1,0:T(8,128)(2,1)S(1)} %copy-done.1, f32[8,32,128]{2,1,0:T(8,128)S(1)} %shard_map.80.inner, f32[8,32,128]{2,1,0:T(8,128)S(1)} %get-tuple-element.29.b, ...), custom_call_target="tpu_custom_call" | custom-call | flops 1000000 | bytes 655360 | tf_op jit(solution)/shard_map/pallas_call | solution.py:1002
  28.1 4.0 %collective-permute-start.4 = (f32[64,128]{1,0:T(8,128)S(1)}, f32[64,128]{1,0:T(8,128)S(1)}, u32[]{:S(2)}, u32[]{:S(2)}) collective-permute-start(f32[64,128]{1,0:T(8,128)S(1)} %get-tuple-element.39), channel_id=1, source_target_pairs={{0,64},{64,128},{128,192},{192,256},{256,320},{320,384},{384,448},... | collective-permute-start | bytes 98312 | tf_op jit(solution)/shard_map/ppermute | solution.py:1018
  32.1 1.3 %collective-permute-start.5 = (f32[64,128]{1,0:T(8,128)S(1)}, f32[64,128]{1,0:T(8,128)S(1)}, u32[]{:S(2)}, u32[]{:S(2)}) collective-permute-start(f32[64,128]{1,0:T(8,128)S(1)} %get-tuple-element.40), channel_id=1, source_target_pairs={{64,0},{128,64},{192,128},{256,192},{320,256},{384,320},{448,384},... | collective-permute-start | bytes 98312 | tf_op jit(solution)/shard_map/ppermute | solution.py:1018
  33.4 1.5 %shard_map.79 = (f32[8,32,128]{2,1,0:T(8,128)}, f32[8,64,128]{2,1,0:T(8,128)S(1)}, f32[1,128]{1,0:T(1,128)S(1)}) custom-call(f32[8]{0:T(128)S(1)} %stack.35.near, f32[8,128]{1,0:T(8,128)S(1)} %get-tuple-element.28.solid, f32[632,128]{1,0:T(8,128)S(1)} %copy-done, f32[8,32,128]{2,1,0:T(8,128)S(1)} %get-tuple-element.29.b, ...), custom_call_target="tpu_custom_call" | custom-call | flops 20000000 | bytes 787456 | tf_op jit(solution)/shard_map/pallas_call | solution.py:1002
  34.9 0.0 collective-permute-done.4.zlo
  34.9 3.7 %collective-permute-done.5.zhi = f32[64,128]{1,0:T(8,128)S(1)} collective-permute-done((f32[64,128]{1,0:T(8,128)S(1)}, f32[64,128]{1,0:T(8,128)S(1)}, u32[]{:S(2)}, u32[]{:S(2)}) %collective-permute-start.5) | collective-permute-done | bytes 32800 | tf_op jit(solution)/shard_map/ppermute | solution.py:1018
  38.6 1.8 %shard_map.82 = (f32[8,64,128]{2,1,0:T(8,128)S(1)}, f32[8,64,128]{2,1,0:T(8,128)S(1)}, f32[8,64,128]{2,1,0:T(8,128)S(1)}, f32[8,64,128]{2,1,0:T(8,128)S(1)}, f32[8,128]{1,0:T(8,128)S(1)}) custom-call(f32[8]{0:T(128)S(1)} %stack.35.near, f32[632,128]{1,0:T(8,128)S(1)} %copy-done, f32[1,128]{1,0:T(1,128)S(1)} %get-tuple-element.37.stat_in, ...), custom_call_target="tpu_custom_call" | custom-call | flops 1000000 | bytes 2105344 | tf_op jit(solution)/shard_map/pallas_call | solution.py:1002
  40.4 4.9 %collective-permute-start.6 = (f32[8,64,128]{2,1,0:T(8,128)S(1)}, f32[8,64,128]{2,1,0:T(8,128)S(1)}, u32[]{:S(2)}, u32[]{:S(2)}) collective-permute-start(f32[8,64,128]{2,1,0:T(8,128)S(1)} %get-tuple-element.44), channel_id=1, source_target_pairs={{0,64},{64,128},{128,192},{192,256},{256,320},{320,384},{384,448},... | collective-permute-start | bytes 786440 | tf_op jit(solution)/shard_map/ppermute | solution.py:1018
  45.3 1.3 %collective-permute-start.7 = (f32[8,64,128]{2,1,0:T(8,128)S(1)}, f32[8,64,128]{2,1,0:T(8,128)S(1)}, u32[]{:S(2)}, u32[]{:S(2)}) collective-permute-start(f32[8,64,128]{2,1,0:T(8,128)S(1)} %get-tuple-element.45), channel_id=1, source_target_pairs={{64,0},{128,64},{192,128},{256,192},{320,256},{384,320},{448,384},... | collective-permute-start | bytes 786440 | tf_op jit(solution)/shard_map/ppermute | solution.py:1018
  46.6 12.9 %all_to_all.39 = f32[8,1,128]{2,1,0:T(1,128)S(1)} all-to-all(f32[8,1,128]{2,1,0:T(1,128)S(1)} %bitcast.26), channel_id=1, replica_groups=mesh['gx'=8,'gy'=64] {'gx'}, dimensions={0} | all-to-all | bytes 8192 | tf_op jit(solution)/shard_map/all_to_all | solution.py:1084
  59.5 0.3 shard_map.83
  59.8 22.0 %all_to_all.40 = f32[64,1,128]{2,1,0:T(1,128)S(1)} all-to-all(f32[64,1,128]{2,1,0:T(1,128)S(1)} %bitcast.21), channel_id=1, replica_groups=mesh['gx'=8,'gy'=64] {'gy'}, dimensions={0} | all-to-all | bytes 65536 | tf_op jit(solution)/shard_map/all_to_all | solution.py:1086
  81.8 2.9 %shard_map.84.coarse = f32[16,128]{1,0:T(8,128)S(1)} custom-call(f32[8]{0:T(128)S(1)} %stack.35.near, f32[64,128]{1,0:T(8,128)S(1)} %bitcast.22), custom_call_target="tpu_custom_call" | custom-call | flops 1000000 | bytes 16384 | tf_op jit(solution)/shard_map/pallas_call | solution.py:1002
  84.7 0.0 collective-permute-done.6.ylo
  84.7 0.0 collective-permute-done.7.yhi
  84.7 2.7 %shard_map.85 = (f32[8,32,128]{2,1,0:T(8,128)S(1)}, f32[8,32,128]{2,1,0:T(8,128)S(1)}, f32[8,32,128]{2,1,0:T(8,128)S(1)}, f32[32,128]{1,0:T(8,128)S(1)}, f32[32,128]{1,0:T(8,128)S(1)}) custom-call(f32[8]{0:T(128)S(1)} %stack.35.near, f32[632,128]{1,0:T(8,128)S(1)} %copy-done, bf16[1040,384]{1,0:T(8,128)(2,1)S(1)} %copy-done.1, ...), custom_call_target="tpu_custom_call" | custom-call | flops 1000000 | bytes 851968 | tf_op jit(solution)/shard_map/pallas_call | solution.py:1002
  87.5 2.2 %collective-permute-start.8 = (f32[32,128]{1,0:T(8,128)S(1)}, f32[32,128]{1,0:T(8,128)S(1)}, u32[]{:S(2)}, u32[]{:S(2)}) collective-permute-start(f32[32,128]{1,0:T(8,128)S(1)} %get-tuple-element.50), channel_id=1, source_target_pairs={{0,64},{64,128},{128,192},{192,256},{256,320},{320,384},{384,448},... | collective-permute-start | bytes 49160 | tf_op jit(solution)/shard_map/ppermute | solution.py:1018
  89.7 1.3 %collective-permute-start.9 = (f32[32,128]{1,0:T(8,128)S(1)}, f32[32,128]{1,0:T(8,128)S(1)}, u32[]{:S(2)}, u32[]{:S(2)}) collective-permute-start(f32[32,128]{1,0:T(8,128)S(1)} %get-tuple-element.51), channel_id=1, source_target_pairs={{64,0},{128,64},{192,128},{256,192},{320,256},{384,320},{448,384},... | collective-permute-start | bytes 49160 | tf_op jit(solution)/shard_map/ppermute | solution.py:1018
  91.0 1.1 shard_map.86
  92.1 0.0 collective-permute-done.8.zlo
  92.1 2.1 %collective-permute-done.9.zhi = f32[32,128]{1,0:T(8,128)S(1)} collective-permute-done((f32[32,128]{1,0:T(8,128)S(1)}, f32[32,128]{1,0:T(8,128)S(1)}, u32[]{:S(2)}, u32[]{:S(2)}) %collective-permute-start.9) | collective-permute-done | bytes 16416 | tf_op jit(solution)/shard_map/ppermute | solution.py:1018
  94.2 0.3 shard_map.87
  94.4 12.0 %all_to_all.41 = f32[16,1,128]{2,1,0:T(1,128)S(1)} all-to-all(f32[16,1,128]{2,1,0:T(1,128)S(1)} %bitcast.24), channel_id=1, replica_groups={{0,1,64,65,128,129,192,193,256,257,320,321,384,385,448,449},{2,3,66,67,..., dimensions={0} | all-to-all | bytes 16384 | tf_op jit(solution)/shard_map/all_to_all | solution.py:1119
  106.5 11.6 %all_to_all.42 = f32[32,1,128]{2,1,0:T(1,128)S(1)} all-to-all(f32[32,1,128]{2,1,0:T(1,128)S(1)} %broadcast_in_dim.2), channel_id=1, replica_groups={{0,2,4,6,8,10,12,14,16,18,20,22,24,26,28,30,32,34,36,38,40,42,44,46,48,..., dimensions={0} | all-to-all | bytes 32768 | tf_op jit(solution)/shard_map/all_to_all | solution.py:1121
  118.0 0.8 shard_map.88
  (3 shorter events, 0.1 us)
Async XLA Ops:
  0.6 19.5 %copy-start.1 = (bf16[1040,384]{1,0:T(8,128)(2,1)S(1)}, bf16[1040,384]{1,0:T(8,128)(2,1)}, u32[]{:S(2)}) copy-start(bf16[1040,384]{1,0:T(8,128)(2,1)} %constant.30.clone.tables) | copy-start | bytes 2396164
  2.4 17.7 %copy-start = (f32[632,128]{1,0:T(8,128)S(1)}, f32[632,128]{1,0:T(8,128)}, u32[]{:S(2)}) copy-start(f32[632,128]{1,0:T(8,128)} %constant.29.clone.packed_in.packed) | copy-start | bytes 970756
  2.4 6.3 %collective-permute-start = (f32[3,32,128]{2,1,0:T(8,128)S(1)}, f32[3,32,128]{2,1,0:T(8,128)S(1)}, u32[]{:S(2)}, u32[]{:S(2)}) collective-permute-start(f32[3,32,128]{2,1,0:T(8,128)S(1)} %get-tuple-element.31), channel_id=1, source_target_pairs={{0,64},{64,128},{128,192},{192,256},{256,320},{320,384},{384,448},... | collective-permute-start | bytes 147464 | tf_op jit(solution)/shard_map/ppermute | solution.py:1018
  7.4 5.5 %collective-permute-start.1 = (f32[3,32,128]{2,1,0:T(8,128)S(1)}, f32[3,32,128]{2,1,0:T(8,128)S(1)}, u32[]{:S(2)}, u32[]{:S(2)}) collective-permute-start(f32[3,32,128]{2,1,0:T(8,128)S(1)} %get-tuple-element.32), channel_id=1, source_target_pairs={{64,0},{128,64},{192,128},{256,192},{320,256},{384,320},{448,384},... | collective-permute-start | bytes 147464 | tf_op jit(solution)/shard_map/ppermute | solution.py:1018
  12.9 8.5 %collective-permute-start.2 = (f32[12,48,128]{2,1,0:T(8,128)S(1)}, f32[12,48,128]{2,1,0:T(8,128)S(1)}, u32[]{:S(2)}, u32[]{:S(2)}) collective-permute-start(f32[12,48,128]{2,1,0:T(8,128)S(1)} %get-tuple-element.33), channel_id=1, source_target_pairs={{0,1},{1,2},{2,3},{3,4},{4,5},{5,6},{6,7},{7,8},{8,9},{9,10},{10,1... | collective-permute-start | bytes 884744 | tf_op jit(solution)/shard_map/ppermute | solution.py:1018
  17.7 8.0 %collective-permute-start.3 = (f32[12,48,128]{2,1,0:T(8,128)S(1)}, f32[12,48,128]{2,1,0:T(8,128)S(1)}, u32[]{:S(2)}, u32[]{:S(2)}) collective-permute-start(f32[12,48,128]{2,1,0:T(8,128)S(1)} %get-tuple-element.34), channel_id=1, source_target_pairs={{1,0},{2,1},{3,2},{4,3},{5,4},{6,5},{7,6},{8,7},{9,8},{10,9},{11,1... | collective-permute-start | bytes 884744 | tf_op jit(solution)/shard_map/ppermute | solution.py:1018
  28.1 6.8 %collective-permute-start.4 = (f32[64,128]{1,0:T(8,128)S(1)}, f32[64,128]{1,0:T(8,128)S(1)}, u32[]{:S(2)}, u32[]{:S(2)}) collective-permute-start(f32[64,128]{1,0:T(8,128)S(1)} %get-tuple-element.39), channel_id=1, source_target_pairs={{0,64},{64,128},{128,192},{192,256},{256,320},{320,384},{384,448},... | collective-permute-start | bytes 98312 | tf_op jit(solution)/shard_map/ppermute | solution.py:1018
  32.1 6.5 %collective-permute-start.5 = (f32[64,128]{1,0:T(8,128)S(1)}, f32[64,128]{1,0:T(8,128)S(1)}, u32[]{:S(2)}, u32[]{:S(2)}) collective-permute-start(f32[64,128]{1,0:T(8,128)S(1)} %get-tuple-element.40), channel_id=1, source_target_pairs={{64,0},{128,64},{192,128},{256,192},{320,256},{384,320},{448,384},... | collective-permute-start | bytes 98312 | tf_op jit(solution)/shard_map/ppermute | solution.py:1018
  40.4 44.3 %collective-permute-start.6 = (f32[8,64,128]{2,1,0:T(8,128)S(1)}, f32[8,64,128]{2,1,0:T(8,128)S(1)}, u32[]{:S(2)}, u32[]{:S(2)}) collective-permute-start(f32[8,64,128]{2,1,0:T(8,128)S(1)} %get-tuple-element.44), channel_id=1, source_target_pairs={{0,64},{64,128},{128,192},{192,256},{256,320},{320,384},{384,448},... | collective-permute-start | bytes 786440 | tf_op jit(solution)/shard_map/ppermute | solution.py:1018
  45.3 39.5 %collective-permute-start.7 = (f32[8,64,128]{2,1,0:T(8,128)S(1)}, f32[8,64,128]{2,1,0:T(8,128)S(1)}, u32[]{:S(2)}, u32[]{:S(2)}) collective-permute-start(f32[8,64,128]{2,1,0:T(8,128)S(1)} %get-tuple-element.45), channel_id=1, source_target_pairs={{64,0},{128,64},{192,128},{256,192},{320,256},{384,320},{448,384},... | collective-permute-start | bytes 786440 | tf_op jit(solution)/shard_map/ppermute | solution.py:1018
  87.5 4.6 %collective-permute-start.8 = (f32[32,128]{1,0:T(8,128)S(1)}, f32[32,128]{1,0:T(8,128)S(1)}, u32[]{:S(2)}, u32[]{:S(2)}) collective-permute-start(f32[32,128]{1,0:T(8,128)S(1)} %get-tuple-element.50), channel_id=1, source_target_pairs={{0,64},{64,128},{128,192},{192,256},{256,320},{320,384},{384,448},... | collective-permute-start | bytes 49160 | tf_op jit(solution)/shard_map/ppermute | solution.py:1018
  89.7 4.5 %collective-permute-start.9 = (f32[32,128]{1,0:T(8,128)S(1)}, f32[32,128]{1,0:T(8,128)S(1)}, u32[]{:S(2)}, u32[]{:S(2)}) collective-permute-start(f32[32,128]{1,0:T(8,128)S(1)} %get-tuple-element.51), channel_id=1, source_target_pairs={{64,0},{128,64},{192,128},{256,192},{320,256},{384,320},{448,384},... | collective-permute-start | bytes 49160 | tf_op jit(solution)/shard_map/ppermute | solution.py:1018

commit v15 on v14

--- a/solution.py
+++ b/solution.py
@@ -612,8 +612,7 @@
     stat[...] = jnp.broadcast_to(stat_in[...] + lane_row(entries), stat.shape)
 
 
-def column_kernel(gathered, out_ref):
-    values = gathered[...]
+def merged_row(values):
     sub = lax.broadcasted_iota(jnp.int32, (8, LANES), 0)
     lane = lax.broadcasted_iota(jnp.int32, (8, LANES), 1)
     after = jnp.where(sub < 7, pltpu.roll(values, 7, 0), 0.0)
@@ -645,7 +644,13 @@
     total = rows[0:1]
     for i in range(1, 8):
         total = total + pltpu.roll(rows[i : i + 1], 16 * i, 1)
-    out_ref[...] = jnp.broadcast_to(total, out_ref.shape)
+    return total
+
+
+def column_kernel(gathered, out_ref):
+    even, odd = (merged_row(gathered[pl.ds(c, 8, stride=2), :]) for c in range(2))
+    row = lax.broadcasted_iota(jnp.int32, out_ref.shape, 0)
+    out_ref[...] = jnp.where(row % 2 == 0, even, odd)
 
 
 def invert(blocks, sub):
@@ -1042,6 +1047,15 @@
     wide_face = (WIDE, LANES)
     rim = (12, TILE, LANES)
 
+    pairs = count_gy // 2
+    columns = [
+        [z * count_gy + 2 * m + c for z in range(count_gx) for c in range(2)] for m in range(pairs)
+    ]
+    layers = [
+        [z * count_gy + 2 * m + c for m in range(pairs)] for z in range(count_gx) for c in range(2)
+    ]
+    axes = ("gx", "gy")
+
     b, l, zlo, zhi, solid = run(
         advect_kernel,
         [block, block, (3, *face), (3, *face), (8, LANES)],
@@ -1076,14 +1090,14 @@
     )
     zl, yl, zlo, zhi, stat = run(
         galerkin_kernel,
-        [wide_block, wide_block, wide_block, wide_block, (count_gx, LANES)],
+        [wide_block, wide_block, wide_block, wide_block, (2 * count_gx, LANES)],
         [near],
         [packed, stat, flux, w, wlo, whi],
     )
     zlo, zhi = shift("gx", zlo, zhi)
-    gathered = lax.all_to_all(stat, "gx", 0, 0, tiled=True)
+    gathered = lax.all_to_all(stat, axes, 0, 0, axis_index_groups=columns, tiled=True)
     (column,) = run(column_kernel, [(count_gy, LANES)], [], [gathered])
-    gathered = lax.all_to_all(column, "gy", 0, 0, tiled=True)
+    gathered = lax.all_to_all(column, axes, 0, 0, axis_index_groups=layers, tiled=True)
     (coarse,) = run(
         functools.partial(coarse_kernel, count_gy),
         [(16, LANES)],
@@ -1108,14 +1122,6 @@
     (sums,) = run(
         face_kernel, [(2 * count_gx, LANES)], [], [packed, flux, b, y, kx, zlo, zhi, sums]
     )
-    pairs = count_gy // 2
-    columns = [
-        [z * count_gy + 2 * m + c for z in range(count_gx) for c in range(2)] for m in range(pairs)
-    ]
-    layers = [
-        [z * count_gy + 2 * m + c for m in range(pairs)] for z in range(count_gx) for c in range(2)
-    ]
-    axes = ("gx", "gy")
     tile = lax.all_to_all(sums, axes, 0, 0, axis_index_groups=columns, tiled=True)
     wide = jnp.broadcast_to(jnp.sum(tile, axis=0, keepdims=True), (pairs, LANES))
     wide = lax.all_to_all(wide, axes, 0, 0, axis_index_groups=layers, tiled=True)

time: 119 us -> 120 us (level)
    all_to_all x1, blocking collectives: 12 us -> 13.4 us  [body(): lax.all_to_all(sums, axes, 0, 0, axis_index_groups=columns, tiled=True)]
where the time goes in v15:
time: 120 us; the launch traced here: 119 us
  blocking collectives  59 us (49%)
  starting transfers between devices  28.3 us (24%)
  Pallas kernels  16.4 us (14%)
  waiting for transfers between devices  14.7 us (12%)
    ppermute x5, starting transfers between devices, shift(): lax.ppermute(high_face, axis, forward)  20.8 us
    all_to_all x1, blocking collectives, body(): lax.all_to_all(column, axes, 0, 0, axis_index_groups=layers, tiled=True)  20.2 us
    pallas_call x12, Pallas kernels, run(): pl.pallas_call(kernel, out_shape=[jax.ShapeDtypeStruct(out, F32) for out...  16.4 us
    ppermute x5, waiting for transfers between devices, shift(): lax.ppermute(low_face, axis, backward)  14.3 us
    all_to_all x1, blocking collectives, body(): lax.all_to_all(stat, axes, 0, 0, axis_index_groups=columns, tiled=True)  13.8 us
    all_to_all x1, blocking collectives, body(): lax.all_to_all(sums, axes, 0, 0, axis_index_groups=columns, tiled=True)  13.4 us
    all_to_all x1, blocking collectives, body(): lax.all_to_all(wide, axes, 0, 0, axis_index_groups=layers, tiled=True)  11.6 us
    ppermute x5, starting transfers between devices, shift(): lax.ppermute(low_face, axis, backward)  7.41 us
  transfers between devices with their start and end apart: 10, of which 5 were waited for; matrix products, arithmetic and copies ran while one was open for 0% of the time, Pallas kernels for 6%

profile of v15, /device:TPU:1, one launch (start us, length us, event | category | flops | bytes accessed | tf_op | source)
XLA Modules:
  0.0 119.4 jit_solution(8185579202056045839)
XLA Ops:
  0.6 0.0 copy-start.1
  0.6 1.8 %shard_map.77 = (f32[8,32,128]{2,1,0:T(8,128)S(1)}, f32[8,32,128]{2,1,0:T(8,128)S(1)}, f32[3,32,128]{2,1,0:T(8,128)S(1)}, f32[3,32,128]{2,1,0:T(8,128)S(1)}, f32[8,128]{1,0:T(8,128)S(1)}) custom-call(f32[8,32,128]{2,1,0:T(8,128)} %lev_in.1, f32[3,8,32,128]{3,2,1,0:T(8,128)} %vel_in.1, f32[8,32,128]{2,1,0:T(8,128)} %src_in.1, ...), custom_call_target="tpu_custom_call" | custom-call | flops 1000000 | bytes 729088 | tf_op jit(solution)/shard_map/pallas_call | solution.py:1007
  2.4 0.0 copy-start
  2.4 5.0 %collective-permute-start = (f32[3,32,128]{2,1,0:T(8,128)S(1)}, f32[3,32,128]{2,1,0:T(8,128)S(1)}, u32[]{:S(2)}, u32[]{:S(2)}) collective-permute-start(f32[3,32,128]{2,1,0:T(8,128)S(1)} %get-tuple-element.31), channel_id=1, source_target_pairs={{0,64},{64,128},{128,192},{192,256},{256,320},{320,384},{384,448},... | collective-permute-start | bytes 147464 | tf_op jit(solution)/shard_map/ppermute | solution.py:1023
  7.4 1.3 %collective-permute-start.1 = (f32[3,32,128]{2,1,0:T(8,128)S(1)}, f32[3,32,128]{2,1,0:T(8,128)S(1)}, u32[]{:S(2)}, u32[]{:S(2)}) collective-permute-start(f32[3,32,128]{2,1,0:T(8,128)S(1)} %get-tuple-element.32), channel_id=1, source_target_pairs={{64,0},{128,64},{192,128},{256,192},{320,256},{384,320},{448,384},... | collective-permute-start | bytes 147464 | tf_op jit(solution)/shard_map/ppermute | solution.py:1023
  8.7 0.0 collective-permute-done.low_z.zlo
  8.7 4.2 %collective-permute-done.1.high_z.zhi = f32[3,32,128]{2,1,0:T(8,128)S(1)} collective-permute-done((f32[3,32,128]{2,1,0:T(8,128)S(1)}, f32[3,32,128]{2,1,0:T(8,128)S(1)}, u32[]{:S(2)}, u32[]{:S(2)}) %collective-permute-start.1) | collective-permute-done | bytes 49184 | tf_op jit(solution)/shard_map/ppermute | solution.py:1023
  12.9 4.8 %collective-permute-start.2 = (f32[12,48,128]{2,1,0:T(8,128)S(1)}, f32[12,48,128]{2,1,0:T(8,128)S(1)}, u32[]{:S(2)}, u32[]{:S(2)}) collective-permute-start(f32[12,48,128]{2,1,0:T(8,128)S(1)} %get-tuple-element.33), channel_id=1, source_target_pairs={{0,1},{1,2},{2,3},{3,4},{4,5},{5,6},{6,7},{7,8},{8,9},{9,10},{10,1... | collective-permute-start | bytes 884744 | tf_op jit(solution)/shard_map/ppermute | solution.py:1023
  17.7 2.2 %collective-permute-start.3 = (f32[12,48,128]{2,1,0:T(8,128)S(1)}, f32[12,48,128]{2,1,0:T(8,128)S(1)}, u32[]{:S(2)}, u32[]{:S(2)}) collective-permute-start(f32[12,48,128]{2,1,0:T(8,128)S(1)} %get-tuple-element.34), channel_id=1, source_target_pairs={{1,0},{2,1},{3,2},{4,3},{5,4},{6,5},{7,6},{8,7},{9,8},{10,9},{11,1... | collective-permute-start | bytes 884744 | tf_op jit(solution)/shard_map/ppermute | solution.py:1023
  20.0 0.1 stack.35.near
  20.1 0.0 copy-done.1
  20.1 0.0 copy-done
  20.1 0.9 shard_map.80.inner
  21.0 0.4 collective-permute-done.2.ylo
  21.4 4.4 %collective-permute-done.3.yhi = f32[12,48,128]{2,1,0:T(8,128)S(1)} collective-permute-done((f32[12,48,128]{2,1,0:T(8,128)S(1)}, f32[12,48,128]{2,1,0:T(8,128)S(1)}, u32[]{:S(2)}, u32[]{:S(2)}) %collective-permute-start.3) | collective-permute-done | bytes 294944 | tf_op jit(solution)/shard_map/ppermute | solution.py:1023
  25.8 2.3 %shard_map.81 = (f32[8,64,128]{2,1,0:T(8,128)S(1)}, f32[64,128]{1,0:T(8,128)S(1)}, f32[64,128]{1,0:T(8,128)S(1)}) custom-call(f32[8]{0:T(128)S(1)} %stack.35.near, f32[632,128]{1,0:T(8,128)S(1)} %copy-done, bf16[1040,384]{1,0:T(8,128)(2,1)S(1)} %copy-done.1, f32[8,32,128]{2,1,0:T(8,128)S(1)} %shard_map.80.inner, f32[8,32,128]{2,1,0:T(8,128)S(1)} %get-tuple-element.29.b, ...), custom_call_target="tpu_custom_call" | custom-call | flops 1000000 | bytes 655360 | tf_op jit(solution)/shard_map/pallas_call | solution.py:1007
  28.1 4.0 %collective-permute-start.4 = (f32[64,128]{1,0:T(8,128)S(1)}, f32[64,128]{1,0:T(8,128)S(1)}, u32[]{:S(2)}, u32[]{:S(2)}) collective-permute-start(f32[64,128]{1,0:T(8,128)S(1)} %get-tuple-element.39), channel_id=1, source_target_pairs={{0,64},{64,128},{128,192},{192,256},{256,320},{320,384},{384,448},... | collective-permute-start | bytes 98312 | tf_op jit(solution)/shard_map/ppermute | solution.py:1023
  32.1 1.3 %collective-permute-start.5 = (f32[64,128]{1,0:T(8,128)S(1)}, f32[64,128]{1,0:T(8,128)S(1)}, u32[]{:S(2)}, u32[]{:S(2)}) collective-permute-start(f32[64,128]{1,0:T(8,128)S(1)} %get-tuple-element.40), channel_id=1, source_target_pairs={{64,0},{128,64},{192,128},{256,192},{320,256},{384,320},{448,384},... | collective-permute-start | bytes 98312 | tf_op jit(solution)/shard_map/ppermute | solution.py:1023
  33.4 1.5 %shard_map.79 = (f32[8,32,128]{2,1,0:T(8,128)}, f32[8,64,128]{2,1,0:T(8,128)S(1)}, f32[1,128]{1,0:T(1,128)S(1)}) custom-call(f32[8]{0:T(128)S(1)} %stack.35.near, f32[8,128]{1,0:T(8,128)S(1)} %get-tuple-element.28.solid, f32[632,128]{1,0:T(8,128)S(1)} %copy-done, f32[8,32,128]{2,1,0:T(8,128)S(1)} %get-tuple-element.29.b, ...), custom_call_target="tpu_custom_call" | custom-call | flops 20000000 | bytes 787456 | tf_op jit(solution)/shard_map/pallas_call | solution.py:1007
  34.9 0.0 collective-permute-done.4.zlo
  34.9 3.7 %collective-permute-done.5.zhi = f32[64,128]{1,0:T(8,128)S(1)} collective-permute-done((f32[64,128]{1,0:T(8,128)S(1)}, f32[64,128]{1,0:T(8,128)S(1)}, u32[]{:S(2)}, u32[]{:S(2)}) %collective-permute-start.5) | collective-permute-done | bytes 32800 | tf_op jit(solution)/shard_map/ppermute | solution.py:1023
  38.6 1.8 %shard_map.82 = (f32[8,64,128]{2,1,0:T(8,128)S(1)}, f32[8,64,128]{2,1,0:T(8,128)S(1)}, f32[8,64,128]{2,1,0:T(8,128)S(1)}, f32[8,64,128]{2,1,0:T(8,128)S(1)}, f32[16,128]{1,0:T(8,128)S(1)}) custom-call(f32[8]{0:T(128)S(1)} %stack.35.near, f32[632,128]{1,0:T(8,128)S(1)} %copy-done, f32[1,128]{1,0:T(1,128)S(1)} %get-tuple-element.37.stat_in, ...), custom_call_target="tpu_custom_call" | custom-call | flops 1000000 | bytes 2113536 | tf_op jit(solution)/shard_map/pallas_call | solution.py:1007
  40.4 4.9 %collective-permute-start.6 = (f32[8,64,128]{2,1,0:T(8,128)S(1)}, f32[8,64,128]{2,1,0:T(8,128)S(1)}, u32[]{:S(2)}, u32[]{:S(2)}) collective-permute-start(f32[8,64,128]{2,1,0:T(8,128)S(1)} %get-tuple-element.44), channel_id=1, source_target_pairs={{0,64},{64,128},{128,192},{192,256},{256,320},{320,384},{384,448},... | collective-permute-start | bytes 786440 | tf_op jit(solution)/shard_map/ppermute | solution.py:1023
  45.3 1.3 %collective-permute-start.7 = (f32[8,64,128]{2,1,0:T(8,128)S(1)}, f32[8,64,128]{2,1,0:T(8,128)S(1)}, u32[]{:S(2)}, u32[]{:S(2)}) collective-permute-start(f32[8,64,128]{2,1,0:T(8,128)S(1)} %get-tuple-element.45), channel_id=1, source_target_pairs={{64,0},{128,64},{192,128},{256,192},{320,256},{384,320},{448,384},... | collective-permute-start | bytes 786440 | tf_op jit(solution)/shard_map/ppermute | solution.py:1023
  46.6 13.8 %all_to_all.39 = f32[16,1,128]{2,1,0:T(1,128)S(1)} all-to-all(f32[16,1,128]{2,1,0:T(1,128)S(1)} %bitcast.24), channel_id=1, replica_groups={{0,1,64,65,128,129,192,193,256,257,320,321,384,385,448,449},{2,3,66,67,..., dimensions={0} | all-to-all | bytes 16384 | tf_op jit(solution)/shard_map/all_to_all | solution.py:1098
  60.4 0.3 shard_map.83
  60.7 20.2 %all_to_all.40 = f32[32,2,128]{2,1,0:T(2,128)S(1)} all-to-all(f32[32,2,128]{2,1,0:T(2,128)S(1)} %bitcast.19), channel_id=1, replica_groups={{0,2,4,6,8,10,12,14,16,18,20,22,24,26,28,30,32,34,36,38,40,42,44,46,48,..., dimensions={0} | all-to-all | bytes 65536 | tf_op jit(solution)/shard_map/all_to_all | solution.py:1100
  80.9 2.9 %shard_map.84.coarse = f32[16,128]{1,0:T(8,128)S(1)} custom-call(f32[8]{0:T(128)S(1)} %stack.35.near, f32[64,128]{1,0:T(8,128)S(1)} %bitcast.20), custom_call_target="tpu_custom_call" | custom-call | flops 1000000 | bytes 16384 | tf_op jit(solution)/shard_map/pallas_call | solution.py:1007
  83.8 0.0 collective-permute-done.6.ylo
  83.8 0.0 collective-permute-done.7.yhi
  83.8 2.7 %shard_map.85 = (f32[8,32,128]{2,1,0:T(8,128)S(1)}, f32[8,32,128]{2,1,0:T(8,128)S(1)}, f32[8,32,128]{2,1,0:T(8,128)S(1)}, f32[32,128]{1,0:T(8,128)S(1)}, f32[32,128]{1,0:T(8,128)S(1)}) custom-call(f32[8]{0:T(128)S(1)} %stack.35.near, f32[632,128]{1,0:T(8,128)S(1)} %copy-done, bf16[1040,384]{1,0:T(8,128)(2,1)S(1)} %copy-done.1, ...), custom_call_target="tpu_custom_call" | custom-call | flops 1000000 | bytes 851968 | tf_op jit(solution)/shard_map/pallas_call | solution.py:1007
  86.6 2.2 %collective-permute-start.8 = (f32[32,128]{1,0:T(8,128)S(1)}, f32[32,128]{1,0:T(8,128)S(1)}, u32[]{:S(2)}, u32[]{:S(2)}) collective-permute-start(f32[32,128]{1,0:T(8,128)S(1)} %get-tuple-element.50), channel_id=1, source_target_pairs={{0,64},{64,128},{128,192},{192,256},{256,320},{320,384},{384,448},... | collective-permute-start | bytes 49160 | tf_op jit(solution)/shard_map/ppermute | solution.py:1023
  88.8 1.3 %collective-permute-start.9 = (f32[32,128]{1,0:T(8,128)S(1)}, f32[32,128]{1,0:T(8,128)S(1)}, u32[]{:S(2)}, u32[]{:S(2)}) collective-permute-start(f32[32,128]{1,0:T(8,128)S(1)} %get-tuple-element.51), channel_id=1, source_target_pairs={{64,0},{128,64},{192,128},{256,192},{320,256},{384,320},{448,384},... | collective-permute-start | bytes 49160 | tf_op jit(solution)/shard_map/ppermute | solution.py:1023
  90.1 1.1 shard_map.86
  91.2 0.0 collective-permute-done.8.zlo
  91.2 2.1 %collective-permute-done.9.zhi = f32[32,128]{1,0:T(8,128)S(1)} collective-permute-done((f32[32,128]{1,0:T(8,128)S(1)}, f32[32,128]{1,0:T(8,128)S(1)}, u32[]{:S(2)}, u32[]{:S(2)}) %collective-permute-start.9) | collective-permute-done | bytes 16416 | tf_op jit(solution)/shard_map/ppermute | solution.py:1023
  93.2 0.3 shard_map.87
  93.5 13.4 %all_to_all.41 = f32[16,1,128]{2,1,0:T(1,128)S(1)} all-to-all(f32[16,1,128]{2,1,0:T(1,128)S(1)} %bitcast.22), channel_id=1, replica_groups={{0,1,64,65,128,129,192,193,256,257,320,321,384,385,448,449},{2,3,66,67,..., dimensions={0} | all-to-all | bytes 16384 | tf_op jit(solution)/shard_map/all_to_all | solution.py:1125
  107.0 11.6 %all_to_all.42 = f32[32,1,128]{2,1,0:T(1,128)S(1)} all-to-all(f32[32,1,128]{2,1,0:T(1,128)S(1)} %broadcast_in_dim.2), channel_id=1, replica_groups={{0,2,4,6,8,10,12,14,16,18,20,22,24,26,28,30,32,34,36,38,40,42,44,46,48,..., dimensions={0} | all-to-all | bytes 32768 | tf_op jit(solution)/shard_map/all_to_all | solution.py:1127
  118.6 0.8 shard_map.88
  (3 shorter events, 0.1 us)
Async XLA Ops:
  0.6 19.5 %copy-start.1 = (bf16[1040,384]{1,0:T(8,128)(2,1)S(1)}, bf16[1040,384]{1,0:T(8,128)(2,1)}, u32[]{:S(2)}) copy-start(bf16[1040,384]{1,0:T(8,128)(2,1)} %constant.30.clone.tables) | copy-start | bytes 2396164
  2.4 17.7 %copy-start = (f32[632,128]{1,0:T(8,128)S(1)}, f32[632,128]{1,0:T(8,128)}, u32[]{:S(2)}) copy-start(f32[632,128]{1,0:T(8,128)} %constant.29.clone.packed_in.packed) | copy-start | bytes 970756
  2.4 6.3 %collective-permute-start = (f32[3,32,128]{2,1,0:T(8,128)S(1)}, f32[3,32,128]{2,1,0:T(8,128)S(1)}, u32[]{:S(2)}, u32[]{:S(2)}) collective-permute-start(f32[3,32,128]{2,1,0:T(8,128)S(1)} %get-tuple-element.31), channel_id=1, source_target_pairs={{0,64},{64,128},{128,192},{192,256},{256,320},{320,384},{384,448},... | collective-permute-start | bytes 147464 | tf_op jit(solution)/shard_map/ppermute | solution.py:1023
  7.4 5.5 %collective-permute-start.1 = (f32[3,32,128]{2,1,0:T(8,128)S(1)}, f32[3,32,128]{2,1,0:T(8,128)S(1)}, u32[]{:S(2)}, u32[]{:S(2)}) collective-permute-start(f32[3,32,128]{2,1,0:T(8,128)S(1)} %get-tuple-element.32), channel_id=1, source_target_pairs={{64,0},{128,64},{192,128},{256,192},{320,256},{384,320},{448,384},... | collective-permute-start | bytes 147464 | tf_op jit(solution)/shard_map/ppermute | solution.py:1023
  12.9 8.5 %collective-permute-start.2 = (f32[12,48,128]{2,1,0:T(8,128)S(1)}, f32[12,48,128]{2,1,0:T(8,128)S(1)}, u32[]{:S(2)}, u32[]{:S(2)}) collective-permute-start(f32[12,48,128]{2,1,0:T(8,128)S(1)} %get-tuple-element.33), channel_id=1, source_target_pairs={{0,1},{1,2},{2,3},{3,4},{4,5},{5,6},{6,7},{7,8},{8,9},{9,10},{10,1... | collective-permute-start | bytes 884744 | tf_op jit(solution)/shard_map/ppermute | solution.py:1023
  17.7 8.0 %collective-permute-start.3 = (f32[12,48,128]{2,1,0:T(8,128)S(1)}, f32[12,48,128]{2,1,0:T(8,128)S(1)}, u32[]{:S(2)}, u32[]{:S(2)}) collective-permute-start(f32[12,48,128]{2,1,0:T(8,128)S(1)} %get-tuple-element.34), channel_id=1, source_target_pairs={{1,0},{2,1},{3,2},{4,3},{5,4},{6,5},{7,6},{8,7},{9,8},{10,9},{11,1... | collective-permute-start | bytes 884744 | tf_op jit(solution)/shard_map/ppermute | solution.py:1023
  28.1 6.8 %collective-permute-start.4 = (f32[64,128]{1,0:T(8,128)S(1)}, f32[64,128]{1,0:T(8,128)S(1)}, u32[]{:S(2)}, u32[]{:S(2)}) collective-permute-start(f32[64,128]{1,0:T(8,128)S(1)} %get-tuple-element.39), channel_id=1, source_target_pairs={{0,64},{64,128},{128,192},{192,256},{256,320},{320,384},{384,448},... | collective-permute-start | bytes 98312 | tf_op jit(solution)/shard_map/ppermute | solution.py:1023
  32.1 6.5 %collective-permute-start.5 = (f32[64,128]{1,0:T(8,128)S(1)}, f32[64,128]{1,0:T(8,128)S(1)}, u32[]{:S(2)}, u32[]{:S(2)}) collective-permute-start(f32[64,128]{1,0:T(8,128)S(1)} %get-tuple-element.40), channel_id=1, source_target_pairs={{64,0},{128,64},{192,128},{256,192},{320,256},{384,320},{448,384},... | collective-permute-start | bytes 98312 | tf_op jit(solution)/shard_map/ppermute | solution.py:1023
  40.4 43.4 %collective-permute-start.6 = (f32[8,64,128]{2,1,0:T(8,128)S(1)}, f32[8,64,128]{2,1,0:T(8,128)S(1)}, u32[]{:S(2)}, u32[]{:S(2)}) collective-permute-start(f32[8,64,128]{2,1,0:T(8,128)S(1)} %get-tuple-element.44), channel_id=1, source_target_pairs={{0,64},{64,128},{128,192},{192,256},{256,320},{320,384},{384,448},... | collective-permute-start | bytes 786440 | tf_op jit(solution)/shard_map/ppermute | solution.py:1023
  45.3 38.6 %collective-permute-start.7 = (f32[8,64,128]{2,1,0:T(8,128)S(1)}, f32[8,64,128]{2,1,0:T(8,128)S(1)}, u32[]{:S(2)}, u32[]{:S(2)}) collective-permute-start(f32[8,64,128]{2,1,0:T(8,128)S(1)} %get-tuple-element.45), channel_id=1, source_target_pairs={{64,0},{128,64},{192,128},{256,192},{320,256},{384,320},{448,384},... | collective-permute-start | bytes 786440 | tf_op jit(solution)/shard_map/ppermute | solution.py:1023
  86.6 4.6 %collective-permute-start.8 = (f32[32,128]{1,0:T(8,128)S(1)}, f32[32,128]{1,0:T(8,128)S(1)}, u32[]{:S(2)}, u32[]{:S(2)}) collective-permute-start(f32[32,128]{1,0:T(8,128)S(1)} %get-tuple-element.50), channel_id=1, source_target_pairs={{0,64},{64,128},{128,192},{192,256},{256,320},{320,384},{384,448},... | collective-permute-start | bytes 49160 | tf_op jit(solution)/shard_map/ppermute | solution.py:1023
  88.8 4.5 %collective-permute-start.9 = (f32[32,128]{1,0:T(8,128)S(1)}, f32[32,128]{1,0:T(8,128)S(1)}, u32[]{:S(2)}, u32[]{:S(2)}) collective-permute-start(f32[32,128]{1,0:T(8,128)S(1)} %get-tuple-element.51), channel_id=1, source_target_pairs={{64,0},{128,64},{192,128},{256,192},{320,256},{384,320},{448,384},... | collective-permute-start | bytes 49160 | tf_op jit(solution)/shard_map/ppermute | solution.py:1023

commit v16 on v14

--- a/solution.py
+++ b/solution.py
@@ -926,6 +926,16 @@
     store_faces(planes, near, w_ref, wlo, whi)
 
 
+def solve_apply_kernel(
+    count, near, gathered, packed, tables, flux, zl, yl, ylo, yhi,
+    coarse, z_ref, y_ref, w_ref, wlo, whi, wide, turned,
+):
+    coarse_kernel(count, near, gathered, coarse, wide, turned)
+    apply_kernel(
+        near, packed, tables, coarse, flux, zl, yl, ylo, yhi, z_ref, y_ref, w_ref, wlo, whi
+    )
+
+
 def second_kernel(near, packed, coarse, flux, b, y, z, w, x_ref, kx_ref, stat):
     columns = [column[RING : RING + ROWS] for column in coarse_columns(near, coarse, 9, 3)]
     field = add_coarse(w[...], coarse_planes(columns, 1.0 - near[0], 1.0 - near[1]))
@@ -1084,18 +1094,12 @@
     gathered = lax.all_to_all(stat, "gx", 0, 0, tiled=True)
     (column,) = run(column_kernel, [(count_gy, LANES)], [], [gathered])
     gathered = lax.all_to_all(column, "gy", 0, 0, tiled=True)
-    (coarse,) = run(
-        functools.partial(coarse_kernel, count_gy),
-        [(16, LANES)],
+    coarse, z, y, w, wlo, whi = run(
+        functools.partial(solve_apply_kernel, count_gy),
+        [(16, LANES), block, block, block, face, face],
         [near],
-        [gathered],
+        [gathered, packed, tables, flux, zl, yl, zlo, zhi],
         [VMEM((LANES, LANES), F32), VMEM((LANES, LANES), F32)],
-    )
-    z, y, w, wlo, whi = run(
-        apply_kernel,
-        [block, block, block, face, face],
-        [near],
-        [packed, tables, coarse, flux, zl, yl, zlo, zhi],
     )
     zlo, zhi = shift("gx", wlo, whi)
     x, kx, sums = run(

time: 119 us -> 118 us (level)
  Pallas kernels: 16.4 us -> 15.2 us
    pallas_call x12 -> x11, Pallas kernels: 16.4 us -> 15.2 us  [run(): pl.pallas_call(kernel, out_shape=[jax.ShapeDtypeStruct(out, F32) for out...]
  transfers between devices with their start and end apart: 10 -> 10, of which waited for: 5 -> 5; matrix products, arithmetic and copies ran while one was open for 0% -> 0% of each run, Pallas kernels for 6% -> 3%
where the time goes in v16:
time: 118 us
  blocking collectives  58.5 us (50%)
  starting transfers between devices  28.3 us (24%)
  Pallas kernels  15.2 us (13%)
  waiting for transfers between devices  14.7 us (12%)
    all_to_all x1, blocking collectives, body(): gathered = lax.all_to_all(column, 'gy', 0, 0, tiled=True)  22 us
    ppermute x5, starting transfers between devices, shift(): lax.ppermute(high_face, axis, forward)  20.8 us
    pallas_call x11, Pallas kernels, run(): pl.pallas_call(kernel, out_shape=[jax.ShapeDtypeStruct(out, F32) for out...  15.2 us
    ppermute x5, waiting for transfers between devices, shift(): lax.ppermute(low_face, axis, backward)  14.3 us
    all_to_all x1, blocking collectives, body(): gathered = lax.all_to_all(stat, 'gx', 0, 0, tiled=True)  12.9 us
    all_to_all x1, blocking collectives, body(): lax.all_to_all(sums, axes, 0, 0, axis_index_groups=columns, tiled=True)  12 us
    all_to_all x1, blocking collectives, body(): lax.all_to_all(wide, axes, 0, 0, axis_index_groups=layers, tiled=True)  11.6 us
    ppermute x5, starting transfers between devices, shift(): lax.ppermute(low_face, axis, backward)  7.41 us
  transfers between devices with their start and end apart: 10, of which 5 were waited for; matrix products, arithmetic and copies ran while one was open for 0% of the time, Pallas kernels for 3%

profile of v16, /device:TPU:1, one launch (start us, length us, event | category | flops | bytes accessed | tf_op | source)
XLA Modules:
  0.0 117.7 jit_solution(10764694532909866729)
XLA Ops:
  0.6 0.0 copy-start.1
  0.6 1.8 %shard_map.77 = (f32[8,32,128]{2,1,0:T(8,128)S(1)}, f32[8,32,128]{2,1,0:T(8,128)S(1)}, f32[3,32,128]{2,1,0:T(8,128)S(1)}, f32[3,32,128]{2,1,0:T(8,128)S(1)}, f32[8,128]{1,0:T(8,128)S(1)}) custom-call(f32[8,32,128]{2,1,0:T(8,128)} %lev_in.1, f32[3,8,32,128]{3,2,1,0:T(8,128)} %vel_in.1, f32[8,32,128]{2,1,0:T(8,128)} %src_in.1, ...), custom_call_target="tpu_custom_call" | custom-call | flops 1000000 | bytes 729088 | tf_op jit(solution)/shard_map/pallas_call | solution.py:1012
  2.4 0.0 copy-start
  2.4 5.0 %collective-permute-start = (f32[3,32,128]{2,1,0:T(8,128)S(1)}, f32[3,32,128]{2,1,0:T(8,128)S(1)}, u32[]{:S(2)}, u32[]{:S(2)}) collective-permute-start(f32[3,32,128]{2,1,0:T(8,128)S(1)} %get-tuple-element.32), channel_id=1, source_target_pairs={{0,64},{64,128},{128,192},{192,256},{256,320},{320,384},{384,448},... | collective-permute-start | bytes 147464 | tf_op jit(solution)/shard_map/ppermute | solution.py:1028
  7.4 1.3 %collective-permute-start.1 = (f32[3,32,128]{2,1,0:T(8,128)S(1)}, f32[3,32,128]{2,1,0:T(8,128)S(1)}, u32[]{:S(2)}, u32[]{:S(2)}) collective-permute-start(f32[3,32,128]{2,1,0:T(8,128)S(1)} %get-tuple-element.33), channel_id=1, source_target_pairs={{64,0},{128,64},{192,128},{256,192},{320,256},{384,320},{448,384},... | collective-permute-start | bytes 147464 | tf_op jit(solution)/shard_map/ppermute | solution.py:1028
  8.7 0.0 collective-permute-done.low_z.zlo
  8.7 4.2 %collective-permute-done.1.high_z.zhi = f32[3,32,128]{2,1,0:T(8,128)S(1)} collective-permute-done((f32[3,32,128]{2,1,0:T(8,128)S(1)}, f32[3,32,128]{2,1,0:T(8,128)S(1)}, u32[]{:S(2)}, u32[]{:S(2)}) %collective-permute-start.1) | collective-permute-done | bytes 49184 | tf_op jit(solution)/shard_map/ppermute | solution.py:1028
  12.9 4.8 %collective-permute-start.2 = (f32[12,48,128]{2,1,0:T(8,128)S(1)}, f32[12,48,128]{2,1,0:T(8,128)S(1)}, u32[]{:S(2)}, u32[]{:S(2)}) collective-permute-start(f32[12,48,128]{2,1,0:T(8,128)S(1)} %get-tuple-element.34), channel_id=1, source_target_pairs={{0,1},{1,2},{2,3},{3,4},{4,5},{5,6},{6,7},{7,8},{8,9},{9,10},{10,1... | collective-permute-start | bytes 884744 | tf_op jit(solution)/shard_map/ppermute | solution.py:1028
  17.7 2.2 %collective-permute-start.3 = (f32[12,48,128]{2,1,0:T(8,128)S(1)}, f32[12,48,128]{2,1,0:T(8,128)S(1)}, u32[]{:S(2)}, u32[]{:S(2)}) collective-permute-start(f32[12,48,128]{2,1,0:T(8,128)S(1)} %get-tuple-element.35), channel_id=1, source_target_pairs={{1,0},{2,1},{3,2},{4,3},{5,4},{6,5},{7,6},{8,7},{9,8},{10,9},{11,1... | collective-permute-start | bytes 884744 | tf_op jit(solution)/shard_map/ppermute | solution.py:1028
  20.0 0.1 stack.35.near
  20.1 0.0 copy-done.1
  20.1 0.0 copy-done
  20.1 0.9 shard_map.80.inner
  21.0 0.4 collective-permute-done.2.ylo
  21.4 4.4 %collective-permute-done.3.yhi = f32[12,48,128]{2,1,0:T(8,128)S(1)} collective-permute-done((f32[12,48,128]{2,1,0:T(8,128)S(1)}, f32[12,48,128]{2,1,0:T(8,128)S(1)}, u32[]{:S(2)}, u32[]{:S(2)}) %collective-permute-start.3) | collective-permute-done | bytes 294944 | tf_op jit(solution)/shard_map/ppermute | solution.py:1028
  25.8 2.3 %shard_map.81 = (f32[8,64,128]{2,1,0:T(8,128)S(1)}, f32[64,128]{1,0:T(8,128)S(1)}, f32[64,128]{1,0:T(8,128)S(1)}) custom-call(f32[8]{0:T(128)S(1)} %stack.35.near, f32[632,128]{1,0:T(8,128)S(1)} %copy-done, bf16[1040,384]{1,0:T(8,128)(2,1)S(1)} %copy-done.1, f32[8,32,128]{2,1,0:T(8,128)S(1)} %shard_map.80.inner, f32[8,32,128]{2,1,0:T(8,128)S(1)} %get-tuple-element.30.b, ...), custom_call_target="tpu_custom_call" | custom-call | flops 1000000 | bytes 655360 | tf_op jit(solution)/shard_map/pallas_call | solution.py:1012
  28.1 4.0 %collective-permute-start.4 = (f32[64,128]{1,0:T(8,128)S(1)}, f32[64,128]{1,0:T(8,128)S(1)}, u32[]{:S(2)}, u32[]{:S(2)}) collective-permute-start(f32[64,128]{1,0:T(8,128)S(1)} %get-tuple-element.40), channel_id=1, source_target_pairs={{0,64},{64,128},{128,192},{192,256},{256,320},{320,384},{384,448},... | collective-permute-start | bytes 98312 | tf_op jit(solution)/shard_map/ppermute | solution.py:1028
  32.1 1.3 %collective-permute-start.5 = (f32[64,128]{1,0:T(8,128)S(1)}, f32[64,128]{1,0:T(8,128)S(1)}, u32[]{:S(2)}, u32[]{:S(2)}) collective-permute-start(f32[64,128]{1,0:T(8,128)S(1)} %get-tuple-element.41), channel_id=1, source_target_pairs={{64,0},{128,64},{192,128},{256,192},{320,256},{384,320},{448,384},... | collective-permute-start | bytes 98312 | tf_op jit(solution)/shard_map/ppermute | solution.py:1028
  33.4 1.5 %shard_map.79 = (f32[8,32,128]{2,1,0:T(8,128)}, f32[8,64,128]{2,1,0:T(8,128)S(1)}, f32[1,128]{1,0:T(1,128)S(1)}) custom-call(f32[8]{0:T(128)S(1)} %stack.35.near, f32[8,128]{1,0:T(8,128)S(1)} %get-tuple-element.29.solid, f32[632,128]{1,0:T(8,128)S(1)} %copy-done, f32[8,32,128]{2,1,0:T(8,128)S(1)} %get-tuple-element.30.b, ...), custom_call_target="tpu_custom_call" | custom-call | flops 20000000 | bytes 787456 | tf_op jit(solution)/shard_map/pallas_call | solution.py:1012
  34.9 0.0 collective-permute-done.4.zlo
  34.9 3.7 %collective-permute-done.5.zhi = f32[64,128]{1,0:T(8,128)S(1)} collective-permute-done((f32[64,128]{1,0:T(8,128)S(1)}, f32[64,128]{1,0:T(8,128)S(1)}, u32[]{:S(2)}, u32[]{:S(2)}) %collective-permute-start.5) | collective-permute-done | bytes 32800 | tf_op jit(solution)/shard_map/ppermute | solution.py:1028
  38.6 1.8 %shard_map.82 = (f32[8,64,128]{2,1,0:T(8,128)S(1)}, f32[8,64,128]{2,1,0:T(8,128)S(1)}, f32[8,64,128]{2,1,0:T(8,128)S(1)}, f32[8,64,128]{2,1,0:T(8,128)S(1)}, f32[8,128]{1,0:T(8,128)S(1)}) custom-call(f32[8]{0:T(128)S(1)} %stack.35.near, f32[632,128]{1,0:T(8,128)S(1)} %copy-done, f32[1,128]{1,0:T(1,128)S(1)} %get-tuple-element.38.stat_in, ...), custom_call_target="tpu_custom_call" | custom-call | flops 1000000 | bytes 2105344 | tf_op jit(solution)/shard_map/pallas_call | solution.py:1012
  40.4 4.9 %collective-permute-start.6 = (f32[8,64,128]{2,1,0:T(8,128)S(1)}, f32[8,64,128]{2,1,0:T(8,128)S(1)}, u32[]{:S(2)}, u32[]{:S(2)}) collective-permute-start(f32[8,64,128]{2,1,0:T(8,128)S(1)} %get-tuple-element.45), channel_id=1, source_target_pairs={{0,64},{64,128},{128,192},{192,256},{256,320},{320,384},{384,448},... | collective-permute-start | bytes 786440 | tf_op jit(solution)/shard_map/ppermute | solution.py:1028
  45.3 1.3 %collective-permute-start.7 = (f32[8,64,128]{2,1,0:T(8,128)S(1)}, f32[8,64,128]{2,1,0:T(8,128)S(1)}, u32[]{:S(2)}, u32[]{:S(2)}) collective-permute-start(f32[8,64,128]{2,1,0:T(8,128)S(1)} %get-tuple-element.46), channel_id=1, source_target_pairs={{64,0},{128,64},{192,128},{256,192},{320,256},{384,320},{448,384},... | collective-permute-start | bytes 786440 | tf_op jit(solution)/shard_map/ppermute | solution.py:1028
  46.6 12.9 %all_to_all.39 = f32[8,1,128]{2,1,0:T(1,128)S(1)} all-to-all(f32[8,1,128]{2,1,0:T(1,128)S(1)} %bitcast.26), channel_id=1, replica_groups=mesh['gx'=8,'gy'=64] {'gx'}, dimensions={0} | all-to-all | bytes 8192 | tf_op jit(solution)/shard_map/all_to_all | solution.py:1094
  59.5 0.3 shard_map.83
  59.8 22.0 %all_to_all.40 = f32[64,1,128]{2,1,0:T(1,128)S(1)} all-to-all(f32[64,1,128]{2,1,0:T(1,128)S(1)} %bitcast.22), channel_id=1, replica_groups=mesh['gx'=8,'gy'=64] {'gy'}, dimensions={0} | all-to-all | bytes 65536 | tf_op jit(solution)/shard_map/all_to_all | solution.py:1096
  81.8 0.0 collective-permute-done.6.ylo
  81.8 0.0 collective-permute-done.7.yhi
  81.8 4.5 %shard_map.84 = (f32[16,128]{1,0:T(8,128)S(1)}, f32[8,32,128]{2,1,0:T(8,128)S(1)}, f32[8,32,128]{2,1,0:T(8,128)S(1)}, f32[8,32,128]{2,1,0:T(8,128)S(1)}, f32[32,128]{1,0:T(8,128)S(1)}, /*index=5*/f32[32,128]{1,0:T(8,128)S(1)}) custom-call(f32[8]{0:T(128)S(1)} %stack.35.near, f32[64,128]{1,0:T(8,128)S(1)} %bitcast.21, f32[632,128]{1,0:T(8,128)S(1)} %copy-done, ...), custom_call_target="tpu_custom_call" | custom-call | flops 1000000 | bytes 868352 | tf_op jit(solution)/shard_map/pallas_call | solution.py:1012
  86.3 2.2 %collective-permute-start.8 = (f32[32,128]{1,0:T(8,128)S(1)}, f32[32,128]{1,0:T(8,128)S(1)}, u32[]{:S(2)}, u32[]{:S(2)}) collective-permute-start(f32[32,128]{1,0:T(8,128)S(1)} %get-tuple-element.52), channel_id=1, source_target_pairs={{0,64},{64,128},{128,192},{192,256},{256,320},{320,384},{384,448},... | collective-permute-start | bytes 49160 | tf_op jit(solution)/shard_map/ppermute | solution.py:1028
  88.5 1.3 %collective-permute-start.9 = (f32[32,128]{1,0:T(8,128)S(1)}, f32[32,128]{1,0:T(8,128)S(1)}, u32[]{:S(2)}, u32[]{:S(2)}) collective-permute-start(f32[32,128]{1,0:T(8,128)S(1)} %get-tuple-element.53), channel_id=1, source_target_pairs={{64,0},{128,64},{192,128},{256,192},{320,256},{384,320},{448,384},... | collective-permute-start | bytes 49160 | tf_op jit(solution)/shard_map/ppermute | solution.py:1028
  89.8 1.1 shard_map.85
  90.9 0.0 collective-permute-done.8.zlo
  90.9 2.1 %collective-permute-done.9.zhi = f32[32,128]{1,0:T(8,128)S(1)} collective-permute-done((f32[32,128]{1,0:T(8,128)S(1)}, f32[32,128]{1,0:T(8,128)S(1)}, u32[]{:S(2)}, u32[]{:S(2)}) %collective-permute-start.9) | collective-permute-done | bytes 16416 | tf_op jit(solution)/shard_map/ppermute | solution.py:1028
  93.0 0.3 shard_map.86
  93.3 12.0 %all_to_all.41 = f32[16,1,128]{2,1,0:T(1,128)S(1)} all-to-all(f32[16,1,128]{2,1,0:T(1,128)S(1)} %bitcast.24), channel_id=1, replica_groups={{0,1,64,65,128,129,192,193,256,257,320,321,384,385,448,449},{2,3,66,67,..., dimensions={0} | all-to-all | bytes 16384 | tf_op jit(solution)/shard_map/all_to_all | solution.py:1123
  105.3 11.6 %all_to_all.42 = f32[32,1,128]{2,1,0:T(1,128)S(1)} all-to-all(f32[32,1,128]{2,1,0:T(1,128)S(1)} %broadcast_in_dim.2), channel_id=1, replica_groups={{0,2,4,6,8,10,12,14,16,18,20,22,24,26,28,30,32,34,36,38,40,42,44,46,48,..., dimensions={0} | all-to-all | bytes 32768 | tf_op jit(solution)/shard_map/all_to_all | solution.py:1125
  116.9 0.8 shard_map.87
  (3 shorter events, 0.1 us)
Async XLA Ops:
  0.6 19.5 %copy-start.1 = (bf16[1040,384]{1,0:T(8,128)(2,1)S(1)}, bf16[1040,384]{1,0:T(8,128)(2,1)}, u32[]{:S(2)}) copy-start(bf16[1040,384]{1,0:T(8,128)(2,1)} %constant.30.clone.tables) | copy-start | bytes 2396164
  2.4 17.7 %copy-start = (f32[632,128]{1,0:T(8,128)S(1)}, f32[632,128]{1,0:T(8,128)}, u32[]{:S(2)}) copy-start(f32[632,128]{1,0:T(8,128)} %constant.29.clone.packed_in.packed) | copy-start | bytes 970756
  2.4 6.3 %collective-permute-start = (f32[3,32,128]{2,1,0:T(8,128)S(1)}, f32[3,32,128]{2,1,0:T(8,128)S(1)}, u32[]{:S(2)}, u32[]{:S(2)}) collective-permute-start(f32[3,32,128]{2,1,0:T(8,128)S(1)} %get-tuple-element.32), channel_id=1, source_target_pairs={{0,64},{64,128},{128,192},{192,256},{256,320},{320,384},{384,448},... | collective-permute-start | bytes 147464 | tf_op jit(solution)/shard_map/ppermute | solution.py:1028
  7.4 5.5 %collective-permute-start.1 = (f32[3,32,128]{2,1,0:T(8,128)S(1)}, f32[3,32,128]{2,1,0:T(8,128)S(1)}, u32[]{:S(2)}, u32[]{:S(2)}) collective-permute-start(f32[3,32,128]{2,1,0:T(8,128)S(1)} %get-tuple-element.33), channel_id=1, source_target_pairs={{64,0},{128,64},{192,128},{256,192},{320,256},{384,320},{448,384},... | collective-permute-start | bytes 147464 | tf_op jit(solution)/shard_map/ppermute | solution.py:1028
  12.9 8.5 %collective-permute-start.2 = (f32[12,48,128]{2,1,0:T(8,128)S(1)}, f32[12,48,128]{2,1,0:T(8,128)S(1)}, u32[]{:S(2)}, u32[]{:S(2)}) collective-permute-start(f32[12,48,128]{2,1,0:T(8,128)S(1)} %get-tuple-element.34), channel_id=1, source_target_pairs={{0,1},{1,2},{2,3},{3,4},{4,5},{5,6},{6,7},{7,8},{8,9},{9,10},{10,1... | collective-permute-start | bytes 884744 | tf_op jit(solution)/shard_map/ppermute | solution.py:1028
  17.7 8.0 %collective-permute-start.3 = (f32[12,48,128]{2,1,0:T(8,128)S(1)}, f32[12,48,128]{2,1,0:T(8,128)S(1)}, u32[]{:S(2)}, u32[]{:S(2)}) collective-permute-start(f32[12,48,128]{2,1,0:T(8,128)S(1)} %get-tuple-element.35), channel_id=1, source_target_pairs={{1,0},{2,1},{3,2},{4,3},{5,4},{6,5},{7,6},{8,7},{9,8},{10,9},{11,1... | collective-permute-start | bytes 884744 | tf_op jit(solution)/shard_map/ppermute | solution.py:1028
  28.1 6.8 %collective-permute-start.4 = (f32[64,128]{1,0:T(8,128)S(1)}, f32[64,128]{1,0:T(8,128)S(1)}, u32[]{:S(2)}, u32[]{:S(2)}) collective-permute-start(f32[64,128]{1,0:T(8,128)S(1)} %get-tuple-element.40), channel_id=1, source_target_pairs={{0,64},{64,128},{128,192},{192,256},{256,320},{320,384},{384,448},... | collective-permute-start | bytes 98312 | tf_op jit(solution)/shard_map/ppermute | solution.py:1028
  32.1 6.5 %collective-permute-start.5 = (f32[64,128]{1,0:T(8,128)S(1)}, f32[64,128]{1,0:T(8,128)S(1)}, u32[]{:S(2)}, u32[]{:S(2)}) collective-permute-start(f32[64,128]{1,0:T(8,128)S(1)} %get-tuple-element.41), channel_id=1, source_target_pairs={{64,0},{128,64},{192,128},{256,192},{320,256},{384,320},{448,384},... | collective-permute-start | bytes 98312 | tf_op jit(solution)/shard_map/ppermute | solution.py:1028
  40.4 41.4 %collective-permute-start.6 = (f32[8,64,128]{2,1,0:T(8,128)S(1)}, f32[8,64,128]{2,1,0:T(8,128)S(1)}, u32[]{:S(2)}, u32[]{:S(2)}) collective-permute-start(f32[8,64,128]{2,1,0:T(8,128)S(1)} %get-tuple-element.45), channel_id=1, source_target_pairs={{0,64},{64,128},{128,192},{192,256},{256,320},{320,384},{384,448},... | collective-permute-start | bytes 786440 | tf_op jit(solution)/shard_map/ppermute | solution.py:1028
  45.3 36.6 %collective-permute-start.7 = (f32[8,64,128]{2,1,0:T(8,128)S(1)}, f32[8,64,128]{2,1,0:T(8,128)S(1)}, u32[]{:S(2)}, u32[]{:S(2)}) collective-permute-start(f32[8,64,128]{2,1,0:T(8,128)S(1)} %get-tuple-element.46), channel_id=1, source_target_pairs={{64,0},{128,64},{192,128},{256,192},{320,256},{384,320},{448,384},... | collective-permute-start | bytes 786440 | tf_op jit(solution)/shard_map/ppermute | solution.py:1028
  86.3 4.6 %collective-permute-start.8 = (f32[32,128]{1,0:T(8,128)S(1)}, f32[32,128]{1,0:T(8,128)S(1)}, u32[]{:S(2)}, u32[]{:S(2)}) collective-permute-start(f32[32,128]{1,0:T(8,128)S(1)} %get-tuple-element.52), channel_id=1, source_target_pairs={{0,64},{64,128},{128,192},{192,256},{256,320},{320,384},{384,448},... | collective-permute-start | bytes 49160 | tf_op jit(solution)/shard_map/ppermute | solution.py:1028
  88.5 4.5 %collective-permute-start.9 = (f32[32,128]{1,0:T(8,128)S(1)}, f32[32,128]{1,0:T(8,128)S(1)}, u32[]{:S(2)}, u32[]{:S(2)}) collective-permute-start(f32[32,128]{1,0:T(8,128)S(1)} %get-tuple-element.53), channel_id=1, source_target_pairs={{64,0},{128,64},{192,128},{256,192},{320,256},{384,320},{448,384},... | collective-permute-start | bytes 49160 | tf_op jit(solution)/shard_map/ppermute | solution.py:1028

commit v17 on v16

--- a/solution.py
+++ b/solution.py
@@ -342,16 +342,7 @@
     return stack(planes)
 
 
-def solve_elements(planes, packed, tables, kind):
-    def table(index):
-        at, rows, width = PLACES[index]
-        return tables[at : at + rows, 0:width]
-
-    fxhh, fxl, bxh, bxl = (table(index) for index in range(4))
-    spectral = left_pairs(table(4 + 2 * kind), along_z(planes, FZ))
-    high, low = parts(jnp.concatenate(spectral, axis=0))
-    wide = dot(jnp.concatenate([high, low], axis=1), fxhh) + dot(high, fxl)
-    step = PLACES[4 + 2 * kind][1]
+def inverse_denominators(packed, step):
     column = packed[AT_EIGEN_Y : AT_EIGEN_Y + step]
     rest = 10 * EX - LANES
     lam = jnp.concatenate(
@@ -361,11 +352,25 @@
         ],
         axis=1,
     )
-    scaled = [
-        wide[step * i : step * (i + 1)]
-        / (SCHWARZ_SCALE * lam + float(SCHWARZ_SCALE * EIGEN[i] + SCHWARZ_SHIFT))
-        for i in range(10)
-    ]
+    shifts = [float(SCHWARZ_SCALE * value + SCHWARZ_SHIFT) for value in EIGEN]
+    return [1.0 / (SCHWARZ_SCALE * lam + shift) for shift in shifts]
+
+
+def solve_elements(planes, packed, tables, kind, inverse=None):
+    def table(index):
+        at, rows, width = PLACES[index]
+        return tables[at : at + rows, 0:width]
+
+    fxhh, fxl, bxh, bxl = (table(index) for index in range(4))
+    spectral = left_pairs(table(4 + 2 * kind), along_z(planes, FZ))
+    high, low = parts(jnp.concatenate(spectral, axis=0))
+    wide = dot(jnp.concatenate([high, low], axis=1), fxhh) + dot(high, fxl)
+    step = PLACES[4 + 2 * kind][1]
+    if inverse is None:
+        scales = inverse_denominators(packed, step)
+    else:
+        scales = [inverse[STEP_A * i : STEP_A * i + step] for i in range(10)]
+    scaled = [wide[step * i : step * (i + 1)] * scales[i] for i in range(10)]
     high, low = parts(jnp.concatenate(scaled, axis=0))
     back = dot(high, bxh) + dot(low, bxh) + dot(high, bxl)
     back = left_pairs(table(5 + 2 * kind), [back[step * i : step * (i + 1)] for i in range(10)])
@@ -557,21 +562,23 @@
     stat[...] = lane_row(entries)
 
 
-def inner_schwarz_kernel(packed, tables, b, zlo, zhi, out_ref):
+def inner_schwarz_kernel(packed, tables, b, zlo, zhi, out_ref, inverse):
     planes = [b[i] for i in range(8)] + [zlo[0], zlo[1], zhi[0], zhi[1]]
+    for i, scale in enumerate(inverse_denominators(packed, STEP_A)):
+        inverse[STEP_A * i : STEP_A * (i + 1)] = scale
     planes = solve_elements(planes, packed, tables, 2)
     for i in range(8):
         out_ref[i] = planes[i]
 
 
 def first_schwarz_kernel(
-    near, packed, tables, inner, b, zlo, zhi, ylo, yhi, w_ref, wlo, whi
+    near, inverse, packed, tables, inner, b, zlo, zhi, ylo, yhi, w_ref, wlo, whi
 ):
     own = [b[i] for i in range(8)] + [zlo[0], zlo[1], zhi[0], zhi[1]]
     planes = [
         jnp.concatenate([ylo[i, 0:TILE_B], own[i], yhi[i, 0:TILE_B]], axis=0) for i in range(12)
     ]
-    planes = solve_elements(planes, packed, tables, 0)
+    planes = solve_elements(planes, packed, tables, 0, inverse)
     row, has_low, has_high = ring_rows(near)
     in_grid = jnp.where(row < RING, has_low, jnp.where(row >= RING + ROWS, has_high, 1.0))
     in_grid = jnp.where(row == RING, has_low, jnp.where(row == RING + ROWS - 1, has_high, in_grid))
@@ -900,7 +907,7 @@
 
 
 def apply_kernel(
-    near, packed, tables, coarse, flux, zl, yl, ylo, yhi,
+    near, inverse, packed, tables, coarse, flux, zl, yl, ylo, yhi,
     z_ref, y_ref, w_ref, wlo, whi,
 ):
     columns = coarse_columns(near, coarse, 0, 5)
@@ -914,7 +921,7 @@
     planes = [applied[i] for i in range(8)]
     planes += face_applied(lower, ylo, packed, (6, 7), 2.0 - 2.0 * near[0])
     planes += face_applied(upper, yhi, packed, (0, 1), 2.0 - 2.0 * near[1])
-    planes = solve_elements(planes, packed, tables, 1)
+    planes = solve_elements(planes, packed, tables, 1, inverse)
     row = lax.broadcasted_iota(jnp.int32, (ROWS, LANES), 0)
     _, has_low, has_high = ring_rows(near)
     in_grid = jnp.where(row == 0, has_low, jnp.where(row == ROWS - 1, has_high, 1.0))
@@ -927,12 +934,13 @@
 
 
 def solve_apply_kernel(
-    count, near, gathered, packed, tables, flux, zl, yl, ylo, yhi,
+    count, near, gathered, inverse, packed, tables, flux, zl, yl, ylo, yhi,
     coarse, z_ref, y_ref, w_ref, wlo, whi, wide, turned,
 ):
     coarse_kernel(count, near, gathered, coarse, wide, turned)
     apply_kernel(
-        near, packed, tables, coarse, flux, zl, yl, ylo, yhi, z_ref, y_ref, w_ref, wlo, whi
+        near, inverse, packed, tables, coarse, flux, zl, yl, ylo, yhi,
+        z_ref, y_ref, w_ref, wlo, whi,
     )
 
 
@@ -1067,14 +1075,14 @@
     zlo, zhi = shift("gx", zlo, zhi)
     ylo, yhi = run(rim_kernel, [rim, rim], [], [solid, b, l, zlo, zhi])
     ylo, yhi = shift("gy", ylo, yhi)
-    (inner,) = run(
-        inner_schwarz_kernel, [block], [], [packed, tables, b, zlo, zhi], flops=20000000
+    inner, inverse = run(
+        inner_schwarz_kernel, [block, (10 * STEP_A, 10 * EX)], [], [packed, tables, b, zlo, zhi], flops=20000000
     )
     w, wlo, whi = run(
         first_schwarz_kernel,
         [wide_block, wide_face, wide_face],
         [near],
-        [packed, tables, inner, b, zlo, zhi, ylo, yhi],
+        [inverse, packed, tables, inner, b, zlo, zhi, ylo, yhi],
     )
     wlo, whi = shift("gx", wlo, whi)
     level_new, flux, stat = run(
@@ -1098,7 +1106,7 @@
         functools.partial(solve_apply_kernel, count_gy),
         [(16, LANES), block, block, block, face, face],
         [near],
-        [gathered, packed, tables, flux, zl, yl, zlo, zhi],
+        [gathered, inverse, packed, tables, flux, zl, yl, zlo, zhi],
         [VMEM((LANES, LANES), F32), VMEM((LANES, LANES), F32)],
     )
     zlo, zhi = shift("gx", wlo, whi)

time: 118 us -> 118 us (level)
  no operation moved by 1% of the time
where the time goes in v17:
time: 118 us
  blocking collectives  58.5 us (50%)
  starting transfers between devices  28.2 us (24%)
  Pallas kernels  15.2 us (13%)
  waiting for transfers between devices  14.7 us (12%)
    all_to_all x1, blocking collectives, body(): gathered = lax.all_to_all(column, 'gy', 0, 0, tiled=True)  22 us
    ppermute x5, starting transfers between devices, shift(): lax.ppermute(high_face, axis, forward)  20.8 us
    pallas_call x11, Pallas kernels, run(): pl.pallas_call(kernel, out_shape=[jax.ShapeDtypeStruct(out, F32) for out...  15.2 us
    ppermute x5, waiting for transfers between devices, shift(): lax.ppermute(low_face, axis, backward)  14.3 us
    all_to_all x1, blocking collectives, body(): gathered = lax.all_to_all(stat, 'gx', 0, 0, tiled=True)  12.9 us
    all_to_all x1, blocking collectives, body(): lax.all_to_all(sums, axes, 0, 0, axis_index_groups=columns, tiled=True)  12 us
    all_to_all x1, blocking collectives, body(): lax.all_to_all(wide, axes, 0, 0, axis_index_groups=layers, tiled=True)  11.6 us
    ppermute x5, starting transfers between devices, shift(): lax.ppermute(low_face, axis, backward)  7.41 us
  transfers between devices with their start and end apart: 10, of which 5 were waited for; matrix products, arithmetic and copies ran while one was open for 0% of the time, Pallas kernels for 3%

profile of v17, /device:TPU:1, one launch (start us, length us, event | category | flops | bytes accessed | tf_op | source)
XLA Modules:
  0.0 117.7 jit_solution(10524159684532487381)
XLA Ops:
  0.6 0.0 copy-start.1
  0.6 1.8 %shard_map.77 = (f32[8,32,128]{2,1,0:T(8,128)S(1)}, f32[8,32,128]{2,1,0:T(8,128)S(1)}, f32[3,32,128]{2,1,0:T(8,128)S(1)}, f32[3,32,128]{2,1,0:T(8,128)S(1)}, f32[8,128]{1,0:T(8,128)S(1)}) custom-call(f32[8,32,128]{2,1,0:T(8,128)} %lev_in.1, f32[3,8,32,128]{3,2,1,0:T(8,128)} %vel_in.1, f32[8,32,128]{2,1,0:T(8,128)} %src_in.1, ...), custom_call_target="tpu_custom_call" | custom-call | flops 1000000 | bytes 729088 | tf_op jit(solution)/shard_map/pallas_call | solution.py:1020
  2.4 0.0 copy-start
  2.4 5.0 %collective-permute-start = (f32[3,32,128]{2,1,0:T(8,128)S(1)}, f32[3,32,128]{2,1,0:T(8,128)S(1)}, u32[]{:S(2)}, u32[]{:S(2)}) collective-permute-start(f32[3,32,128]{2,1,0:T(8,128)S(1)} %get-tuple-element.34), channel_id=1, source_target_pairs={{0,64},{64,128},{128,192},{192,256},{256,320},{320,384},{384,448},... | collective-permute-start | bytes 147464 | tf_op jit(solution)/shard_map/ppermute | solution.py:1036
  7.4 1.3 %collective-permute-start.1 = (f32[3,32,128]{2,1,0:T(8,128)S(1)}, f32[3,32,128]{2,1,0:T(8,128)S(1)}, u32[]{:S(2)}, u32[]{:S(2)}) collective-permute-start(f32[3,32,128]{2,1,0:T(8,128)S(1)} %get-tuple-element.35), channel_id=1, source_target_pairs={{64,0},{128,64},{192,128},{256,192},{320,256},{384,320},{448,384},... | collective-permute-start | bytes 147464 | tf_op jit(solution)/shard_map/ppermute | solution.py:1036
  8.7 0.0 collective-permute-done.low_z.zlo
  8.7 4.2 %collective-permute-done.1.high_z.zhi = f32[3,32,128]{2,1,0:T(8,128)S(1)} collective-permute-done((f32[3,32,128]{2,1,0:T(8,128)S(1)}, f32[3,32,128]{2,1,0:T(8,128)S(1)}, u32[]{:S(2)}, u32[]{:S(2)}) %collective-permute-start.1) | collective-permute-done | bytes 49184 | tf_op jit(solution)/shard_map/ppermute | solution.py:1036
  12.9 4.8 %collective-permute-start.2 = (f32[12,48,128]{2,1,0:T(8,128)S(1)}, f32[12,48,128]{2,1,0:T(8,128)S(1)}, u32[]{:S(2)}, u32[]{:S(2)}) collective-permute-start(f32[12,48,128]{2,1,0:T(8,128)S(1)} %get-tuple-element.36), channel_id=1, source_target_pairs={{0,1},{1,2},{2,3},{3,4},{4,5},{5,6},{6,7},{7,8},{8,9},{9,10},{10,1... | collective-permute-start | bytes 884744 | tf_op jit(solution)/shard_map/ppermute | solution.py:1036
  17.7 2.2 %collective-permute-start.3 = (f32[12,48,128]{2,1,0:T(8,128)S(1)}, f32[12,48,128]{2,1,0:T(8,128)S(1)}, u32[]{:S(2)}, u32[]{:S(2)}) collective-permute-start(f32[12,48,128]{2,1,0:T(8,128)S(1)} %get-tuple-element.37), channel_id=1, source_target_pairs={{1,0},{2,1},{3,2},{4,3},{5,4},{6,5},{7,6},{8,7},{9,8},{10,9},{11,1... | collective-permute-start | bytes 884744 | tf_op jit(solution)/shard_map/ppermute | solution.py:1036
  20.0 0.1 stack.35.near
  20.1 0.0 copy-done.1
  20.1 0.0 copy-done
  20.1 0.9 shard_map.80
  21.0 0.3 collective-permute-done.2.ylo
  21.4 4.4 %collective-permute-done.3.yhi = f32[12,48,128]{2,1,0:T(8,128)S(1)} collective-permute-done((f32[12,48,128]{2,1,0:T(8,128)S(1)}, f32[12,48,128]{2,1,0:T(8,128)S(1)}, u32[]{:S(2)}, u32[]{:S(2)}) %collective-permute-start.3) | collective-permute-done | bytes 294944 | tf_op jit(solution)/shard_map/ppermute | solution.py:1036
  25.8 2.3 %shard_map.81 = (f32[8,64,128]{2,1,0:T(8,128)S(1)}, f32[64,128]{1,0:T(8,128)S(1)}, f32[64,128]{1,0:T(8,128)S(1)}) custom-call(f32[8]{0:T(128)S(1)} %stack.35.near, f32[800,160]{1,0:T(8,128)S(1)} %get-tuple-element.41.inverse, f32[632,128]{1,0:T(8,128)S(1)} %copy-done, bf16[1040,384]{1,0:T(8,128)(2,1)S(1)} %copy-done.1, ...), custom_call_target="tpu_custom_call" | custom-call | flops 1000000 | bytes 655360 | tf_op jit(solution)/shard_map/pallas_call | solution.py:1020
  28.1 4.0 %collective-permute-start.4 = (f32[64,128]{1,0:T(8,128)S(1)}, f32[64,128]{1,0:T(8,128)S(1)}, u32[]{:S(2)}, u32[]{:S(2)}) collective-permute-start(f32[64,128]{1,0:T(8,128)S(1)} %get-tuple-element.44), channel_id=1, source_target_pairs={{0,64},{64,128},{128,192},{192,256},{256,320},{320,384},{384,448},... | collective-permute-start | bytes 98312 | tf_op jit(solution)/shard_map/ppermute | solution.py:1036
  32.1 1.3 %collective-permute-start.5 = (f32[64,128]{1,0:T(8,128)S(1)}, f32[64,128]{1,0:T(8,128)S(1)}, u32[]{:S(2)}, u32[]{:S(2)}) collective-permute-start(f32[64,128]{1,0:T(8,128)S(1)} %get-tuple-element.45), channel_id=1, source_target_pairs={{64,0},{128,64},{192,128},{256,192},{320,256},{384,320},{448,384},... | collective-permute-start | bytes 98312 | tf_op jit(solution)/shard_map/ppermute | solution.py:1036
  33.4 1.5 %shard_map.79 = (f32[8,32,128]{2,1,0:T(8,128)}, f32[8,64,128]{2,1,0:T(8,128)S(1)}, f32[1,128]{1,0:T(1,128)S(1)}) custom-call(f32[8]{0:T(128)S(1)} %stack.35.near, f32[8,128]{1,0:T(8,128)S(1)} %get-tuple-element.31.solid, f32[632,128]{1,0:T(8,128)S(1)} %copy-done, f32[8,32,128]{2,1,0:T(8,128)S(1)} %get-tuple-element.32.b, ...), custom_call_target="tpu_custom_call" | custom-call | flops 20000000 | bytes 787456 | tf_op jit(solution)/shard_map/pallas_call | solution.py:1020
  34.9 0.0 collective-permute-done.4.zlo
  34.9 3.7 %collective-permute-done.5.zhi = f32[64,128]{1,0:T(8,128)S(1)} collective-permute-done((f32[64,128]{1,0:T(8,128)S(1)}, f32[64,128]{1,0:T(8,128)S(1)}, u32[]{:S(2)}, u32[]{:S(2)}) %collective-permute-start.5) | collective-permute-done | bytes 32800 | tf_op jit(solution)/shard_map/ppermute | solution.py:1036
  38.6 1.8 %shard_map.82 = (f32[8,64,128]{2,1,0:T(8,128)S(1)}, f32[8,64,128]{2,1,0:T(8,128)S(1)}, f32[8,64,128]{2,1,0:T(8,128)S(1)}, f32[8,64,128]{2,1,0:T(8,128)S(1)}, f32[8,128]{1,0:T(8,128)S(1)}) custom-call(f32[8]{0:T(128)S(1)} %stack.35.near, f32[632,128]{1,0:T(8,128)S(1)} %copy-done, f32[1,128]{1,0:T(1,128)S(1)} %get-tuple-element.40.stat_in, ...), custom_call_target="tpu_custom_call" | custom-call | flops 1000000 | bytes 2105344 | tf_op jit(solution)/shard_map/pallas_call | solution.py:1020
  40.4 4.9 %collective-permute-start.6 = (f32[8,64,128]{2,1,0:T(8,128)S(1)}, f32[8,64,128]{2,1,0:T(8,128)S(1)}, u32[]{:S(2)}, u32[]{:S(2)}) collective-permute-start(f32[8,64,128]{2,1,0:T(8,128)S(1)} %get-tuple-element.49), channel_id=1, source_target_pairs={{0,64},{64,128},{128,192},{192,256},{256,320},{320,384},{384,448},... | collective-permute-start | bytes 786440 | tf_op jit(solution)/shard_map/ppermute | solution.py:1036
  45.3 1.3 %collective-permute-start.7 = (f32[8,64,128]{2,1,0:T(8,128)S(1)}, f32[8,64,128]{2,1,0:T(8,128)S(1)}, u32[]{:S(2)}, u32[]{:S(2)}) collective-permute-start(f32[8,64,128]{2,1,0:T(8,128)S(1)} %get-tuple-element.50), channel_id=1, source_target_pairs={{64,0},{128,64},{192,128},{256,192},{320,256},{384,320},{448,384},... | collective-permute-start | bytes 786440 | tf_op jit(solution)/shard_map/ppermute | solution.py:1036
  46.6 12.9 %all_to_all.39 = f32[8,1,128]{2,1,0:T(1,128)S(1)} all-to-all(f32[8,1,128]{2,1,0:T(1,128)S(1)} %bitcast.26), channel_id=1, replica_groups=mesh['gx'=8,'gy'=64] {'gx'}, dimensions={0} | all-to-all | bytes 8192 | tf_op jit(solution)/shard_map/all_to_all | solution.py:1102
  59.5 0.3 shard_map.83
  59.8 22.0 %all_to_all.40 = f32[64,1,128]{2,1,0:T(1,128)S(1)} all-to-all(f32[64,1,128]{2,1,0:T(1,128)S(1)} %bitcast.22), channel_id=1, replica_groups=mesh['gx'=8,'gy'=64] {'gy'}, dimensions={0} | all-to-all | bytes 65536 | tf_op jit(solution)/shard_map/all_to_all | solution.py:1104
  81.8 0.0 collective-permute-done.6.ylo
  81.8 0.0 collective-permute-done.7.yhi
  81.8 4.5 %shard_map.84 = (f32[16,128]{1,0:T(8,128)S(1)}, f32[8,32,128]{2,1,0:T(8,128)S(1)}, f32[8,32,128]{2,1,0:T(8,128)S(1)}, f32[8,32,128]{2,1,0:T(8,128)S(1)}, f32[32,128]{1,0:T(8,128)S(1)}, /*index=5*/f32[32,128]{1,0:T(8,128)S(1)}) custom-call(f32[8]{0:T(128)S(1)} %stack.35.near, f32[64,128]{1,0:T(8,128)S(1)} %bitcast.21, ...), custom_call_target="tpu_custom_call" | custom-call | flops 1000000 | bytes 868352 | tf_op jit(solution)/shard_map/pallas_call | solution.py:1020
  86.3 2.2 %collective-permute-start.8 = (f32[32,128]{1,0:T(8,128)S(1)}, f32[32,128]{1,0:T(8,128)S(1)}, u32[]{:S(2)}, u32[]{:S(2)}) collective-permute-start(f32[32,128]{1,0:T(8,128)S(1)} %get-tuple-element.56), channel_id=1, source_target_pairs={{0,64},{64,128},{128,192},{192,256},{256,320},{320,384},{384,448},... | collective-permute-start | bytes 49160 | tf_op jit(solution)/shard_map/ppermute | solution.py:1036
  88.5 1.3 %collective-permute-start.9 = (f32[32,128]{1,0:T(8,128)S(1)}, f32[32,128]{1,0:T(8,128)S(1)}, u32[]{:S(2)}, u32[]{:S(2)}) collective-permute-start(f32[32,128]{1,0:T(8,128)S(1)} %get-tuple-element.57), channel_id=1, source_target_pairs={{64,0},{128,64},{192,128},{256,192},{320,256},{384,320},{448,384},... | collective-permute-start | bytes 49160 | tf_op jit(solution)/shard_map/ppermute | solution.py:1036
  89.8 1.1 shard_map.85
  90.9 0.0 collective-permute-done.8.zlo
  90.9 2.1 %collective-permute-done.9.zhi = f32[32,128]{1,0:T(8,128)S(1)} collective-permute-done((f32[32,128]{1,0:T(8,128)S(1)}, f32[32,128]{1,0:T(8,128)S(1)}, u32[]{:S(2)}, u32[]{:S(2)}) %collective-permute-start.9) | collective-permute-done | bytes 16416 | tf_op jit(solution)/shard_map/ppermute | solution.py:1036
  93.0 0.3 shard_map.86
  93.3 12.0 %all_to_all.41 = f32[16,1,128]{2,1,0:T(1,128)S(1)} all-to-all(f32[16,1,128]{2,1,0:T(1,128)S(1)} %bitcast.24), channel_id=1, replica_groups={{0,1,64,65,128,129,192,193,256,257,320,321,384,385,448,449},{2,3,66,67,..., dimensions={0} | all-to-all | bytes 16384 | tf_op jit(solution)/shard_map/all_to_all | solution.py:1131
  105.3 11.6 %all_to_all.42 = f32[32,1,128]{2,1,0:T(1,128)S(1)} all-to-all(f32[32,1,128]{2,1,0:T(1,128)S(1)} %broadcast_in_dim.2), channel_id=1, replica_groups={{0,2,4,6,8,10,12,14,16,18,20,22,24,26,28,30,32,34,36,38,40,42,44,46,48,..., dimensions={0} | all-to-all | bytes 32768 | tf_op jit(solution)/shard_map/all_to_all | solution.py:1133
  116.9 0.8 shard_map.87
  (3 shorter events, 0.1 us)
Async XLA Ops:
  0.6 19.5 %copy-start.1 = (bf16[1040,384]{1,0:T(8,128)(2,1)S(1)}, bf16[1040,384]{1,0:T(8,128)(2,1)}, u32[]{:S(2)}) copy-start(bf16[1040,384]{1,0:T(8,128)(2,1)} %constant.30.clone.tables) | copy-start | bytes 2396164
  2.4 17.7 %copy-start = (f32[632,128]{1,0:T(8,128)S(1)}, f32[632,128]{1,0:T(8,128)}, u32[]{:S(2)}) copy-start(f32[632,128]{1,0:T(8,128)} %constant.29.clone.packed_in.packed) | copy-start | bytes 970756
  2.4 6.3 %collective-permute-start = (f32[3,32,128]{2,1,0:T(8,128)S(1)}, f32[3,32,128]{2,1,0:T(8,128)S(1)}, u32[]{:S(2)}, u32[]{:S(2)}) collective-permute-start(f32[3,32,128]{2,1,0:T(8,128)S(1)} %get-tuple-element.34), channel_id=1, source_target_pairs={{0,64},{64,128},{128,192},{192,256},{256,320},{320,384},{384,448},... | collective-permute-start | bytes 147464 | tf_op jit(solution)/shard_map/ppermute | solution.py:1036
  7.4 5.5 %collective-permute-start.1 = (f32[3,32,128]{2,1,0:T(8,128)S(1)}, f32[3,32,128]{2,1,0:T(8,128)S(1)}, u32[]{:S(2)}, u32[]{:S(2)}) collective-permute-start(f32[3,32,128]{2,1,0:T(8,128)S(1)} %get-tuple-element.35), channel_id=1, source_target_pairs={{64,0},{128,64},{192,128},{256,192},{320,256},{384,320},{448,384},... | collective-permute-start | bytes 147464 | tf_op jit(solution)/shard_map/ppermute | solution.py:1036
  12.9 8.5 %collective-permute-start.2 = (f32[12,48,128]{2,1,0:T(8,128)S(1)}, f32[12,48,128]{2,1,0:T(8,128)S(1)}, u32[]{:S(2)}, u32[]{:S(2)}) collective-permute-start(f32[12,48,128]{2,1,0:T(8,128)S(1)} %get-tuple-element.36), channel_id=1, source_target_pairs={{0,1},{1,2},{2,3},{3,4},{4,5},{5,6},{6,7},{7,8},{8,9},{9,10},{10,1... | collective-permute-start | bytes 884744 | tf_op jit(solution)/shard_map/ppermute | solution.py:1036
  17.7 8.0 %collective-permute-start.3 = (f32[12,48,128]{2,1,0:T(8,128)S(1)}, f32[12,48,128]{2,1,0:T(8,128)S(1)}, u32[]{:S(2)}, u32[]{:S(2)}) collective-permute-start(f32[12,48,128]{2,1,0:T(8,128)S(1)} %get-tuple-element.37), channel_id=1, source_target_pairs={{1,0},{2,1},{3,2},{4,3},{5,4},{6,5},{7,6},{8,7},{9,8},{10,9},{11,1... | collective-permute-start | bytes 884744 | tf_op jit(solution)/shard_map/ppermute | solution.py:1036
  28.1 6.8 %collective-permute-start.4 = (f32[64,128]{1,0:T(8,128)S(1)}, f32[64,128]{1,0:T(8,128)S(1)}, u32[]{:S(2)}, u32[]{:S(2)}) collective-permute-start(f32[64,128]{1,0:T(8,128)S(1)} %get-tuple-element.44), channel_id=1, source_target_pairs={{0,64},{64,128},{128,192},{192,256},{256,320},{320,384},{384,448},... | collective-permute-start | bytes 98312 | tf_op jit(solution)/shard_map/ppermute | solution.py:1036
  32.1 6.5 %collective-permute-start.5 = (f32[64,128]{1,0:T(8,128)S(1)}, f32[64,128]{1,0:T(8,128)S(1)}, u32[]{:S(2)}, u32[]{:S(2)}) collective-permute-start(f32[64,128]{1,0:T(8,128)S(1)} %get-tuple-element.45), channel_id=1, source_target_pairs={{64,0},{128,64},{192,128},{256,192},{320,256},{384,320},{448,384},... | collective-permute-start | bytes 98312 | tf_op jit(solution)/shard_map/ppermute | solution.py:1036
  40.4 41.4 %collective-permute-start.6 = (f32[8,64,128]{2,1,0:T(8,128)S(1)}, f32[8,64,128]{2,1,0:T(8,128)S(1)}, u32[]{:S(2)}, u32[]{:S(2)}) collective-permute-start(f32[8,64,128]{2,1,0:T(8,128)S(1)} %get-tuple-element.49), channel_id=1, source_target_pairs={{0,64},{64,128},{128,192},{192,256},{256,320},{320,384},{384,448},... | collective-permute-start | bytes 786440 | tf_op jit(solution)/shard_map/ppermute | solution.py:1036
  45.3 36.6 %collective-permute-start.7 = (f32[8,64,128]{2,1,0:T(8,128)S(1)}, f32[8,64,128]{2,1,0:T(8,128)S(1)}, u32[]{:S(2)}, u32[]{:S(2)}) collective-permute-start(f32[8,64,128]{2,1,0:T(8,128)S(1)} %get-tuple-element.50), channel_id=1, source_target_pairs={{64,0},{128,64},{192,128},{256,192},{320,256},{384,320},{448,384},... | collective-permute-start | bytes 786440 | tf_op jit(solution)/shard_map/ppermute | solution.py:1036
  86.3 4.6 %collective-permute-start.8 = (f32[32,128]{1,0:T(8,128)S(1)}, f32[32,128]{1,0:T(8,128)S(1)}, u32[]{:S(2)}, u32[]{:S(2)}) collective-permute-start(f32[32,128]{1,0:T(8,128)S(1)} %get-tuple-element.56), channel_id=1, source_target_pairs={{0,64},{64,128},{128,192},{192,256},{256,320},{320,384},{384,448},... | collective-permute-start | bytes 49160 | tf_op jit(solution)/shard_map/ppermute | solution.py:1036
  88.5 4.5 %collective-permute-start.9 = (f32[32,128]{1,0:T(8,128)S(1)}, f32[32,128]{1,0:T(8,128)S(1)}, u32[]{:S(2)}, u32[]{:S(2)}) collective-permute-start(f32[32,128]{1,0:T(8,128)S(1)} %get-tuple-element.57), channel_id=1, source_target_pairs={{64,0},{128,64},{192,128},{256,192},{320,256},{384,320},{448,384},... | collective-permute-start | bytes 49160 | tf_op jit(solution)/shard_map/ppermute | solution.py:1036
